TPU v7x, 256 devices: a whole 4x4x8 slice. The times are simulated.
256 devices in a mesh: slab: 16 (over x, y_lo, core), tile: 16 (over z, y_hi).
Axes of the slice: x: 4, y: 4 (y_hi: 2, y_lo: 2; y = y_hi * 2 + y_lo), z: 8, core: 2. Of those that a mesh axis runs over, the one named last changes fastest.
Arguments:
- volume: bfloat16 [128, 2048, 2048], P('slab', None, 'tile'), may hold values from -6 to 6
- measured: bfloat16 [2, 192, 8, 2048], P(None, 'slab', None, 'tile'), may hold values from -6 to 6
- ray_weight: bfloat16 [2, 192, 2048], P(None, 'slab', 'tile'), may hold values from -0.75 to 0.75
- view_owner: int32 [2, 192, 1], P(None, 'slab'), may hold values from 0 to 15; in each aligned block of 12 rows (0 to 11, 12 to 23, ..., all dimensions but the last counted through in order) at most 2 rows name the same one
- band_offset: int32 [2, 192], P(None, 'slab'), may hold values from 0 to 127, as said below
- band_width: int32 [2, 192], P(None, 'slab'), may hold values from 1 to 64
- beta: float32 [1], replicated, may hold values from 0.3 to 1
Outputs:
- gradient: bfloat16 [128, 2048, 2048], P('slab', None, 'tile')
Inputs may be any that keep to these rules, and one draw needn't show every extreme that they name: `view_owner`: among the views of one batch acquired on one slab (aligned blocks of 12 views), no slab is named more than 2 times. band_offset + band_width <= 128 for every view.
All inputs are finite; a program needn't handle non-finite values.
Results may differ from a plain program's by a relative error of at most 0.0053.
Values may be sent and summed in bfloat16 or wider, within the bound.
No kernel may reach another device: no remote copies, remote signals or barrier semaphores. Data moves between devices by JAX's collectives and lax.ppermute only.
A program may use at most 128 MiB of HBM per device.

v0:
```python
import jax
import jax.numpy as jnp
from jax import lax
from jax.sharding import PartitionSpec as P

NY = 2048
BAND = 128
BATCHES = 2
CAPP = 2


def extended(cells, sides, width):
    for axis, dim in sides:
        count = lax.axis_size(axis)
        ends = count - 1
        head = lax.slice_in_dim(cells, 0, width, axis=dim)
        tail = lax.slice_in_dim(cells, cells.shape[dim] - width, cells.shape[dim], axis=dim)
        cells = jnp.concatenate(
            [
                lax.ppermute(tail, axis, [(i, (i + 1) % count) for i in range(ends)]),
                cells,
                lax.ppermute(head, axis, [((i + 1) % count, i) for i in range(ends)]),
            ],
            axis=dim,
        )
    return cells


def penalty(diff):
    return diff / jnp.sqrt(1.0 + diff * diff)


def band_matrices(offsets, widths):
    column = jnp.arange(2 * BAND, dtype=jnp.int32)[None, :, None]
    channel = jnp.arange(BAND, dtype=jnp.int32)[None, None, :]
    delta = channel + BAND - column - offsets[:, None, None]
    inside = (delta >= 0) & (delta < widths[:, None, None])
    recip = (1.0 / widths.astype(jnp.float32)).astype(jnp.bfloat16)
    return jnp.where(inside, recip[:, None, None], jnp.zeros((), jnp.bfloat16))


def forward_band(rows, mats):
    count, depth, extent = rows.shape
    blocks = rows.reshape(count, depth, extent // BAND, BAND)
    before = jnp.concatenate([jnp.zeros_like(blocks[:, :, :1]), blocks[:, :, :-1]], axis=2)
    paired = jnp.concatenate([before, blocks], axis=3)
    out = jnp.einsum(
        "jznc,jcd->jznd", paired, mats, preferred_element_type=jnp.float32, precision=None
    )
    return out.reshape(count, depth, extent)


def backward_band(rows, mats):
    count, depth, extent = rows.shape
    blocks = rows.reshape(count, depth, extent // BAND, BAND)
    spread = jnp.einsum("jznd,jcd->jznc", blocks, mats, preferred_element_type=jnp.float32)
    later = jnp.concatenate(
        [spread[:, :, 1:, :BAND], jnp.zeros_like(spread[:, :, :1, :BAND])], axis=2
    )
    return (spread[:, :, :, BAND:] + later).reshape(count, depth, extent)


def shards(volume, measured, ray_weight, view_owner, band_offset, band_width, beta):
    slab_count = lax.axis_size("slab")
    depth, extent, strip = volume.shape
    views_here = view_owner.shape[1]
    capacity = slab_count * CAPP
    data = jnp.zeros((depth, extent, strip), jnp.float32)
    for batch in range(BATCHES):
        owners = view_owner[batch, :, 0]
        onehot = (owners[:, None] == jnp.arange(slab_count, dtype=jnp.int32)[None, :]).astype(
            jnp.int32
        )
        ranks = jnp.sum(onehot * (jnp.cumsum(onehot, axis=0) - 1), axis=1)
        slots = owners * CAPP + ranks
        select = (jnp.arange(capacity, dtype=jnp.int32)[:, None] == slots[None, :]).astype(
            jnp.int32
        )
        picker = select.astype(jnp.bfloat16)
        sent_weights = jnp.dot(
            picker, ray_weight[batch], preferred_element_type=jnp.float32
        ).astype(jnp.bfloat16)
        sent_rows = jnp.dot(
            picker, measured[batch].reshape(views_here, -1), preferred_element_type=jnp.float32
        ).astype(jnp.bfloat16)
        filled = jnp.sum(select, axis=1)
        sent_offsets = jnp.sum(select * band_offset[batch][None, :], axis=1)
        sent_widths = jnp.sum(select * band_width[batch][None, :], axis=1) + 1 - filled
        params = jnp.stack([sent_offsets, sent_widths], axis=1).astype(jnp.bfloat16)
        got_weights, got_params, got_rows = (
            lax.all_to_all(
                sent_weights.reshape(slab_count, CAPP, strip),
                "slab",
                split_axis=0,
                concat_axis=0,
                tiled=True,
            ),
            lax.all_to_all(
                params.reshape(slab_count, CAPP, 2), "slab", split_axis=0, concat_axis=0, tiled=True
            ),
            lax.all_to_all(
                sent_rows.reshape(slab_count, CAPP, -1),
                "slab",
                split_axis=0,
                concat_axis=0,
                tiled=True,
            ),
        )
        got_weights = got_weights.reshape(capacity, strip)
        got_params = got_params.reshape(capacity, 2).astype(jnp.int32)
        offsets = got_params[:, 0]
        widths = got_params[:, 1]
        rows_here = got_rows.reshape(capacity, depth, -1)
        partial_value = jnp.einsum(
            "jy,zxy->jzx", got_weights, volume, preferred_element_type=jnp.float32
        ).astype(jnp.bfloat16)
        mats = band_matrices(offsets, widths)
        sums = lax.psum_scatter(
            forward_band(partial_value, mats), "tile", scatter_dimension=2, tiled=True
        )
        residual = (sums - rows_here.astype(jnp.float32)).astype(jnp.bfloat16)
        whole_rows = lax.all_gather(residual, "tile", axis=2, tiled=True)
        images = backward_band(whole_rows, mats).astype(jnp.bfloat16)
        data = data + jnp.einsum(
            "jy,jzx->zxy", got_weights, images, preferred_element_type=jnp.float32
        )
    padded = extended(volume, (("slab", 0), ("tile", 2)), 1).astype(jnp.float32)
    center = padded[1:-1, :, 1:-1]
    slice_index = lax.axis_index("slab") * depth + jnp.arange(depth, dtype=jnp.int32)[:, None, None]
    column_index = (
        lax.axis_index("tile") * strip + jnp.arange(strip, dtype=jnp.int32)[None, None, :]
    )
    total_depth = depth * slab_count
    regular = jnp.where(slice_index > 0, penalty(center - padded[:-2, :, 1:-1]), 0.0)
    regular = regular + jnp.where(
        slice_index < total_depth - 1, penalty(center - padded[2:, :, 1:-1]), 0.0
    )
    regular = regular + jnp.where(column_index > 0, penalty(center - padded[1:-1, :, :-2]), 0.0)
    regular = regular + jnp.where(column_index < NY - 1, penalty(center - padded[1:-1, :, 2:]), 0.0)
    along_x = penalty(jnp.diff(center, axis=1))
    regular = (
        regular
        + jnp.pad(along_x, ((0, 0), (1, 0), (0, 0)))
        - jnp.pad(along_x, ((0, 0), (0, 1), (0, 0)))
    )
    return (data + beta[0] * regular).astype(jnp.bfloat16)


def solution(mesh):
    in_specs = (
        P("slab", None, "tile"),
        P(None, "slab", None, "tile"),
        P(None, "slab", "tile"),
        P(None, "slab", None),
        P(None, "slab"),
        P(None, "slab"),
        P(),
    )
    out_specs = P("slab", None, "tile")
    return jax.shard_map(shards, mesh=mesh, in_specs=in_specs, out_specs=out_specs, check_vma=False)
```

profile of v0, /device:TPU:8, one launch (start us, length us, event | category | flops | bytes accessed | tf_op | source)
XLA Modules:
  0.0 659.8 jit_solution(3916435099906286732)
XLA Ops:
  10.0 5.8 all-to-all-start.1
  17.4 3.0 all-to-all-done.1
  20.4 4.7 all-to-all-start
  25.5 4.3 all-to-all-done
  29.8 3.7 convolution_convert_fusion.1
  37.9 4.7 all-to-all-start.4
  43.4 3.9 all-to-all-done.4
  47.3 4.7 all-to-all-start.3
  52.4 4.4 all-to-all-done.3
  56.7 3.7 convolution_convert_fusion
  65.2 1.9 collective-permute-start
  67.1 3.6 collective-permute-start.1
  71.7 4.8 all-to-all-start.2
  77.5 5.9 all-to-all-done.2
  83.3 4.8 all-to-all-start.5
  89.1 4.5 constant_dynamic-update-slice_fusion.1
  93.6 155.6 %reduce-scatter.3.cloned.1.call-done = f32[32,8,128]{2,1,0:T(8,128)} async-done(((f32[32,8,2048]{2,1,0:T(8,128)}), f32[32,8,128]{2,1,0:T(8,128)}) %reduce-scatter.3.cloned.1.call-update) | async-done | bytes 131088 | tf_op jit(solution)/shard_map/reduce_scatter | solution.py:118
  251.6 9.6 %fusion.67 = (bf16[10,2048,1]{2,1,0:T(8,128)(2,1)}, bf16[10,2048,1]{2,1,0:T(8,128)(2,1)}) fusion(bf16[10,2048,128]{2,1,0:T(8,128)(2,1)} %constant_dynamic-update-slice_fusion), kind=kLoop, calls=%fused_computation.127 | loop fusion | bytes 163840 | tf_op jit(solution)/shard_map/slice | solution.py:17
  261.3 4.8 copy.73
  267.4 4.8 copy.72
  272.2 6.2 collective-permute-start.2
  279.2 3.6 copy.75
  282.8 3.6 copy.74
  286.5 16.3 %maximum_convert_fusion = f32[10,2048,130]{2,1,0:T(8,128)} fusion(bf16[10,2048,1]{2,1,0:T(8,128)(2,1)} %copy.75, bf16[10,2048,128]{2,1,0:T(8,128)(2,1)} %constant_dynamic-update-slice_fusion, bf16[10,2048,1]{2,1,0:T(8,128)(2,1)} %copy.74), kind=kLoop, calls=%fused_computation | loop fusion | flops 15974400 | bytes 15974400 | tf_op jit(solution)/shard_map/convert_element_type | solution.py:127
  302.7 156.1 %reduce-scatter.5.cloned.1.call-done = f32[32,8,128]{2,1,0:T(8,128)} async-done(((f32[32,8,2048]{2,1,0:T(8,128)}), f32[32,8,128]{2,1,0:T(8,128)}) %reduce-scatter.5.cloned.1.call-update) | async-done | bytes 131088 | tf_op jit(solution)/shard_map/reduce_scatter | solution.py:118
  460.4 17.2 %rsqrt_multiply_fusion = f32[8,2047,128]{2,1,0:T(8,128)} fusion(f32[10,2048,130]{2,1,0:T(8,128)} %maximum_convert_fusion), kind=kLoop, calls=%fused_computation.7 | loop fusion | flops 8384512 | bytes 25153536 | tf_op jit(solution)/shard_map/div | solution.py:30
  477.6 57.0 %all-gather.3.cloned.1.call-done = bf16[32,8,2048]{2,1,0:T(8,128)(2,1)} async-done(((bf16[32,8,128]{2,1,0:T(8,128)(2,1)}), bf16[32,8,2048]{2,1,0:T(8,128)(2,1)}) %all-gather.3.cloned.1.call-update) | async-done | bytes 1048592 | tf_op jit(solution)/shard_map/all_gather | solution.py:122
  534.6 2.2 fusion.22
  537.9 4.7 fusion.35
  542.7 66.0 %all-gather.5.cloned.1.call-done = bf16[32,8,2048]{2,1,0:T(8,128)(2,1)} async-done(((bf16[32,8,128]{2,1,0:T(8,128)(2,1)}), bf16[32,8,2048]{2,1,0:T(8,128)(2,1)}) %all-gather.5.cloned.1.call-update) | async-done | bytes 1048592 | tf_op jit(solution)/shard_map/all_gather | solution.py:122
  608.7 2.2 fusion.25
  612.0 41.2 %add_convert_fusion = bf16[8,2048,128]{2,1,0:T(8,128)(2,1)} fusion(f32[8,2047,128]{2,1,0:T(8,128)} %rsqrt_multiply_fusion, f32[10,2048,130]{2,1,0:T(8,128)} %maximum_convert_fusion, f32[8,2048,128]{2,1,0:T(8,128)} %fusion.35, bf16[32,128,1]{1,0,2:T(8,128)(2,1)S(1)} %bitcast.127, f32[]{:T(128)} %bitcast.111, pred[8]{0:T(512)(128)(4,1)S(1)} %get-tuple-element.35, ...), kind=kOutput, calls=%fused_computation.6 | convolution fusion | flops 195035136 | bytes 63967508 | tf_op jit(solution)/shard_map/jy,jzx->zxy/dot_general | solution.py:124
  (87 shorter events, 25.8 us)
Async XLA Ops:
  10.0 10.5 %all-to-all-start.1 = ((bf16[16,2,2]{1,2,0:T(2,128)(2,1)}), bf16[16,2,2]{1,2,0:T(2,128)(2,1)S(1)}, u32[]{:S(2)}, u32[]{:S(2)}) async-start(bf16[16,2,2]{1,2,0:T(2,128)(2,1)} %copy.61), calls=%async_computation.1 | async-start | bytes 16384 | tf_op jit(solution)/shard_map/all_to_all | solution.py:98
  20.4 9.4 %all-to-all-start = ((bf16[16,2,128]{2,1,0:T(2,128)(2,1)}), bf16[16,2,128]{2,1,0:T(2,128)(2,1)S(1)}, u32[]{:S(2)}, u32[]{:S(2)}) async-start(bf16[16,2,128]{2,1,0:T(2,128)(2,1)} %bitcast.2), calls=%async_computation | async-start | bytes 16384 | tf_op jit(solution)/shard_map/all_to_all | solution.py:91
  25.2 224.0 %reduce-scatter.3.cloned.1.call-start = ((), (), s32[]{:S(2)}) async-start(), calls=%async_computation.8 | async-start | bytes 2228224 | tf_op jit(solution)/shard_map/reduce_scatter | solution.py:118
  37.9 9.5 %all-to-all-start.4 = ((bf16[16,2,2]{1,2,0:T(2,128)(2,1)}), bf16[16,2,2]{1,2,0:T(2,128)(2,1)S(1)}, u32[]{:S(2)}, u32[]{:S(2)}) async-start(bf16[16,2,2]{1,2,0:T(2,128)(2,1)} %copy.68), calls=%async_computation.5 | async-start | bytes 16384 | tf_op jit(solution)/shard_map/all_to_all | solution.py:98
  47.3 9.4 %all-to-all-start.3 = ((bf16[16,2,128]{2,1,0:T(2,128)(2,1)}), bf16[16,2,128]{2,1,0:T(2,128)(2,1)S(1)}, u32[]{:S(2)}, u32[]{:S(2)}) async-start(bf16[16,2,128]{2,1,0:T(2,128)(2,1)} %bitcast.13), calls=%async_computation.4 | async-start | bytes 16384 | tf_op jit(solution)/shard_map/all_to_all | solution.py:91
  52.0 406.8 %reduce-scatter.5.cloned.1.call-start = ((), (), s32[]{:S(2)}) async-start(), calls=%async_computation.10 | async-start | bytes 2228224 | tf_op jit(solution)/shard_map/reduce_scatter | solution.py:118
  62.3 8.4 %copy-start = (bf16[2,12,8,128]{3,2,1,0:T(8,128)(2,1)S(1)}, bf16[2,12,8,128]{3,2,1,0:T(8,128)(2,1)}, u32[]{:S(2)}) copy-start(bf16[2,12,8,128]{3,2,1,0:T(8,128)(2,1)} %param.8) | copy-start | bytes 147460
  65.2 23.1 %collective-permute-start = (bf16[1,2048,128]{2,1,0:T(8,128)(2,1)S(1)}, bf16[1,2048,128]{2,1,0:T(8,128)(2,1)S(1)}, u32[]{:S(2)}, u32[]{:S(2)}) collective-permute-start(bf16[1,2048,128]{2,1,0:T(8,128)(2,1)S(1)} %get-tuple-element.14), channel_id=1, source_target_pairs={{0,16},{16,32},{32,48},{48,64},{64,80},{80,96},{96,112},{112,128},... | collective-permute-start | bytes 1572872 | tf_op jit(solution)/shard_map/ppermute | solution.py:20
  67.1 183.7 %collective-permute-start.1 = (bf16[1,2048,128]{2,1,0:T(8,128)(2,1)S(1)}, bf16[1,2048,128]{2,1,0:T(8,128)(2,1)S(1)}, u32[]{:S(2)}, u32[]{:S(2)}) collective-permute-start(bf16[1,2048,128]{2,1,0:T(8,128)(2,1)S(1)} %get-tuple-element.13), channel_id=1, source_target_pairs={{16,0},{32,16},{48,32},{64,48},{80,64},{96,80},{112,96},{128,112},... | collective-permute-start | bytes 1572872 | tf_op jit(solution)/shard_map/ppermute | solution.py:22
  71.7 11.6 %all-to-all-start.2 = ((bf16[16,2,1024]{2,1,0:T(2,128)(2,1)}), bf16[16,2,1024]{2,1,0:T(2,128)(2,1)S(1)}, u32[]{:S(2)}, u32[]{:S(2)}) async-start(bf16[16,2,1024]{2,1,0:T(2,128)(2,1)} %reshape.199), calls=%async_computation.3 | async-start | bytes 131072 | tf_op jit(solution)/shard_map/all_to_all | solution.py:101
  83.3 195.8 %all-to-all-start.5 = ((bf16[16,2,1024]{2,1,0:T(2,128)(2,1)}), bf16[16,2,1024]{2,1,0:T(2,128)(2,1)S(1)}, u32[]{:S(2)}, u32[]{:S(2)}) async-start(bf16[16,2,1024]{2,1,0:T(2,128)(2,1)} %reshape.205), calls=%async_computation.7 | async-start | bytes 131072 | tf_op jit(solution)/shard_map/all_to_all | solution.py:101
  88.2 446.4 %all-gather.3.cloned.1.call-start = ((), (), s32[]{:S(2)}) async-start(), calls=%async_computation.9 | async-start | bytes 1114112 | tf_op jit(solution)/shard_map/all_gather | solution.py:122
  250.8 357.9 %all-gather.5.cloned.1.call-start = ((), (), s32[]{:S(2)}) async-start(), calls=%async_computation.11 | async-start | bytes 1114112 | tf_op jit(solution)/shard_map/all_gather | solution.py:122
  266.1 13.1 %collective-permute-start.3 = (bf16[10,2048,1]{1,0,2:T(8,128)(2,1)S(1)}, bf16[10,2048,1]{1,0,2:T(8,128)(2,1)S(1)}, u32[]{:S(2)}, u32[]{:S(2)}) collective-permute-start(bf16[10,2048,1]{1,0,2:T(8,128)(2,1)S(1)} %copy.73), channel_id=1, source_target_pairs={{1,0},{2,1},{3,2},{4,3},{5,4},{6,5},{7,6},{8,7},{9,8},{10,9},{11,1... | collective-permute-start | bytes 122888 | tf_op jit(solution)/shard_map/ppermute | solution.py:22
  272.2 10.6 %collective-permute-start.2 = (bf16[10,2048,1]{1,0,2:T(8,128)(2,1)S(1)}, bf16[10,2048,1]{1,0,2:T(8,128)(2,1)S(1)}, u32[]{:S(2)}, u32[]{:S(2)}) collective-permute-start(bf16[10,2048,1]{1,0,2:T(8,128)(2,1)S(1)} %copy.72), channel_id=1, source_target_pairs={{0,1},{1,2},{2,3},{3,4},{4,5},{5,6},{6,7},{7,8},{8,9},{9,10},{10,1... | collective-permute-start | bytes 122888 | tf_op jit(solution)/shard_map/ppermute | solution.py:20
Sparse Core Ops, SparseCore 0:
  37.0 212.1 reduce-scatter.2
  253.1 205.6 reduce-scatter.4
  461.3 73.2 all-gather.2
  536.9 71.7 all-gather.4
where the time goes:
time: 662 us; the launch traced here: 660 us
  waiting for transfers between devices  456 us (69%)
  matrix products  62.5 us (9%)
  local copies, waits for them, and re-layouts  45.3 us (7%)
  starting transfers between devices  42.8 us (6%)
  other arithmetic  38.7 us (6%)
  between operations  14.2 us (2%)
    reduce_scatter x2, waiting for transfers between devices, shards(): lax.psum_scatter(forward_band(partial_value, mats), 'tile', scatter_dimen...  312 us
    all_gather x2, waiting for transfers between devices, shards(): whole_rows = lax.all_gather(residual, 'tile', axis=2, tiled=True)  123 us
    dot_general x2, matrix products, shards(): jnp.einsum('jy,jzx->zxy', got_weights, images, preferred_element_type=jnp...  45.9 us
    div x1, other arithmetic, penalty(): return diff / jnp.sqrt(1.0 + diff * diff)  17.2 us
    convert_element_type x1, other arithmetic, shards(): padded = extended(volume, (('slab', 0), ('tile', 2)), 1).astype(jnp.float32)  16.3 us
    slice x2, local copies, waits for them, and re-layouts, extended(): lax.slice_in_dim(cells, cells.shape[dim] - width, cells.shape[dim], axis=...  14.5 us
  transfers between devices with their start and end apart: 14, of which 9 were waited for; matrix products, arithmetic and copies ran while one was open for 14% of the time, Pallas kernels for 0%

commit v1 on v0

v1 whole, which is shorter than its diff:
```python
import functools

import jax
import jax.numpy as jnp
from jax import lax
from jax.experimental import pallas as pl
from jax.experimental.pallas import tpu as pltpu
from jax.sharding import PartitionSpec as P

BAND = 128
BATCHES = 2
CAPP = 2
SLOTS = BATCHES * CAPP
ROWS = 16
RUN = SLOTS * 8
PIECES = 4
XT = 256
F32 = jnp.float32
BF16 = jnp.bfloat16
VMEM = pl.BlockSpec(memory_space=pltpu.VMEM)
SMEM = pl.BlockSpec(memory_space=pltpu.SMEM)
ANY = pl.BlockSpec(memory_space=pl.ANY)


def cost(flops, moved):
    return pl.CostEstimate(flops=flops, bytes_accessed=moved, transcendentals=0)


def iota(shape, dim):
    return lax.broadcasted_iota(jnp.int32, shape, dim)


def pack_kernel(owner_ref, offset_ref, width_ref, weight_ref, measured_ref, out_ref, count_ref):
    out_ref[...] = jnp.zeros_like(out_ref)
    slabs = out_ref.shape[0]
    views = owner_ref.shape[1]
    row = iota((ROWS, BAND), 0)
    lane = iota((ROWS, BAND), 1)
    empty = jnp.zeros((8, BAND), F32)
    for batch in range(BATCHES):
        for slab in range(slabs):
            count_ref[slab] = 0
        for view in range(views):
            owner = owner_ref[batch, view]
            rank = count_ref[owner]
            count_ref[owner] = rank + 1
            rows = jnp.concatenate([measured_ref[batch, view].astype(F32), empty], axis=0)
            band = jnp.where(
                lane == 0,
                offset_ref[batch, view].astype(F32),
                jnp.where(lane == 1, width_ref[batch, view].astype(F32), 0.0),
            )
            rows = jnp.where(row == 8, weight_ref[view].astype(F32)[batch : batch + 1], jnp.where(row == 9, band, rows))
            out_ref[owner, batch * CAPP + rank] = rows.astype(BF16)


def pack(owner, offset, width, weight, measured, slabs):
    return pl.pallas_call(
        pack_kernel,
        out_shape=jax.ShapeDtypeStruct((slabs, SLOTS, ROWS, BAND), BF16),
        in_specs=[SMEM, SMEM, SMEM, VMEM, VMEM],
        out_specs=VMEM,
        scratch_shapes=[pltpu.SMEM((slabs,), jnp.int32)],
        name="pack_messages",
    )(owner, offset, width, jnp.transpose(weight, (1, 0, 2)), measured)


def joined(block):
    return jnp.concatenate([block[z] for z in range(block.shape[0])], axis=1)


def edge_kernel(volume_ref, order_ref, first_ref, last_ref, bottom_ref, top_ref):
    depth, _, strip = volume_ref.shape
    shape = (2 * depth, depth * strip)
    row, lane = iota(shape, 0), iota(shape, 1)
    target = jnp.where(row < depth, row * strip, (row - depth) * strip + strip - 1)
    pick = jnp.where(lane == target, 1.0, 0.0).astype(BF16)
    out = lax.dot_general(
        pick, joined(volume_ref), (((1,), (1,)), ((), ())), preferred_element_type=F32
    )
    first_ref[...] = out[:depth]
    last_ref[...] = out[depth:]
    bottom_ref[...] = volume_ref[0]
    top_ref[...] = volume_ref[depth - 1]


def edges(volume, order):
    depth, extent, strip = volume.shape
    line = jax.ShapeDtypeStruct((depth, extent), F32)
    plane = jax.ShapeDtypeStruct((extent, strip), BF16)
    line_spec = pl.BlockSpec((depth, XT), lambda i: (0, i))
    plane_spec = pl.BlockSpec((XT, strip), lambda i: (i, 0))
    return pl.pallas_call(
        edge_kernel,
        grid=(extent // XT,),
        out_shape=(line, line, plane, plane),
        in_specs=[pl.BlockSpec((depth, XT, strip), lambda i: (0, i, 0)), ANY],
        out_specs=(line_spec, line_spec, plane_spec, plane_spec),
        cost_estimate=cost(2 * 256 * volume.size, 3 * volume.size),
        name="strip_edges",
    )(volume, order)


def spread_weights(tiles, out_ref, first, depth):
    rows = tiles.shape[0] * depth
    weights = jnp.broadcast_to(
        tiles.astype(F32)[:, 8:9, :], (tiles.shape[0], depth, BAND)
    ).reshape(rows, BAND)
    slice_of = lax.rem(iota((rows, BAND), 0), depth)
    for z in range(depth):
        out_ref[first : first + rows, z * BAND : (z + 1) * BAND] = jnp.where(
            slice_of == z, weights, 0.0
        ).astype(BF16)


def hops(tiles):
    half = tiles // 4
    return [0] + [sign * hop for hop in range(1, half) for sign in (1, -1)] + [half]


def forward_kernel(tiles, place_ref, got_ref, volume_ref, *refs):
    spread_ref, outs = refs[0], refs[1:]
    me = place_ref[1]

    @pl.when(pl.program_id(0) == 0)
    def _():
        row = 0
        for hop in hops(tiles):
            tile = lax.rem(me + 2 * hop + tiles, tiles)
            for source in (tile, tile ^ 1):
                spread_weights(got_ref[pl.ds(source * SLOTS, SLOTS)], spread_ref, row, 8)
                row += RUN

    out = lax.dot_general(
        spread_ref[...], joined(volume_ref), (((1,), (1,)), ((), ())), preferred_element_type=F32
    ).astype(BF16)
    row = 0
    for ref in outs:
        ref[...] = out[row : row + ref.shape[0]]
        row += ref.shape[0]


def forward(place, got, volume, tiles):
    depth, extent, strip = volume.shape
    slots = got.shape[0]
    rows = [2 * RUN] * (tiles // 2 - 1) + [RUN] * 2
    spread = (slots * depth, depth * strip)
    return pl.pallas_call(
        functools.partial(forward_kernel, tiles),
        grid=(extent // XT,),
        out_shape=[jax.ShapeDtypeStruct(spread, BF16)]
        + [jax.ShapeDtypeStruct((count, extent), BF16) for count in rows],
        in_specs=[
            SMEM,
            pl.BlockSpec(got.shape, lambda i: (0, 0, 0)),
            pl.BlockSpec((depth, XT, strip), lambda i: (0, i, 0)),
        ],
        out_specs=[pl.BlockSpec(spread, lambda i: (0, 0))]
        + [pl.BlockSpec((count, XT), lambda i: (0, i)) for count in rows],
        cost_estimate=cost(2 * slots * depth * volume.size, 3 * volume.size),
        name="forward",
    )(place, got, volume)


def sums_kernel(from_below_ref, up_ref, from_above_ref, down_ref, *refs):
    up_out_ref, down_out_ref = refs[-2:]
    part = from_below_ref.shape[0]
    rows = up_ref.shape[0]
    up_out_ref[:part] = (from_below_ref[...].astype(F32) + up_ref[:part].astype(F32)).astype(BF16)
    low = rows - part
    down_out_ref[low:] = (from_above_ref[...].astype(F32) + down_ref[low:].astype(F32)).astype(BF16)
    if low:
        up_out_ref[part:] = up_ref[part:]
        down_out_ref[:low] = down_ref[:low]


def ring_sums(from_below, up, from_above, down, *order):
    out = jax.ShapeDtypeStruct(up.shape, BF16)
    return pl.pallas_call(
        sums_kernel,
        out_shape=(out, out),
        in_specs=[VMEM] * 4 + [ANY] * len(order),
        out_specs=(VMEM, VMEM),
        cost_estimate=cost(2 * up.size, 8 * up.size),
        name="ring_sums",
    )(from_below, up, from_above, down, *order)


def last_sums_kernel(from_below_ref, from_above_ref, own_ref, *refs):
    kept_ref, sent_ref = refs[-2:]
    total = (
        from_below_ref[...].astype(F32) + from_above_ref[...].astype(F32) + own_ref[...].astype(F32)
    )
    kept_ref[...] = total[:RUN]
    sent_ref[...] = total[RUN:].astype(BF16)


def last_sums(from_below, from_above, own, *order):
    extent = own.shape[1]
    return pl.pallas_call(
        last_sums_kernel,
        out_shape=(
            jax.ShapeDtypeStruct((RUN, extent), F32),
            jax.ShapeDtypeStruct((RUN, extent), BF16),
        ),
        in_specs=[VMEM] * 3 + [ANY] * len(order),
        out_specs=(VMEM, VMEM),
        cost_estimate=cost(2 * own.size, 8 * own.size),
        name="last_sums",
    )(from_below, from_above, own, *order)


def residual_kernel(kept_ref, arrived_ref, views_ref, *refs):
    out_ref = refs[-1]
    extent = kept_ref.shape[1]
    blocks = extent // BAND
    empty = jnp.zeros((8, BAND), F32)
    for slot in range(SLOTS):
        low = slot * 8
        total = kept_ref[low : low + 8] + arrived_ref[...].astype(F32)[low : low + 8]
        band = views_ref[0, slot].astype(F32)
        offset = band[9:10, 0:1].astype(jnp.int32)
        width = jnp.maximum(band[9:10, 1:2], 1.0)
        recip = 1.0 / width
        width = width.astype(jnp.int32)

        def inside(delta):
            delta = delta - offset
            return jnp.where((delta >= 0) & (delta < width), recip, 0.0).astype(BF16)

        shape = (2 * BAND, BAND)
        onward = inside(iota(shape, 1) + BAND - iota(shape, 0))
        back = inside(iota(shape, 0) - iota(shape, 1))
        parts = [total[:, n * BAND : (n + 1) * BAND] for n in range(blocks)]
        here = jnp.concatenate(parts, axis=0)
        before = jnp.concatenate([empty] + parts[:-1], axis=0)
        paired = jnp.concatenate([before, here], axis=1)
        high = paired.astype(BF16)
        rest = (paired - high.astype(F32)).astype(BF16)
        sums = jnp.dot(high, onward, preferred_element_type=F32) + jnp.dot(
            rest, onward, preferred_element_type=F32
        )
        rows = jnp.concatenate(
            [views_ref[n, slot].astype(F32)[:8] for n in range(blocks)], axis=0
        )
        residual = (sums - rows).astype(BF16).astype(F32)
        later = jnp.concatenate([residual[8:], empty], axis=0)
        both = jnp.concatenate([residual, later], axis=1).astype(BF16)
        image = jnp.dot(both, back, preferred_element_type=F32)
        image = jnp.concatenate([image[n * 8 : (n + 1) * 8] for n in range(blocks)], axis=1)
        if slot % 2 == 0:
            even = image
        else:
            out_ref[low - 8 : low + 8] = jnp.concatenate([even, image], axis=0).astype(BF16)


def residual_images(kept, arrived, views, *order):
    return pl.pallas_call(
        residual_kernel,
        out_shape=jax.ShapeDtypeStruct(arrived.shape, BF16),
        in_specs=[VMEM] * 3 + [ANY] * len(order),
        out_specs=VMEM,
        cost_estimate=cost(4 * 8 * 16 * 256 * 128 * 6, 2 * views.size),
        name="residual_images",
    )(kept, arrived, views, *order)


def penalty(diff):
    return diff * lax.rsqrt(1.0 + diff * diff)


def regularizer_kernel(
    first_tile,
    count,
    place_ref,
    beta_ref,
    block_ref,
    before_ref,
    after_ref,
    below_ref,
    above_ref,
    first_ref,
    last_ref,
    left_ref,
    right_ref,
    *refs,
):
    out_ref, under_ref, side_ref = refs[-3:]
    depth, tile, strip = block_ref.shape
    at = pl.program_id(0) + first_tile
    beta = beta_ref[0]
    has_below = (place_ref[0] > 0).astype(F32)
    has_above = (place_ref[0] < place_ref[3] - 1).astype(F32)
    has_left = (place_ref[1] > 0).astype(F32)
    has_right = (place_ref[1] < place_ref[2] - 1).astype(F32)
    has_before = (at > 0).astype(F32)
    has_after = (at < count - 1).astype(F32)
    spacing = strip // 8

    on_left = penalty(first_ref[...] - left_ref[...]) * has_left
    on_right = penalty(right_ref[...] - last_ref[...]) * has_right
    end = iota((spacing, tile), 0)
    rows = []
    for level in range(8):
        up = (level + 1) % 8
        rows.append(
            jnp.where(
                end == 0,
                on_left[level : level + 1],
                jnp.where(end == spacing - 1, on_right[up : up + 1], 0.0),
            )
        )
    side_ref[...] = jnp.concatenate(rows, axis=0).T
    under_ref[...] = (
        penalty(block_ref[0].astype(F32) - below_ref[...].astype(F32)) * has_below
    )
    row = iota((tile, strip), 0)
    lane = iota((tile, strip), 1)

    def body(z, carry):
        center = block_ref[z].astype(F32)
        top = z == depth - 1
        upper = jnp.where(top, above_ref[...], block_ref[jnp.minimum(z + 1, depth - 1)])
        over = penalty(upper.astype(F32) - center) * jnp.where(top, has_above, 1.0)
        total = under_ref[...] - over
        under_ref[...] = over
        ahead = after_ref[z].astype(F32)[0:1]
        behind = penalty(center[0:1] - before_ref[z].astype(F32)[15:16]) * has_before
        along = penalty(jnp.where(row == tile - 1, ahead, pltpu.roll(center, tile - 1, 0)) - center)
        along = jnp.where(row == tile - 1, along * has_after, along)
        total = total + jnp.where(row == 0, behind, pltpu.roll(along, 1, 0)) - along
        side = pltpu.roll(side_ref[...], lax.rem(strip - z * spacing, strip), 1)
        across = penalty(pltpu.roll(center, strip - 1, 1) - center)
        across = jnp.where(lane == strip - 1, side, across)
        total = total + jnp.where(lane == 0, side, pltpu.roll(across, 1, 1)) - across
        out_ref[z] = (total * beta).astype(BF16)
        return carry

    lax.fori_loop(0, depth, body, 0, unroll=2)


def regularizer(index, done, place, beta, volume, below, above, lines, *order):
    depth, extent, strip = volume.shape
    count = extent // XT
    length = count // PIECES
    start = index * length
    edge = XT // 16
    line = pl.BlockSpec((depth, XT), lambda i: (0, start + i))
    plane = pl.BlockSpec((XT, strip), lambda i: (start + i, 0))
    block = pl.BlockSpec((depth, XT, strip), lambda i: (0, start + i, 0))
    ends = [
        lambda i: (0, jnp.maximum((start + i) * edge - 1, 0), 0),
        lambda i: (0, jnp.minimum((start + i + 1) * edge, count * edge - 1), 0),
    ]
    specs = [SMEM, SMEM, block]
    specs += [pl.BlockSpec((depth, 16, strip), where) for where in ends]
    specs += [plane] * 2 + [line] * 4 + [ANY] * len(order)
    before = [] if done is None else [done]
    return pl.pallas_call(
        functools.partial(regularizer_kernel, start, count),
        grid=(length,),
        out_shape=jax.ShapeDtypeStruct(volume.shape, BF16),
        in_specs=specs + [ANY] * len(before),
        out_specs=block,
        scratch_shapes=[pltpu.VMEM((XT, strip), F32), pltpu.VMEM((XT, strip), F32)],
        input_output_aliases={len(specs): 0} if before else {},
        cost_estimate=cost(30 * volume.size // PIECES, 8 * volume.size // PIECES),
        name="regularizer",
    )(place, beta, volume, volume, volume, below, above, *lines, *order, *before)


def gradient_kernel(count, spread_ref, *refs):
    chunk_refs = refs[:count]
    regular_ref, out_ref = refs[count:]
    depth, tile, strip = out_ref.shape
    rows = jnp.concatenate([ref[...] for ref in chunk_refs], axis=0)
    out = lax.dot_general(
        rows, spread_ref[...], (((0,), (0,)), ((), ())), preferred_element_type=F32
    )
    for z in range(depth):
        regular = regular_ref[z].astype(F32)
        out_ref[z] = (out[:, z * strip : (z + 1) * strip] + regular).astype(BF16)


def gradient(spread, chunks, regular):
    depth, extent, strip = regular.shape
    block = pl.BlockSpec((depth, XT, strip), lambda i: (0, i, 0))
    size = depth * extent * strip
    return pl.pallas_call(
        functools.partial(gradient_kernel, len(chunks)),
        grid=(extent // XT,),
        out_shape=jax.ShapeDtypeStruct(regular.shape, BF16),
        in_specs=[pl.BlockSpec(spread.shape, lambda i: (0, 0))]
        + [pl.BlockSpec((chunk.shape[0], XT), lambda i: (0, i)) for chunk in chunks]
        + [block],
        out_specs=block,
        cost_estimate=cost(2 * spread.shape[0] * size, 5 * size),
        name="gradient",
    )(spread, *chunks, regular)


def shards(volume, measured, ray_weight, view_owner, band_offset, band_width, beta):
    slabs = lax.axis_size("slab")
    tiles = lax.axis_size("tile")
    slab, tile = lax.axis_index("slab"), lax.axis_index("tile")
    place = jnp.stack([slab, tile, jnp.int32(tiles), jnp.int32(slabs)])

    def along_z(block, by):
        return lax.ppermute(block, "tile", [(i, (i + 2 * by) % tiles) for i in range(tiles)])

    def along_y(block):
        return lax.ppermute(block, "tile", [(i, i ^ 1) for i in range(tiles)])

    packed = pack(view_owner[:, :, 0], band_offset, band_width, ray_weight, measured, slabs)
    got = lax.all_to_all(packed, "slab", split_axis=0, concat_axis=0, tiled=True)
    first, last, bottom, top = edges(volume, packed)
    got, first, last, bottom, top = lax.optimization_barrier((got, first, last, bottom, top))

    spread, *outs = forward(place, got.reshape(slabs * SLOTS, ROWS, BAND), volume, tiles)
    own = dict(zip(hops(tiles)[:-1], outs))
    up, down = outs[-2:]
    first, last, up = lax.optimization_barrier((first, last, up))
    from_below, from_above = along_z(up, 1), along_z(down, -1)
    left = lax.ppermute(last, "tile", [(i, i + 1) for i in range(tiles - 1)])
    right = lax.ppermute(first, "tile", [(i + 1, i) for i in range(tiles - 1)])
    lines = (first, last, left, right)

    up, down = ring_sums(from_below, own[3], from_above, own[-3], left)
    bottom, top, up = lax.optimization_barrier((bottom, top, up))
    from_below, from_above = along_z(up, 1), along_z(down, -1)
    below = lax.ppermute(top, "slab", [(i, i + 1) for i in range(slabs - 1)])
    above = lax.ppermute(bottom, "slab", [(i + 1, i) for i in range(slabs - 1)])

    up, down = ring_sums(from_below, own[2], from_above, own[-2], right)
    got, up = lax.optimization_barrier((got, up))
    from_below, from_above = along_z(up, 1), along_z(down, -1)
    views = lax.all_to_all(got, "tile", split_axis=0, concat_axis=0, tiled=True)

    up, down = ring_sums(from_below, own[1], from_above, own[-1], below, above)
    from_below, from_above = along_z(up, 1), along_z(down, -1)
    regular = None

    def piece(index, after):
        return regularizer(index, regular, place, beta, volume, below, above, lines, after)

    kept, sent = last_sums(from_below, from_above, own[0], views)
    arrived = along_y(sent)
    regular = piece(0, sent)
    images = residual_images(kept, arrived, views, regular)

    partner = along_y(images)
    regular = piece(1, images)
    pair = jnp.concatenate([images, partner], axis=0)
    chunks = [pair]
    up, down = pair, pair
    for hop in range(1, tiles // 4):
        if hop <= 2:
            up, down, regular = lax.optimization_barrier((up, down, regular))
            after = up
        up, down = along_z(up, 1), along_z(down, -1)
        chunks += [down, up]
        if hop <= 2:
            regular = piece(hop + 1, after)
    up, down, regular = lax.optimization_barrier((up, down, regular))
    chunks += [along_z(up[:RUN], 1), along_z(down[RUN:], -1)]
    return gradient(spread, chunks, regular)


def solution(mesh):
    in_specs = (
        P("slab", None, "tile"),
        P(None, "slab", None, "tile"),
        P(None, "slab", "tile"),
        P(None, "slab", None),
        P(None, "slab"),
        P(None, "slab"),
        P(),
    )
    out_specs = P("slab", None, "tile")
    return jax.shard_map(shards, mesh=mesh, in_specs=in_specs, out_specs=out_specs, check_vma=False)
```

time: 662 us -> 157 us (0.24)
  the two profiles are of different devices: /device:TPU:8 before, /device:TPU:110 now
where the time goes in v1:
time: 157 us; the launch traced here: 156 us
  Pallas kernels  58.5 us (37%)
  starting transfers between devices  54.5 us (35%)
  waiting for transfers between devices  36.2 us (23%)
  local copies, waits for them, and re-layouts  5.32 us (3%)
    ppermute x16, starting transfers between devices, along_z(): lax.ppermute(block, 'tile', [(i, (i + 2 * by) % tiles) for i in range(til...  25.8 us
    pallas_call x4, Pallas kernels, regularizer(): pl.pallas_call(functools.partial(regularizer_kernel, start, count), grid=...  21.9 us
    ppermute x16, waiting for transfers between devices, along_z(): lax.ppermute(block, 'tile', [(i, (i + 2 * by) % tiles) for i in range(til...  19 us
    ppermute x1, waiting for transfers between devices, shards(): right = lax.ppermute(first, 'tile', [(i + 1, i) for i in range(tiles - 1)])  9.62 us
    pallas_call x1, Pallas kernels, gradient(): pl.pallas_call(functools.partial(gradient_kernel, len(chunks)), grid=(ext...  9.13 us
    pallas_call x1, Pallas kernels, forward(): pl.pallas_call(functools.partial(forward_kernel, tiles), grid=(extent //...  8.37 us
    all_to_all x1, starting transfers between devices, shards(): views = lax.all_to_all(got, 'tile', split_axis=0, concat_axis=0, tiled=True)  7.78 us
    pallas_call x1, Pallas kernels, edges(): pl.pallas_call(edge_kernel, grid=(extent // XT,), out_shape=(line, line,...  6.67 us
  transfers between devices with their start and end apart: 24, of which 10 were waited for; matrix products, arithmetic and copies ran while one was open for 0% of the time, Pallas kernels for 21%

profile of v1, /device:TPU:110, one launch (start us, length us, event | category | flops | bytes accessed | tf_op | source)
XLA Modules:
  0.0 156.1 jit_solution(9981406574157063335)
XLA Ops:
  1.7 5.7 %all-to-all-start = ((bf16[16,4,16,128]{3,2,1,0:T(8,128)(2,1)}), bf16[16,4,16,128]{3,2,1,0:T(8,128)(2,1)S(1)}, u32[]{:S(2)}, u32[]{:S(2)}) async-start(bf16[16,4,16,128]{3,2,1,0:T(8,128)(2,1)} %pack_messages.1.order_ref), calls=%async_computation | async-start | bytes 524288 | tf_op jit(solution)/shard_map/all_to_all | solution.py:415
  7.4 6.7 %strip_edges.1 = (f32[8,2048]{1,0:T(8,128)}, f32[8,2048]{1,0:T(8,128)}, bf16[2048,128]{1,0:T(8,128)(2,1)}, bf16[2048,128]{1,0:T(8,128)(2,1)}) custom-call(bf16[8,2048,128]{2,1,0:T(8,128)(2,1)} %after_ref.7, bf16[16,4,16,128]{3,2,1,0:T(8,128)(2,1)} %pack_messages.1.order_ref), custom_call_target="tpu_custom_call" | custom-call | flops 1073741824 | bytes 6291456 | tf_op jit(solution)/shard_map/strip_edges/pallas_call | solution.py:93
  15.4 8.4 %forward.1 = (bf16[512,1024]{1,0:T(8,128)(2,1)}, bf16[64,2048]{1,0:T(8,128)(2,1)}, bf16[64,2048]{1,0:T(8,128)(2,1)}, bf16[64,2048]{1,0:T(8,128)(2,1)}, bf16[64,2...) custom-call(s32[4]{0:T(128)} %pad_add_fusion.place_ref, ...), custom_call_target="tpu_custom_call" | custom-call | flops 2147483648 | bytes 6291456 | tf_op jit(solution)/shard_map/forward/pallas_call | solution.py:148
  23.8 3.2 %collective-permute-start = (bf16[32,2048]{1,0:T(8,128)(2,1)}, bf16[32,2048]{1,0:T(8,128)(2,1)S(1)}, u32[]{:S(2)}, u32[]{:S(2)}) collective-permute-start(bf16[32,2048]{1,0:T(8,128)(2,1)} %get-tuple-element.60), channel_id=1, source_target_pairs={{0,2},{1,3},{2,4},{3,5},{4,6},{5,7},{6,8},{7,9},{8,10},{9,11},{10,... | collective-permute-start | bytes 393224 | tf_op jit(solution)/shard_map/ppermute | solution.py:409
  27.0 4.2 %collective-permute-start.2 = (f32[8,2048]{1,0:T(8,128)S(1)}, f32[8,2048]{1,0:T(8,128)S(1)}, u32[]{:S(2)}, u32[]{:S(2)}) collective-permute-start(f32[8,2048]{1,0:T(8,128)S(1)} %copy-done.8), channel_id=1, source_target_pairs={{0,1},{1,2},{2,3},{3,4},{4,5},{5,6},{6,7},{7,8},{8,9},{9,10},{10,1... | collective-permute-start | bytes 196616 | tf_op jit(solution)/shard_map/ppermute | solution.py:424
  31.2 4.3 %collective-permute-done.2.refs_0_.left_ref = f32[8,2048]{1,0:T(8,128)S(1)} collective-permute-done((f32[8,2048]{1,0:T(8,128)S(1)}, f32[8,2048]{1,0:T(8,128)S(1)}, u32[]{:S(2)}, u32[]{:S(2)}) %collective-permute-start.2) | collective-permute-done | bytes 65568 | tf_op jit(solution)/shard_map/ppermute | solution.py:424
  36.2 2.0 %ring_sums.3 = (bf16[64,2048]{1,0:T(8,128)(2,1)}, bf16[64,2048]{1,0:T(8,128)(2,1)}) custom-call(bf16[32,2048]{1,0:T(8,128)(2,1)} %copy-done.25, bf16[64,2048]{1,0:T(8,128)(2,1)} %get-tuple-element.61.up_ref, bf16[32,2048]{1,0:T(8,128)(2,1)} %copy-done.26, bf16[64,2048]{1,0:T(8,128)(2,1)} %get-tuple-element.63.down_ref, f32[8,2048]{1,0:T(8,128)} %copy-done.5), custom_call_target="tpu_custom_call" | custom-call | flops 262144 | bytes 1048576 | tf_op jit(solution)/shard_map/ring_sums/pallas_call | solution.py:179
  38.2 4.4 %collective-permute-start.3 = (bf16[64,2048]{1,0:T(8,128)(2,1)}, bf16[64,2048]{1,0:T(8,128)(2,1)S(1)}, u32[]{:S(2)}, u32[]{:S(2)}) collective-permute-start(bf16[64,2048]{1,0:T(8,128)(2,1)} %get-tuple-element.66), channel_id=1, source_target_pairs={{0,2},{1,3},{2,4},{3,5},{4,6},{5,7},{6,8},{7,9},{8,10},{9,11},{10,... | collective-permute-start | bytes 786440 | tf_op jit(solution)/shard_map/ppermute | solution.py:409
  44.6 3.6 %collective-permute-start.9 = (bf16[2048,128]{1,0:T(8,128)(2,1)S(1)}, bf16[2048,128]{1,0:T(8,128)(2,1)S(1)}, u32[]{:S(2)}, u32[]{:S(2)}) collective-permute-start(bf16[2048,128]{1,0:T(8,128)(2,1)S(1)} %copy-done.27), channel_id=1, source_target_pairs={{16,0},{32,16},{48,32},{64,48},{80,64},{96,80},{112,96},{128,112},... | collective-permute-start | bytes 1572872 | tf_op jit(solution)/shard_map/ppermute | solution.py:432
  48.2 1.9 %collective-permute-start.5 = (f32[8,2048]{1,0:T(8,128)S(1)}, f32[8,2048]{1,0:T(8,128)S(1)}, u32[]{:S(2)}, u32[]{:S(2)}) collective-permute-start(f32[8,2048]{1,0:T(8,128)S(1)} %copy-done.7), channel_id=1, source_target_pairs={{1,0},{2,1},{3,2},{4,3},{5,4},{6,5},{7,6},{8,7},{9,8},{10,9},{11,1... | collective-permute-start | bytes 196616 | tf_op jit(solution)/shard_map/ppermute | solution.py:425
  50.2 9.6 %collective-permute-done.5.refs_0_.right_ref = f32[8,2048]{1,0:T(8,128)S(1)} collective-permute-done((f32[8,2048]{1,0:T(8,128)S(1)}, f32[8,2048]{1,0:T(8,128)S(1)}, u32[]{:S(2)}, u32[]{:S(2)}) %collective-permute-start.5) | collective-permute-done | bytes 65568 | tf_op jit(solution)/shard_map/ppermute | solution.py:425
  60.6 2.1 %ring_sums.4 = (bf16[64,2048]{1,0:T(8,128)(2,1)}, bf16[64,2048]{1,0:T(8,128)(2,1)}) custom-call(bf16[64,2048]{1,0:T(8,128)(2,1)} %copy-done.16, bf16[64,2048]{1,0:T(8,128)(2,1)} %get-tuple-element.67.up_ref, bf16[64,2048]{1,0:T(8,128)(2,1)} %copy-done.17, bf16[64,2048]{1,0:T(8,128)(2,1)} %get-tuple-element.69.down_ref, f32[8,2048]{1,0:T(8,128)} %copy-done.4), custom_call_target="tpu_custom_call" | custom-call | flops 262144 | bytes 1048576 | tf_op jit(solution)/shard_map/ring_sums/pallas_call | solution.py:179
  62.7 3.2 %collective-permute-start.6 = (bf16[64,2048]{1,0:T(8,128)(2,1)}, bf16[64,2048]{1,0:T(8,128)(2,1)S(1)}, u32[]{:S(2)}, u32[]{:S(2)}) collective-permute-start(bf16[64,2048]{1,0:T(8,128)(2,1)} %get-tuple-element.72), channel_id=1, source_target_pairs={{0,2},{1,3},{2,4},{3,5},{4,6},{5,7},{6,8},{7,9},{8,10},{9,11},{10,... | collective-permute-start | bytes 786440 | tf_op jit(solution)/shard_map/ppermute | solution.py:409
  65.9 7.8 %all-to-all-start.1 = ((bf16[16,4,16,128]{3,2,1,0:T(8,128)(2,1)}), bf16[16,4,16,128]{3,2,1,0:T(8,128)(2,1)S(1)}, u32[]{:S(2)}, u32[]{:S(2)}) async-start(bf16[16,4,16,128]{3,2,1,0:T(8,128)(2,1)} %copy-done.10), calls=%async_computation.1 | async-start | bytes 524288 | tf_op jit(solution)/shard_map/all_to_all | solution.py:437
  73.7 2.8 %collective-permute-done.7.from_above_ref = bf16[64,2048]{1,0:T(8,128)(2,1)S(1)} collective-permute-done((bf16[64,2048]{1,0:T(8,128)(2,1)}, bf16[64,2048]{1,0:T(8,128)(2,1)S(1)}, u32[]{:S(2)}, u32[]{:S(2)}) %collective-permute-start.7) | collective-permute-done | bytes 262176 | tf_op jit(solution)/shard_map/ppermute | solution.py:409
  77.6 2.1 %ring_sums.5 = (bf16[64,2048]{1,0:T(8,128)(2,1)}, bf16[64,2048]{1,0:T(8,128)(2,1)}) custom-call(bf16[64,2048]{1,0:T(8,128)(2,1)} %copy-done.20, bf16[64,2048]{1,0:T(8,128)(2,1)} %get-tuple-element.73.up_ref, bf16[64,2048]{1,0:T(8,128)(2,1)} %copy-done.21, bf16[64,2048]{1,0:T(8,128)(2,1)} %get-tuple-element.75.down_ref, bf16[2048,128]{1,0:T(8,128)(2,1)} %copy-done, ...), custom_call_target="tpu_custom_call" | custom-call | flops 262144 | bytes 1048576 | tf_op jit(solution)/shard_map/ring_sums/pallas_call | solution.py:179
  79.7 1.9 %collective-permute-start.11 = (bf16[64,2048]{1,0:T(8,128)(2,1)}, bf16[64,2048]{1,0:T(8,128)(2,1)S(1)}, u32[]{:S(2)}, u32[]{:S(2)}) collective-permute-start(bf16[64,2048]{1,0:T(8,128)(2,1)} %get-tuple-element.79), channel_id=1, source_target_pairs={{0,14},{1,15},{2,0},{3,1},{4,2},{5,3},{6,4},{7,5},{8,6},{9,7},{10,... | collective-permute-start | bytes 786440 | tf_op jit(solution)/shard_map/ppermute | solution.py:409
  81.7 2.7 %all-to-all-done.1.refs_0_.views_ref = bf16[16,4,16,128]{3,2,1,0:T(8,128)(2,1)S(1)} async-done(((bf16[16,4,16,128]{3,2,1,0:T(8,128)(2,1)}), bf16[16,4,16,128]{3,2,1,0:T(8,128)(2,1)S(1)}, u32[]{:S(2)}, u32[]{:S(2)}) %all-to-all-start.1) | async-done | bytes 262176 | tf_op jit(solution)/shard_map/all_to_all | solution.py:437
  90.2 2.8 %collective-permute-start.12 = (bf16[32,2048]{1,0:T(8,128)(2,1)}, bf16[32,2048]{1,0:T(8,128)(2,1)S(1)}, u32[]{:S(2)}, u32[]{:S(2)}) collective-permute-start(bf16[32,2048]{1,0:T(8,128)(2,1)} %get-tuple-element.83.refs_0_), channel_id=1, source_target_pairs={{0,1},{1,0},{2,3},{3,2},{4,5},{5,4},{6,7},{7,6},{8,9},{9,8},{10,11... | collective-permute-start | bytes 393224 | tf_op jit(solution)/shard_map/ppermute | solution.py:412
  93.6 5.5 %regularizer.4.refs_0_.refs_1_ = bf16[8,2048,128]{2,1,0:T(8,128)(2,1)} custom-call(s32[4]{0:T(128)} %pad_add_fusion.place_ref, f32[1]{0:T(128)S(6)} %copy.14.beta_ref, bf16[8,2048,128]{2,1,0:T(8,128)(2,1)} %after_ref.7, bf16[8,2048,128]{2,1,0:T(8,128)(2,1)} %after_ref.7, bf16[8,2048,128]{2,1,0:T(8,128)(2,1)} %after_ref.7, bf16[2048,128]{1,0:T(8,128)(2,1)} %copy-done, ...), custom_call_target="tpu_custom_call" | custom-call | flops 15728640 | bytes 4194304 | tf_op jit(solution)/shard_map/regularizer/pallas_call | solution.py:359
  99.8 2.7 %residual_images.1.refs_0_ = bf16[32,2048]{1,0:T(8,128)(2,1)} custom-call(f32[32,2048]{1,0:T(8,128)} %get-tuple-element.82.kept_ref, bf16[32,2048]{1,0:T(8,128)(2,1)} %copy-done.24, bf16[16,4,16,128]{3,2,1,0:T(8,128)(2,1)} %copy-done.3, bf16[8,2048,128]{2,1,0:T(8,128)(2,1)} %regularizer.4.refs_0_.refs_1_), custom_call_target="tpu_custom_call" | custom-call | flops 100663296 | bytes 262144 | tf_op jit(solution)/shard_map/residual_images/pallas_call | solution.py:258
  103.2 5.4 %regularizer.5.refs_1_ = bf16[8,2048,128]{2,1,0:T(8,128)(2,1)} custom-call(s32[4]{0:T(128)} %pad_add_fusion.place_ref, f32[1]{0:T(128)S(6)} %copy.14.beta_ref, bf16[8,2048,128]{2,1,0:T(8,128)(2,1)} %after_ref.7, bf16[8,2048,128]{2,1,0:T(8,128)(2,1)} %after_ref.7, bf16[8,2048,128]{2,1,0:T(8,128)(2,1)} %after_ref.7, ...), custom_call_target="tpu_custom_call", output_to_operand_aliasing={{}: (12, {})} | custom-call | flops 15728640 | bytes 4194304 | tf_op jit(solution)/shard_map/regularizer/pallas_call | solution.py:359
  109.7 3.1 %collective-permute-start.15 = (bf16[64,2048]{1,0:T(8,128)(2,1)S(1)}, bf16[64,2048]{1,0:T(8,128)(2,1)S(1)}, u32[]{:S(2)}, u32[]{:S(2)}) collective-permute-start(bf16[64,2048]{1,0:T(8,128)(2,1)S(1)} %pad_maximum_fusion.refs_0_), channel_id=1, source_target_pairs={{0,2},{1,3},{2,4},{3,5},{4,6},{5,7},{6,8},{7,9},{8,10},{9,11},{10,... | collective-permute-start | bytes 786440 | tf_op jit(solution)/shard_map/ppermute | solution.py:409
  112.7 5.5 %regularizer.6.refs_1_ = bf16[8,2048,128]{2,1,0:T(8,128)(2,1)} custom-call(s32[4]{0:T(128)} %pad_add_fusion.place_ref, f32[1]{0:T(128)S(6)} %copy.14.beta_ref, bf16[8,2048,128]{2,1,0:T(8,128)(2,1)} %after_ref.7, bf16[8,2048,128]{2,1,0:T(8,128)(2,1)} %after_ref.7, bf16[8,2048,128]{2,1,0:T(8,128)(2,1)} %after_ref.7, ...), custom_call_target="tpu_custom_call", output_to_operand_aliasing={{}: (12, {})} | custom-call | flops 15728640 | bytes 4194304 | tf_op jit(solution)/shard_map/regularizer/pallas_call | solution.py:359
  118.3 3.3 %collective-permute-start.17 = (bf16[64,2048]{1,0:T(8,128)(2,1)S(1)}, bf16[64,2048]{1,0:T(8,128)(2,1)S(1)}, u32[]{:S(2)}, u32[]{:S(2)}) collective-permute-start(bf16[64,2048]{1,0:T(8,128)(2,1)S(1)} %collective-permute-done.15.refs_0_.refs_2_), channel_id=1, source_target_pairs={{0,2},{1,3},{2,4},{3,5},{4,6},{5,7},{6,8},{7,9},{8,10},{9,11},{10,... | collective-permute-start | bytes 786440 | tf_op jit(solution)/shard_map/ppermute | solution.py:409
  121.6 6.9 %collective-permute-done.16.refs_3_ = bf16[64,2048]{1,0:T(8,128)(2,1)S(1)} collective-permute-done((bf16[64,2048]{1,0:T(8,128)(2,1)S(1)}, bf16[64,2048]{1,0:T(8,128)(2,1)S(1)}, u32[]{:S(2)}, u32[]{:S(2)}) %collective-permute-start.16) | collective-permute-done | bytes 262176 | tf_op jit(solution)/shard_map/ppermute | solution.py:409
  128.5 3.2 %collective-permute-start.19 = (bf16[64,2048]{1,0:T(8,128)(2,1)S(1)}, bf16[64,2048]{1,0:T(8,128)(2,1)S(1)}, u32[]{:S(2)}, u32[]{:S(2)}) collective-permute-start(bf16[64,2048]{1,0:T(8,128)(2,1)S(1)} %collective-permute-done.17.refs_4_), channel_id=1, source_target_pairs={{0,2},{1,3},{2,4},{3,5},{4,6},{5,7},{6,8},{7,9},{8,10},{9,11},{10,... | collective-permute-start | bytes 786440 | tf_op jit(solution)/shard_map/ppermute | solution.py:409
  131.7 5.5 %regularizer.7.refs_9_ = bf16[8,2048,128]{2,1,0:T(8,128)(2,1)} custom-call(s32[4]{0:T(128)} %pad_add_fusion.place_ref, f32[1]{0:T(128)S(6)} %copy.14.beta_ref, bf16[8,2048,128]{2,1,0:T(8,128)(2,1)} %after_ref.7, bf16[8,2048,128]{2,1,0:T(8,128)(2,1)} %after_ref.7, bf16[8,2048,128]{2,1,0:T(8,128)(2,1)} %after_ref.7, ...), custom_call_target="tpu_custom_call", output_to_operand_aliasing={{}: (12, {})} | custom-call | flops 15728640 | bytes 4194304 | tf_op jit(solution)/shard_map/regularizer/pallas_call | solution.py:359
  137.3 2.7 %collective-permute-start.20 = (bf16[32,2048]{1,0:T(8,128)(2,1)S(1)}, bf16[32,2048]{1,0:T(8,128)(2,1)S(1)}, u32[]{:S(2)}, u32[]{:S(2)}) collective-permute-start(bf16[32,2048]{1,0:T(8,128)(2,1)S(1)} %slice.6), channel_id=1, source_target_pairs={{0,2},{1,3},{2,4},{3,5},{4,6},{5,7},{6,8},{7,9},{8,10},{9,11},{10,... | collective-permute-start | bytes 393224 | tf_op jit(solution)/shard_map/ppermute | solution.py:409
  140.1 2.4 %collective-permute-done.20.refs_7_ = bf16[32,2048]{1,0:T(8,128)(2,1)S(1)} collective-permute-done((bf16[32,2048]{1,0:T(8,128)(2,1)S(1)}, bf16[32,2048]{1,0:T(8,128)(2,1)S(1)}, u32[]{:S(2)}, u32[]{:S(2)}) %collective-permute-start.20) | collective-permute-done | bytes 131104 | tf_op jit(solution)/shard_map/ppermute | solution.py:409
  142.6 3.7 %collective-permute-done.21.refs_8_ = bf16[32,2048]{1,0:T(8,128)(2,1)S(1)} collective-permute-done((bf16[32,2048]{1,0:T(8,128)(2,1)S(1)}, bf16[32,2048]{1,0:T(8,128)(2,1)S(1)}, u32[]{:S(2)}, u32[]{:S(2)}) %collective-permute-start.21) | collective-permute-done | bytes 131104 | tf_op jit(solution)/shard_map/ppermute | solution.py:409
  147.0 9.1 %gradient.1 = bf16[8,2048,128]{2,1,0:T(8,128)(2,1)} custom-call(bf16[512,1024]{1,0:T(8,128)(2,1)} %get-tuple-element.54.spread_ref, bf16[64,2048]{1,0:T(8,128)(2,1)} %copy-done.2, bf16[64,2048]{1,0:T(8,128)(2,1)} %copy-done.13, bf16[64,2048]{1,0:T(8,128)(2,1)} %copy-done.9, bf16[64,2048]{1,0:T(8,128)(2,1)} %copy-done.14, bf16[64,2048]{1,0:T(8,128)(2,1)} %copy-done.15, ...), custom_call_target="tpu_custom_call" | custom-call | flops 2147483648 | bytes 10485760 | tf_op jit(solution)/shard_map/gradient/pallas_call | solution.py:389
  (92 shorter events, 16.6 us)
Async XLA Ops:
  1.7 13.0 %all-to-all-start = ((bf16[16,4,16,128]{3,2,1,0:T(8,128)(2,1)}), bf16[16,4,16,128]{3,2,1,0:T(8,128)(2,1)S(1)}, u32[]{:S(2)}, u32[]{:S(2)}) async-start(bf16[16,4,16,128]{3,2,1,0:T(8,128)(2,1)} %pack_messages.1.order_ref), calls=%async_computation | async-start | bytes 524288 | tf_op jit(solution)/shard_map/all_to_all | solution.py:415
  14.0 12.9 %copy-start.8 = (f32[8,2048]{1,0:T(8,128)S(1)}, f32[8,2048]{1,0:T(8,128)}, u32[]{:S(2)}) copy-start(f32[8,2048]{1,0:T(8,128)} %get-tuple-element.64.last_ref) | copy-start | bytes 196612
  15.4 27.3 %copy-start.28 = (bf16[2048,128]{1,0:T(8,128)(2,1)S(1)}, bf16[2048,128]{1,0:T(8,128)(2,1)}, u32[]{:S(2)}) copy-start(bf16[2048,128]{1,0:T(8,128)(2,1)} %get-tuple-element.76) | copy-start | bytes 1572868
  15.4 29.2 %copy-start.27 = (bf16[2048,128]{1,0:T(8,128)(2,1)S(1)}, bf16[2048,128]{1,0:T(8,128)(2,1)}, u32[]{:S(2)}) copy-start(bf16[2048,128]{1,0:T(8,128)(2,1)} %get-tuple-element.77) | copy-start | bytes 1572868
  15.4 32.9 %copy-start.7 = (f32[8,2048]{1,0:T(8,128)S(1)}, f32[8,2048]{1,0:T(8,128)}, u32[]{:S(2)}) copy-start(f32[8,2048]{1,0:T(8,128)} %get-tuple-element.70.first_ref) | copy-start | bytes 196612
  23.8 11.8 %collective-permute-start = (bf16[32,2048]{1,0:T(8,128)(2,1)}, bf16[32,2048]{1,0:T(8,128)(2,1)S(1)}, u32[]{:S(2)}, u32[]{:S(2)}) collective-permute-start(bf16[32,2048]{1,0:T(8,128)(2,1)} %get-tuple-element.60), channel_id=1, source_target_pairs={{0,2},{1,3},{2,4},{3,5},{4,6},{5,7},{6,8},{7,9},{8,10},{9,11},{10,... | collective-permute-start | bytes 393224 | tf_op jit(solution)/shard_map/ppermute | solution.py:409
  26.9 8.6 %collective-permute-start.1 = (bf16[32,2048]{1,0:T(8,128)(2,1)}, bf16[32,2048]{1,0:T(8,128)(2,1)S(1)}, u32[]{:S(2)}, u32[]{:S(2)}) collective-permute-start(bf16[32,2048]{1,0:T(8,128)(2,1)} %get-tuple-element.62), channel_id=1, source_target_pairs={{0,14},{1,15},{2,0},{3,1},{4,2},{5,3},{6,4},{7,5},{8,6},{9,7},{10,... | collective-permute-start | bytes 393224 | tf_op jit(solution)/shard_map/ppermute | solution.py:409
  27.0 8.6 %collective-permute-start.2 = (f32[8,2048]{1,0:T(8,128)S(1)}, f32[8,2048]{1,0:T(8,128)S(1)}, u32[]{:S(2)}, u32[]{:S(2)}) collective-permute-start(f32[8,2048]{1,0:T(8,128)S(1)} %copy-done.8), channel_id=1, source_target_pairs={{0,1},{1,2},{2,3},{3,4},{4,5},{5,6},{6,7},{7,8},{8,9},{9,10},{10,1... | collective-permute-start | bytes 196616 | tf_op jit(solution)/shard_map/ppermute | solution.py:424
  38.2 21.6 %collective-permute-start.3 = (bf16[64,2048]{1,0:T(8,128)(2,1)}, bf16[64,2048]{1,0:T(8,128)(2,1)S(1)}, u32[]{:S(2)}, u32[]{:S(2)}) collective-permute-start(bf16[64,2048]{1,0:T(8,128)(2,1)} %get-tuple-element.66), channel_id=1, source_target_pairs={{0,2},{1,3},{2,4},{3,5},{4,6},{5,7},{6,8},{7,9},{8,10},{9,11},{10,... | collective-permute-start | bytes 786440 | tf_op jit(solution)/shard_map/ppermute | solution.py:409
  42.7 17.2 %collective-permute-start.4 = (bf16[64,2048]{1,0:T(8,128)(2,1)}, bf16[64,2048]{1,0:T(8,128)(2,1)S(1)}, u32[]{:S(2)}, u32[]{:S(2)}) collective-permute-start(bf16[64,2048]{1,0:T(8,128)(2,1)} %get-tuple-element.68), channel_id=1, source_target_pairs={{0,14},{1,15},{2,0},{3,1},{4,2},{5,3},{6,4},{7,5},{8,6},{9,7},{10,... | collective-permute-start | bytes 786440 | tf_op jit(solution)/shard_map/ppermute | solution.py:409
  42.7 33.9 %collective-permute-start.8 = (bf16[2048,128]{1,0:T(8,128)(2,1)S(1)}, bf16[2048,128]{1,0:T(8,128)(2,1)S(1)}, u32[]{:S(2)}, u32[]{:S(2)}) collective-permute-start(bf16[2048,128]{1,0:T(8,128)(2,1)S(1)} %copy-done.28), channel_id=1, source_target_pairs={{0,16},{16,32},{32,48},{48,64},{64,80},{80,96},{96,112},{112,128},... | collective-permute-start | bytes 1572872 | tf_op jit(solution)/shard_map/ppermute | solution.py:431
  44.6 31.9 %collective-permute-start.9 = (bf16[2048,128]{1,0:T(8,128)(2,1)S(1)}, bf16[2048,128]{1,0:T(8,128)(2,1)S(1)}, u32[]{:S(2)}, u32[]{:S(2)}) collective-permute-start(bf16[2048,128]{1,0:T(8,128)(2,1)S(1)} %copy-done.27), channel_id=1, source_target_pairs={{16,0},{32,16},{48,32},{64,48},{80,64},{96,80},{112,96},{128,112},... | collective-permute-start | bytes 1572872 | tf_op jit(solution)/shard_map/ppermute | solution.py:432
  48.2 11.5 %collective-permute-start.5 = (f32[8,2048]{1,0:T(8,128)S(1)}, f32[8,2048]{1,0:T(8,128)S(1)}, u32[]{:S(2)}, u32[]{:S(2)}) collective-permute-start(f32[8,2048]{1,0:T(8,128)S(1)} %copy-done.7), channel_id=1, source_target_pairs={{1,0},{2,1},{3,2},{4,3},{5,4},{6,5},{7,6},{8,7},{9,8},{10,9},{11,1... | collective-permute-start | bytes 196616 | tf_op jit(solution)/shard_map/ppermute | solution.py:425
  62.7 11.0 %collective-permute-start.6 = (bf16[64,2048]{1,0:T(8,128)(2,1)}, bf16[64,2048]{1,0:T(8,128)(2,1)S(1)}, u32[]{:S(2)}, u32[]{:S(2)}) collective-permute-start(bf16[64,2048]{1,0:T(8,128)(2,1)} %get-tuple-element.72), channel_id=1, source_target_pairs={{0,2},{1,3},{2,4},{3,5},{4,6},{5,7},{6,8},{7,9},{8,10},{9,11},{10,... | collective-permute-start | bytes 786440 | tf_op jit(solution)/shard_map/ppermute | solution.py:409
  65.9 10.6 %collective-permute-start.7 = (bf16[64,2048]{1,0:T(8,128)(2,1)}, bf16[64,2048]{1,0:T(8,128)(2,1)S(1)}, u32[]{:S(2)}, u32[]{:S(2)}) collective-permute-start(bf16[64,2048]{1,0:T(8,128)(2,1)} %get-tuple-element.74), channel_id=1, source_target_pairs={{0,14},{1,15},{2,0},{3,1},{4,2},{5,3},{6,4},{7,5},{8,6},{9,7},{10,... | collective-permute-start | bytes 786440 | tf_op jit(solution)/shard_map/ppermute | solution.py:409
  65.9 18.4 %all-to-all-start.1 = ((bf16[16,4,16,128]{3,2,1,0:T(8,128)(2,1)}), bf16[16,4,16,128]{3,2,1,0:T(8,128)(2,1)S(1)}, u32[]{:S(2)}, u32[]{:S(2)}) async-start(bf16[16,4,16,128]{3,2,1,0:T(8,128)(2,1)} %copy-done.10), calls=%async_computation.1 | async-start | bytes 524288 | tf_op jit(solution)/shard_map/all_to_all | solution.py:437
  79.6 6.6 %collective-permute-start.10 = (bf16[64,2048]{1,0:T(8,128)(2,1)}, bf16[64,2048]{1,0:T(8,128)(2,1)S(1)}, u32[]{:S(2)}, u32[]{:S(2)}) collective-permute-start(bf16[64,2048]{1,0:T(8,128)(2,1)} %get-tuple-element.78), channel_id=1, source_target_pairs={{0,2},{1,3},{2,4},{3,5},{4,6},{5,7},{6,8},{7,9},{8,10},{9,11},{10,... | collective-permute-start | bytes 786440 | tf_op jit(solution)/shard_map/ppermute | solution.py:409
  79.7 7.8 %collective-permute-start.11 = (bf16[64,2048]{1,0:T(8,128)(2,1)}, bf16[64,2048]{1,0:T(8,128)(2,1)S(1)}, u32[]{:S(2)}, u32[]{:S(2)}) collective-permute-start(bf16[64,2048]{1,0:T(8,128)(2,1)} %get-tuple-element.79), channel_id=1, source_target_pairs={{0,14},{1,15},{2,0},{3,1},{4,2},{5,3},{6,4},{7,5},{8,6},{9,7},{10,... | collective-permute-start | bytes 786440 | tf_op jit(solution)/shard_map/ppermute | solution.py:409
  90.2 9.0 %collective-permute-start.12 = (bf16[32,2048]{1,0:T(8,128)(2,1)}, bf16[32,2048]{1,0:T(8,128)(2,1)S(1)}, u32[]{:S(2)}, u32[]{:S(2)}) collective-permute-start(bf16[32,2048]{1,0:T(8,128)(2,1)} %get-tuple-element.83.refs_0_), channel_id=1, source_target_pairs={{0,1},{1,0},{2,3},{3,2},{4,5},{5,4},{6,7},{7,6},{8,9},{9,8},{10,11... | collective-permute-start | bytes 393224 | tf_op jit(solution)/shard_map/ppermute | solution.py:412
  102.5 6.7 %collective-permute-start.13 = (bf16[32,2048]{1,0:T(8,128)(2,1)}, bf16[32,2048]{1,0:T(8,128)(2,1)S(1)}, u32[]{:S(2)}, u32[]{:S(2)}) collective-permute-start(bf16[32,2048]{1,0:T(8,128)(2,1)} %residual_images.1.refs_0_), channel_id=1, source_target_pairs={{0,1},{1,0},{2,3},{3,2},{4,5},{5,4},{6,7},{7,6},{8,9},{9,8},{10,11... | collective-permute-start | bytes 393224 | tf_op jit(solution)/shard_map/ppermute | solution.py:412
  109.2 9.0 %collective-permute-start.14 = (bf16[64,2048]{1,0:T(8,128)(2,1)S(1)}, bf16[64,2048]{1,0:T(8,128)(2,1)S(1)}, u32[]{:S(2)}, u32[]{:S(2)}) collective-permute-start(bf16[64,2048]{1,0:T(8,128)(2,1)S(1)} %pad_maximum_fusion.refs_0_), channel_id=1, source_target_pairs={{0,14},{1,15},{2,0},{3,1},{4,2},{5,3},{6,4},{7,5},{8,6},{9,7},{10,... | collective-permute-start | bytes 786440 | tf_op jit(solution)/shard_map/ppermute | solution.py:409
  109.7 8.6 %collective-permute-start.15 = (bf16[64,2048]{1,0:T(8,128)(2,1)S(1)}, bf16[64,2048]{1,0:T(8,128)(2,1)S(1)}, u32[]{:S(2)}, u32[]{:S(2)}) collective-permute-start(bf16[64,2048]{1,0:T(8,128)(2,1)S(1)} %pad_maximum_fusion.refs_0_), channel_id=1, source_target_pairs={{0,2},{1,3},{2,4},{3,5},{4,6},{5,7},{6,8},{7,9},{8,10},{9,11},{10,... | collective-permute-start | bytes 786440 | tf_op jit(solution)/shard_map/ppermute | solution.py:409
  118.2 28.1 %copy-start.13 = (bf16[64,2048]{1,0:T(8,128)(2,1)}, bf16[64,2048]{1,0:T(8,128)(2,1)S(1)}, u32[]{:S(2)}) copy-start(bf16[64,2048]{1,0:T(8,128)(2,1)S(1)} %collective-permute-done.14.refs_1_) | copy-start | bytes 786436
  118.2 13.5 %copy-start.9 = (bf16[64,2048]{1,0:T(8,128)(2,1)}, bf16[64,2048]{1,0:T(8,128)(2,1)S(1)}, u32[]{:S(2)}) copy-start(bf16[64,2048]{1,0:T(8,128)(2,1)S(1)} %collective-permute-done.15.refs_0_.refs_2_) | copy-start | bytes 786436
  118.2 10.2 %collective-permute-start.16 = (bf16[64,2048]{1,0:T(8,128)(2,1)S(1)}, bf16[64,2048]{1,0:T(8,128)(2,1)S(1)}, u32[]{:S(2)}, u32[]{:S(2)}) collective-permute-start(bf16[64,2048]{1,0:T(8,128)(2,1)S(1)} %collective-permute-done.14.refs_1_), channel_id=1, source_target_pairs={{0,14},{1,15},{2,0},{3,1},{4,2},{5,3},{6,4},{7,5},{8,6},{9,7},{10,... | collective-permute-start | bytes 786440 | tf_op jit(solution)/shard_map/ppermute | solution.py:409
  118.3 10.2 %collective-permute-start.17 = (bf16[64,2048]{1,0:T(8,128)(2,1)S(1)}, bf16[64,2048]{1,0:T(8,128)(2,1)S(1)}, u32[]{:S(2)}, u32[]{:S(2)}) collective-permute-start(bf16[64,2048]{1,0:T(8,128)(2,1)S(1)} %collective-permute-done.15.refs_0_.refs_2_), channel_id=1, source_target_pairs={{0,2},{1,3},{2,4},{3,5},{4,6},{5,7},{6,8},{7,9},{8,10},{9,11},{10,... | collective-permute-start | bytes 786440 | tf_op jit(solution)/shard_map/ppermute | solution.py:409
  128.5 8.8 %collective-permute-start.18 = (bf16[64,2048]{1,0:T(8,128)(2,1)S(1)}, bf16[64,2048]{1,0:T(8,128)(2,1)S(1)}, u32[]{:S(2)}, u32[]{:S(2)}) collective-permute-start(bf16[64,2048]{1,0:T(8,128)(2,1)S(1)} %collective-permute-done.16.refs_3_), channel_id=1, source_target_pairs={{0,14},{1,15},{2,0},{3,1},{4,2},{5,3},{6,4},{7,5},{8,6},{9,7},{10,... | collective-permute-start | bytes 786440 | tf_op jit(solution)/shard_map/ppermute | solution.py:409
  128.5 8.8 %collective-permute-start.19 = (bf16[64,2048]{1,0:T(8,128)(2,1)S(1)}, bf16[64,2048]{1,0:T(8,128)(2,1)S(1)}, u32[]{:S(2)}, u32[]{:S(2)}) collective-permute-start(bf16[64,2048]{1,0:T(8,128)(2,1)S(1)} %collective-permute-done.17.refs_4_), channel_id=1, source_target_pairs={{0,2},{1,3},{2,4},{3,5},{4,6},{5,7},{6,8},{7,9},{8,10},{9,11},{10,... | collective-permute-start | bytes 786440 | tf_op jit(solution)/shard_map/ppermute | solution.py:409
  137.2 9.1 %copy-start.11 = (bf16[64,2048]{1,0:T(8,128)(2,1)}, bf16[64,2048]{1,0:T(8,128)(2,1)S(1)}, u32[]{:S(2)}) copy-start(bf16[64,2048]{1,0:T(8,128)(2,1)S(1)} %collective-permute-done.18.refs_5_) | copy-start | bytes 786436
  137.3 9.1 %copy-start.12 = (bf16[64,2048]{1,0:T(8,128)(2,1)}, bf16[64,2048]{1,0:T(8,128)(2,1)S(1)}, u32[]{:S(2)}) copy-start(bf16[64,2048]{1,0:T(8,128)(2,1)S(1)} %collective-permute-done.19.refs_6_) | copy-start | bytes 786436
  137.3 5.3 %collective-permute-start.20 = (bf16[32,2048]{1,0:T(8,128)(2,1)S(1)}, bf16[32,2048]{1,0:T(8,128)(2,1)S(1)}, u32[]{:S(2)}, u32[]{:S(2)}) collective-permute-start(bf16[32,2048]{1,0:T(8,128)(2,1)S(1)} %slice.6), channel_id=1, source_target_pairs={{0,2},{1,3},{2,4},{3,5},{4,6},{5,7},{6,8},{7,9},{8,10},{9,11},{10,... | collective-permute-start | bytes 393224 | tf_op jit(solution)/shard_map/ppermute | solution.py:409
  140.0 6.3 %collective-permute-start.21 = (bf16[32,2048]{1,0:T(8,128)(2,1)S(1)}, bf16[32,2048]{1,0:T(8,128)(2,1)S(1)}, u32[]{:S(2)}, u32[]{:S(2)}) collective-permute-start(bf16[32,2048]{1,0:T(8,128)(2,1)S(1)} %slice.7), channel_id=1, source_target_pairs={{0,14},{1,15},{2,0},{3,1},{4,2},{5,3},{6,4},{7,5},{8,6},{9,7},{10,... | collective-permute-start | bytes 393224 | tf_op jit(solution)/shard_map/ppermute | solution.py:409
  (21 other events, 48.3 us)

commit v2 on v1

v2 whole, which is shorter than its diff:
```python
import functools

import jax
import jax.numpy as jnp
from jax import lax
from jax.experimental import pallas as pl
from jax.experimental.pallas import tpu as pltpu
from jax.sharding import PartitionSpec as P

BAND = 128
BATCHES = 2
CAPP = 2
SLOTS = BATCHES * CAPP
ROWS = 16
RUN = SLOTS * 8
PAIR = 2 * RUN
LINES = 16
PIECES = 4


def limit(mib):
    return pltpu.CompilerParams(vmem_limit_bytes=mib << 20)

XT = 256
F32 = jnp.float32
BF16 = jnp.bfloat16
VMEM = pl.BlockSpec(memory_space=pltpu.VMEM)
SMEM = pl.BlockSpec(memory_space=pltpu.SMEM)
ANY = pl.BlockSpec(memory_space=pl.ANY)


def cost(flops, moved):
    return pl.CostEstimate(flops=flops, bytes_accessed=moved, transcendentals=0)


def iota(shape, dim):
    return lax.broadcasted_iota(jnp.int32, shape, dim)


def pack_kernel(owner_ref, offset_ref, width_ref, weight_ref, measured_ref, out_ref, count_ref):
    out_ref[...] = jnp.zeros_like(out_ref)
    slabs = out_ref.shape[0]
    views = owner_ref.shape[1]
    row = iota((ROWS, BAND), 0)
    lane = iota((ROWS, BAND), 1)
    empty = jnp.zeros((8, BAND), F32)
    for batch in range(BATCHES):
        for slab in range(slabs):
            count_ref[slab] = 0
        for view in range(views):
            owner = owner_ref[batch, view]
            rank = count_ref[owner]
            count_ref[owner] = rank + 1
            rows = jnp.concatenate([measured_ref[batch, view].astype(F32), empty], axis=0)
            band = jnp.where(
                lane == 0,
                offset_ref[batch, view].astype(F32),
                jnp.where(lane == 1, width_ref[batch, view].astype(F32), 0.0),
            )
            rows = jnp.where(row == 8, weight_ref[view].astype(F32)[batch : batch + 1], jnp.where(row == 9, band, rows))
            out_ref[owner, batch * CAPP + rank] = rows.astype(BF16)


def pack(owner, offset, width, weight, measured, slabs):
    return pl.pallas_call(
        pack_kernel,
        out_shape=jax.ShapeDtypeStruct((slabs, SLOTS, ROWS, BAND), BF16),
        in_specs=[SMEM, SMEM, SMEM, VMEM, VMEM],
        out_specs=VMEM,
        scratch_shapes=[pltpu.SMEM((slabs,), jnp.int32)],
        name="pack_messages",
    )(owner, offset, width, jnp.transpose(weight, (1, 0, 2)), measured)


def joined(block):
    return jnp.concatenate([block[z] for z in range(block.shape[0])], axis=1)


def spread_weights(tiles, out_ref, first, depth):
    rows = tiles.shape[0] * depth
    weights = jnp.broadcast_to(
        tiles.astype(F32)[:, 8:9, :], (tiles.shape[0], depth, BAND)
    ).reshape(rows, BAND)
    slice_of = lax.rem(iota((rows, BAND), 0), depth)
    for z in range(depth):
        out_ref[first : first + rows, z * BAND : (z + 1) * BAND] = jnp.where(
            slice_of == z, weights, 0.0
        ).astype(BF16)


def hops(tiles):
    half = tiles // 4
    return [0] + [sign * hop for hop in range(1, half) for sign in (1, -1)] + [half]


def fill_spread(tiles, me, got_ref, spread_ref):
    row = 0
    for hop in hops(tiles):
        tile = lax.rem(me + 2 * hop + tiles, tiles)
        for source in (tile, tile ^ 1):
            spread_weights(got_ref[pl.ds(source * SLOTS, SLOTS)], spread_ref, row, 8)
            row += RUN
    shape = (LINES, spread_ref.shape[1])
    line = iota(shape, 0)
    target = jnp.where(line < 8, line * BAND, (line - 8) * BAND + BAND - 1)
    spread_ref[row:] = jnp.where(iota(shape, 1) == target, 1.0, 0.0).astype(BF16)


def spread_kernel(tiles, place_ref, got_ref, order_ref, out_ref):
    fill_spread(tiles, place_ref[1], got_ref, out_ref)


def spread_rows(place, got, tiles, order):
    shape = (got.shape[0] * 8 + LINES, 8 * BAND)
    return pl.pallas_call(
        functools.partial(spread_kernel, tiles),
        out_shape=jax.ShapeDtypeStruct(shape, BF16),
        in_specs=[SMEM, VMEM, ANY],
        out_specs=VMEM,
        compiler_params=limit(16),
        cost_estimate=cost(4 * shape[0] * shape[1], 4 * shape[0] * shape[1]),
        name="spread_rows",
    )(place, got, order)


def forward_kernel(tiles, place_ref, got_ref, volume_ref, *refs):
    outs, spread_ref = refs[:-1], refs[-1]

    @pl.when(pl.program_id(0) == 0)
    def _():
        fill_spread(tiles, place_ref[1], got_ref, spread_ref)

    out = lax.dot_general(
        spread_ref[...], joined(volume_ref), (((1,), (1,)), ((), ())), preferred_element_type=F32
    ).astype(BF16)
    row = 0
    for ref in outs:
        count = min(ref.shape[0], PAIR)
        ref[:count] = out[row : row + count]
        if ref.shape[0] > PAIR:
            ref[PAIR:] = out[-LINES:]
        row += count


def forward(place, got, volume, tiles, *order):
    depth, extent, strip = volume.shape
    slots = got.shape[0]
    rows = [PAIR] + [PAIR + LINES] * 2 + [PAIR] * (tiles // 2 - 4) + [RUN] * 2

    def kernel(place_ref, got_ref, volume_ref, *refs):
        forward_kernel(tiles, place_ref, got_ref, volume_ref, *refs[len(order) :])

    return pl.pallas_call(
        kernel,
        grid=(extent // XT,),
        out_shape=[jax.ShapeDtypeStruct((count, extent), BF16) for count in rows],
        in_specs=[
            SMEM,
            pl.BlockSpec(got.shape, lambda i: (0, 0, 0)),
            pl.BlockSpec((depth, XT, strip), lambda i: (0, i, 0)),
        ]
        + [ANY] * len(order),
        out_specs=[pl.BlockSpec((count, XT), lambda i: (0, i)) for count in rows],
        scratch_shapes=[pltpu.VMEM((slots * depth + LINES, depth * strip), BF16)],
        cost_estimate=cost(2 * slots * depth * volume.size, 3 * volume.size),
        name="forward",
    )(place, got, volume, *order)


def sums_kernel(up_ref, up_near_ref, up_far_ref, down_ref, down_near_ref, down_far_ref, *refs):
    up_out_ref, down_out_ref = refs[-2:]

    def add(*parts):
        return functools.reduce(jnp.add, [part.astype(F32) for part in parts]).astype(BF16)

    up_out_ref[:RUN] = add(up_ref[:RUN], up_near_ref[:RUN], up_far_ref[...])
    up_out_ref[RUN:] = add(up_ref[RUN:], up_near_ref[RUN:])
    down_out_ref[:RUN] = add(down_ref[:RUN], down_near_ref[:RUN])
    down_out_ref[RUN:] = add(down_ref[RUN:], down_near_ref[RUN:], down_far_ref[...])


def round_sums(*operands):
    out = jax.ShapeDtypeStruct(operands[0].shape, BF16)
    return pl.pallas_call(
        sums_kernel,
        out_shape=(out, out),
        in_specs=[VMEM] * 6 + [ANY] * (len(operands) - 6),
        out_specs=(VMEM, VMEM),
        compiler_params=limit(16),
        cost_estimate=cost(6 * out.size, 14 * out.size),
        name="round_sums",
    )(*operands)


def last_sums_kernel(
    place_ref, own_ref, mine_ref, below_ref, above_ref, up_ref, down_ref, *refs
):
    kept_ref, sent_ref = refs[-2:]
    total = (
        own_ref[...].astype(F32)
        + below_ref[:PAIR].astype(F32)
        + above_ref[:PAIR].astype(F32)
        + up_ref[...].astype(F32)
        + down_ref[...].astype(F32)
    )
    kept_ref[...] = total[:RUN]
    sent_ref[:RUN] = total[RUN:].astype(BF16)
    mine, below, above = [ref[PAIR:].astype(F32) for ref in (mine_ref, below_ref, above_ref)]
    even = place_ref[1] % 2 == 0
    left = jnp.where(even, mine[8:], below[8:])
    right = jnp.where(even, above[:8], mine[:8])
    sent_ref[RUN:] = jnp.concatenate([left, right], axis=0).astype(BF16)


def last_sums(place, own, mine, below, above, up, down, *order):
    extent = own.shape[1]
    return pl.pallas_call(
        last_sums_kernel,
        out_shape=(
            jax.ShapeDtypeStruct((RUN, extent), F32),
            jax.ShapeDtypeStruct((RUN + LINES, extent), BF16),
        ),
        in_specs=[SMEM] + [VMEM] * 6 + [ANY] * len(order),
        out_specs=(VMEM, VMEM),
        compiler_params=limit(16),
        cost_estimate=cost(5 * own.size, 14 * own.size),
        name="last_sums",
    )(place, own, mine, below, above, up, down, *order)


def residual_kernel(kept_ref, arrived_ref, views_ref, *refs):
    out_ref = refs[-1]
    extent = kept_ref.shape[1]
    blocks = extent // BAND
    empty = jnp.zeros((8, BAND), F32)
    arrived = arrived_ref[:RUN].astype(F32)
    for slot in range(SLOTS):
        low = slot * 8
        total = kept_ref[low : low + 8] + arrived[low : low + 8]
        band = views_ref[0, slot].astype(F32)
        offset = band[9:10, 0:1].astype(jnp.int32)
        width = jnp.maximum(band[9:10, 1:2], 1.0)
        recip = 1.0 / width
        width = width.astype(jnp.int32)

        def inside(delta):
            delta = delta - offset
            return jnp.where((delta >= 0) & (delta < width), recip, 0.0).astype(BF16)

        shape = (2 * BAND, BAND)
        onward = inside(iota(shape, 1) + BAND - iota(shape, 0))
        back = inside(iota(shape, 0) - iota(shape, 1))
        parts = [total[:, n * BAND : (n + 1) * BAND] for n in range(blocks)]
        here = jnp.concatenate(parts, axis=0)
        before = jnp.concatenate([empty] + parts[:-1], axis=0)
        paired = jnp.concatenate([before, here], axis=1)
        high = paired.astype(BF16)
        rest = (paired - high.astype(F32)).astype(BF16)
        sums = jnp.dot(high, onward, preferred_element_type=F32) + jnp.dot(
            rest, onward, preferred_element_type=F32
        )
        rows = jnp.concatenate(
            [views_ref[n, slot].astype(F32)[:8] for n in range(blocks)], axis=0
        )
        residual = (sums - rows).astype(BF16).astype(F32)
        later = jnp.concatenate([residual[8:], empty], axis=0)
        both = jnp.concatenate([residual, later], axis=1).astype(BF16)
        image = jnp.dot(both, back, preferred_element_type=F32)
        image = jnp.concatenate([image[n * 8 : (n + 1) * 8] for n in range(blocks)], axis=1)
        if slot % 2 == 0:
            even = image
        else:
            out_ref[low - 8 : low + 8] = jnp.concatenate([even, image], axis=0).astype(BF16)


def residual_images(kept, arrived, views, *order):
    return pl.pallas_call(
        residual_kernel,
        out_shape=jax.ShapeDtypeStruct(kept.shape, BF16),
        in_specs=[VMEM] * 3 + [ANY] * len(order),
        out_specs=VMEM,
        compiler_params=limit(16),
        cost_estimate=cost(4 * 8 * 16 * 256 * 128 * 6, 2 * views.size),
        name="residual_images",
    )(kept, arrived, views, *order)


def penalty(diff):
    return diff * lax.rsqrt(1.0 + diff * diff)


def regularizer_kernel(
    first_tile,
    count,
    place_ref,
    beta_ref,
    block_ref,
    before_ref,
    after_ref,
    below_ref,
    above_ref,
    *refs,
):
    out_ref, under_ref = refs[-2:]
    depth, tile, strip = block_ref.shape
    at = pl.program_id(0) + first_tile
    beta = beta_ref[0]
    has_below = (place_ref[0] > 0).astype(F32)
    has_above = (place_ref[0] < place_ref[3] - 1).astype(F32)
    has_before = (at > 0).astype(F32)
    has_after = (at < count - 1).astype(F32)
    under_ref[...] = penalty(block_ref[0].astype(F32) - below_ref[0].astype(F32)) * has_below
    row = iota((tile, strip), 0)
    lane = iota((tile, strip), 1)

    def body(z, carry):
        center = block_ref[z].astype(F32)
        top = z == depth - 1
        upper = jnp.where(top, above_ref[0], block_ref[jnp.minimum(z + 1, depth - 1)])
        over = penalty(upper.astype(F32) - center) * jnp.where(top, has_above, 1.0)
        total = under_ref[...] - over
        under_ref[...] = over
        ahead = after_ref[z].astype(F32)[0:1]
        behind = penalty(center[0:1] - before_ref[z].astype(F32)[15:16]) * has_before
        along = penalty(jnp.where(row == tile - 1, ahead, pltpu.roll(center, tile - 1, 0)) - center)
        along = jnp.where(row == tile - 1, along * has_after, along)
        total = total + jnp.where(row == 0, behind, pltpu.roll(along, 1, 0)) - along
        across = penalty(pltpu.roll(center, strip - 1, 1) - center)
        across = jnp.where(lane == strip - 1, 0.0, across)
        total = total + pltpu.roll(across, 1, 1) - across
        out_ref[z] = (total * beta).astype(BF16)
        return carry

    lax.fori_loop(0, depth, body, 0, unroll=2)


def regularizer(index, done, place, beta, volume, below, above, *order):
    depth, extent, strip = volume.shape
    count = extent // XT
    length = count // PIECES
    start = index * length
    edge = XT // 16
    plane = pl.BlockSpec((1, XT, strip), lambda i: (0, start + i, 0))
    block = pl.BlockSpec((depth, XT, strip), lambda i: (0, start + i, 0))
    ends = [
        lambda i: (0, jnp.maximum((start + i) * edge - 1, 0), 0),
        lambda i: (0, jnp.minimum((start + i + 1) * edge, count * edge - 1), 0),
    ]
    specs = [SMEM, SMEM, block]
    specs += [pl.BlockSpec((depth, 16, strip), where) for where in ends]
    specs += [plane] * 2 + [ANY] * len(order)
    before = [] if done is None else [done]
    return pl.pallas_call(
        functools.partial(regularizer_kernel, start, count),
        grid=(length,),
        out_shape=jax.ShapeDtypeStruct(volume.shape, BF16),
        in_specs=specs + [ANY] * len(before),
        out_specs=block,
        scratch_shapes=[pltpu.VMEM((XT, strip), F32)],
        input_output_aliases={len(specs): 0} if before else {},
        cost_estimate=cost(30 * volume.size // PIECES, 8 * volume.size // PIECES),
        name="regularizer",
    )(place, beta, volume, volume, volume, below, above, *order, *before)


def gradient_kernel(place_ref, beta_ref, spread_ref, mine_ref, beside_ref, *refs):
    chunk_refs = refs[:-2]
    regular_ref, out_ref = refs[-2:]
    depth, tile, strip = out_ref.shape
    beta = beta_ref[0]
    has_left = (place_ref[1] > 0).astype(F32)
    has_right = (place_ref[1] < place_ref[2] - 1).astype(F32)
    mine, beside = mine_ref[...].astype(F32), beside_ref[...].astype(F32)
    on_left = penalty(mine[:8] - beside[:8]) * (has_left * beta)
    on_right = penalty(mine[8:] - beside[8:]) * (has_right * beta)
    ends = jnp.concatenate([on_left, on_right], axis=0).astype(BF16)
    rows = jnp.concatenate([ref[...] for ref in chunk_refs] + [ends], axis=0)
    out = lax.dot_general(
        rows, spread_ref[...], (((0,), (0,)), ((), ())), preferred_element_type=F32
    )
    for z in range(depth):
        regular = regular_ref[z].astype(F32)
        out_ref[z] = (out[:, z * strip : (z + 1) * strip] + regular).astype(BF16)


def gradient(place, beta, spread, mine, arrived, chunks, regular):
    depth, extent, strip = regular.shape
    block = pl.BlockSpec((depth, XT, strip), lambda i: (0, i, 0))
    size = depth * extent * strip
    return pl.pallas_call(
        gradient_kernel,
        grid=(extent // XT,),
        out_shape=jax.ShapeDtypeStruct(regular.shape, BF16),
        in_specs=[
            SMEM,
            SMEM,
            pl.BlockSpec(spread.shape, lambda i: (0, 0)),
            pl.BlockSpec((LINES, XT), lambda i: (PAIR // LINES, i)),
            pl.BlockSpec((LINES, XT), lambda i: (RUN // LINES, i)),
        ]
        + [pl.BlockSpec((chunk.shape[0], XT), lambda i: (0, i)) for chunk in chunks]
        + [block],
        out_specs=block,
        compiler_params=limit(16),
        cost_estimate=cost(2 * spread.shape[0] * size, 5 * size),
        name="gradient",
    )(place, beta, spread, mine, arrived, *chunks, regular)


def shards(volume, measured, ray_weight, view_owner, band_offset, band_width, beta):
    slabs = lax.axis_size("slab")
    tiles = lax.axis_size("tile")
    slab, tile = lax.axis_index("slab"), lax.axis_index("tile")
    depth = volume.shape[0]
    place = jnp.stack([slab, tile, jnp.int32(tiles), jnp.int32(slabs)])

    def along_z(block, by):
        return lax.ppermute(block, "tile", [(i, (i + 2 * by) % tiles) for i in range(tiles)])

    def along_y(block):
        return lax.ppermute(block, "tile", [(i, i ^ 1) for i in range(tiles)])

    packed = pack(view_owner[:, :, 0], band_offset, band_width, ray_weight, measured, slabs)
    packed, after = lax.optimization_barrier((packed, volume))
    got = lax.all_to_all(packed, "slab", split_axis=0, concat_axis=0, tiled=True)
    top, bottom = after[depth - 1 :], after[:1]
    below = lax.ppermute(top, "slab", [(i, i + 1) for i in range(slabs - 1)])
    above = lax.ppermute(bottom, "slab", [(i + 1, i) for i in range(slabs - 1)])
    flat = got.reshape(slabs * SLOTS, ROWS, BAND)

    own, up1, down1, up2, down2, up3, down3, far_up, far_down = forward(
        place, flat, volume, tiles, top, bottom
    )
    mine = up1
    near = along_z(up3, 1), along_z(down3, -1)
    far = along_z(far_up, 2), along_z(far_down, -2)
    one = along_z(up1, 1), along_z(down1, -1)
    regular = regularizer(0, None, place, beta, volume, below, above, far_up)
    up, down = round_sums(up2, near[0], far[0], down2, near[1], far[1], regular)
    got, up = lax.optimization_barrier((got, up))
    two = along_z(up, 2), along_z(down, -2)
    views = lax.all_to_all(got, "tile", split_axis=0, concat_axis=0, tiled=True)
    kept, sent = last_sums(place, own, up1, *one, *two, views)
    arrived = along_y(sent)
    regular = regularizer(1, regular, place, beta, volume, below, above, sent)
    images = residual_images(kept, arrived, views, regular)

    partner = along_y(images)
    regular = regularizer(2, regular, place, beta, volume, below, above, images)
    pair = jnp.concatenate([images, partner], axis=0)
    pair, regular = lax.optimization_barrier((pair, regular))
    up2, down2 = along_z(pair, 2), along_z(pair, -2)
    up1, down1 = along_z(pair, 1), along_z(pair, -1)
    spread = spread_rows(place, flat, tiles, pair)
    regular = regularizer(3, regular, place, beta, volume, below, above, pair, spread)
    up2, down2, regular = lax.optimization_barrier((up2, down2, regular))
    up3, down3 = along_z(up2, 1), along_z(down2, -1)
    far_up, far_down = along_z(up2[:RUN], 2), along_z(down2[RUN:], -2)
    chunks = [pair, down1, up1, down2, up2, down3, up3, far_up, far_down]
    return gradient(place, beta, spread, mine, arrived, chunks, regular)


def solution(mesh):
    in_specs = (
        P("slab", None, "tile"),
        P(None, "slab", None, "tile"),
        P(None, "slab", "tile"),
        P(None, "slab", None),
        P(None, "slab"),
        P(None, "slab"),
        P(),
    )
    out_specs = P("slab", None, "tile")
    return jax.shard_map(shards, mesh=mesh, in_specs=in_specs, out_specs=out_specs, check_vma=False)
```

time: 157 us -> 142 us (0.904)
  the two profiles are of different devices: /device:TPU:110 before, /device:TPU:8 now
where the time goes in v2:
time: 142 us; the launch traced here: 141 us
  starting transfers between devices  56.1 us (40%)
  Pallas kernels  39.1 us (28%)
  waiting for transfers between devices  31.2 us (22%)
  local copies, waits for them, and re-layouts  11.8 us (8%)
  other arithmetic  1.51 us (1%)
    ppermute x16, waiting for transfers between devices, along_z(): lax.ppermute(block, 'tile', [(i, (i + 2 * by) % tiles) for i in range(til...  31.2 us
    ppermute x16, starting transfers between devices, along_z(): lax.ppermute(block, 'tile', [(i, (i + 2 * by) % tiles) for i in range(til...  30.2 us
    pallas_call x4, Pallas kernels, regularizer(): pl.pallas_call(functools.partial(regularizer_kernel, start, count), grid=...  19.3 us
    unnamed x42, local copies, waits for them, and re-layouts  10.6 us
    all_to_all x1, starting transfers between devices, shards(): views = lax.all_to_all(got, 'tile', split_axis=0, concat_axis=0, tiled=True)  8.24 us
    pallas_call x1, Pallas kernels, forward(): pl.pallas_call(kernel, grid=(extent // XT,), out_shape=[jax.ShapeDtypeStr...  8.02 us
    pallas_call x1, Pallas kernels, gradient(): pl.pallas_call(gradient_kernel, grid=(extent // XT,), out_shape=jax.Shape...  7.24 us
    all_to_all x1, starting transfers between devices, shards(): lax.all_to_all(packed, 'slab', split_axis=0, concat_axis=0, tiled=True)  6.11 us
  transfers between devices with their start and end apart: 22, of which 10 were waited for; matrix products, arithmetic and copies ran while one was open for 1% of the time, Pallas kernels for 20%

profile of v2, /device:TPU:8, one launch (start us, length us, event | category | flops | bytes accessed | tf_op | source)
XLA Modules:
  0.0 140.7 jit_solution(17444808932221406970)
XLA Ops:
  0.0 1.7 %pack_messages.1 = bf16[16,4,16,128]{3,2,1,0:T(8,128)(2,1)} custom-call(s32[2,12]{1,0:T(2,128)} %bitcast.6, s32[2,12]{1,0:T(2,128)} %offset_ref.1, s32[2,12]{1,0:T(2,128)} %width_ref.1, bf16[12,2,128]{2,1,0:T(2,128)(2,1)} %bitcast.5, bf16[2,12,8,128]{3,2,1,0:T(8,128)(2,1)} %measured_ref.1), custom_call_target="tpu_custom_call" | custom-call | tf_op jit(solution)/shard_map/pack_messages/pallas_call | solution.py:65
  1.7 6.1 %all-to-all-start = ((bf16[16,4,16,128]{3,2,1,0:T(8,128)(2,1)}), bf16[16,4,16,128]{3,2,1,0:T(8,128)(2,1)}, u32[]{:S(2)}, u32[]{:S(2)}) async-start(bf16[16,4,16,128]{3,2,1,0:T(8,128)(2,1)} %pack_messages.1), calls=%async_computation | async-start | bytes 524288 | tf_op jit(solution)/shard_map/all_to_all | solution.py:425
  9.1 2.1 %collective-permute-start.6 = (bf16[1,2048,128]{2,1,0:T(8,128)(2,1)S(1)}, bf16[1,2048,128]{2,1,0:T(8,128)(2,1)S(1)}, u32[]{:S(2)}, u32[]{:S(2)}) collective-permute-start(bf16[1,2048,128]{2,1,0:T(8,128)(2,1)S(1)} %get-tuple-element.50.refs_0_), channel_id=1, source_target_pairs={{0,16},{16,32},{32,48},{48,64},{64,80},{80,96},{96,112},{112,128},... | collective-permute-start | bytes 1572872 | tf_op jit(solution)/shard_map/ppermute | solution.py:427
  11.1 3.5 %collective-permute-start.7 = (bf16[1,2048,128]{2,1,0:T(8,128)(2,1)S(1)}, bf16[1,2048,128]{2,1,0:T(8,128)(2,1)S(1)}, u32[]{:S(2)}, u32[]{:S(2)}) collective-permute-start(bf16[1,2048,128]{2,1,0:T(8,128)(2,1)S(1)} %get-tuple-element.49.refs_1_), channel_id=1, source_target_pairs={{16,0},{32,16},{48,32},{64,48},{80,64},{96,80},{112,96},{128,112},... | collective-permute-start | bytes 1572872 | tf_op jit(solution)/shard_map/ppermute | solution.py:428
  15.3 8.0 %forward.1 = (bf16[64,2048]{1,0:T(8,128)(2,1)}, bf16[80,2048]{1,0:T(8,128)(2,1)}, bf16[80,2048]{1,0:T(8,128)(2,1)}, bf16[64,2048]{1,0:T(8,128)(2,1)}, bf16[64,20...) custom-call(s32[4]{0:T(128)} %pad_add_fusion.place_ref, ...), custom_call_target="tpu_custom_call" | custom-call | flops 2147483648 | bytes 6291456 | tf_op jit(solution)/shard_map/forward/pallas_call | solution.py:153
  23.3 1.7 %collective-permute-start.2 = (bf16[64,2048]{1,0:T(8,128)(2,1)}, bf16[64,2048]{1,0:T(8,128)(2,1)S(1)}, u32[]{:S(2)}, u32[]{:S(2)}) collective-permute-start(bf16[64,2048]{1,0:T(8,128)(2,1)} %get-tuple-element.33), channel_id=1, source_target_pairs={{0,2},{1,3},{2,4},{3,5},{4,6},{5,7},{6,8},{7,9},{8,10},{9,11},{10,... | collective-permute-start | bytes 786440 | tf_op jit(solution)/shard_map/ppermute | solution.py:418
  25.0 4.0 %collective-permute-start.4 = (bf16[64,2048]{1,0:T(8,128)(2,1)}, bf16[64,2048]{1,0:T(8,128)(2,1)S(1)}, u32[]{:S(2)}, u32[]{:S(2)}) collective-permute-start(bf16[64,2048]{1,0:T(8,128)(2,1)} %get-tuple-element.36), channel_id=1, source_target_pairs={{0,14},{1,15},{2,0},{3,1},{4,2},{5,3},{6,4},{7,5},{8,6},{9,7},{10,... | collective-permute-start | bytes 786440 | tf_op jit(solution)/shard_map/ppermute | solution.py:418
  29.0 4.1 %collective-permute-start.5 = (bf16[32,2048]{1,0:T(8,128)(2,1)}, bf16[32,2048]{1,0:T(8,128)(2,1)S(1)}, u32[]{:S(2)}, u32[]{:S(2)}) collective-permute-start(bf16[32,2048]{1,0:T(8,128)(2,1)} %get-tuple-element.37), channel_id=1, source_target_pairs={{0,12},{1,13},{2,14},{3,15},{4,0},{5,1},{6,2},{7,3},{8,4},{9,5},{1... | collective-permute-start | bytes 393224 | tf_op jit(solution)/shard_map/ppermute | solution.py:418
  34.6 4.9 %regularizer.4.refs_0_.refs_1_ = bf16[8,2048,128]{2,1,0:T(8,128)(2,1)} custom-call(s32[4]{0:T(128)} %pad_add_fusion.place_ref, f32[1]{0:T(128)S(6)} %copy.14.beta_ref, bf16[8,2048,128]{2,1,0:T(8,128)(2,1)} %after_ref.7, bf16[8,2048,128]{2,1,0:T(8,128)(2,1)} %after_ref.7, bf16[8,2048,128]{2,1,0:T(8,128)(2,1)} %after_ref.7, bf16[1,2048,128]{2,1,0:T(8,128)(2,1)} %copy-done.16, ...), custom_call_target="tpu_custom_call" | custom-call | flops 15728640 | bytes 4194304 | tf_op jit(solution)/shard_map/regularizer/pallas_call | solution.py:353
  40.5 2.2 %copy-done = bf16[8,2048,128]{2,1,0:T(8,128)(2,1)S(1)} copy-done((bf16[8,2048,128]{2,1,0:T(8,128)(2,1)S(1)}, bf16[8,2048,128]{2,1,0:T(8,128)(2,1)}, u32[]{:S(2)}) %copy-start) | copy-done | bytes 4194328
  42.9 8.2 %all-to-all-start.1 = ((bf16[16,4,16,128]{3,2,1,0:T(8,128)(2,1)}), bf16[16,4,16,128]{3,2,1,0:T(8,128)(2,1)S(1)}, u32[]{:S(2)}, u32[]{:S(2)}) async-start(bf16[16,4,16,128]{3,2,1,0:T(8,128)(2,1)} %all-to-all-done), calls=%async_computation.1 | async-start | bytes 524288 | tf_op jit(solution)/shard_map/all_to_all | solution.py:442
  51.1 2.0 %collective-permute-start = (bf16[80,2048]{1,0:T(8,128)(2,1)S(1)}, bf16[80,2048]{1,0:T(8,128)(2,1)S(1)}, u32[]{:S(2)}, u32[]{:S(2)}) collective-permute-start(bf16[80,2048]{1,0:T(8,128)(2,1)S(1)} %copy-done.7), channel_id=1, source_target_pairs={{0,2},{1,3},{2,4},{3,5},{4,6},{5,7},{6,8},{7,9},{8,10},{9,11},{10,... | collective-permute-start | bytes 983048 | tf_op jit(solution)/shard_map/ppermute | solution.py:418
  54.4 1.6 %collective-permute-start.8 = (bf16[64,2048]{1,0:T(8,128)(2,1)S(1)}, bf16[64,2048]{1,0:T(8,128)(2,1)S(1)}, u32[]{:S(2)}, u32[]{:S(2)}) collective-permute-start(bf16[64,2048]{1,0:T(8,128)(2,1)S(1)} %get-tuple-element.39), channel_id=1, source_target_pairs={{0,4},{1,5},{2,6},{3,7},{4,8},{5,9},{6,10},{7,11},{8,12},{9,13},{1... | collective-permute-start | bytes 786440 | tf_op jit(solution)/shard_map/ppermute | solution.py:418
  56.1 2.5 %collective-permute-start.9 = (bf16[64,2048]{1,0:T(8,128)(2,1)S(1)}, bf16[64,2048]{1,0:T(8,128)(2,1)S(1)}, u32[]{:S(2)}, u32[]{:S(2)}) collective-permute-start(bf16[64,2048]{1,0:T(8,128)(2,1)S(1)} %get-tuple-element.40), channel_id=1, source_target_pairs={{0,12},{1,13},{2,14},{3,15},{4,0},{5,1},{6,2},{7,3},{8,4},{9,5},{1... | collective-permute-start | bytes 786440 | tf_op jit(solution)/shard_map/ppermute | solution.py:418
  58.6 10.3 %collective-permute-done.below_ref = bf16[80,2048]{1,0:T(8,128)(2,1)S(1)} collective-permute-done((bf16[80,2048]{1,0:T(8,128)(2,1)S(1)}, bf16[80,2048]{1,0:T(8,128)(2,1)S(1)}, u32[]{:S(2)}, u32[]{:S(2)}) %collective-permute-start) | collective-permute-done | bytes 327712 | tf_op jit(solution)/shard_map/ppermute | solution.py:418
  68.9 7.4 %collective-permute-done.8.up_ref = bf16[64,2048]{1,0:T(8,128)(2,1)S(1)} collective-permute-done((bf16[64,2048]{1,0:T(8,128)(2,1)S(1)}, bf16[64,2048]{1,0:T(8,128)(2,1)S(1)}, u32[]{:S(2)}, u32[]{:S(2)}) %collective-permute-start.8) | collective-permute-done | bytes 262176 | tf_op jit(solution)/shard_map/ppermute | solution.py:418
  77.3 3.5 %collective-permute-start.10 = (bf16[48,2048]{1,0:T(8,128)(2,1)S(1)}, bf16[48,2048]{1,0:T(8,128)(2,1)S(1)}, u32[]{:S(2)}, u32[]{:S(2)}) collective-permute-start(bf16[48,2048]{1,0:T(8,128)(2,1)S(1)} %get-tuple-element.43.refs_0_), channel_id=1, source_target_pairs={{0,1},{1,0},{2,3},{3,2},{4,5},{5,4},{6,7},{7,6},{8,9},{9,8},{10,11... | collective-permute-start | bytes 589832 | tf_op jit(solution)/shard_map/ppermute | solution.py:421
  80.8 4.8 %regularizer.5.refs_0_.refs_1_ = bf16[8,2048,128]{2,1,0:T(8,128)(2,1)} custom-call(s32[4]{0:T(128)} %pad_add_fusion.place_ref, f32[1]{0:T(128)S(6)} %copy.14.beta_ref, bf16[8,2048,128]{2,1,0:T(8,128)(2,1)} %after_ref.7, bf16[8,2048,128]{2,1,0:T(8,128)(2,1)} %after_ref.7, bf16[8,2048,128]{2,1,0:T(8,128)(2,1)} %after_ref.7, ...), custom_call_target="tpu_custom_call", output_to_operand_aliasing={{}: (8, {})} | custom-call | flops 15728640 | bytes 4194304 | tf_op jit(solution)/shard_map/regularizer/pallas_call | solution.py:353
  85.6 2.2 %copy-done.1 = bf16[8,2048,128]{2,1,0:T(8,128)(2,1)S(1)} copy-done((bf16[8,2048,128]{2,1,0:T(8,128)(2,1)S(1)}, bf16[8,2048,128]{2,1,0:T(8,128)(2,1)}, u32[]{:S(2)}) %copy-start.1) | copy-done | bytes 4194328
  88.7 2.5 %collective-permute-start.11 = (bf16[32,2048]{1,0:T(8,128)(2,1)S(1)}, bf16[32,2048]{1,0:T(8,128)(2,1)S(1)}, u32[]{:S(2)}, u32[]{:S(2)}) collective-permute-start(bf16[32,2048]{1,0:T(8,128)(2,1)S(1)} %residual_images.1.refs_0_), channel_id=1, source_target_pairs={{0,1},{1,0},{2,3},{3,2},{4,5},{5,4},{6,7},{7,6},{8,9},{9,8},{10,11... | collective-permute-start | bytes 393224 | tf_op jit(solution)/shard_map/ppermute | solution.py:421
  91.2 4.8 %regularizer.6.refs_2_ = bf16[8,2048,128]{2,1,0:T(8,128)(2,1)} custom-call(s32[4]{0:T(128)} %pad_add_fusion.place_ref, f32[1]{0:T(128)S(6)} %copy.14.beta_ref, bf16[8,2048,128]{2,1,0:T(8,128)(2,1)} %after_ref.7, bf16[8,2048,128]{2,1,0:T(8,128)(2,1)} %after_ref.7, bf16[8,2048,128]{2,1,0:T(8,128)(2,1)} %after_ref.7, ...), custom_call_target="tpu_custom_call", output_to_operand_aliasing={{}: (8, {})} | custom-call | flops 15728640 | bytes 4194304 | tf_op jit(solution)/shard_map/regularizer/pallas_call | solution.py:353
  96.9 3.8 %collective-permute-start.14 = (bf16[64,2048]{1,0:T(8,128)(2,1)S(1)}, bf16[64,2048]{1,0:T(8,128)(2,1)S(1)}, u32[]{:S(2)}, u32[]{:S(2)}) collective-permute-start(bf16[64,2048]{1,0:T(8,128)(2,1)S(1)} %pad_maximum_fusion.order_ref.refs_0_), channel_id=1, source_target_pairs={{0,4},{1,5},{2,6},{3,7},{4,8},{5,9},{6,10},{7,11},{8,12},{9,13},{1... | collective-permute-start | bytes 786440 | tf_op jit(solution)/shard_map/ppermute | solution.py:418
  101.3 1.5 %collective-permute-start.12 = (bf16[64,2048]{1,0:T(8,128)(2,1)S(1)}, bf16[64,2048]{1,0:T(8,128)(2,1)S(1)}, u32[]{:S(2)}, u32[]{:S(2)}) collective-permute-start(bf16[64,2048]{1,0:T(8,128)(2,1)S(1)} %pad_maximum_fusion.order_ref.refs_0_), channel_id=1, source_target_pairs={{0,14},{1,15},{2,0},{3,1},{4,2},{5,3},{6,4},{7,5},{8,6},{9,7},{10,... | collective-permute-start | bytes 786440 | tf_op jit(solution)/shard_map/ppermute | solution.py:418
  105.5 4.8 %regularizer.7.refs_9_ = bf16[8,2048,128]{2,1,0:T(8,128)(2,1)} custom-call(s32[4]{0:T(128)} %pad_add_fusion.place_ref, f32[1]{0:T(128)S(6)} %copy.14.beta_ref, bf16[8,2048,128]{2,1,0:T(8,128)(2,1)} %after_ref.7, bf16[8,2048,128]{2,1,0:T(8,128)(2,1)} %after_ref.7, bf16[8,2048,128]{2,1,0:T(8,128)(2,1)} %after_ref.7, ...), custom_call_target="tpu_custom_call", output_to_operand_aliasing={{}: (9, {})} | custom-call | flops 15728640 | bytes 4194304 | tf_op jit(solution)/shard_map/regularizer/pallas_call | solution.py:353
  110.3 2.7 %collective-permute-done.14.refs_4_ = bf16[64,2048]{1,0:T(8,128)(2,1)S(1)} collective-permute-done((bf16[64,2048]{1,0:T(8,128)(2,1)S(1)}, bf16[64,2048]{1,0:T(8,128)(2,1)S(1)}, u32[]{:S(2)}, u32[]{:S(2)}) %collective-permute-start.14) | collective-permute-done | bytes 262176 | tf_op jit(solution)/shard_map/ppermute | solution.py:418
  113.0 1.9 %collective-permute-done.15.refs_3_ = bf16[64,2048]{1,0:T(8,128)(2,1)S(1)} collective-permute-done((bf16[64,2048]{1,0:T(8,128)(2,1)S(1)}, bf16[64,2048]{1,0:T(8,128)(2,1)S(1)}, u32[]{:S(2)}, u32[]{:S(2)}) %collective-permute-start.15) | collective-permute-done | bytes 262176 | tf_op jit(solution)/shard_map/ppermute | solution.py:418
  116.9 2.0 %collective-permute-start.18 = (bf16[32,2048]{1,0:T(8,128)(2,1)S(1)}, bf16[32,2048]{1,0:T(8,128)(2,1)S(1)}, u32[]{:S(2)}, u32[]{:S(2)}) collective-permute-start(bf16[32,2048]{1,0:T(8,128)(2,1)S(1)} %slice.14), channel_id=1, source_target_pairs={{0,4},{1,5},{2,6},{3,7},{4,8},{5,9},{6,10},{7,11},{8,12},{9,13},{1... | collective-permute-start | bytes 393224 | tf_op jit(solution)/shard_map/ppermute | solution.py:418
  119.5 2.5 %collective-permute-start.19 = (bf16[32,2048]{1,0:T(8,128)(2,1)S(1)}, bf16[32,2048]{1,0:T(8,128)(2,1)S(1)}, u32[]{:S(2)}, u32[]{:S(2)}) collective-permute-start(bf16[32,2048]{1,0:T(8,128)(2,1)S(1)} %slice.15), channel_id=1, source_target_pairs={{0,12},{1,13},{2,14},{3,15},{4,0},{5,1},{6,2},{7,3},{8,4},{9,5},{1... | collective-permute-start | bytes 393224 | tf_op jit(solution)/shard_map/ppermute | solution.py:418
  122.0 4.9 %collective-permute-done.18.refs_7_ = bf16[32,2048]{1,0:T(8,128)(2,1)S(1)} collective-permute-done((bf16[32,2048]{1,0:T(8,128)(2,1)S(1)}, bf16[32,2048]{1,0:T(8,128)(2,1)S(1)}, u32[]{:S(2)}, u32[]{:S(2)}) %collective-permute-start.18) | collective-permute-done | bytes 131104 | tf_op jit(solution)/shard_map/ppermute | solution.py:418
  126.9 2.2 %collective-permute-done.19.refs_8_ = bf16[32,2048]{1,0:T(8,128)(2,1)S(1)} collective-permute-done((bf16[32,2048]{1,0:T(8,128)(2,1)S(1)}, bf16[32,2048]{1,0:T(8,128)(2,1)S(1)}, u32[]{:S(2)}, u32[]{:S(2)}) %collective-permute-start.19) | collective-permute-done | bytes 131104 | tf_op jit(solution)/shard_map/ppermute | solution.py:418
  129.1 2.2 %copy-done.2 = bf16[8,2048,128]{2,1,0:T(8,128)(2,1)S(1)} copy-done((bf16[8,2048,128]{2,1,0:T(8,128)(2,1)S(1)}, bf16[8,2048,128]{2,1,0:T(8,128)(2,1)}, u32[]{:S(2)}) %copy-start.2) | copy-done | bytes 4194328
  133.5 7.2 %gradient.1 = bf16[8,2048,128]{2,1,0:T(8,128)(2,1)} custom-call(s32[4]{0:T(128)S(1)} %copy-done.15, f32[1]{0:T(128)S(6)} %copy.14.beta_ref, bf16[528,1024]{1,0:T(8,128)(2,1)S(1)} %copy-done.4, bf16[80,2048]{1,0:T(8,128)(2,1)S(1)} %copy-done.7, bf16[48,2048]{1,0:T(8,128)(2,1)S(1)} %collective-permute-done.10.arrived_ref.beside_ref, ...), custom_call_target="tpu_custom_call" | custom-call | flops 2214592512 | bytes 10485760 | tf_op jit(solution)/shard_map/gradient/pallas_call | solution.py:390
  (71 shorter events, 16.1 us)
Async XLA Ops:
  1.7 13.6 %all-to-all-start = ((bf16[16,4,16,128]{3,2,1,0:T(8,128)(2,1)}), bf16[16,4,16,128]{3,2,1,0:T(8,128)(2,1)}, u32[]{:S(2)}, u32[]{:S(2)}) async-start(bf16[16,4,16,128]{3,2,1,0:T(8,128)(2,1)} %pack_messages.1), calls=%async_computation | async-start | bytes 524288 | tf_op jit(solution)/shard_map/all_to_all | solution.py:425
  9.1 6.2 %copy-start.18 = (bf16[1,2048,128]{2,1,0:T(8,128)(2,1)}, bf16[1,2048,128]{2,1,0:T(8,128)(2,1)S(1)}, u32[]{:S(2)}) copy-start(bf16[1,2048,128]{2,1,0:T(8,128)(2,1)S(1)} %get-tuple-element.49.refs_1_) | copy-start | bytes 1572868
  9.1 19.9 %collective-permute-start.6 = (bf16[1,2048,128]{2,1,0:T(8,128)(2,1)S(1)}, bf16[1,2048,128]{2,1,0:T(8,128)(2,1)S(1)}, u32[]{:S(2)}, u32[]{:S(2)}) collective-permute-start(bf16[1,2048,128]{2,1,0:T(8,128)(2,1)S(1)} %get-tuple-element.50.refs_0_), channel_id=1, source_target_pairs={{0,16},{16,32},{32,48},{48,64},{64,80},{80,96},{96,112},{112,128},... | collective-permute-start | bytes 1572872 | tf_op jit(solution)/shard_map/ppermute | solution.py:427
  11.1 22.7 %collective-permute-start.7 = (bf16[1,2048,128]{2,1,0:T(8,128)(2,1)S(1)}, bf16[1,2048,128]{2,1,0:T(8,128)(2,1)S(1)}, u32[]{:S(2)}, u32[]{:S(2)}) collective-permute-start(bf16[1,2048,128]{2,1,0:T(8,128)(2,1)S(1)} %get-tuple-element.49.refs_1_), channel_id=1, source_target_pairs={{16,0},{32,16},{48,32},{64,48},{80,64},{96,80},{112,96},{128,112},... | collective-permute-start | bytes 1572872 | tf_op jit(solution)/shard_map/ppermute | solution.py:428
  23.3 17.2 %collective-permute-start.2 = (bf16[64,2048]{1,0:T(8,128)(2,1)}, bf16[64,2048]{1,0:T(8,128)(2,1)S(1)}, u32[]{:S(2)}, u32[]{:S(2)}) collective-permute-start(bf16[64,2048]{1,0:T(8,128)(2,1)} %get-tuple-element.33), channel_id=1, source_target_pairs={{0,2},{1,3},{2,4},{3,5},{4,6},{5,7},{6,8},{7,9},{8,10},{9,11},{10,... | collective-permute-start | bytes 786440 | tf_op jit(solution)/shard_map/ppermute | solution.py:418
  25.0 15.5 %collective-permute-start.4 = (bf16[64,2048]{1,0:T(8,128)(2,1)}, bf16[64,2048]{1,0:T(8,128)(2,1)S(1)}, u32[]{:S(2)}, u32[]{:S(2)}) collective-permute-start(bf16[64,2048]{1,0:T(8,128)(2,1)} %get-tuple-element.36), channel_id=1, source_target_pairs={{0,14},{1,15},{2,0},{3,1},{4,2},{5,3},{6,4},{7,5},{8,6},{9,7},{10,... | collective-permute-start | bytes 786440 | tf_op jit(solution)/shard_map/ppermute | solution.py:418
  29.0 11.3 %collective-permute-start.3 = (bf16[32,2048]{1,0:T(8,128)(2,1)}, bf16[32,2048]{1,0:T(8,128)(2,1)S(1)}, u32[]{:S(2)}, u32[]{:S(2)}) collective-permute-start(bf16[32,2048]{1,0:T(8,128)(2,1)} %get-tuple-element.34.refs_0_), channel_id=1, source_target_pairs={{0,4},{1,5},{2,6},{3,7},{4,8},{5,9},{6,10},{7,11},{8,12},{9,13},{1... | collective-permute-start | bytes 393224 | tf_op jit(solution)/shard_map/ppermute | solution.py:418
  29.0 11.5 %collective-permute-start.5 = (bf16[32,2048]{1,0:T(8,128)(2,1)}, bf16[32,2048]{1,0:T(8,128)(2,1)S(1)}, u32[]{:S(2)}, u32[]{:S(2)}) collective-permute-start(bf16[32,2048]{1,0:T(8,128)(2,1)} %get-tuple-element.37), channel_id=1, source_target_pairs={{0,12},{1,13},{2,14},{3,15},{4,0},{5,1},{6,2},{7,3},{8,4},{9,5},{1... | collective-permute-start | bytes 393224 | tf_op jit(solution)/shard_map/ppermute | solution.py:418
  33.8 6.7 %copy-start.10 = (bf16[64,2048]{1,0:T(8,128)(2,1)S(1)}, bf16[64,2048]{1,0:T(8,128)(2,1)}, u32[]{:S(2)}) copy-start(bf16[64,2048]{1,0:T(8,128)(2,1)} %get-tuple-element.32.up_ref) | copy-start | bytes 786436
  33.8 6.7 %copy-start.11 = (bf16[64,2048]{1,0:T(8,128)(2,1)S(1)}, bf16[64,2048]{1,0:T(8,128)(2,1)}, u32[]{:S(2)}) copy-start(bf16[64,2048]{1,0:T(8,128)(2,1)} %get-tuple-element.35.down_ref) | copy-start | bytes 786436
  34.6 16.5 %copy-start.7 = (bf16[80,2048]{1,0:T(8,128)(2,1)S(1)}, bf16[80,2048]{1,0:T(8,128)(2,1)}, u32[]{:S(2)}) copy-start(bf16[80,2048]{1,0:T(8,128)(2,1)} %get-tuple-element.30.mine_ref) | copy-start | bytes 983044
  34.6 18.5 %copy-start.20 = (bf16[80,2048]{1,0:T(8,128)(2,1)S(1)}, bf16[80,2048]{1,0:T(8,128)(2,1)}, u32[]{:S(2)}) copy-start(bf16[80,2048]{1,0:T(8,128)(2,1)} %get-tuple-element.31) | copy-start | bytes 983044
  34.6 42.0 %copy-start.9 = (bf16[64,2048]{1,0:T(8,128)(2,1)S(1)}, bf16[64,2048]{1,0:T(8,128)(2,1)}, u32[]{:S(2)}) copy-start(bf16[64,2048]{1,0:T(8,128)(2,1)} %get-tuple-element.29.own_ref) | copy-start | bytes 786436
  39.5 37.1 %copy-start.13 = (s32[4]{0:T(128)S(1)}, s32[4]{0:T(128)}, u32[]{:S(2)}) copy-start(s32[4]{0:T(128)} %pad_add_fusion.place_ref) | copy-start | bytes 52
  42.9 33.7 %all-to-all-start.1 = ((bf16[16,4,16,128]{3,2,1,0:T(8,128)(2,1)}), bf16[16,4,16,128]{3,2,1,0:T(8,128)(2,1)S(1)}, u32[]{:S(2)}, u32[]{:S(2)}) async-start(bf16[16,4,16,128]{3,2,1,0:T(8,128)(2,1)} %all-to-all-done), calls=%async_computation.1 | async-start | bytes 524288 | tf_op jit(solution)/shard_map/all_to_all | solution.py:442
  51.1 17.8 %collective-permute-start = (bf16[80,2048]{1,0:T(8,128)(2,1)S(1)}, bf16[80,2048]{1,0:T(8,128)(2,1)S(1)}, u32[]{:S(2)}, u32[]{:S(2)}) collective-permute-start(bf16[80,2048]{1,0:T(8,128)(2,1)S(1)} %copy-done.7), channel_id=1, source_target_pairs={{0,2},{1,3},{2,4},{3,5},{4,6},{5,7},{6,8},{7,9},{8,10},{9,11},{10,... | collective-permute-start | bytes 983048 | tf_op jit(solution)/shard_map/ppermute | solution.py:418
  53.1 15.8 %collective-permute-start.1 = (bf16[80,2048]{1,0:T(8,128)(2,1)S(1)}, bf16[80,2048]{1,0:T(8,128)(2,1)S(1)}, u32[]{:S(2)}, u32[]{:S(2)}) collective-permute-start(bf16[80,2048]{1,0:T(8,128)(2,1)S(1)} %copy-done.20), channel_id=1, source_target_pairs={{0,14},{1,15},{2,0},{3,1},{4,2},{5,3},{6,4},{7,5},{8,6},{9,7},{10,... | collective-permute-start | bytes 983048 | tf_op jit(solution)/shard_map/ppermute | solution.py:418
  54.4 21.8 %collective-permute-start.8 = (bf16[64,2048]{1,0:T(8,128)(2,1)S(1)}, bf16[64,2048]{1,0:T(8,128)(2,1)S(1)}, u32[]{:S(2)}, u32[]{:S(2)}) collective-permute-start(bf16[64,2048]{1,0:T(8,128)(2,1)S(1)} %get-tuple-element.39), channel_id=1, source_target_pairs={{0,4},{1,5},{2,6},{3,7},{4,8},{5,9},{6,10},{7,11},{8,12},{9,13},{1... | collective-permute-start | bytes 786440 | tf_op jit(solution)/shard_map/ppermute | solution.py:418
  56.1 20.5 %collective-permute-start.9 = (bf16[64,2048]{1,0:T(8,128)(2,1)S(1)}, bf16[64,2048]{1,0:T(8,128)(2,1)S(1)}, u32[]{:S(2)}, u32[]{:S(2)}) collective-permute-start(bf16[64,2048]{1,0:T(8,128)(2,1)S(1)} %get-tuple-element.40), channel_id=1, source_target_pairs={{0,12},{1,13},{2,14},{3,15},{4,0},{5,1},{6,2},{7,3},{8,4},{9,5},{1... | collective-permute-start | bytes 786440 | tf_op jit(solution)/shard_map/ppermute | solution.py:418
  77.3 8.3 %collective-permute-start.10 = (bf16[48,2048]{1,0:T(8,128)(2,1)S(1)}, bf16[48,2048]{1,0:T(8,128)(2,1)S(1)}, u32[]{:S(2)}, u32[]{:S(2)}) collective-permute-start(bf16[48,2048]{1,0:T(8,128)(2,1)S(1)} %get-tuple-element.43.refs_0_), channel_id=1, source_target_pairs={{0,1},{1,0},{2,3},{3,2},{4,5},{5,4},{6,7},{7,6},{8,9},{9,8},{10,11... | collective-permute-start | bytes 589832 | tf_op jit(solution)/shard_map/ppermute | solution.py:421
  88.7 14.6 %copy-start.14 = (s32[4]{0:T(128)S(1)}, s32[4]{0:T(128)}, u32[]{:S(2)}) copy-start(s32[4]{0:T(128)} %pad_add_fusion.place_ref) | copy-start | bytes 52
  88.7 7.3 %collective-permute-start.11 = (bf16[32,2048]{1,0:T(8,128)(2,1)S(1)}, bf16[32,2048]{1,0:T(8,128)(2,1)S(1)}, u32[]{:S(2)}, u32[]{:S(2)}) collective-permute-start(bf16[32,2048]{1,0:T(8,128)(2,1)S(1)} %residual_images.1.refs_0_), channel_id=1, source_target_pairs={{0,1},{1,0},{2,3},{3,2},{4,5},{5,4},{6,7},{7,6},{8,9},{9,8},{10,11... | collective-permute-start | bytes 393224 | tf_op jit(solution)/shard_map/ppermute | solution.py:421
  96.9 7.6 %copy-start.5 = (bf16[64,2048]{1,0:T(8,128)(2,1)}, bf16[64,2048]{1,0:T(8,128)(2,1)S(1)}, u32[]{:S(2)}) copy-start(bf16[64,2048]{1,0:T(8,128)(2,1)S(1)} %pad_maximum_fusion.order_ref.refs_0_) | copy-start | bytes 786436
  96.9 16.1 %collective-permute-start.14 = (bf16[64,2048]{1,0:T(8,128)(2,1)S(1)}, bf16[64,2048]{1,0:T(8,128)(2,1)S(1)}, u32[]{:S(2)}, u32[]{:S(2)}) collective-permute-start(bf16[64,2048]{1,0:T(8,128)(2,1)S(1)} %pad_maximum_fusion.order_ref.refs_0_), channel_id=1, source_target_pairs={{0,4},{1,5},{2,6},{3,7},{4,8},{5,9},{6,10},{7,11},{8,12},{9,13},{1... | collective-permute-start | bytes 786440 | tf_op jit(solution)/shard_map/ppermute | solution.py:418
  100.7 14.1 %collective-permute-start.15 = (bf16[64,2048]{1,0:T(8,128)(2,1)S(1)}, bf16[64,2048]{1,0:T(8,128)(2,1)S(1)}, u32[]{:S(2)}, u32[]{:S(2)}) collective-permute-start(bf16[64,2048]{1,0:T(8,128)(2,1)S(1)} %pad_maximum_fusion.order_ref.refs_0_), channel_id=1, source_target_pairs={{0,12},{1,13},{2,14},{3,15},{4,0},{5,1},{6,2},{7,3},{8,4},{9,5},{1... | collective-permute-start | bytes 786440 | tf_op jit(solution)/shard_map/ppermute | solution.py:418
  101.3 18.2 %collective-permute-start.12 = (bf16[64,2048]{1,0:T(8,128)(2,1)S(1)}, bf16[64,2048]{1,0:T(8,128)(2,1)S(1)}, u32[]{:S(2)}, u32[]{:S(2)}) collective-permute-start(bf16[64,2048]{1,0:T(8,128)(2,1)S(1)} %pad_maximum_fusion.order_ref.refs_0_), channel_id=1, source_target_pairs={{0,14},{1,15},{2,0},{3,1},{4,2},{5,3},{6,4},{7,5},{8,6},{9,7},{10,... | collective-permute-start | bytes 786440 | tf_op jit(solution)/shard_map/ppermute | solution.py:418
  102.8 19.2 %collective-permute-start.13 = (bf16[64,2048]{1,0:T(8,128)(2,1)S(1)}, bf16[64,2048]{1,0:T(8,128)(2,1)S(1)}, u32[]{:S(2)}, u32[]{:S(2)}) collective-permute-start(bf16[64,2048]{1,0:T(8,128)(2,1)S(1)} %pad_maximum_fusion.order_ref.refs_0_), channel_id=1, source_target_pairs={{0,2},{1,3},{2,4},{3,5},{4,6},{5,7},{6,8},{7,9},{8,10},{9,11},{10,... | collective-permute-start | bytes 786440 | tf_op jit(solution)/shard_map/ppermute | solution.py:418
  105.5 23.6 %copy-start.15 = (s32[4]{0:T(128)S(1)}, s32[4]{0:T(128)}, u32[]{:S(2)}) copy-start(s32[4]{0:T(128)} %pad_add_fusion.place_ref) | copy-start | bytes 52
  114.9 14.2 %collective-permute-start.16 = (bf16[64,2048]{1,0:T(8,128)(2,1)S(1)}, bf16[64,2048]{1,0:T(8,128)(2,1)S(1)}, u32[]{:S(2)}, u32[]{:S(2)}) collective-permute-start(bf16[64,2048]{1,0:T(8,128)(2,1)S(1)} %collective-permute-done.15.refs_3_), channel_id=1, source_target_pairs={{0,14},{1,15},{2,0},{3,1},{4,2},{5,3},{6,4},{7,5},{8,6},{9,7},{10,... | collective-permute-start | bytes 786440 | tf_op jit(solution)/shard_map/ppermute | solution.py:418
  115.7 13.4 %collective-permute-start.17 = (bf16[64,2048]{1,0:T(8,128)(2,1)S(1)}, bf16[64,2048]{1,0:T(8,128)(2,1)S(1)}, u32[]{:S(2)}, u32[]{:S(2)}) collective-permute-start(bf16[64,2048]{1,0:T(8,128)(2,1)S(1)} %collective-permute-done.14.refs_4_), channel_id=1, source_target_pairs={{0,2},{1,3},{2,4},{3,5},{4,6},{5,7},{6,8},{7,9},{8,10},{9,11},{10,... | collective-permute-start | bytes 786440 | tf_op jit(solution)/shard_map/ppermute | solution.py:418
  116.9 10.0 %collective-permute-start.18 = (bf16[32,2048]{1,0:T(8,128)(2,1)S(1)}, bf16[32,2048]{1,0:T(8,128)(2,1)S(1)}, u32[]{:S(2)}, u32[]{:S(2)}) collective-permute-start(bf16[32,2048]{1,0:T(8,128)(2,1)S(1)} %slice.14), channel_id=1, source_target_pairs={{0,4},{1,5},{2,6},{3,7},{4,8},{5,9},{6,10},{7,11},{8,12},{9,13},{1... | collective-permute-start | bytes 393224 | tf_op jit(solution)/shard_map/ppermute | solution.py:418
  119.5 9.6 %collective-permute-start.19 = (bf16[32,2048]{1,0:T(8,128)(2,1)S(1)}, bf16[32,2048]{1,0:T(8,128)(2,1)S(1)}, u32[]{:S(2)}, u32[]{:S(2)}) collective-permute-start(bf16[32,2048]{1,0:T(8,128)(2,1)S(1)} %slice.15), channel_id=1, source_target_pairs={{0,12},{1,13},{2,14},{3,15},{4,0},{5,1},{6,2},{7,3},{8,4},{9,5},{1... | collective-permute-start | bytes 393224 | tf_op jit(solution)/shard_map/ppermute | solution.py:418
  (11 other events, 27.5 us)

commit v3 on v2

--- a/solution.py
+++ b/solution.py
@@ -15,6 +15,7 @@
 RUN = SLOTS * 8
 PAIR = 2 * RUN
 LINES = 16
+EDGE = 16
 PIECES = 4
 
 
@@ -27,6 +28,7 @@
 VMEM = pl.BlockSpec(memory_space=pltpu.VMEM)
 SMEM = pl.BlockSpec(memory_space=pltpu.SMEM)
 ANY = pl.BlockSpec(memory_space=pl.ANY)
+HBM = pl.BlockSpec(memory_space=pltpu.HBM)
 
 
 def cost(flops, moved):
@@ -76,6 +78,48 @@
     return jnp.concatenate([block[z] for z in range(block.shape[0])], axis=1)
 
 
+def streamed(ref, buffer_ref, sem_ref, first, edge=0):
+    step, steps = pl.program_id(0), pl.num_programs(0)
+    extent = ref.shape[1]
+
+    def copies(index):
+        slot = lax.rem(index, 2)
+        start = (first + index) * XT
+        parts = [(start, edge, XT)]
+        if edge:
+            parts.append((jnp.maximum(start - edge, 0), 0, edge))
+            parts.append((jnp.minimum(start + XT, extent - edge), edge + XT, edge))
+        return [
+            pltpu.make_async_copy(
+                ref.at[:, pl.ds(pl.multiple_of(source, 16), size)],
+                buffer_ref.at[slot, :, pl.ds(target, size)],
+                sem_ref.at[slot, part],
+            )
+            for part, (source, target, size) in enumerate(parts)
+        ]
+
+    @pl.when(step == 0)
+    def _():
+        for copy in copies(step):
+            copy.start()
+
+    @pl.when(step + 1 < steps)
+    def _():
+        for copy in copies(step + 1):
+            copy.start()
+
+    for copy in copies(step):
+        copy.wait()
+    return buffer_ref.at[lax.rem(step, 2)]
+
+
+def stream_scratch(depth, strip, edge=0):
+    return [
+        pltpu.VMEM((2, depth, XT + 2 * edge, strip), BF16),
+        pltpu.SemaphoreType.DMA((2, 3 if edge else 1)),
+    ]
+
+
 def spread_weights(tiles, out_ref, first, depth):
     rows = tiles.shape[0] * depth
     weights = jnp.broadcast_to(
@@ -106,32 +150,37 @@
     spread_ref[row:] = jnp.where(iota(shape, 1) == target, 1.0, 0.0).astype(BF16)
 
 
-def spread_kernel(tiles, place_ref, got_ref, order_ref, out_ref):
+def spread_kernel(tiles, place_ref, got_ref, order_ref, out_ref, views_ref):
     fill_spread(tiles, place_ref[1], got_ref, out_ref)
+    views_ref[...] = got_ref[...]
 
 
 def spread_rows(place, got, tiles, order):
     shape = (got.shape[0] * 8 + LINES, 8 * BAND)
     return pl.pallas_call(
         functools.partial(spread_kernel, tiles),
-        out_shape=jax.ShapeDtypeStruct(shape, BF16),
+        out_shape=(
+            jax.ShapeDtypeStruct(shape, BF16),
+            jax.ShapeDtypeStruct(got.shape, BF16),
+        ),
         in_specs=[SMEM, VMEM, ANY],
-        out_specs=VMEM,
-        compiler_params=limit(16),
+        out_specs=(VMEM, VMEM),
+        compiler_params=limit(8),
         cost_estimate=cost(4 * shape[0] * shape[1], 4 * shape[0] * shape[1]),
         name="spread_rows",
     )(place, got, order)
 
 
 def forward_kernel(tiles, place_ref, got_ref, volume_ref, *refs):
-    outs, spread_ref = refs[:-1], refs[-1]
+    outs, (spread_ref, buffer_ref, sem_ref) = refs[:-3], refs[-3:]
+    block_ref = streamed(volume_ref, buffer_ref, sem_ref, 0)
 
     @pl.when(pl.program_id(0) == 0)
     def _():
         fill_spread(tiles, place_ref[1], got_ref, spread_ref)
 
     out = lax.dot_general(
-        spread_ref[...], joined(volume_ref), (((1,), (1,)), ((), ())), preferred_element_type=F32
+        spread_ref[...], joined(block_ref), (((1,), (1,)), ((), ())), preferred_element_type=F32
     ).astype(BF16)
     row = 0
     for ref in outs:
@@ -157,11 +206,13 @@
         in_specs=[
             SMEM,
             pl.BlockSpec(got.shape, lambda i: (0, 0, 0)),
-            pl.BlockSpec((depth, XT, strip), lambda i: (0, i, 0)),
+            HBM,
         ]
         + [ANY] * len(order),
         out_specs=[pl.BlockSpec((count, XT), lambda i: (0, i)) for count in rows],
-        scratch_shapes=[pltpu.VMEM((slots * depth + LINES, depth * strip), BF16)],
+        scratch_shapes=[pltpu.VMEM((slots * depth + LINES, depth * strip), BF16)]
+        + stream_scratch(depth, strip),
+        compiler_params=limit(10),
         cost_estimate=cost(2 * slots * depth * volume.size, 3 * volume.size),
         name="forward",
     )(place, got, volume, *order)
@@ -186,7 +237,7 @@
         out_shape=(out, out),
         in_specs=[VMEM] * 6 + [ANY] * (len(operands) - 6),
         out_specs=(VMEM, VMEM),
-        compiler_params=limit(16),
+        compiler_params=limit(8),
         cost_estimate=cost(6 * out.size, 14 * out.size),
         name="round_sums",
     )(*operands)
@@ -222,7 +273,7 @@
         ),
         in_specs=[SMEM] + [VMEM] * 6 + [ANY] * len(order),
         out_specs=(VMEM, VMEM),
-        compiler_params=limit(16),
+        compiler_params=limit(8),
         cost_estimate=cost(5 * own.size, 14 * own.size),
         name="last_sums",
     )(place, own, mine, below, above, up, down, *order)
@@ -279,10 +330,27 @@
         out_shape=jax.ShapeDtypeStruct(kept.shape, BF16),
         in_specs=[VMEM] * 3 + [ANY] * len(order),
         out_specs=VMEM,
-        compiler_params=limit(16),
+        compiler_params=limit(8),
         cost_estimate=cost(4 * 8 * 16 * 256 * 128 * 6, 2 * views.size),
         name="residual_images",
     )(kept, arrived, views, *order)
+
+
+def join_kernel(first_ref, second_ref, order_ref, out_ref):
+    out_ref[:RUN] = first_ref[...]
+    out_ref[RUN:] = second_ref[...]
+
+
+def join(first, second, order):
+    return pl.pallas_call(
+        join_kernel,
+        out_shape=jax.ShapeDtypeStruct((PAIR, first.shape[1]), BF16),
+        in_specs=[VMEM, VMEM, ANY],
+        out_specs=VMEM,
+        compiler_params=limit(8),
+        cost_estimate=cost(0, 8 * first.size),
+        name="join",
+    )(first, second, order)
 
 
 def penalty(diff):
@@ -294,34 +362,37 @@
     count,
     place_ref,
     beta_ref,
-    block_ref,
-    before_ref,
-    after_ref,
+    volume_ref,
     below_ref,
     above_ref,
     *refs,
 ):
-    out_ref, under_ref = refs[-2:]
-    depth, tile, strip = block_ref.shape
+    out_ref, token_ref, under_ref, buffer_ref, sem_ref = refs[-5:]
+    block_ref = streamed(volume_ref, buffer_ref, sem_ref, first_tile, EDGE)
+    depth, strip, tile = block_ref.shape[0], block_ref.shape[2], XT
     at = pl.program_id(0) + first_tile
     beta = beta_ref[0]
     has_below = (place_ref[0] > 0).astype(F32)
     has_above = (place_ref[0] < place_ref[3] - 1).astype(F32)
     has_before = (at > 0).astype(F32)
     has_after = (at < count - 1).astype(F32)
-    under_ref[...] = penalty(block_ref[0].astype(F32) - below_ref[0].astype(F32)) * has_below
+    here = pl.ds(EDGE, tile)
+    under_ref[...] = (
+        penalty(block_ref[0, here].astype(F32) - below_ref[0].astype(F32)) * has_below
+    )
     row = iota((tile, strip), 0)
     lane = iota((tile, strip), 1)
 
     def body(z, carry):
-        center = block_ref[z].astype(F32)
+        center = block_ref[z, here].astype(F32)
         top = z == depth - 1
-        upper = jnp.where(top, above_ref[0], block_ref[jnp.minimum(z + 1, depth - 1)])
+        upper = jnp.where(top, above_ref[0], block_ref[jnp.minimum(z + 1, depth - 1), here])
         over = penalty(upper.astype(F32) - center) * jnp.where(top, has_above, 1.0)
         total = under_ref[...] - over
         under_ref[...] = over
-        ahead = after_ref[z].astype(F32)[0:1]
-        behind = penalty(center[0:1] - before_ref[z].astype(F32)[15:16]) * has_before
+        ahead = block_ref[z, pl.ds(EDGE + tile, EDGE)].astype(F32)[0:1]
+        behind = block_ref[z, pl.ds(0, EDGE)].astype(F32)[EDGE - 1 :]
+        behind = penalty(center[0:1] - behind) * has_before
         along = penalty(jnp.where(row == tile - 1, ahead, pltpu.roll(center, tile - 1, 0)) - center)
         along = jnp.where(row == tile - 1, along * has_after, along)
         total = total + jnp.where(row == 0, behind, pltpu.roll(along, 1, 0)) - along
@@ -332,6 +403,7 @@
         return carry
 
     lax.fori_loop(0, depth, body, 0, unroll=2)
+    token_ref[...] = under_ref[:8]
 
 
 def regularizer(index, done, place, beta, volume, below, above, *order):
@@ -339,33 +411,29 @@
     count = extent // XT
     length = count // PIECES
     start = index * length
-    edge = XT // 16
     plane = pl.BlockSpec((1, XT, strip), lambda i: (0, start + i, 0))
     block = pl.BlockSpec((depth, XT, strip), lambda i: (0, start + i, 0))
-    ends = [
-        lambda i: (0, jnp.maximum((start + i) * edge - 1, 0), 0),
-        lambda i: (0, jnp.minimum((start + i + 1) * edge, count * edge - 1), 0),
-    ]
-    specs = [SMEM, SMEM, block]
-    specs += [pl.BlockSpec((depth, 16, strip), where) for where in ends]
+    specs = [SMEM, SMEM, HBM]
     specs += [plane] * 2 + [ANY] * len(order)
     before = [] if done is None else [done]
     return pl.pallas_call(
         functools.partial(regularizer_kernel, start, count),
         grid=(length,),
-        out_shape=jax.ShapeDtypeStruct(volume.shape, BF16),
-        in_specs=specs + [ANY] * len(before),
-        out_specs=block,
-        scratch_shapes=[pltpu.VMEM((XT, strip), F32)],
+        out_shape=(pltpu.HBM(volume.shape, BF16), jax.ShapeDtypeStruct((8, strip), F32)),
+        in_specs=specs + [HBM] * len(before),
+        out_specs=(block, pl.BlockSpec((8, strip), lambda i: (0, 0))),
+        scratch_shapes=[pltpu.VMEM((XT, strip), F32)] + stream_scratch(depth, strip, EDGE),
+        compiler_params=limit(8),
         input_output_aliases={len(specs): 0} if before else {},
         cost_estimate=cost(30 * volume.size // PIECES, 8 * volume.size // PIECES),
         name="regularizer",
-    )(place, beta, volume, volume, volume, below, above, *order, *before)
+    )(place, beta, volume, below, above, *order, *before)
 
 
 def gradient_kernel(place_ref, beta_ref, spread_ref, mine_ref, beside_ref, *refs):
-    chunk_refs = refs[:-2]
-    regular_ref, out_ref = refs[-2:]
+    chunk_refs = refs[:-4]
+    whole_ref, out_ref, buffer_ref, sem_ref = refs[-4:]
+    regular_ref = streamed(whole_ref, buffer_ref, sem_ref, 0)
     depth, tile, strip = out_ref.shape
     beta = beta_ref[0]
     has_left = (place_ref[1] > 0).astype(F32)
@@ -399,9 +467,10 @@
             pl.BlockSpec((LINES, XT), lambda i: (RUN // LINES, i)),
         ]
         + [pl.BlockSpec((chunk.shape[0], XT), lambda i: (0, i)) for chunk in chunks]
-        + [block],
+        + [HBM],
         out_specs=block,
-        compiler_params=limit(16),
+        scratch_shapes=stream_scratch(depth, strip),
+        compiler_params=limit(12),
         cost_estimate=cost(2 * spread.shape[0] * size, 5 * size),
         name="gradient",
     )(place, beta, spread, mine, arrived, *chunks, regular)
@@ -427,6 +496,7 @@
     below = lax.ppermute(top, "slab", [(i, i + 1) for i in range(slabs - 1)])
     above = lax.ppermute(bottom, "slab", [(i + 1, i) for i in range(slabs - 1)])
     flat = got.reshape(slabs * SLOTS, ROWS, BAND)
+    volume = pltpu.with_memory_space_constraint(volume, pltpu.HBM)
 
     own, up1, down1, up2, down2, up3, down3, far_up, far_down = forward(
         place, flat, volume, tiles, top, bottom
@@ -435,28 +505,27 @@
     near = along_z(up3, 1), along_z(down3, -1)
     far = along_z(far_up, 2), along_z(far_down, -2)
     one = along_z(up1, 1), along_z(down1, -1)
-    regular = regularizer(0, None, place, beta, volume, below, above, far_up)
-    up, down = round_sums(up2, near[0], far[0], down2, near[1], far[1], regular)
-    got, up = lax.optimization_barrier((got, up))
+    regular, token = regularizer(0, None, place, beta, volume, below, above, far_up)
+    up, down = round_sums(up2, near[0], far[0], down2, near[1], far[1], token, *one)
     two = along_z(up, 2), along_z(down, -2)
-    views = lax.all_to_all(got, "tile", split_axis=0, concat_axis=0, tiled=True)
+    spread, views = spread_rows(place, flat, tiles, up)
+    views = views.reshape(got.shape)
+    views = lax.all_to_all(views, "tile", split_axis=0, concat_axis=0, tiled=True)
     kept, sent = last_sums(place, own, up1, *one, *two, views)
     arrived = along_y(sent)
-    regular = regularizer(1, regular, place, beta, volume, below, above, sent)
-    images = residual_images(kept, arrived, views, regular)
+    regular, token = regularizer(1, regular, place, beta, volume, below, above, sent)
+    images = residual_images(kept, arrived, views, token)
 
     partner = along_y(images)
-    regular = regularizer(2, regular, place, beta, volume, below, above, images)
-    pair = jnp.concatenate([images, partner], axis=0)
-    pair, regular = lax.optimization_barrier((pair, regular))
+    regular, token = regularizer(2, regular, place, beta, volume, below, above, images)
+    pair = join(images, partner, token)
     up2, down2 = along_z(pair, 2), along_z(pair, -2)
     up1, down1 = along_z(pair, 1), along_z(pair, -1)
-    spread = spread_rows(place, flat, tiles, pair)
-    regular = regularizer(3, regular, place, beta, volume, below, above, pair, spread)
-    up2, down2, regular = lax.optimization_barrier((up2, down2, regular))
+    regular, token = regularizer(3, regular, place, beta, volume, below, above, pair)
     up3, down3 = along_z(up2, 1), along_z(down2, -1)
     far_up, far_down = along_z(up2[:RUN], 2), along_z(down2[RUN:], -2)
     chunks = [pair, down1, up1, down2, up2, down3, up3, far_up, far_down]
+    regular = pltpu.with_memory_space_constraint(regular, pltpu.HBM)
     return gradient(place, beta, spread, mine, arrived, chunks, regular)
 
 

time: 142 us -> 146 us (1.028)
  waiting for transfers between devices: 31.2 us -> 37 us
  local copies, waits for them, and re-layouts: 11.8 us -> 7.67 us
  Pallas kernels: 39.1 us -> 43.2 us
    ppermute x16, waiting for transfers between devices: 31.2 us -> 36.1 us  [along_z(): lax.ppermute(block, 'tile', [(i, (i + 2 * by) % tiles) for i in range(til...]
    unnamed x42 -> x18, local copies, waits for them, and re-layouts: 10.6 us -> 6.38 us
    pallas_call x4, Pallas kernels: 19.3 us -> 21.6 us  [regularizer(): pl.pallas_call(functools.partial(regularizer_kernel, start, count), grid=...]
    pallas_call x1, Pallas kernels: 7.24 us -> 9.53 us  [gradient(): pl.pallas_call(gradient_kernel, grid=(extent // XT,), out_shape=jax.Shape...]
    ppermute x16, starting transfers between devices: 30.2 us -> 32.3 us  [along_z(): lax.ppermute(block, 'tile', [(i, (i + 2 * by) % tiles) for i in range(til...]
    ppermute x1, starting transfers between devices: 3.51 us -> 2.02 us  [shards(): above = lax.ppermute(bottom, 'slab', [(i + 1, i) for i in range(slabs - 1)])]
  transfers between devices with their start and end apart: 22 -> 22, of which waited for: 10 -> 9; matrix products, arithmetic and copies ran while one was open for 1% -> 1% of each run, Pallas kernels for 20% -> 20%
where the time goes in v3:
time: 146 us; the launch traced here: 144 us
  starting transfers between devices  55.5 us (38%)
  Pallas kernels  43.2 us (30%)
  waiting for transfers between devices  37 us (25%)
  local copies, waits for them, and re-layouts  7.67 us (5%)
    ppermute x16, waiting for transfers between devices, along_z(): lax.ppermute(block, 'tile', [(i, (i + 2 * by) % tiles) for i in range(til...  36.1 us
    ppermute x16, starting transfers between devices, along_z(): lax.ppermute(block, 'tile', [(i, (i + 2 * by) % tiles) for i in range(til...  32.3 us
    pallas_call x4, Pallas kernels, regularizer(): pl.pallas_call(functools.partial(regularizer_kernel, start, count), grid=...  21.6 us
    pallas_call x1, Pallas kernels, gradient(): pl.pallas_call(gradient_kernel, grid=(extent // XT,), out_shape=jax.Shape...  9.53 us
    all_to_all x1, starting transfers between devices, shards(): lax.all_to_all(views, 'tile', split_axis=0, concat_axis=0, tiled=True)  7.97 us
    pallas_call x1, Pallas kernels, forward(): pl.pallas_call(kernel, grid=(extent // XT,), out_shape=[jax.ShapeDtypeStr...  7.82 us
    unnamed x18, local copies, waits for them, and re-layouts  6.38 us
    all_to_all x1, starting transfers between devices, shards(): lax.all_to_all(packed, 'slab', split_axis=0, concat_axis=0, tiled=True)  5.77 us
  transfers between devices with their start and end apart: 22, of which 9 were waited for; matrix products, arithmetic and copies ran while one was open for 1% of the time, Pallas kernels for 20%

profile of v3, /device:TPU:8, one launch (start us, length us, event | category | flops | bytes accessed | tf_op | source)
XLA Modules:
  0.0 144.4 jit_solution(3440377052506189764)
XLA Ops:
  0.0 1.7 %pack_messages.1 = bf16[16,4,16,128]{3,2,1,0:T(8,128)(2,1)} custom-call(s32[2,12]{1,0:T(2,128)} %bitcast.10, s32[2,12]{1,0:T(2,128)} %offset_ref.1, s32[2,12]{1,0:T(2,128)} %width_ref.1, bf16[12,2,128]{2,1,0:T(2,128)(2,1)} %bitcast.9, bf16[2,12,8,128]{3,2,1,0:T(8,128)(2,1)} %measured_ref.1), custom_call_target="tpu_custom_call" | custom-call | tf_op jit(solution)/shard_map/pack_messages/pallas_call | solution.py:67
  1.7 5.8 %all-to-all-start = ((bf16[16,4,16,128]{3,2,1,0:T(8,128)(2,1)}), bf16[16,4,16,128]{3,2,1,0:T(8,128)(2,1)S(1)}, u32[]{:S(2)}, u32[]{:S(2)}) async-start(bf16[16,4,16,128]{3,2,1,0:T(8,128)(2,1)} %pack_messages.1), calls=%async_computation | async-start | bytes 524288 | tf_op jit(solution)/shard_map/all_to_all | solution.py:494
  7.5 1.3 fusion
  8.7 2.0 %collective-permute-start.5 = (bf16[1,2048,128]{2,1,0:T(8,128)(2,1)S(1)}, bf16[1,2048,128]{2,1,0:T(8,128)(2,1)S(1)}, u32[]{:S(2)}, u32[]{:S(2)}) collective-permute-start(bf16[1,2048,128]{2,1,0:T(8,128)(2,1)S(1)} %get-tuple-element.53.refs_1_), channel_id=1, source_target_pairs={{16,0},{32,16},{48,32},{64,48},{80,64},{96,80},{112,96},{128,112},... | collective-permute-start | bytes 1572872 | tf_op jit(solution)/shard_map/ppermute | solution.py:497
  10.8 2.3 %collective-permute-start.4 = (bf16[1,2048,128]{2,1,0:T(8,128)(2,1)S(1)}, bf16[1,2048,128]{2,1,0:T(8,128)(2,1)S(1)}, u32[]{:S(2)}, u32[]{:S(2)}) collective-permute-start(bf16[1,2048,128]{2,1,0:T(8,128)(2,1)S(1)} %get-tuple-element.54.refs_0_), channel_id=1, source_target_pairs={{0,16},{16,32},{32,48},{48,64},{64,80},{80,96},{96,112},{112,128},... | collective-permute-start | bytes 1572872 | tf_op jit(solution)/shard_map/ppermute | solution.py:496
  14.0 7.8 %forward.1 = (bf16[64,2048]{1,0:T(8,128)(2,1)S(1)}, bf16[80,2048]{1,0:T(8,128)(2,1)S(1)}, bf16[80,2048]{1,0:T(8,128)(2,1)S(1)}, bf16[64,2048]{1,0:T(8,128)(2,1)S...) custom-call(s32[4]{0:T(128)S(1)} %pad_add_fusion.place_ref, ...), custom_call_target="tpu_custom_call" | custom-call | flops 2147483648 | bytes 6291456 | tf_op jit(solution)/shard_map/forward/pallas_call | solution.py:202
  22.5 6.3 %collective-permute-start.3 = (bf16[32,2048]{1,0:T(8,128)(2,1)S(1)}, bf16[32,2048]{1,0:T(8,128)(2,1)S(1)}, u32[]{:S(2)}, u32[]{:S(2)}) collective-permute-start(bf16[32,2048]{1,0:T(8,128)(2,1)S(1)} %get-tuple-element.36), channel_id=1, source_target_pairs={{0,12},{1,13},{2,14},{3,15},{4,0},{5,1},{6,2},{7,3},{8,4},{9,5},{1... | collective-permute-start | bytes 393224 | tf_op jit(solution)/shard_map/ppermute | solution.py:487
  28.8 1.0 collective-permute-start.7
  29.8 1.0 collective-permute-start.6
  30.8 4.1 %collective-permute-done.3.down_far_ref = bf16[32,2048]{1,0:T(8,128)(2,1)S(1)} collective-permute-done((bf16[32,2048]{1,0:T(8,128)(2,1)S(1)}, bf16[32,2048]{1,0:T(8,128)(2,1)S(1)}, u32[]{:S(2)}, u32[]{:S(2)}) %collective-permute-start.3) | collective-permute-done | bytes 131104 | tf_op jit(solution)/shard_map/ppermute | solution.py:487
  34.9 3.2 %collective-permute-start.2 = (bf16[64,2048]{1,0:T(8,128)(2,1)S(1)}, bf16[64,2048]{1,0:T(8,128)(2,1)S(1)}, u32[]{:S(2)}, u32[]{:S(2)}) collective-permute-start(bf16[64,2048]{1,0:T(8,128)(2,1)S(1)} %get-tuple-element.35), channel_id=1, source_target_pairs={{0,14},{1,15},{2,0},{3,1},{4,2},{5,3},{6,4},{7,5},{8,6},{9,7},{10,... | collective-permute-start | bytes 786440 | tf_op jit(solution)/shard_map/ppermute | solution.py:487
  39.3 5.4 %regularizer.4 = (bf16[8,2048,128]{2,1,0:T(8,128)(2,1)}, f32[8,128]{1,0:T(8,128)S(1)}) custom-call(s32[4]{0:T(128)S(1)} %pad_add_fusion.place_ref, f32[1]{0:T(128)S(6)} %copy.14.beta_ref, bf16[8,2048,128]{2,1,0:T(8,128)(2,1)} %volume_ref.9, bf16[1,2048,128]{2,1,0:T(8,128)(2,1)S(1)} %collective-permute-done.4.below_ref, ...), custom_call_target="tpu_custom_call" | custom-call | flops 15728640 | bytes 4194304 | tf_op jit(solution)/shard_map/regularizer/pallas_call | solution.py:419
  44.7 5.0 %collective-permute-done.1.up_far_ref = bf16[32,2048]{1,0:T(8,128)(2,1)S(1)} collective-permute-done((bf16[32,2048]{1,0:T(8,128)(2,1)S(1)}, bf16[32,2048]{1,0:T(8,128)(2,1)S(1)}, u32[]{:S(2)}, u32[]{:S(2)}) %collective-permute-start.1) | collective-permute-done | bytes 131104 | tf_op jit(solution)/shard_map/ppermute | solution.py:487
  52.4 8.0 %all-to-all-start.1 = ((bf16[16,4,16,128]{3,2,1,0:T(8,128)(2,1)}), bf16[16,4,16,128]{3,2,1,0:T(8,128)(2,1)S(1)}, u32[]{:S(2)}, u32[]{:S(2)}) async-start(bf16[16,4,16,128]{3,2,1,0:T(8,128)(2,1)} %bitcast.8), calls=%async_computation.1 | async-start | bytes 524288 | tf_op jit(solution)/shard_map/all_to_all | solution.py:513
  60.4 4.0 %collective-permute-start.9 = (bf16[64,2048]{1,0:T(8,128)(2,1)}, bf16[64,2048]{1,0:T(8,128)(2,1)S(1)}, u32[]{:S(2)}, u32[]{:S(2)}) collective-permute-start(bf16[64,2048]{1,0:T(8,128)(2,1)} %copy-done.8), channel_id=1, source_target_pairs={{0,12},{1,13},{2,14},{3,15},{4,0},{5,1},{6,2},{7,3},{8,4},{9,5},{1... | collective-permute-start | bytes 786440 | tf_op jit(solution)/shard_map/ppermute | solution.py:487
  64.4 16.2 %collective-permute-done.9.down_ref = bf16[64,2048]{1,0:T(8,128)(2,1)S(1)} collective-permute-done((bf16[64,2048]{1,0:T(8,128)(2,1)}, bf16[64,2048]{1,0:T(8,128)(2,1)S(1)}, u32[]{:S(2)}, u32[]{:S(2)}) %collective-permute-start.9) | collective-permute-done | bytes 262176 | tf_op jit(solution)/shard_map/ppermute | solution.py:487
  82.1 0.9 copy-done.1
  83.0 0.9 copy-done.3
  84.0 0.9 copy-done.5
  85.7 3.1 %collective-permute-start.10 = (bf16[48,2048]{1,0:T(8,128)(2,1)S(1)}, bf16[48,2048]{1,0:T(8,128)(2,1)S(1)}, u32[]{:S(2)}, u32[]{:S(2)}) collective-permute-start(bf16[48,2048]{1,0:T(8,128)(2,1)S(1)} %get-tuple-element.45.refs_0_), channel_id=1, source_target_pairs={{0,1},{1,0},{2,3},{3,2},{4,5},{5,4},{6,7},{7,6},{8,9},{9,8},{10,11... | collective-permute-start | bytes 589832 | tf_op jit(solution)/shard_map/ppermute | solution.py:490
  88.7 5.4 %regularizer.5 = (bf16[8,2048,128]{2,1,0:T(8,128)(2,1)}, f32[8,128]{1,0:T(8,128)S(1)}) custom-call(s32[4]{0:T(128)S(1)} %pad_add_fusion.place_ref, f32[1]{0:T(128)S(6)} %copy.14.beta_ref, bf16[8,2048,128]{2,1,0:T(8,128)(2,1)} %volume_ref.9, bf16[1,2048,128]{2,1,0:T(8,128)(2,1)S(1)} %collective-permute-done.4.below_ref, ...), custom_call_target="tpu_custom_call", output_to_operand_aliasing={{0}: (6, {})} | custom-call | flops 15728640 | bytes 4194304 | tf_op jit(solution)/shard_map/regularizer/pallas_call | solution.py:419
  95.1 2.1 %collective-permute-start.11 = (bf16[32,2048]{1,0:T(8,128)(2,1)S(1)}, bf16[32,2048]{1,0:T(8,128)(2,1)S(1)}, u32[]{:S(2)}, u32[]{:S(2)}) collective-permute-start(bf16[32,2048]{1,0:T(8,128)(2,1)S(1)} %residual_images.1.refs_0_.first_ref), channel_id=1, source_target_pairs={{0,1},{1,0},{2,3},{3,2},{4,5},{5,4},{6,7},{7,6},{8,9},{9,8},{10,11... | collective-permute-start | bytes 393224 | tf_op jit(solution)/shard_map/ppermute | solution.py:490
  97.1 5.4 %regularizer.6 = (bf16[8,2048,128]{2,1,0:T(8,128)(2,1)}, f32[8,128]{1,0:T(8,128)S(1)}) custom-call(s32[4]{0:T(128)S(1)} %pad_add_fusion.place_ref, f32[1]{0:T(128)S(6)} %copy.14.beta_ref, bf16[8,2048,128]{2,1,0:T(8,128)(2,1)} %volume_ref.9, bf16[1,2048,128]{2,1,0:T(8,128)(2,1)S(1)} %collective-permute-done.4.below_ref, ...), custom_call_target="tpu_custom_call", output_to_operand_aliasing={{0}: (6, {})} | custom-call | flops 15728640 | bytes 4194304 | tf_op jit(solution)/shard_map/regularizer/pallas_call | solution.py:419
  102.6 4.5 %collective-permute-start.15 = (bf16[64,2048]{1,0:T(8,128)(2,1)S(1)}, bf16[64,2048]{1,0:T(8,128)(2,1)S(1)}, u32[]{:S(2)}, u32[]{:S(2)}) collective-permute-start(bf16[64,2048]{1,0:T(8,128)(2,1)S(1)} %join.1.refs_0_), channel_id=1, source_target_pairs={{0,4},{1,5},{2,6},{3,7},{4,8},{5,9},{6,10},{7,11},{8,12},{9,13},{1... | collective-permute-start | bytes 786440 | tf_op jit(solution)/shard_map/ppermute | solution.py:487
  107.1 1.3 collective-permute-start.13
  108.4 2.0 %collective-permute-start.12 = (bf16[64,2048]{1,0:T(8,128)(2,1)S(1)}, bf16[64,2048]{1,0:T(8,128)(2,1)S(1)}, u32[]{:S(2)}, u32[]{:S(2)}) collective-permute-start(bf16[64,2048]{1,0:T(8,128)(2,1)S(1)} %join.1.refs_0_), channel_id=1, source_target_pairs={{0,14},{1,15},{2,0},{3,1},{4,2},{5,3},{6,4},{7,5},{8,6},{9,7},{10,... | collective-permute-start | bytes 786440 | tf_op jit(solution)/shard_map/ppermute | solution.py:487
  110.3 9.2 %collective-permute-done.15.refs_4_ = bf16[64,2048]{1,0:T(8,128)(2,1)S(1)} collective-permute-done((bf16[64,2048]{1,0:T(8,128)(2,1)S(1)}, bf16[64,2048]{1,0:T(8,128)(2,1)S(1)}, u32[]{:S(2)}, u32[]{:S(2)}) %collective-permute-start.15) | collective-permute-done | bytes 262176 | tf_op jit(solution)/shard_map/ppermute | solution.py:487
  119.5 4.3 %collective-permute-start.16 = (bf16[64,2048]{1,0:T(8,128)(2,1)S(1)}, bf16[64,2048]{1,0:T(8,128)(2,1)S(1)}, u32[]{:S(2)}, u32[]{:S(2)}) collective-permute-start(bf16[64,2048]{1,0:T(8,128)(2,1)S(1)} %collective-permute-done.14.refs_3_), channel_id=1, source_target_pairs={{0,14},{1,15},{2,0},{3,1},{4,2},{5,3},{6,4},{7,5},{8,6},{9,7},{10,... | collective-permute-start | bytes 786440 | tf_op jit(solution)/shard_map/ppermute | solution.py:487
  124.3 3.8 %collective-permute-start.19 = (bf16[32,2048]{1,0:T(8,128)(2,1)S(1)}, bf16[32,2048]{1,0:T(8,128)(2,1)S(1)}, u32[]{:S(2)}, u32[]{:S(2)}) collective-permute-start(bf16[32,2048]{1,0:T(8,128)(2,1)S(1)} %slice.17), channel_id=1, source_target_pairs={{0,12},{1,13},{2,14},{3,15},{4,0},{5,1},{6,2},{7,3},{8,4},{9,5},{1... | collective-permute-start | bytes 393224 | tf_op jit(solution)/shard_map/ppermute | solution.py:487
  128.1 5.4 %regularizer.7 = (bf16[8,2048,128]{2,1,0:T(8,128)(2,1)}, f32[8,128]{1,0:T(8,128)}) custom-call(s32[4]{0:T(128)S(1)} %pad_add_fusion.place_ref, f32[1]{0:T(128)S(6)} %copy.14.beta_ref, bf16[8,2048,128]{2,1,0:T(8,128)(2,1)} %volume_ref.9, bf16[1,2048,128]{2,1,0:T(8,128)(2,1)S(1)} %collective-permute-done.4.below_ref, ...), custom_call_target="tpu_custom_call", output_to_operand_aliasing={{0}: (6, {})} | custom-call | flops 15728640 | bytes 4194304 | tf_op jit(solution)/shard_map/regularizer/pallas_call | solution.py:419
  133.7 1.0 collective-permute-done.19.refs_8_
  134.7 9.5 %gradient.1 = bf16[8,2048,128]{2,1,0:T(8,128)(2,1)} custom-call(s32[4]{0:T(128)S(1)} %pad_add_fusion.place_ref, f32[1]{0:T(128)S(6)} %copy.14.beta_ref, bf16[528,1024]{1,0:T(8,128)(2,1)S(1)} %get-tuple-element.41.spread_ref, bf16[80,2048]{1,0:T(8,128)(2,1)S(1)} %get-tuple-element.38.mine_ref, ...), custom_call_target="tpu_custom_call" | custom-call | flops 2214592512 | bytes 10485760 | tf_op jit(solution)/shard_map/gradient/pallas_call | solution.py:458
  (47 shorter events, 8.5 us)
Async XLA Ops:
  1.7 12.3 %all-to-all-start = ((bf16[16,4,16,128]{3,2,1,0:T(8,128)(2,1)}), bf16[16,4,16,128]{3,2,1,0:T(8,128)(2,1)S(1)}, u32[]{:S(2)}, u32[]{:S(2)}) async-start(bf16[16,4,16,128]{3,2,1,0:T(8,128)(2,1)} %pack_messages.1), calls=%async_computation | async-start | bytes 524288 | tf_op jit(solution)/shard_map/all_to_all | solution.py:494
  8.7 26.2 %collective-permute-start.5 = (bf16[1,2048,128]{2,1,0:T(8,128)(2,1)S(1)}, bf16[1,2048,128]{2,1,0:T(8,128)(2,1)S(1)}, u32[]{:S(2)}, u32[]{:S(2)}) collective-permute-start(bf16[1,2048,128]{2,1,0:T(8,128)(2,1)S(1)} %get-tuple-element.53.refs_1_), channel_id=1, source_target_pairs={{16,0},{32,16},{48,32},{64,48},{80,64},{96,80},{112,96},{128,112},... | collective-permute-start | bytes 1572872 | tf_op jit(solution)/shard_map/ppermute | solution.py:497
  10.8 27.4 %collective-permute-start.4 = (bf16[1,2048,128]{2,1,0:T(8,128)(2,1)S(1)}, bf16[1,2048,128]{2,1,0:T(8,128)(2,1)S(1)}, u32[]{:S(2)}, u32[]{:S(2)}) collective-permute-start(bf16[1,2048,128]{2,1,0:T(8,128)(2,1)S(1)} %get-tuple-element.54.refs_0_), channel_id=1, source_target_pairs={{0,16},{16,32},{32,48},{48,64},{64,80},{80,96},{96,112},{112,128},... | collective-permute-start | bytes 1572872 | tf_op jit(solution)/shard_map/ppermute | solution.py:496
  21.8 0.7 copy-start
  22.5 12.4 %collective-permute-start.3 = (bf16[32,2048]{1,0:T(8,128)(2,1)S(1)}, bf16[32,2048]{1,0:T(8,128)(2,1)S(1)}, u32[]{:S(2)}, u32[]{:S(2)}) collective-permute-start(bf16[32,2048]{1,0:T(8,128)(2,1)S(1)} %get-tuple-element.36), channel_id=1, source_target_pairs={{0,12},{1,13},{2,14},{3,15},{4,0},{5,1},{6,2},{7,3},{8,4},{9,5},{1... | collective-permute-start | bytes 393224 | tf_op jit(solution)/shard_map/ppermute | solution.py:487
  28.8 21.2 %collective-permute-start.7 = (bf16[80,2048]{1,0:T(8,128)(2,1)S(1)}, bf16[80,2048]{1,0:T(8,128)(2,1)S(1)}, u32[]{:S(2)}, u32[]{:S(2)}) collective-permute-start(bf16[80,2048]{1,0:T(8,128)(2,1)S(1)} %get-tuple-element.39), channel_id=1, source_target_pairs={{0,14},{1,15},{2,0},{3,1},{4,2},{5,3},{6,4},{7,5},{8,6},{9,7},{10,... | collective-permute-start | bytes 983048 | tf_op jit(solution)/shard_map/ppermute | solution.py:487
  29.8 20.2 %collective-permute-start.6 = (bf16[80,2048]{1,0:T(8,128)(2,1)S(1)}, bf16[80,2048]{1,0:T(8,128)(2,1)S(1)}, u32[]{:S(2)}, u32[]{:S(2)}) collective-permute-start(bf16[80,2048]{1,0:T(8,128)(2,1)S(1)} %get-tuple-element.38.mine_ref), channel_id=1, source_target_pairs={{0,2},{1,3},{2,4},{3,5},{4,6},{5,7},{6,8},{7,9},{8,10},{9,11},{10,... | collective-permute-start | bytes 983048 | tf_op jit(solution)/shard_map/ppermute | solution.py:487
  34.9 15.1 %collective-permute-start = (bf16[64,2048]{1,0:T(8,128)(2,1)S(1)}, bf16[64,2048]{1,0:T(8,128)(2,1)S(1)}, u32[]{:S(2)}, u32[]{:S(2)}) collective-permute-start(bf16[64,2048]{1,0:T(8,128)(2,1)S(1)} %get-tuple-element.32), channel_id=1, source_target_pairs={{0,2},{1,3},{2,4},{3,5},{4,6},{5,7},{6,8},{7,9},{8,10},{9,11},{10,... | collective-permute-start | bytes 786440 | tf_op jit(solution)/shard_map/ppermute | solution.py:487
  34.9 15.1 %collective-permute-start.2 = (bf16[64,2048]{1,0:T(8,128)(2,1)S(1)}, bf16[64,2048]{1,0:T(8,128)(2,1)S(1)}, u32[]{:S(2)}, u32[]{:S(2)}) collective-permute-start(bf16[64,2048]{1,0:T(8,128)(2,1)S(1)} %get-tuple-element.35), channel_id=1, source_target_pairs={{0,14},{1,15},{2,0},{3,1},{4,2},{5,3},{6,4},{7,5},{8,6},{9,7},{10,... | collective-permute-start | bytes 786440 | tf_op jit(solution)/shard_map/ppermute | solution.py:487
  38.1 11.6 %collective-permute-start.1 = (bf16[32,2048]{1,0:T(8,128)(2,1)S(1)}, bf16[32,2048]{1,0:T(8,128)(2,1)S(1)}, u32[]{:S(2)}, u32[]{:S(2)}) collective-permute-start(bf16[32,2048]{1,0:T(8,128)(2,1)S(1)} %get-tuple-element.33.refs_0_), channel_id=1, source_target_pairs={{0,4},{1,5},{2,6},{3,7},{4,8},{5,9},{6,10},{7,11},{8,12},{9,13},{1... | collective-permute-start | bytes 393224 | tf_op jit(solution)/shard_map/ppermute | solution.py:487
  50.2 0.7 copy-start.8
  50.9 0.8 copy-start.6
  51.7 0.7 copy-start.7
  52.4 29.7 %all-to-all-start.1 = ((bf16[16,4,16,128]{3,2,1,0:T(8,128)(2,1)}), bf16[16,4,16,128]{3,2,1,0:T(8,128)(2,1)S(1)}, u32[]{:S(2)}, u32[]{:S(2)}) async-start(bf16[16,4,16,128]{3,2,1,0:T(8,128)(2,1)} %bitcast.8), calls=%async_computation.1 | async-start | bytes 524288 | tf_op jit(solution)/shard_map/all_to_all | solution.py:513
  60.4 20.3 %collective-permute-start.9 = (bf16[64,2048]{1,0:T(8,128)(2,1)}, bf16[64,2048]{1,0:T(8,128)(2,1)S(1)}, u32[]{:S(2)}, u32[]{:S(2)}) collective-permute-start(bf16[64,2048]{1,0:T(8,128)(2,1)} %copy-done.8), channel_id=1, source_target_pairs={{0,12},{1,13},{2,14},{3,15},{4,0},{5,1},{6,2},{7,3},{8,4},{9,5},{1... | collective-permute-start | bytes 786440 | tf_op jit(solution)/shard_map/ppermute | solution.py:487
  64.4 17.0 %collective-permute-start.8 = (bf16[64,2048]{1,0:T(8,128)(2,1)}, bf16[64,2048]{1,0:T(8,128)(2,1)S(1)}, u32[]{:S(2)}, u32[]{:S(2)}) collective-permute-start(bf16[64,2048]{1,0:T(8,128)(2,1)} %copy-done.6), channel_id=1, source_target_pairs={{0,4},{1,5},{2,6},{3,7},{4,8},{5,9},{6,10},{7,11},{8,12},{9,13},{1... | collective-permute-start | bytes 786440 | tf_op jit(solution)/shard_map/ppermute | solution.py:487
  80.7 0.7 copy-start.2
  81.4 0.7 copy-start.4
  82.1 1.0 copy-start.1
  83.0 0.9 copy-start.3
  84.0 0.9 copy-start.5
  85.7 8.5 %collective-permute-start.10 = (bf16[48,2048]{1,0:T(8,128)(2,1)S(1)}, bf16[48,2048]{1,0:T(8,128)(2,1)S(1)}, u32[]{:S(2)}, u32[]{:S(2)}) collective-permute-start(bf16[48,2048]{1,0:T(8,128)(2,1)S(1)} %get-tuple-element.45.refs_0_), channel_id=1, source_target_pairs={{0,1},{1,0},{2,3},{3,2},{4,5},{5,4},{6,7},{7,6},{8,9},{9,8},{10,11... | collective-permute-start | bytes 589832 | tf_op jit(solution)/shard_map/ppermute | solution.py:490
  95.1 7.5 %collective-permute-start.11 = (bf16[32,2048]{1,0:T(8,128)(2,1)S(1)}, bf16[32,2048]{1,0:T(8,128)(2,1)S(1)}, u32[]{:S(2)}, u32[]{:S(2)}) collective-permute-start(bf16[32,2048]{1,0:T(8,128)(2,1)S(1)} %residual_images.1.refs_0_.first_ref), channel_id=1, source_target_pairs={{0,1},{1,0},{2,3},{3,2},{4,5},{5,4},{6,7},{7,6},{8,9},{9,8},{10,11... | collective-permute-start | bytes 393224 | tf_op jit(solution)/shard_map/ppermute | solution.py:490
  102.6 17.0 %collective-permute-start.15 = (bf16[64,2048]{1,0:T(8,128)(2,1)S(1)}, bf16[64,2048]{1,0:T(8,128)(2,1)S(1)}, u32[]{:S(2)}, u32[]{:S(2)}) collective-permute-start(bf16[64,2048]{1,0:T(8,128)(2,1)S(1)} %join.1.refs_0_), channel_id=1, source_target_pairs={{0,4},{1,5},{2,6},{3,7},{4,8},{5,9},{6,10},{7,11},{8,12},{9,13},{1... | collective-permute-start | bytes 786440 | tf_op jit(solution)/shard_map/ppermute | solution.py:487
  107.1 12.4 %collective-permute-start.14 = (bf16[64,2048]{1,0:T(8,128)(2,1)S(1)}, bf16[64,2048]{1,0:T(8,128)(2,1)S(1)}, u32[]{:S(2)}, u32[]{:S(2)}) collective-permute-start(bf16[64,2048]{1,0:T(8,128)(2,1)S(1)} %join.1.refs_0_), channel_id=1, source_target_pairs={{0,12},{1,13},{2,14},{3,15},{4,0},{5,1},{6,2},{7,3},{8,4},{9,5},{1... | collective-permute-start | bytes 786440 | tf_op jit(solution)/shard_map/ppermute | solution.py:487
  107.1 17.2 %collective-permute-start.13 = (bf16[64,2048]{1,0:T(8,128)(2,1)S(1)}, bf16[64,2048]{1,0:T(8,128)(2,1)S(1)}, u32[]{:S(2)}, u32[]{:S(2)}) collective-permute-start(bf16[64,2048]{1,0:T(8,128)(2,1)S(1)} %join.1.refs_0_), channel_id=1, source_target_pairs={{0,2},{1,3},{2,4},{3,5},{4,6},{5,7},{6,8},{7,9},{8,10},{9,11},{10,... | collective-permute-start | bytes 786440 | tf_op jit(solution)/shard_map/ppermute | solution.py:487
  108.4 25.1 %collective-permute-start.12 = (bf16[64,2048]{1,0:T(8,128)(2,1)S(1)}, bf16[64,2048]{1,0:T(8,128)(2,1)S(1)}, u32[]{:S(2)}, u32[]{:S(2)}) collective-permute-start(bf16[64,2048]{1,0:T(8,128)(2,1)S(1)} %join.1.refs_0_), channel_id=1, source_target_pairs={{0,14},{1,15},{2,0},{3,1},{4,2},{5,3},{6,4},{7,5},{8,6},{9,7},{10,... | collective-permute-start | bytes 786440 | tf_op jit(solution)/shard_map/ppermute | solution.py:487
  119.5 15.2 %collective-permute-start.17 = (bf16[64,2048]{1,0:T(8,128)(2,1)S(1)}, bf16[64,2048]{1,0:T(8,128)(2,1)S(1)}, u32[]{:S(2)}, u32[]{:S(2)}) collective-permute-start(bf16[64,2048]{1,0:T(8,128)(2,1)S(1)} %collective-permute-done.15.refs_4_), channel_id=1, source_target_pairs={{0,2},{1,3},{2,4},{3,5},{4,6},{5,7},{6,8},{7,9},{8,10},{9,11},{10,... | collective-permute-start | bytes 786440 | tf_op jit(solution)/shard_map/ppermute | solution.py:487
  119.5 15.2 %collective-permute-start.16 = (bf16[64,2048]{1,0:T(8,128)(2,1)S(1)}, bf16[64,2048]{1,0:T(8,128)(2,1)S(1)}, u32[]{:S(2)}, u32[]{:S(2)}) collective-permute-start(bf16[64,2048]{1,0:T(8,128)(2,1)S(1)} %collective-permute-done.14.refs_3_), channel_id=1, source_target_pairs={{0,14},{1,15},{2,0},{3,1},{4,2},{5,3},{6,4},{7,5},{8,6},{9,7},{10,... | collective-permute-start | bytes 786440 | tf_op jit(solution)/shard_map/ppermute | solution.py:487
  123.8 9.9 %collective-permute-start.18 = (bf16[32,2048]{1,0:T(8,128)(2,1)S(1)}, bf16[32,2048]{1,0:T(8,128)(2,1)S(1)}, u32[]{:S(2)}, u32[]{:S(2)}) collective-permute-start(bf16[32,2048]{1,0:T(8,128)(2,1)S(1)} %slice.16), channel_id=1, source_target_pairs={{0,4},{1,5},{2,6},{3,7},{4,8},{5,9},{6,10},{7,11},{8,12},{9,13},{1... | collective-permute-start | bytes 393224 | tf_op jit(solution)/shard_map/ppermute | solution.py:487
  124.3 10.4 %collective-permute-start.19 = (bf16[32,2048]{1,0:T(8,128)(2,1)S(1)}, bf16[32,2048]{1,0:T(8,128)(2,1)S(1)}, u32[]{:S(2)}, u32[]{:S(2)}) collective-permute-start(bf16[32,2048]{1,0:T(8,128)(2,1)S(1)} %slice.17), channel_id=1, source_target_pairs={{0,12},{1,13},{2,14},{3,15},{4,0},{5,1},{6,2},{7,3},{8,4},{9,5},{1... | collective-permute-start | bytes 393224 | tf_op jit(solution)/shard_map/ppermute | solution.py:487

commit v4 on v3

--- a/solution.py
+++ b/solution.py
@@ -78,37 +78,35 @@
     return jnp.concatenate([block[z] for z in range(block.shape[0])], axis=1)
 
 
-def streamed(ref, buffer_ref, sem_ref, first, edge=0):
-    step, steps = pl.program_id(0), pl.num_programs(0)
+def tile_copies(ref, buffer_ref, sem_ref, index, first=0, edge=0):
+    slot = lax.rem(index, 2)
     extent = ref.shape[1]
-
-    def copies(index):
-        slot = lax.rem(index, 2)
-        start = (first + index) * XT
-        parts = [(start, edge, XT)]
-        if edge:
-            parts.append((jnp.maximum(start - edge, 0), 0, edge))
-            parts.append((jnp.minimum(start + XT, extent - edge), edge + XT, edge))
-        return [
-            pltpu.make_async_copy(
-                ref.at[:, pl.ds(pl.multiple_of(source, 16), size)],
-                buffer_ref.at[slot, :, pl.ds(target, size)],
-                sem_ref.at[slot, part],
-            )
-            for part, (source, target, size) in enumerate(parts)
-        ]
-
-    @pl.when(step == 0)
-    def _():
-        for copy in copies(step):
-            copy.start()
-
+    start = (first + index) * XT
+    parts = [(start, edge, XT)]
+    if edge:
+        parts.append((jnp.maximum(start - edge, 0), 0, edge))
+        parts.append((jnp.minimum(start + XT, extent - edge), edge + XT, edge))
+    return [
+        pltpu.make_async_copy(
+            ref.at[:, pl.ds(pl.multiple_of(source, 16), size)],
+            buffer_ref.at[slot, :, pl.ds(target, size)],
+            sem_ref.at[slot, part],
+        )
+        for part, (source, target, size) in enumerate(parts)
+    ]
+
+
+def start(copies):
+    for copy in copies:
+        copy.start()
+
+
+def streamed(ref, buffer_ref, sem_ref, step, steps, first=0, edge=0):
     @pl.when(step + 1 < steps)
     def _():
-        for copy in copies(step + 1):
-            copy.start()
-
-    for copy in copies(step):
+        start(tile_copies(ref, buffer_ref, sem_ref, step + 1, first, edge))
+
+    for copy in tile_copies(ref, buffer_ref, sem_ref, step, first, edge):
         copy.wait()
     return buffer_ref.at[lax.rem(step, 2)]
 
@@ -150,66 +148,89 @@
     spread_ref[row:] = jnp.where(iota(shape, 1) == target, 1.0, 0.0).astype(BF16)
 
 
-def spread_kernel(tiles, place_ref, got_ref, order_ref, out_ref, views_ref):
+def spread_kernel(tiles, place_ref, got_ref, order_ref, out_ref):
     fill_spread(tiles, place_ref[1], got_ref, out_ref)
-    views_ref[...] = got_ref[...]
 
 
 def spread_rows(place, got, tiles, order):
     shape = (got.shape[0] * 8 + LINES, 8 * BAND)
     return pl.pallas_call(
         functools.partial(spread_kernel, tiles),
-        out_shape=(
-            jax.ShapeDtypeStruct(shape, BF16),
-            jax.ShapeDtypeStruct(got.shape, BF16),
-        ),
+        out_shape=jax.ShapeDtypeStruct(shape, BF16),
         in_specs=[SMEM, VMEM, ANY],
-        out_specs=(VMEM, VMEM),
+        out_specs=VMEM,
         compiler_params=limit(8),
         cost_estimate=cost(4 * shape[0] * shape[1], 4 * shape[0] * shape[1]),
         name="spread_rows",
     )(place, got, order)
 
 
+def measured_rows(got_ref, source):
+    rows = got_ref[pl.ds(source * SLOTS, SLOTS)].astype(F32)[:, :8]
+    return rows.reshape(RUN, BAND).astype(BF16)
+
+
+PLACES = {
+    0: [(0, 0), (0, RUN)],
+    1: [(3, PAIR), (3, PAIR + RUN)],
+    -1: [(4, PAIR), (4, PAIR + RUN)],
+    2: [(1, 0), (1, RUN)],
+    -2: [(2, 0), (2, RUN)],
+    3: [(3, 0), (3, RUN)],
+    -3: [(4, 0), (4, RUN)],
+    4: [(5, 0), (6, 0)],
+}
+NEAR = 2 * PAIR + LINES
+
+
 def forward_kernel(tiles, place_ref, got_ref, volume_ref, *refs):
     outs, (spread_ref, buffer_ref, sem_ref) = refs[:-3], refs[-3:]
-    block_ref = streamed(volume_ref, buffer_ref, sem_ref, 0)
-
-    @pl.when(pl.program_id(0) == 0)
-    def _():
-        fill_spread(tiles, place_ref[1], got_ref, spread_ref)
-
-    out = lax.dot_general(
-        spread_ref[...], joined(block_ref), (((1,), (1,)), ((), ())), preferred_element_type=F32
-    ).astype(BF16)
-    row = 0
-    for ref in outs:
-        count = min(ref.shape[0], PAIR)
-        ref[:count] = out[row : row + count]
-        if ref.shape[0] > PAIR:
-            ref[PAIR:] = out[-LINES:]
-        row += count
+    extent = volume_ref.shape[1]
+    me = place_ref[1]
+    start(tile_copies(volume_ref, buffer_ref, sem_ref, 0))
+    fill_spread(tiles, me, got_ref, spread_ref)
+    where = [(outs[index], row) for hop in hops(tiles) for index, row in PLACES[hop]]
+    beyond = pl.ds(extent, BAND)
+    for index, hop in enumerate(hops(tiles)):
+        tile = lax.rem(me + 2 * hop + tiles, tiles)
+        for turn, source in enumerate((tile, tile ^ 1)):
+            ref, row = where[2 * index + turn]
+            ref[row : row + RUN, beyond] = measured_rows(got_ref, source)
+    for ref in outs[3:5]:
+        ref[NEAR - LINES :, beyond] = jnp.zeros((LINES, BAND), BF16)
+    steps = extent // XT
+
+    def body(step, carry):
+        block_ref = streamed(volume_ref, buffer_ref, sem_ref, step, steps)
+        out = lax.dot_general(
+            spread_ref[...],
+            joined(block_ref),
+            (((1,), (1,)), ((), ())),
+            preferred_element_type=F32,
+        ).astype(BF16)
+        here = pl.ds(pl.multiple_of(step * XT, XT), XT)
+        for index, (ref, row) in enumerate(where):
+            ref[row : row + RUN, here] = out[index * RUN : (index + 1) * RUN]
+        for ref in outs[3:5]:
+            ref[NEAR - LINES :, here] = out[-LINES:]
+        return carry
+
+    lax.fori_loop(0, steps, body, 0)
 
 
 def forward(place, got, volume, tiles, *order):
     depth, extent, strip = volume.shape
     slots = got.shape[0]
-    rows = [PAIR] + [PAIR + LINES] * 2 + [PAIR] * (tiles // 2 - 4) + [RUN] * 2
+    rows = [PAIR] * 3 + [NEAR] * 2 + [RUN] * 2
 
     def kernel(place_ref, got_ref, volume_ref, *refs):
         forward_kernel(tiles, place_ref, got_ref, volume_ref, *refs[len(order) :])
 
     return pl.pallas_call(
         kernel,
-        grid=(extent // XT,),
-        out_shape=[jax.ShapeDtypeStruct((count, extent), BF16) for count in rows],
-        in_specs=[
-            SMEM,
-            pl.BlockSpec(got.shape, lambda i: (0, 0, 0)),
-            HBM,
-        ]
-        + [ANY] * len(order),
-        out_specs=[pl.BlockSpec((count, XT), lambda i: (0, i)) for count in rows],
+        out_shape=[jax.ShapeDtypeStruct((count, extent + BAND), BF16) for count in rows],
+        in_specs=[SMEM, VMEM, HBM] + [ANY] * len(order),
+        out_specs=[VMEM] * len(rows),
         scratch_shapes=[pltpu.VMEM((slots * depth + LINES, depth * strip), BF16)]
         + stream_scratch(depth, strip),
         compiler_params=limit(10),
@@ -219,19 +240,27 @@
 
 
 def sums_kernel(up_ref, up_near_ref, up_far_ref, down_ref, down_near_ref, down_far_ref, *refs):
-    up_out_ref, down_out_ref = refs[-2:]
-
-    def add(*parts):
-        return functools.reduce(jnp.add, [part.astype(F32) for part in parts]).astype(BF16)
-
-    up_out_ref[:RUN] = add(up_ref[:RUN], up_near_ref[:RUN], up_far_ref[...])
-    up_out_ref[RUN:] = add(up_ref[RUN:], up_near_ref[RUN:])
-    down_out_ref[:RUN] = add(down_ref[:RUN], down_near_ref[:RUN])
-    down_out_ref[RUN:] = add(down_ref[RUN:], down_near_ref[RUN:], down_far_ref[...])
+    extent = up_ref.shape[1] - BAND
+    for own_ref, near_ref, far_ref, low, out_ref in (
+        (up_ref, up_near_ref, up_far_ref, 0, refs[-2]),
+        (down_ref, down_near_ref, down_far_ref, RUN, refs[-1]),
+    ):
+        for row in (0, RUN):
+            rows = slice(row, row + RUN)
+            total = own_ref[rows, :extent].astype(F32) + near_ref[rows, :extent].astype(F32)
+            last = jnp.zeros((RUN, BAND), BF16)
+            if row == low:
+                total = total + far_ref[:, :extent].astype(F32)
+                last = far_ref[:, extent:]
+            out_ref[rows, :extent] = total.astype(BF16)
+            out_ref[rows, extent : extent + BAND] = own_ref[rows, extent:]
+            out_ref[rows, extent + BAND : extent + 2 * BAND] = near_ref[rows, extent:]
+            out_ref[rows, extent + 2 * BAND :] = last
 
 
 def round_sums(*operands):
-    out = jax.ShapeDtypeStruct(operands[0].shape, BF16)
+    rows, lanes = operands[0].shape
+    out = jax.ShapeDtypeStruct((rows, lanes + 2 * BAND), BF16)
     return pl.pallas_call(
         sums_kernel,
         out_shape=(out, out),
@@ -243,52 +272,88 @@
     )(*operands)
 
 
+STRIPS = (0, -1, 1, -2, 2, -3, 3, 4)
+
+
 def last_sums_kernel(
     place_ref, own_ref, mine_ref, below_ref, above_ref, up_ref, down_ref, *refs
 ):
-    kept_ref, sent_ref = refs[-2:]
-    total = (
-        own_ref[...].astype(F32)
-        + below_ref[:PAIR].astype(F32)
-        + above_ref[:PAIR].astype(F32)
-        + up_ref[...].astype(F32)
-        + down_ref[...].astype(F32)
-    )
-    kept_ref[...] = total[:RUN]
-    sent_ref[:RUN] = total[RUN:].astype(BF16)
-    mine, below, above = [ref[PAIR:].astype(F32) for ref in (mine_ref, below_ref, above_ref)]
+    kept_ref, strips_ref, sent_ref = refs[-3:]
+    extent = own_ref.shape[1] - BAND
+    for row in (0, RUN):
+        rows, beside = slice(row, row + RUN), slice(PAIR + row, PAIR + row + RUN)
+        total = (
+            own_ref[rows, :extent].astype(F32)
+            + below_ref[beside, :extent].astype(F32)
+            + above_ref[beside, :extent].astype(F32)
+            + up_ref[rows, :extent].astype(F32)
+            + down_ref[rows, :extent].astype(F32)
+        )
+        near, far = slice(extent, extent + BAND), slice(extent + BAND, extent + 2 * BAND)
+        across = slice(extent + 2 * BAND, extent + 3 * BAND)
+        strips = [
+            own_ref[rows, near],
+            below_ref[beside, near],
+            above_ref[beside, near],
+            up_ref[rows, near],
+            down_ref[rows, near],
+            up_ref[rows, far],
+            down_ref[rows, far],
+            up_ref[rows, across] if row == 0 else down_ref[rows, across],
+        ]
+        if row == 0:
+            kept_ref[...] = total
+            for index, strip in enumerate(strips):
+                strips_ref[:, index * BAND : (index + 1) * BAND] = strip
+        else:
+            sent_ref[:RUN] = total.astype(BF16)
+            halves = [strip[low : low + 16] for strip in strips for low in (0, 16)]
+            sent_ref[RUN + LINES :] = jnp.concatenate(halves, axis=1)
+    mine, below, above = [
+        ref[NEAR - LINES :, :extent].astype(F32) for ref in (mine_ref, below_ref, above_ref)
+    ]
     even = place_ref[1] % 2 == 0
     left = jnp.where(even, mine[8:], below[8:])
     right = jnp.where(even, above[:8], mine[:8])
-    sent_ref[RUN:] = jnp.concatenate([left, right], axis=0).astype(BF16)
+    sent_ref[RUN : RUN + LINES] = jnp.concatenate([left, right], axis=0).astype(BF16)
 
 
 def last_sums(place, own, mine, below, above, up, down, *order):
-    extent = own.shape[1]
+    extent = own.shape[1] - BAND
     return pl.pallas_call(
         last_sums_kernel,
         out_shape=(
             jax.ShapeDtypeStruct((RUN, extent), F32),
-            jax.ShapeDtypeStruct((RUN + LINES, extent), BF16),
+            jax.ShapeDtypeStruct((RUN, len(STRIPS) * BAND), BF16),
+            jax.ShapeDtypeStruct((RUN + LINES + 16, extent), BF16),
         ),
         in_specs=[SMEM] + [VMEM] * 6 + [ANY] * len(order),
-        out_specs=(VMEM, VMEM),
+        out_specs=(VMEM,) * 3,
         compiler_params=limit(8),
         cost_estimate=cost(5 * own.size, 14 * own.size),
         name="last_sums",
     )(place, own, mine, below, above, up, down, *order)
 
 
-def residual_kernel(kept_ref, arrived_ref, views_ref, *refs):
-    out_ref = refs[-1]
+def residual_kernel(place_ref, kept_ref, strips_ref, arrived_ref, got_ref, *refs):
+    out_ref, measured_ref = refs[-2:]
     extent = kept_ref.shape[1]
     blocks = extent // BAND
+    me = place_ref[1]
+    for index, hop in enumerate(STRIPS):
+        tile = lax.rem(me + 2 * hop + blocks, blocks)
+        measured_ref[tile] = strips_ref[:, index * BAND : (index + 1) * BAND].astype(F32)
+        for half in (0, 1):
+            lanes = slice((2 * index + half) * BAND, (2 * index + half + 1) * BAND)
+            measured_ref[tile ^ 1, half * 16 : (half + 1) * 16] = arrived_ref[
+                RUN + LINES :, lanes
+            ].astype(F32)
     empty = jnp.zeros((8, BAND), F32)
     arrived = arrived_ref[:RUN].astype(F32)
     for slot in range(SLOTS):
         low = slot * 8
         total = kept_ref[low : low + 8] + arrived[low : low + 8]
-        band = views_ref[0, slot].astype(F32)
+        band = got_ref[me * SLOTS + slot].astype(F32)
         offset = band[9:10, 0:1].astype(jnp.int32)
         width = jnp.maximum(band[9:10, 1:2], 1.0)
         recip = 1.0 / width
@@ -310,9 +375,7 @@
         sums = jnp.dot(high, onward, preferred_element_type=F32) + jnp.dot(
             rest, onward, preferred_element_type=F32
         )
-        rows = jnp.concatenate(
-            [views_ref[n, slot].astype(F32)[:8] for n in range(blocks)], axis=0
-        )
+        rows = measured_ref[:, low : low + 8].reshape(blocks * 8, BAND)
         residual = (sums - rows).astype(BF16).astype(F32)
         later = jnp.concatenate([residual[8:], empty], axis=0)
         both = jnp.concatenate([residual, later], axis=1).astype(BF16)
@@ -324,16 +387,17 @@
             out_ref[low - 8 : low + 8] = jnp.concatenate([even, image], axis=0).astype(BF16)
 
 
-def residual_images(kept, arrived, views, *order):
+def residual_images(place, kept, strips, arrived, got, *order):
     return pl.pallas_call(
         residual_kernel,
         out_shape=jax.ShapeDtypeStruct(kept.shape, BF16),
-        in_specs=[VMEM] * 3 + [ANY] * len(order),
+        in_specs=[SMEM] + [VMEM] * 4 + [ANY] * len(order),
         out_specs=VMEM,
+        scratch_shapes=[pltpu.VMEM((kept.shape[1] // BAND, RUN, BAND), F32)],
         compiler_params=limit(8),
-        cost_estimate=cost(4 * 8 * 16 * 256 * 128 * 6, 2 * views.size),
+        cost_estimate=cost(4 * 8 * 16 * 256 * 128 * 6, 12 * kept.size),
         name="residual_images",
-    )(kept, arrived, views, *order)
+    )(place, kept, strips, arrived, got, *order)
 
 
 def join_kernel(first_ref, second_ref, order_ref, out_ref):
@@ -368,7 +432,13 @@
     *refs,
 ):
     out_ref, token_ref, under_ref, buffer_ref, sem_ref = refs[-5:]
-    block_ref = streamed(volume_ref, buffer_ref, sem_ref, first_tile, EDGE)
+    step, steps = pl.program_id(0), pl.num_programs(0)
+
+    @pl.when(step == 0)
+    def _():
+        start(tile_copies(volume_ref, buffer_ref, sem_ref, 0, first_tile, EDGE))
+
+    block_ref = streamed(volume_ref, buffer_ref, sem_ref, step, steps, first_tile, EDGE)
     depth, strip, tile = block_ref.shape[0], block_ref.shape[2], XT
     at = pl.program_id(0) + first_tile
     beta = beta_ref[0]
@@ -410,14 +480,14 @@
     depth, extent, strip = volume.shape
     count = extent // XT
     length = count // PIECES
-    start = index * length
-    plane = pl.BlockSpec((1, XT, strip), lambda i: (0, start + i, 0))
-    block = pl.BlockSpec((depth, XT, strip), lambda i: (0, start + i, 0))
+    origin = index * length
+    plane = pl.BlockSpec((1, XT, strip), lambda i: (0, origin + i, 0))
+    block = pl.BlockSpec((depth, XT, strip), lambda i: (0, origin + i, 0))
     specs = [SMEM, SMEM, HBM]
     specs += [plane] * 2 + [ANY] * len(order)
     before = [] if done is None else [done]
     return pl.pallas_call(
-        functools.partial(regularizer_kernel, start, count),
+        functools.partial(regularizer_kernel, origin, count),
         grid=(length,),
         out_shape=(pltpu.HBM(volume.shape, BF16), jax.ShapeDtypeStruct((8, strip), F32)),
         in_specs=specs + [HBM] * len(before),
@@ -431,45 +501,61 @@
 
 
 def gradient_kernel(place_ref, beta_ref, spread_ref, mine_ref, beside_ref, *refs):
-    chunk_refs = refs[:-4]
-    whole_ref, out_ref, buffer_ref, sem_ref = refs[-4:]
-    regular_ref = streamed(whole_ref, buffer_ref, sem_ref, 0)
-    depth, tile, strip = out_ref.shape
+    chunk_refs = refs[:-6]
+    whole_ref, out_ref, buffer_ref, sem_ref, result_ref, result_sem_ref = refs[-6:]
+    depth, extent, strip = whole_ref.shape
+    steps = extent // XT
     beta = beta_ref[0]
     has_left = (place_ref[1] > 0).astype(F32)
     has_right = (place_ref[1] < place_ref[2] - 1).astype(F32)
-    mine, beside = mine_ref[...].astype(F32), beside_ref[...].astype(F32)
-    on_left = penalty(mine[:8] - beside[:8]) * (has_left * beta)
-    on_right = penalty(mine[8:] - beside[8:]) * (has_right * beta)
-    ends = jnp.concatenate([on_left, on_right], axis=0).astype(BF16)
-    rows = jnp.concatenate([ref[...] for ref in chunk_refs] + [ends], axis=0)
-    out = lax.dot_general(
-        rows, spread_ref[...], (((0,), (0,)), ((), ())), preferred_element_type=F32
-    )
-    for z in range(depth):
-        regular = regular_ref[z].astype(F32)
-        out_ref[z] = (out[:, z * strip : (z + 1) * strip] + regular).astype(BF16)
+    start(tile_copies(whole_ref, buffer_ref, sem_ref, 0))
+
+    def result(step):
+        slot = lax.rem(step, 2)
+        here = pl.ds(pl.multiple_of(step * XT, XT), XT)
+        return pltpu.make_async_copy(
+            result_ref.at[slot], out_ref.at[:, here], result_sem_ref.at[slot]
+        )
+
+    def body(step, carry):
+        here = pl.ds(pl.multiple_of(step * XT, XT), XT)
+        mine = mine_ref[NEAR - LINES :, here].astype(F32)
+        beside = beside_ref[RUN : RUN + LINES, here].astype(F32)
+        on_left = penalty(mine[:8] - beside[:8]) * (has_left * beta)
+        on_right = penalty(mine[8:] - beside[8:]) * (has_right * beta)
+        ends = jnp.concatenate([on_left, on_right], axis=0).astype(BF16)
+        rows = jnp.concatenate([ref[:, here] for ref in chunk_refs] + [ends], axis=0)
+        out = lax.dot_general(
+            rows, spread_ref[...], (((0,), (0,)), ((), ())), preferred_element_type=F32
+        )
+        regular_ref = streamed(whole_ref, buffer_ref, sem_ref, step, steps)
+
+        @pl.when(step >= 2)
+        def _():
+            result(step - 2).wait()
+
+        slot = lax.rem(step, 2)
+        for z in range(depth):
+            regular = regular_ref[z].astype(F32)
+            result_ref[slot, z] = (out[:, z * strip : (z + 1) * strip] + regular).astype(BF16)
+        result(step).start()
+        return carry
+
+    lax.fori_loop(0, steps, body, 0)
+    result(jnp.int32(steps - 2)).wait()
+    result(jnp.int32(steps - 1)).wait()
 
 
 def gradient(place, beta, spread, mine, arrived, chunks, regular):
     depth, extent, strip = regular.shape
-    block = pl.BlockSpec((depth, XT, strip), lambda i: (0, i, 0))
     size = depth * extent * strip
     return pl.pallas_call(
         gradient_kernel,
-        grid=(extent // XT,),
         out_shape=jax.ShapeDtypeStruct(regular.shape, BF16),
-        in_specs=[
-            SMEM,
-            SMEM,
-            pl.BlockSpec(spread.shape, lambda i: (0, 0)),
-            pl.BlockSpec((LINES, XT), lambda i: (PAIR // LINES, i)),
-            pl.BlockSpec((LINES, XT), lambda i: (RUN // LINES, i)),
-        ]
-        + [pl.BlockSpec((chunk.shape[0], XT), lambda i: (0, i)) for chunk in chunks]
-        + [HBM],
-        out_specs=block,
-        scratch_shapes=stream_scratch(depth, strip),
+        in_specs=[SMEM, SMEM] + [VMEM] * (3 + len(chunks)) + [HBM],
+        out_specs=ANY,
+        scratch_shapes=stream_scratch(depth, strip)
+        + [pltpu.VMEM((2, depth, XT, strip), BF16), pltpu.SemaphoreType.DMA((2,))],
         compiler_params=limit(12),
         cost_estimate=cost(2 * spread.shape[0] * size, 5 * size),
         name="gradient",
@@ -498,35 +584,34 @@
     flat = got.reshape(slabs * SLOTS, ROWS, BAND)
     volume = pltpu.with_memory_space_constraint(volume, pltpu.HBM)
 
-    own, up1, down1, up2, down2, up3, down3, far_up, far_down = forward(
+    own, up2, down2, near_up, near_down, far_up, far_down = forward(
         place, flat, volume, tiles, top, bottom
     )
-    mine = up1
-    near = along_z(up3, 1), along_z(down3, -1)
+    near_up, near_down, far_up, far_down, below, above = lax.optimization_barrier(
+        (near_up, near_down, far_up, far_down, below, above)
+    )
+    near = along_z(near_up, 1), along_z(near_down, -1)
     far = along_z(far_up, 2), along_z(far_down, -2)
-    one = along_z(up1, 1), along_z(down1, -1)
     regular, token = regularizer(0, None, place, beta, volume, below, above, far_up)
-    up, down = round_sums(up2, near[0], far[0], down2, near[1], far[1], token, *one)
+    up, down = round_sums(up2, near[0], far[0], down2, near[1], far[1], token)
     two = along_z(up, 2), along_z(down, -2)
-    spread, views = spread_rows(place, flat, tiles, up)
-    views = views.reshape(got.shape)
-    views = lax.all_to_all(views, "tile", split_axis=0, concat_axis=0, tiled=True)
-    kept, sent = last_sums(place, own, up1, *one, *two, views)
+    regular, token = regularizer(1, regular, place, beta, volume, below, above, up)
+    kept, strips, sent = last_sums(place, own, near_up, *near, *two, token)
     arrived = along_y(sent)
-    regular, token = regularizer(1, regular, place, beta, volume, below, above, sent)
-    images = residual_images(kept, arrived, views, token)
+    images = residual_images(place, kept, strips, arrived, flat)
 
     partner = along_y(images)
     regular, token = regularizer(2, regular, place, beta, volume, below, above, images)
     pair = join(images, partner, token)
     up2, down2 = along_z(pair, 2), along_z(pair, -2)
     up1, down1 = along_z(pair, 1), along_z(pair, -1)
-    regular, token = regularizer(3, regular, place, beta, volume, below, above, pair)
+    spread = spread_rows(place, flat, tiles, pair)
+    regular, token = regularizer(3, regular, place, beta, volume, below, above, pair, spread)
     up3, down3 = along_z(up2, 1), along_z(down2, -1)
     far_up, far_down = along_z(up2[:RUN], 2), along_z(down2[RUN:], -2)
     chunks = [pair, down1, up1, down2, up2, down3, up3, far_up, far_down]
     regular = pltpu.with_memory_space_constraint(regular, pltpu.HBM)
-    return gradient(place, beta, spread, mine, arrived, chunks, regular)
+    return gradient(place, beta, spread, near_up, arrived, chunks, regular)
 
 
 def solution(mesh):

time: 146 us -> 137 us (0.938)
  starting transfers between devices: 55.5 us -> 43.3 us
  waiting for transfers between devices: 37 us -> 47.5 us
  local copies, waits for them, and re-layouts: 7.67 us -> 1.29 us
  Pallas kernels: 43.2 us -> 41.4 us
    all_to_all x1 -> x0, starting transfers between devices: 7.97 us -> none  [shards(): lax.all_to_all(views, 'tile', split_axis=0, concat_axis=0, tiled=True)]
    all_to_all x1, waiting for transfers between devices: 0.79 us -> 7.3 us  [shards(): lax.all_to_all(packed, 'slab', split_axis=0, concat_axis=0, tiled=True)]
    unnamed x18 -> x0, local copies, waits for them, and re-layouts: 6.38 us -> none
    ppermute x2, waiting for transfers between devices: 0.01 us -> 6.27 us  [along_y(): return lax.ppermute(block, 'tile', [(i, i ^ 1) for i in range(tiles)])]
    ppermute x16 -> x14, starting transfers between devices: 32.3 us -> 27 us  [along_z(): lax.ppermute(block, 'tile', [(i, (i + 2 * by) % tiles) for i in range(til...]
    pallas_call x7, Pallas kernels: 39.7 us -> 37.3 us  [the longest x4 21.6 us: regularizer(): pl.pallas_call(functools.partial(regularizer_kernel, origin, count), grid...]
    ppermute x16 -> x14, waiting for transfers between devices: 36.1 us -> 33.9 us  [along_z(): lax.ppermute(block, 'tile', [(i, (i + 2 * by) % tiles) for i in range(til...]
    ppermute x1, starting transfers between devices: 2.02 us -> 3.64 us  [shards(): above = lax.ppermute(bottom, 'slab', [(i + 1, i) for i in range(slabs - 1)])]
  transfers between devices with their start and end apart: 22 -> 19, of which waited for: 9 -> 9; matrix products, arithmetic and copies ran while one was open for 1% -> 0% of each run, Pallas kernels for 20% -> 22%
where the time goes in v4:
time: 137 us; the launch traced here: 134 us
  waiting for transfers between devices  47.5 us (35%)
  starting transfers between devices  43.3 us (32%)
  Pallas kernels  41.4 us (30%)
    ppermute x14, waiting for transfers between devices, along_z(): lax.ppermute(block, 'tile', [(i, (i + 2 * by) % tiles) for i in range(til...  33.9 us
    ppermute x14, starting transfers between devices, along_z(): lax.ppermute(block, 'tile', [(i, (i + 2 * by) % tiles) for i in range(til...  27 us
    pallas_call x4, Pallas kernels, regularizer(): pl.pallas_call(functools.partial(regularizer_kernel, origin, count), grid...  21.6 us
    pallas_call x1, Pallas kernels, gradient(): pl.pallas_call(gradient_kernel, out_shape=jax.ShapeDtypeStruct(regular.sh...  7.69 us
    all_to_all x1, waiting for transfers between devices, shards(): lax.all_to_all(packed, 'slab', split_axis=0, concat_axis=0, tiled=True)  7.3 us
    pallas_call x1, Pallas kernels, forward(): pl.pallas_call(kernel, out_shape=[jax.ShapeDtypeStruct((count, extent + B...  7.24 us
    ppermute x2, waiting for transfers between devices, along_y(): return lax.ppermute(block, 'tile', [(i, i ^ 1) for i in range(tiles)])  6.27 us
    all_to_all x1, starting transfers between devices, shards(): lax.all_to_all(packed, 'slab', split_axis=0, concat_axis=0, tiled=True)  5.79 us
  transfers between devices with their start and end apart: 19, of which 9 were waited for; matrix products, arithmetic and copies ran while one was open for 0% of the time, Pallas kernels for 22%

profile of v4, /device:TPU:8, one launch (start us, length us, event | category | flops | bytes accessed | tf_op | source)
XLA Modules:
  0.0 134.4 jit_solution(860643581047501882)
XLA Ops:
  0.0 1.7 %pack_messages.1 = bf16[16,4,16,128]{3,2,1,0:T(8,128)(2,1)} custom-call(s32[2,12]{1,0:T(2,128)} %bitcast.9, s32[2,12]{1,0:T(2,128)} %offset_ref.1, s32[2,12]{1,0:T(2,128)} %width_ref.1, bf16[12,2,128]{2,1,0:T(2,128)(2,1)} %bitcast.8, bf16[2,12,8,128]{3,2,1,0:T(8,128)(2,1)} %measured_ref.1), custom_call_target="tpu_custom_call" | custom-call | tf_op jit(solution)/shard_map/pack_messages/pallas_call | solution.py:67
  1.7 1.3 fusion
  3.0 1.9 %collective-permute-start = (bf16[1,2048,128]{2,1,0:T(8,128)(2,1)S(1)}, bf16[1,2048,128]{2,1,0:T(8,128)(2,1)S(1)}, u32[]{:S(2)}, u32[]{:S(2)}) collective-permute-start(bf16[1,2048,128]{2,1,0:T(8,128)(2,1)S(1)} %get-tuple-element.60.refs_0_), channel_id=1, source_target_pairs={{0,16},{16,32},{32,48},{48,64},{64,80},{80,96},{96,112},{112,128},... | collective-permute-start | bytes 1572872 | tf_op jit(solution)/shard_map/ppermute | solution.py:582
  4.9 3.6 %collective-permute-start.1 = (bf16[1,2048,128]{2,1,0:T(8,128)(2,1)S(1)}, bf16[1,2048,128]{2,1,0:T(8,128)(2,1)S(1)}, u32[]{:S(2)}, u32[]{:S(2)}) collective-permute-start(bf16[1,2048,128]{2,1,0:T(8,128)(2,1)S(1)} %get-tuple-element.59.refs_1_), channel_id=1, source_target_pairs={{16,0},{32,16},{48,32},{64,48},{80,64},{96,80},{112,96},{128,112},... | collective-permute-start | bytes 1572872 | tf_op jit(solution)/shard_map/ppermute | solution.py:583
  8.5 5.8 %all-to-all-start = ((bf16[16,4,16,128]{3,2,1,0:T(8,128)(2,1)}), bf16[16,4,16,128]{3,2,1,0:T(8,128)(2,1)S(1)}, u32[]{:S(2)}, u32[]{:S(2)}) async-start(bf16[16,4,16,128]{3,2,1,0:T(8,128)(2,1)} %pack_messages.1), calls=%async_computation | async-start | bytes 524288 | tf_op jit(solution)/shard_map/all_to_all | solution.py:580
  14.4 7.3 %all-to-all-done = bf16[16,4,16,128]{3,2,1,0:T(8,128)(2,1)S(1)} async-done(((bf16[16,4,16,128]{3,2,1,0:T(8,128)(2,1)}), bf16[16,4,16,128]{3,2,1,0:T(8,128)(2,1)S(1)}, u32[]{:S(2)}, u32[]{:S(2)}) %all-to-all-start) | async-done | bytes 262176 | tf_op jit(solution)/shard_map/all_to_all | solution.py:580
  21.7 7.2 %forward.1 = (bf16[64,2176]{1,0:T(8,128)(2,1)S(1)}, bf16[64,2176]{1,0:T(8,128)(2,1)S(1)}, bf16[64,2176]{1,0:T(8,128)(2,1)S(1)}, bf16[144,2176]{1,0:T(8,128)(2,1)...) custom-call(s32[4]{0:T(128)S(1)} %pad_add_fusion.place_ref, ...), custom_call_target="tpu_custom_call" | custom-call | flops 2147483648 | bytes 6291456 | tf_op jit(solution)/shard_map/forward/pallas_call | solution.py:229
  29.0 2.0 %collective-permute-start.2 = (bf16[144,2176]{1,0:T(8,128)(2,1)S(1)}, bf16[144,2176]{1,0:T(8,128)(2,1)S(1)}, u32[]{:S(2)}, u32[]{:S(2)}) collective-permute-start(bf16[144,2176]{1,0:T(8,128)(2,1)S(1)} %get-tuple-element.39.mine_ref), channel_id=1, source_target_pairs={{0,2},{1,3},{2,4},{3,5},{4,6},{5,7},{6,8},{7,9},{8,10},{9,11},{10,... | collective-permute-start | bytes 1880072 | tf_op jit(solution)/shard_map/ppermute | solution.py:573
  31.0 4.0 %collective-permute-start.3 = (bf16[144,2176]{1,0:T(8,128)(2,1)S(1)}, bf16[144,2176]{1,0:T(8,128)(2,1)S(1)}, u32[]{:S(2)}, u32[]{:S(2)}) collective-permute-start(bf16[144,2176]{1,0:T(8,128)(2,1)S(1)} %get-tuple-element.40), channel_id=1, source_target_pairs={{0,14},{1,15},{2,0},{3,1},{4,2},{5,3},{6,4},{7,5},{8,6},{9,7},{10,... | collective-permute-start | bytes 1880072 | tf_op jit(solution)/shard_map/ppermute | solution.py:573
  35.0 4.1 %collective-permute-start.5 = (bf16[32,2176]{1,0:T(8,128)(2,1)S(1)}, bf16[32,2176]{1,0:T(8,128)(2,1)S(1)}, u32[]{:S(2)}, u32[]{:S(2)}) collective-permute-start(bf16[32,2176]{1,0:T(8,128)(2,1)S(1)} %get-tuple-element.44), channel_id=1, source_target_pairs={{0,12},{1,13},{2,14},{3,15},{4,0},{5,1},{6,2},{7,3},{8,4},{9,5},{1... | collective-permute-start | bytes 417800 | tf_op jit(solution)/shard_map/ppermute | solution.py:573
  39.8 5.5 %regularizer.4 = (bf16[8,2048,128]{2,1,0:T(8,128)(2,1)}, f32[8,128]{1,0:T(8,128)S(1)}) custom-call(s32[4]{0:T(128)S(1)} %pad_add_fusion.place_ref, f32[1]{0:T(128)S(6)} %copy.14.beta_ref, bf16[8,2048,128]{2,1,0:T(8,128)(2,1)} %volume_ref.9, bf16[1,2048,128]{2,1,0:T(8,128)(2,1)S(1)} %collective-permute-done.below_ref, ...), custom_call_target="tpu_custom_call" | custom-call | flops 15728640 | bytes 4194304 | tf_op jit(solution)/shard_map/regularizer/pallas_call | solution.py:489
  45.3 8.9 %collective-permute-done.4.up_far_ref = bf16[32,2176]{1,0:T(8,128)(2,1)S(1)} collective-permute-done((bf16[32,2176]{1,0:T(8,128)(2,1)S(1)}, bf16[32,2176]{1,0:T(8,128)(2,1)S(1)}, u32[]{:S(2)}, u32[]{:S(2)}) %collective-permute-start.4) | collective-permute-done | bytes 139296 | tf_op jit(solution)/shard_map/ppermute | solution.py:573
  54.8 5.3 %collective-permute-start.6 = (bf16[64,2432]{1,0:T(8,128)(2,1)S(1)}, bf16[64,2432]{1,0:T(8,128)(2,1)S(1)}, u32[]{:S(2)}, u32[]{:S(2)}) collective-permute-start(bf16[64,2432]{1,0:T(8,128)(2,1)S(1)} %get-tuple-element.48.refs_0_), channel_id=1, source_target_pairs={{0,4},{1,5},{2,6},{3,7},{4,8},{5,9},{6,10},{7,11},{8,12},{9,13},{1... | collective-permute-start | bytes 933896 | tf_op jit(solution)/shard_map/ppermute | solution.py:573
  60.1 5.4 %regularizer.5 = (bf16[8,2048,128]{2,1,0:T(8,128)(2,1)}, f32[8,128]{1,0:T(8,128)S(1)}) custom-call(s32[4]{0:T(128)S(1)} %pad_add_fusion.place_ref, f32[1]{0:T(128)S(6)} %copy.14.beta_ref, bf16[8,2048,128]{2,1,0:T(8,128)(2,1)} %volume_ref.9, bf16[1,2048,128]{2,1,0:T(8,128)(2,1)S(1)} %collective-permute-done.below_ref, ...), custom_call_target="tpu_custom_call", output_to_operand_aliasing={{0}: (6, {})} | custom-call | flops 15728640 | bytes 4194304 | tf_op jit(solution)/shard_map/regularizer/pallas_call | solution.py:489
  65.5 7.6 %collective-permute-done.6.up_ref = bf16[64,2432]{1,0:T(8,128)(2,1)S(1)} collective-permute-done((bf16[64,2432]{1,0:T(8,128)(2,1)S(1)}, bf16[64,2432]{1,0:T(8,128)(2,1)S(1)}, u32[]{:S(2)}, u32[]{:S(2)}) %collective-permute-start.6) | collective-permute-done | bytes 311328 | tf_op jit(solution)/shard_map/ppermute | solution.py:573
  73.1 1.5 %collective-permute-done.7.down_ref = bf16[64,2432]{1,0:T(8,128)(2,1)S(1)} collective-permute-done((bf16[64,2432]{1,0:T(8,128)(2,1)S(1)}, bf16[64,2432]{1,0:T(8,128)(2,1)S(1)}, u32[]{:S(2)}, u32[]{:S(2)}) %collective-permute-start.7) | collective-permute-done | bytes 311328 | tf_op jit(solution)/shard_map/ppermute | solution.py:573
  75.3 2.4 %collective-permute-start.8 = (bf16[64,2048]{1,0:T(8,128)(2,1)S(1)}, bf16[64,2048]{1,0:T(8,128)(2,1)S(1)}, u32[]{:S(2)}, u32[]{:S(2)}) collective-permute-start(bf16[64,2048]{1,0:T(8,128)(2,1)S(1)} %get-tuple-element.54), channel_id=1, source_target_pairs={{0,1},{1,0},{2,3},{3,2},{4,5},{5,4},{6,7},{7,6},{8,9},{9,8},{10,11... | collective-permute-start | bytes 786440 | tf_op jit(solution)/shard_map/ppermute | solution.py:576
  77.7 6.3 %collective-permute-done.8.arrived_ref.beside_ref = bf16[64,2048]{1,0:T(8,128)(2,1)S(1)} collective-permute-done((bf16[64,2048]{1,0:T(8,128)(2,1)S(1)}, bf16[64,2048]{1,0:T(8,128)(2,1)S(1)}, u32[]{:S(2)}, u32[]{:S(2)}) %collective-permute-start.8) | collective-permute-done | bytes 262176 | tf_op jit(solution)/shard_map/ppermute | solution.py:576
  84.0 1.4 %residual_images.1.refs_0_.first_ref = bf16[32,2048]{1,0:T(8,128)(2,1)S(1)} custom-call(s32[4]{0:T(128)S(1)} %pad_add_fusion.place_ref, f32[32,2048]{1,0:T(8,128)S(1)} %get-tuple-element.52.kept_ref, bf16[32,1024]{1,0:T(8,128)(2,1)S(1)} %get-tuple-element.53.strips_ref, bf16[64,2048]{1,0:T(8,128)(2,1)S(1)} %collective-permute-done.8.arrived_ref.beside_ref, ...), custom_call_target="tpu_custom_call" | custom-call | flops 100663296 | bytes 786432 | tf_op jit(solution)/shard_map/residual_images/pallas_call | solution.py:391
  85.4 2.5 %collective-permute-start.9 = (bf16[32,2048]{1,0:T(8,128)(2,1)S(1)}, bf16[32,2048]{1,0:T(8,128)(2,1)S(1)}, u32[]{:S(2)}, u32[]{:S(2)}) collective-permute-start(bf16[32,2048]{1,0:T(8,128)(2,1)S(1)} %residual_images.1.refs_0_.first_ref), channel_id=1, source_target_pairs={{0,1},{1,0},{2,3},{3,2},{4,5},{5,4},{6,7},{7,6},{8,9},{9,8},{10,11... | collective-permute-start | bytes 393224 | tf_op jit(solution)/shard_map/ppermute | solution.py:576
  87.9 5.4 %regularizer.6 = (bf16[8,2048,128]{2,1,0:T(8,128)(2,1)}, f32[8,128]{1,0:T(8,128)S(1)}) custom-call(s32[4]{0:T(128)S(1)} %pad_add_fusion.place_ref, f32[1]{0:T(128)S(6)} %copy.14.beta_ref, bf16[8,2048,128]{2,1,0:T(8,128)(2,1)} %volume_ref.9, bf16[1,2048,128]{2,1,0:T(8,128)(2,1)S(1)} %collective-permute-done.below_ref, ...), custom_call_target="tpu_custom_call", output_to_operand_aliasing={{0}: (6, {})} | custom-call | flops 15728640 | bytes 4194304 | tf_op jit(solution)/shard_map/regularizer/pallas_call | solution.py:489
  93.3 2.8 %collective-permute-start.12 = (bf16[64,2048]{1,0:T(8,128)(2,1)S(1)}, bf16[64,2048]{1,0:T(8,128)(2,1)S(1)}, u32[]{:S(2)}, u32[]{:S(2)}) collective-permute-start(bf16[64,2048]{1,0:T(8,128)(2,1)S(1)} %join.1.order_ref.refs_0_), channel_id=1, source_target_pairs={{0,12},{1,13},{2,14},{3,15},{4,0},{5,1},{6,2},{7,3},{8,4},{9,5},{1... | collective-permute-start | bytes 786440 | tf_op jit(solution)/shard_map/ppermute | solution.py:573
  97.0 1.4 %collective-permute-start.11 = (bf16[64,2048]{1,0:T(8,128)(2,1)S(1)}, bf16[64,2048]{1,0:T(8,128)(2,1)S(1)}, u32[]{:S(2)}, u32[]{:S(2)}) collective-permute-start(bf16[64,2048]{1,0:T(8,128)(2,1)S(1)} %join.1.order_ref.refs_0_), channel_id=1, source_target_pairs={{0,2},{1,3},{2,4},{3,5},{4,6},{5,7},{6,8},{7,9},{8,10},{9,11},{10,... | collective-permute-start | bytes 786440 | tf_op jit(solution)/shard_map/ppermute | solution.py:573
  98.4 7.8 %collective-permute-done.12.refs_3_ = bf16[64,2048]{1,0:T(8,128)(2,1)S(1)} collective-permute-done((bf16[64,2048]{1,0:T(8,128)(2,1)S(1)}, bf16[64,2048]{1,0:T(8,128)(2,1)S(1)}, u32[]{:S(2)}, u32[]{:S(2)}) %collective-permute-start.12) | collective-permute-done | bytes 262176 | tf_op jit(solution)/shard_map/ppermute | solution.py:573
  106.1 2.2 %collective-permute-start.14 = (bf16[64,2048]{1,0:T(8,128)(2,1)S(1)}, bf16[64,2048]{1,0:T(8,128)(2,1)S(1)}, u32[]{:S(2)}, u32[]{:S(2)}) collective-permute-start(bf16[64,2048]{1,0:T(8,128)(2,1)S(1)} %collective-permute-done.12.refs_3_), channel_id=1, source_target_pairs={{0,14},{1,15},{2,0},{3,1},{4,2},{5,3},{6,4},{7,5},{8,6},{9,7},{10,... | collective-permute-start | bytes 786440 | tf_op jit(solution)/shard_map/ppermute | solution.py:573
  108.4 4.6 %collective-permute-done.13.refs_4_ = bf16[64,2048]{1,0:T(8,128)(2,1)S(1)} collective-permute-done((bf16[64,2048]{1,0:T(8,128)(2,1)S(1)}, bf16[64,2048]{1,0:T(8,128)(2,1)S(1)}, u32[]{:S(2)}, u32[]{:S(2)}) %collective-permute-start.13) | collective-permute-done | bytes 262176 | tf_op jit(solution)/shard_map/ppermute | solution.py:573
  113.0 1.4 %collective-permute-start.16 = (bf16[32,2048]{1,0:T(8,128)(2,1)S(1)}, bf16[32,2048]{1,0:T(8,128)(2,1)S(1)}, u32[]{:S(2)}, u32[]{:S(2)}) collective-permute-start(bf16[32,2048]{1,0:T(8,128)(2,1)S(1)} %slice.16), channel_id=1, source_target_pairs={{0,4},{1,5},{2,6},{3,7},{4,8},{5,9},{6,10},{7,11},{8,12},{9,13},{1... | collective-permute-start | bytes 393224 | tf_op jit(solution)/shard_map/ppermute | solution.py:573
  114.5 2.9 %collective-permute-start.17 = (bf16[32,2048]{1,0:T(8,128)(2,1)S(1)}, bf16[32,2048]{1,0:T(8,128)(2,1)S(1)}, u32[]{:S(2)}, u32[]{:S(2)}) collective-permute-start(bf16[32,2048]{1,0:T(8,128)(2,1)S(1)} %slice.17), channel_id=1, source_target_pairs={{0,12},{1,13},{2,14},{3,15},{4,0},{5,1},{6,2},{7,3},{8,4},{9,5},{1... | collective-permute-start | bytes 393224 | tf_op jit(solution)/shard_map/ppermute | solution.py:573
  117.3 0.8 spread_rows.1.refs_1_.spread_ref
  118.1 5.4 %regularizer.7 = (bf16[8,2048,128]{2,1,0:T(8,128)(2,1)}, f32[8,128]{1,0:T(8,128)}) custom-call(s32[4]{0:T(128)S(1)} %pad_add_fusion.place_ref, f32[1]{0:T(128)S(6)} %copy.14.beta_ref, bf16[8,2048,128]{2,1,0:T(8,128)(2,1)} %volume_ref.9, bf16[1,2048,128]{2,1,0:T(8,128)(2,1)S(1)} %collective-permute-done.below_ref, ...), custom_call_target="tpu_custom_call", output_to_operand_aliasing={{0}: (7, {})} | custom-call | flops 15728640 | bytes 4194304 | tf_op jit(solution)/shard_map/regularizer/pallas_call | solution.py:489
  123.5 3.0 %collective-permute-done.16.refs_7_ = bf16[32,2048]{1,0:T(8,128)(2,1)S(1)} collective-permute-done((bf16[32,2048]{1,0:T(8,128)(2,1)S(1)}, bf16[32,2048]{1,0:T(8,128)(2,1)S(1)}, u32[]{:S(2)}, u32[]{:S(2)}) %collective-permute-start.16) | collective-permute-done | bytes 131104 | tf_op jit(solution)/shard_map/ppermute | solution.py:573
  126.6 7.7 %gradient.1 = bf16[8,2048,128]{2,1,0:T(8,128)(2,1)} custom-call(s32[4]{0:T(128)S(1)} %pad_add_fusion.place_ref, f32[1]{0:T(128)S(6)} %copy.14.beta_ref, bf16[528,1024]{1,0:T(8,128)(2,1)S(1)} %spread_rows.1.refs_1_.spread_ref, bf16[144,2176]{1,0:T(8,128)(2,1)S(1)} %get-tuple-element.39.mine_ref, ...), custom_call_target="tpu_custom_call" | custom-call | flops 2214592512 | bytes 10485760 | tf_op jit(solution)/shard_map/gradient/pallas_call | solution.py:552
  (23 shorter events, 2.4 us)
Async XLA Ops:
  3.0 26.0 %collective-permute-start = (bf16[1,2048,128]{2,1,0:T(8,128)(2,1)S(1)}, bf16[1,2048,128]{2,1,0:T(8,128)(2,1)S(1)}, u32[]{:S(2)}, u32[]{:S(2)}) collective-permute-start(bf16[1,2048,128]{2,1,0:T(8,128)(2,1)S(1)} %get-tuple-element.60.refs_0_), channel_id=1, source_target_pairs={{0,16},{16,32},{32,48},{48,64},{64,80},{80,96},{96,112},{112,128},... | collective-permute-start | bytes 1572872 | tf_op jit(solution)/shard_map/ppermute | solution.py:582
  4.9 24.1 %collective-permute-start.1 = (bf16[1,2048,128]{2,1,0:T(8,128)(2,1)S(1)}, bf16[1,2048,128]{2,1,0:T(8,128)(2,1)S(1)}, u32[]{:S(2)}, u32[]{:S(2)}) collective-permute-start(bf16[1,2048,128]{2,1,0:T(8,128)(2,1)S(1)} %get-tuple-element.59.refs_1_), channel_id=1, source_target_pairs={{16,0},{32,16},{48,32},{64,48},{80,64},{96,80},{112,96},{128,112},... | collective-permute-start | bytes 1572872 | tf_op jit(solution)/shard_map/ppermute | solution.py:583
  8.5 13.2 %all-to-all-start = ((bf16[16,4,16,128]{3,2,1,0:T(8,128)(2,1)}), bf16[16,4,16,128]{3,2,1,0:T(8,128)(2,1)S(1)}, u32[]{:S(2)}, u32[]{:S(2)}) async-start(bf16[16,4,16,128]{3,2,1,0:T(8,128)(2,1)} %pack_messages.1), calls=%async_computation | async-start | bytes 524288 | tf_op jit(solution)/shard_map/all_to_all | solution.py:580
  29.0 25.7 %collective-permute-start.2 = (bf16[144,2176]{1,0:T(8,128)(2,1)S(1)}, bf16[144,2176]{1,0:T(8,128)(2,1)S(1)}, u32[]{:S(2)}, u32[]{:S(2)}) collective-permute-start(bf16[144,2176]{1,0:T(8,128)(2,1)S(1)} %get-tuple-element.39.mine_ref), channel_id=1, source_target_pairs={{0,2},{1,3},{2,4},{3,5},{4,6},{5,7},{6,8},{7,9},{8,10},{9,11},{10,... | collective-permute-start | bytes 1880072 | tf_op jit(solution)/shard_map/ppermute | solution.py:573
  31.0 23.7 %collective-permute-start.3 = (bf16[144,2176]{1,0:T(8,128)(2,1)S(1)}, bf16[144,2176]{1,0:T(8,128)(2,1)S(1)}, u32[]{:S(2)}, u32[]{:S(2)}) collective-permute-start(bf16[144,2176]{1,0:T(8,128)(2,1)S(1)} %get-tuple-element.40), channel_id=1, source_target_pairs={{0,14},{1,15},{2,0},{3,1},{4,2},{5,3},{6,4},{7,5},{8,6},{9,7},{10,... | collective-permute-start | bytes 1880072 | tf_op jit(solution)/shard_map/ppermute | solution.py:573
  35.0 19.2 %collective-permute-start.4 = (bf16[32,2176]{1,0:T(8,128)(2,1)S(1)}, bf16[32,2176]{1,0:T(8,128)(2,1)S(1)}, u32[]{:S(2)}, u32[]{:S(2)}) collective-permute-start(bf16[32,2176]{1,0:T(8,128)(2,1)S(1)} %get-tuple-element.42.refs_0_), channel_id=1, source_target_pairs={{0,4},{1,5},{2,6},{3,7},{4,8},{5,9},{6,10},{7,11},{8,12},{9,13},{1... | collective-permute-start | bytes 417800 | tf_op jit(solution)/shard_map/ppermute | solution.py:573
  35.0 19.6 %collective-permute-start.5 = (bf16[32,2176]{1,0:T(8,128)(2,1)S(1)}, bf16[32,2176]{1,0:T(8,128)(2,1)S(1)}, u32[]{:S(2)}, u32[]{:S(2)}) collective-permute-start(bf16[32,2176]{1,0:T(8,128)(2,1)S(1)} %get-tuple-element.44), channel_id=1, source_target_pairs={{0,12},{1,13},{2,14},{3,15},{4,0},{5,1},{6,2},{7,3},{8,4},{9,5},{1... | collective-permute-start | bytes 417800 | tf_op jit(solution)/shard_map/ppermute | solution.py:573
  54.8 18.2 %collective-permute-start.6 = (bf16[64,2432]{1,0:T(8,128)(2,1)S(1)}, bf16[64,2432]{1,0:T(8,128)(2,1)S(1)}, u32[]{:S(2)}, u32[]{:S(2)}) collective-permute-start(bf16[64,2432]{1,0:T(8,128)(2,1)S(1)} %get-tuple-element.48.refs_0_), channel_id=1, source_target_pairs={{0,4},{1,5},{2,6},{3,7},{4,8},{5,9},{6,10},{7,11},{8,12},{9,13},{1... | collective-permute-start | bytes 933896 | tf_op jit(solution)/shard_map/ppermute | solution.py:573
  60.1 14.4 %collective-permute-start.7 = (bf16[64,2432]{1,0:T(8,128)(2,1)S(1)}, bf16[64,2432]{1,0:T(8,128)(2,1)S(1)}, u32[]{:S(2)}, u32[]{:S(2)}) collective-permute-start(bf16[64,2432]{1,0:T(8,128)(2,1)S(1)} %get-tuple-element.49), channel_id=1, source_target_pairs={{0,12},{1,13},{2,14},{3,15},{4,0},{5,1},{6,2},{7,3},{8,4},{9,5},{1... | collective-permute-start | bytes 933896 | tf_op jit(solution)/shard_map/ppermute | solution.py:573
  75.3 8.7 %collective-permute-start.8 = (bf16[64,2048]{1,0:T(8,128)(2,1)S(1)}, bf16[64,2048]{1,0:T(8,128)(2,1)S(1)}, u32[]{:S(2)}, u32[]{:S(2)}) collective-permute-start(bf16[64,2048]{1,0:T(8,128)(2,1)S(1)} %get-tuple-element.54), channel_id=1, source_target_pairs={{0,1},{1,0},{2,3},{3,2},{4,5},{5,4},{6,7},{7,6},{8,9},{9,8},{10,11... | collective-permute-start | bytes 786440 | tf_op jit(solution)/shard_map/ppermute | solution.py:576
  85.4 7.9 %collective-permute-start.9 = (bf16[32,2048]{1,0:T(8,128)(2,1)S(1)}, bf16[32,2048]{1,0:T(8,128)(2,1)S(1)}, u32[]{:S(2)}, u32[]{:S(2)}) collective-permute-start(bf16[32,2048]{1,0:T(8,128)(2,1)S(1)} %residual_images.1.refs_0_.first_ref), channel_id=1, source_target_pairs={{0,1},{1,0},{2,3},{3,2},{4,5},{5,4},{6,7},{7,6},{8,9},{9,8},{10,11... | collective-permute-start | bytes 393224 | tf_op jit(solution)/shard_map/ppermute | solution.py:576
  93.3 12.8 %collective-permute-start.12 = (bf16[64,2048]{1,0:T(8,128)(2,1)S(1)}, bf16[64,2048]{1,0:T(8,128)(2,1)S(1)}, u32[]{:S(2)}, u32[]{:S(2)}) collective-permute-start(bf16[64,2048]{1,0:T(8,128)(2,1)S(1)} %join.1.order_ref.refs_0_), channel_id=1, source_target_pairs={{0,12},{1,13},{2,14},{3,15},{4,0},{5,1},{6,2},{7,3},{8,4},{9,5},{1... | collective-permute-start | bytes 786440 | tf_op jit(solution)/shard_map/ppermute | solution.py:573
  96.1 16.9 %collective-permute-start.13 = (bf16[64,2048]{1,0:T(8,128)(2,1)S(1)}, bf16[64,2048]{1,0:T(8,128)(2,1)S(1)}, u32[]{:S(2)}, u32[]{:S(2)}) collective-permute-start(bf16[64,2048]{1,0:T(8,128)(2,1)S(1)} %join.1.order_ref.refs_0_), channel_id=1, source_target_pairs={{0,4},{1,5},{2,6},{3,7},{4,8},{5,9},{6,10},{7,11},{8,12},{9,13},{1... | collective-permute-start | bytes 786440 | tf_op jit(solution)/shard_map/ppermute | solution.py:573
  96.3 18.1 %collective-permute-start.10 = (bf16[64,2048]{1,0:T(8,128)(2,1)S(1)}, bf16[64,2048]{1,0:T(8,128)(2,1)S(1)}, u32[]{:S(2)}, u32[]{:S(2)}) collective-permute-start(bf16[64,2048]{1,0:T(8,128)(2,1)S(1)} %join.1.order_ref.refs_0_), channel_id=1, source_target_pairs={{0,14},{1,15},{2,0},{3,1},{4,2},{5,3},{6,4},{7,5},{8,6},{9,7},{10,... | collective-permute-start | bytes 786440 | tf_op jit(solution)/shard_map/ppermute | solution.py:573
  97.0 26.6 %collective-permute-start.11 = (bf16[64,2048]{1,0:T(8,128)(2,1)S(1)}, bf16[64,2048]{1,0:T(8,128)(2,1)S(1)}, u32[]{:S(2)}, u32[]{:S(2)}) collective-permute-start(bf16[64,2048]{1,0:T(8,128)(2,1)S(1)} %join.1.order_ref.refs_0_), channel_id=1, source_target_pairs={{0,2},{1,3},{2,4},{3,5},{4,6},{5,7},{6,8},{7,9},{8,10},{9,11},{10,... | collective-permute-start | bytes 786440 | tf_op jit(solution)/shard_map/ppermute | solution.py:573
  106.1 20.5 %collective-permute-start.14 = (bf16[64,2048]{1,0:T(8,128)(2,1)S(1)}, bf16[64,2048]{1,0:T(8,128)(2,1)S(1)}, u32[]{:S(2)}, u32[]{:S(2)}) collective-permute-start(bf16[64,2048]{1,0:T(8,128)(2,1)S(1)} %collective-permute-done.12.refs_3_), channel_id=1, source_target_pairs={{0,14},{1,15},{2,0},{3,1},{4,2},{5,3},{6,4},{7,5},{8,6},{9,7},{10,... | collective-permute-start | bytes 786440 | tf_op jit(solution)/shard_map/ppermute | solution.py:573
  113.0 13.6 %collective-permute-start.15 = (bf16[64,2048]{1,0:T(8,128)(2,1)S(1)}, bf16[64,2048]{1,0:T(8,128)(2,1)S(1)}, u32[]{:S(2)}, u32[]{:S(2)}) collective-permute-start(bf16[64,2048]{1,0:T(8,128)(2,1)S(1)} %collective-permute-done.13.refs_4_), channel_id=1, source_target_pairs={{0,2},{1,3},{2,4},{3,5},{4,6},{5,7},{6,8},{7,9},{8,10},{9,11},{10,... | collective-permute-start | bytes 786440 | tf_op jit(solution)/shard_map/ppermute | solution.py:573
  113.0 13.6 %collective-permute-start.16 = (bf16[32,2048]{1,0:T(8,128)(2,1)S(1)}, bf16[32,2048]{1,0:T(8,128)(2,1)S(1)}, u32[]{:S(2)}, u32[]{:S(2)}) collective-permute-start(bf16[32,2048]{1,0:T(8,128)(2,1)S(1)} %slice.16), channel_id=1, source_target_pairs={{0,4},{1,5},{2,6},{3,7},{4,8},{5,9},{6,10},{7,11},{8,12},{9,13},{1... | collective-permute-start | bytes 393224 | tf_op jit(solution)/shard_map/ppermute | solution.py:573
  114.5 12.1 %collective-permute-start.17 = (bf16[32,2048]{1,0:T(8,128)(2,1)S(1)}, bf16[32,2048]{1,0:T(8,128)(2,1)S(1)}, u32[]{:S(2)}, u32[]{:S(2)}) collective-permute-start(bf16[32,2048]{1,0:T(8,128)(2,1)S(1)} %slice.17), channel_id=1, source_target_pairs={{0,12},{1,13},{2,14},{3,15},{4,0},{5,1},{6,2},{7,3},{8,4},{9,5},{1... | collective-permute-start | bytes 393224 | tf_op jit(solution)/shard_map/ppermute | solution.py:573

commit v5 on v4

--- a/solution.py
+++ b/solution.py
@@ -170,34 +170,19 @@
     return rows.reshape(RUN, BAND).astype(BF16)
 
 
-PLACES = {
-    0: [(0, 0), (0, RUN)],
-    1: [(3, PAIR), (3, PAIR + RUN)],
-    -1: [(4, PAIR), (4, PAIR + RUN)],
-    2: [(1, 0), (1, RUN)],
-    -2: [(2, 0), (2, RUN)],
-    3: [(3, 0), (3, RUN)],
-    -3: [(4, 0), (4, RUN)],
-    4: [(5, 0), (6, 0)],
-}
-NEAR = 2 * PAIR + LINES
-
-
 def forward_kernel(tiles, place_ref, got_ref, volume_ref, *refs):
-    outs, (spread_ref, buffer_ref, sem_ref) = refs[:-3], refs[-3:]
+    outs, (ends_ref, spread_ref, buffer_ref, sem_ref, last_ref, first_ref) = refs[:-6], refs[-6:]
     extent = volume_ref.shape[1]
     me = place_ref[1]
     start(tile_copies(volume_ref, buffer_ref, sem_ref, 0))
     fill_spread(tiles, me, got_ref, spread_ref)
-    where = [(outs[index], row) for hop in hops(tiles) for index, row in PLACES[hop]]
+    where = [(ref, row) for ref in outs for row in range(0, ref.shape[0], RUN)]
     beyond = pl.ds(extent, BAND)
     for index, hop in enumerate(hops(tiles)):
         tile = lax.rem(me + 2 * hop + tiles, tiles)
         for turn, source in enumerate((tile, tile ^ 1)):
             ref, row = where[2 * index + turn]
             ref[row : row + RUN, beyond] = measured_rows(got_ref, source)
-    for ref in outs[3:5]:
-        ref[NEAR - LINES :, beyond] = jnp.zeros((LINES, BAND), BF16)
     steps = extent // XT
 
     def body(step, carry):
@@ -211,96 +196,95 @@
         here = pl.ds(pl.multiple_of(step * XT, XT), XT)
         for index, (ref, row) in enumerate(where):
             ref[row : row + RUN, here] = out[index * RUN : (index + 1) * RUN]
-        for ref in outs[3:5]:
-            ref[NEAR - LINES :, here] = out[-LINES:]
+        ends_ref[:, here] = out[-LINES:]
+        ends = out[-LINES:].astype(F32)
+        there = pl.ds(pl.multiple_of(step * 8, 8), 8)
+        first_ref[there] = ends[:8]
+        last_ref[there] = ends[8:]
         return carry
 
     lax.fori_loop(0, steps, body, 0)
+    outs[1][:, extent + BAND :] = last_ref[...].astype(BF16)
+    outs[2][:, extent + BAND :] = first_ref[...].astype(BF16)
 
 
 def forward(place, got, volume, tiles, *order):
     depth, extent, strip = volume.shape
     slots = got.shape[0]
-    rows = [PAIR] * 3 + [NEAR] * 2 + [RUN] * 2
+    rows = [PAIR] * (tiles // 2 - 1) + [RUN] * 2
+    lanes = [extent + BAND + (XT if index in (1, 2) else 0) for index in range(len(rows))]
 
     def kernel(place_ref, got_ref, volume_ref, *refs):
         forward_kernel(tiles, place_ref, got_ref, volume_ref, *refs[len(order) :])
 
     return pl.pallas_call(
         kernel,
-        out_shape=[jax.ShapeDtypeStruct((count, extent + BAND), BF16) for count in rows],
+        out_shape=[jax.ShapeDtypeStruct(shape, BF16) for shape in zip(rows, lanes)]
+        + [jax.ShapeDtypeStruct((LINES, extent), BF16)],
         in_specs=[SMEM, VMEM, HBM] + [ANY] * len(order),
-        out_specs=[VMEM] * len(rows),
+        out_specs=[VMEM] * (len(rows) + 1),
         scratch_shapes=[pltpu.VMEM((slots * depth + LINES, depth * strip), BF16)]
-        + stream_scratch(depth, strip),
+        + stream_scratch(depth, strip)
+        + [pltpu.VMEM((extent // XT * 8, XT), F32)] * 2,
         compiler_params=limit(10),
         cost_estimate=cost(2 * slots * depth * volume.size, 3 * volume.size),
         name="forward",
     )(place, got, volume, *order)
 
 
-def sums_kernel(up_ref, up_near_ref, up_far_ref, down_ref, down_near_ref, down_far_ref, *refs):
-    extent = up_ref.shape[1] - BAND
-    for own_ref, near_ref, far_ref, low, out_ref in (
-        (up_ref, up_near_ref, up_far_ref, 0, refs[-2]),
-        (down_ref, down_near_ref, down_far_ref, RUN, refs[-1]),
+def sums_kernel(extent, from_below_ref, up_ref, from_above_ref, down_ref, *refs):
+    for came_ref, own_ref, low, out_ref in (
+        (from_below_ref, up_ref, 0, refs[-2]),
+        (from_above_ref, down_ref, RUN, refs[-1]),
     ):
+        came_lanes = came_ref.shape[1] - extent
+        past = extent + BAND
         for row in (0, RUN):
             rows = slice(row, row + RUN)
-            total = own_ref[rows, :extent].astype(F32) + near_ref[rows, :extent].astype(F32)
-            last = jnp.zeros((RUN, BAND), BF16)
-            if row == low:
-                total = total + far_ref[:, :extent].astype(F32)
-                last = far_ref[:, extent:]
+            total = own_ref[rows, :extent].astype(F32)
+            strips = jnp.zeros((RUN, came_lanes), BF16)
+            if came_ref.shape[0] > RUN or row == low:
+                came = rows if came_ref.shape[0] > RUN else slice(0, RUN)
+                total = total + came_ref[came, :extent].astype(F32)
+                strips = came_ref[came, extent:]
             out_ref[rows, :extent] = total.astype(BF16)
-            out_ref[rows, extent : extent + BAND] = own_ref[rows, extent:]
-            out_ref[rows, extent + BAND : extent + 2 * BAND] = near_ref[rows, extent:]
-            out_ref[rows, extent + 2 * BAND :] = last
-
-
-def round_sums(*operands):
-    rows, lanes = operands[0].shape
-    out = jax.ShapeDtypeStruct((rows, lanes + 2 * BAND), BF16)
-    return pl.pallas_call(
-        sums_kernel,
+            out_ref[rows, extent:past] = own_ref[rows, extent:past]
+            out_ref[rows, past : past + came_lanes] = strips
+        if own_ref.shape[1] > past:
+            out_ref[:, past + came_lanes :] = own_ref[:, past:]
+
+
+def ring_sums(from_below, up, from_above, down, extent, *order):
+    out = jax.ShapeDtypeStruct((PAIR, up.shape[1] + from_below.shape[1] - extent), BF16)
+    return pl.pallas_call(
+        functools.partial(sums_kernel, extent),
         out_shape=(out, out),
-        in_specs=[VMEM] * 6 + [ANY] * (len(operands) - 6),
+        in_specs=[VMEM] * 4 + [ANY] * len(order),
         out_specs=(VMEM, VMEM),
         compiler_params=limit(8),
-        cost_estimate=cost(6 * out.size, 14 * out.size),
-        name="round_sums",
-    )(*operands)
+        cost_estimate=cost(6 * out.size, 12 * out.size),
+        name="ring_sums",
+    )(from_below, up, from_above, down, *order)
 
 
 STRIPS = (0, -1, 1, -2, 2, -3, 3, 4)
 
 
-def last_sums_kernel(
-    place_ref, own_ref, mine_ref, below_ref, above_ref, up_ref, down_ref, *refs
-):
+def last_sums_kernel(place_ref, own_ref, ends_ref, below_ref, above_ref, *refs):
     kept_ref, strips_ref, sent_ref = refs[-3:]
-    extent = own_ref.shape[1] - BAND
+    extent = ends_ref.shape[1]
+    blocks = [slice(extent + n * BAND, extent + (n + 1) * BAND) for n in range(4)]
     for row in (0, RUN):
-        rows, beside = slice(row, row + RUN), slice(PAIR + row, PAIR + row + RUN)
+        rows = slice(row, row + RUN)
         total = (
             own_ref[rows, :extent].astype(F32)
-            + below_ref[beside, :extent].astype(F32)
-            + above_ref[beside, :extent].astype(F32)
-            + up_ref[rows, :extent].astype(F32)
-            + down_ref[rows, :extent].astype(F32)
+            + below_ref[rows, :extent].astype(F32)
+            + above_ref[rows, :extent].astype(F32)
         )
-        near, far = slice(extent, extent + BAND), slice(extent + BAND, extent + 2 * BAND)
-        across = slice(extent + 2 * BAND, extent + 3 * BAND)
-        strips = [
-            own_ref[rows, near],
-            below_ref[beside, near],
-            above_ref[beside, near],
-            up_ref[rows, near],
-            down_ref[rows, near],
-            up_ref[rows, far],
-            down_ref[rows, far],
-            up_ref[rows, across] if row == 0 else down_ref[rows, across],
-        ]
+        strips = [own_ref[rows, blocks[0]]]
+        for n in range(3):
+            strips += [below_ref[rows, blocks[n]], above_ref[rows, blocks[n]]]
+        strips.append((below_ref if row == 0 else above_ref)[rows, blocks[3]])
         if row == 0:
             kept_ref[...] = total
             for index, strip in enumerate(strips):
@@ -309,17 +293,20 @@
             sent_ref[:RUN] = total.astype(BF16)
             halves = [strip[low : low + 16] for strip in strips for low in (0, 16)]
             sent_ref[RUN + LINES :] = jnp.concatenate(halves, axis=1)
-    mine, below, above = [
-        ref[NEAR - LINES :, :extent].astype(F32) for ref in (mine_ref, below_ref, above_ref)
-    ]
+
+    def column(ref):
+        tiled = ref[:, blocks[3].stop :].astype(F32)
+        return jnp.concatenate([tiled[n * 8 : (n + 1) * 8] for n in range(extent // XT)], axis=1)
+
+    mine = ends_ref[...].astype(F32)
     even = place_ref[1] % 2 == 0
-    left = jnp.where(even, mine[8:], below[8:])
-    right = jnp.where(even, above[:8], mine[:8])
+    left = jnp.where(even, mine[8:], column(below_ref))
+    right = jnp.where(even, column(above_ref), mine[:8])
     sent_ref[RUN : RUN + LINES] = jnp.concatenate([left, right], axis=0).astype(BF16)
 
 
-def last_sums(place, own, mine, below, above, up, down, *order):
-    extent = own.shape[1] - BAND
+def last_sums(place, own, ends, below, above, *order):
+    extent = ends.shape[1]
     return pl.pallas_call(
         last_sums_kernel,
         out_shape=(
@@ -327,12 +314,12 @@
             jax.ShapeDtypeStruct((RUN, len(STRIPS) * BAND), BF16),
             jax.ShapeDtypeStruct((RUN + LINES + 16, extent), BF16),
         ),
-        in_specs=[SMEM] + [VMEM] * 6 + [ANY] * len(order),
+        in_specs=[SMEM] + [VMEM] * 4 + [ANY] * len(order),
         out_specs=(VMEM,) * 3,
         compiler_params=limit(8),
         cost_estimate=cost(5 * own.size, 14 * own.size),
         name="last_sums",
-    )(place, own, mine, below, above, up, down, *order)
+    )(place, own, ends, below, above, *order)
 
 
 def residual_kernel(place_ref, kept_ref, strips_ref, arrived_ref, got_ref, *refs):
@@ -400,23 +387,6 @@
     )(place, kept, strips, arrived, got, *order)
 
 
-def join_kernel(first_ref, second_ref, order_ref, out_ref):
-    out_ref[:RUN] = first_ref[...]
-    out_ref[RUN:] = second_ref[...]
-
-
-def join(first, second, order):
-    return pl.pallas_call(
-        join_kernel,
-        out_shape=jax.ShapeDtypeStruct((PAIR, first.shape[1]), BF16),
-        in_specs=[VMEM, VMEM, ANY],
-        out_specs=VMEM,
-        compiler_params=limit(8),
-        cost_estimate=cost(0, 8 * first.size),
-        name="join",
-    )(first, second, order)
-
-
 def penalty(diff):
     return diff * lax.rsqrt(1.0 + diff * diff)
 
@@ -519,7 +489,7 @@
 
     def body(step, carry):
         here = pl.ds(pl.multiple_of(step * XT, XT), XT)
-        mine = mine_ref[NEAR - LINES :, here].astype(F32)
+        mine = mine_ref[:, here].astype(F32)
         beside = beside_ref[RUN : RUN + LINES, here].astype(F32)
         on_left = penalty(mine[:8] - beside[:8]) * (has_left * beta)
         on_right = penalty(mine[8:] - beside[8:]) * (has_right * beta)
@@ -584,34 +554,36 @@
     flat = got.reshape(slabs * SLOTS, ROWS, BAND)
     volume = pltpu.with_memory_space_constraint(volume, pltpu.HBM)
 
-    own, up2, down2, near_up, near_down, far_up, far_down = forward(
+    own, up1, down1, up2, down2, up3, down3, up, down, ends = forward(
         place, flat, volume, tiles, top, bottom
     )
-    near_up, near_down, far_up, far_down, below, above = lax.optimization_barrier(
-        (near_up, near_down, far_up, far_down, below, above)
-    )
-    near = along_z(near_up, 1), along_z(near_down, -1)
-    far = along_z(far_up, 2), along_z(far_down, -2)
-    regular, token = regularizer(0, None, place, beta, volume, below, above, far_up)
-    up, down = round_sums(up2, near[0], far[0], down2, near[1], far[1], token)
-    two = along_z(up, 2), along_z(down, -2)
-    regular, token = regularizer(1, regular, place, beta, volume, below, above, up)
-    kept, strips, sent = last_sums(place, own, near_up, *near, *two, token)
+    extent = ends.shape[1]
+    spread = spread_rows(place, flat, tiles, ends)
+    order, regular = [spread], None
+    for index, (own_up, own_down) in enumerate([(up3, down3), (up2, down2), (up1, down1)]):
+        came = along_z(up, 1), along_z(down, -1)
+        up, down = ring_sums(came[0], own_up, came[1], own_down, extent, *order)
+        regular, token = regularizer(index, regular, place, beta, volume, below, above, up)
+        order = [token]
+    came = along_z(up, 1), along_z(down, -1)
+    kept, strips, sent = last_sums(place, own, ends, *came, *order)
     arrived = along_y(sent)
-    images = residual_images(place, kept, strips, arrived, flat)
+    regular, token = regularizer(3, regular, place, beta, volume, below, above, sent)
+    images = residual_images(place, kept, strips, arrived, flat, token)
 
     partner = along_y(images)
-    regular, token = regularizer(2, regular, place, beta, volume, below, above, images)
-    pair = join(images, partner, token)
-    up2, down2 = along_z(pair, 2), along_z(pair, -2)
-    up1, down1 = along_z(pair, 1), along_z(pair, -1)
-    spread = spread_rows(place, flat, tiles, pair)
-    regular, token = regularizer(3, regular, place, beta, volume, below, above, pair, spread)
-    up3, down3 = along_z(up2, 1), along_z(down2, -1)
-    far_up, far_down = along_z(up2[:RUN], 2), along_z(down2[RUN:], -2)
-    chunks = [pair, down1, up1, down2, up2, down3, up3, far_up, far_down]
+    rings = []
+    for first, past in ((images, 1), (partner, -1)):
+        up, down = first, first
+        ring = {0: first}
+        for hop in range(1, tiles // 4):
+            up, down = along_z(up, 1), along_z(down, -1)
+            ring[-hop], ring[hop] = up, down
+        ring[tiles // 4] = along_z(up, 1) if past == 1 else along_z(down, -1)
+        rings.append(ring)
+    chunks = [ring[hop] for hop in hops(tiles) for ring in rings]
     regular = pltpu.with_memory_space_constraint(regular, pltpu.HBM)
-    return gradient(place, beta, spread, near_up, arrived, chunks, regular)
+    return gradient(place, beta, spread, ends, arrived, chunks, regular)
 
 
 def solution(mesh):

time: 137 us -> 117 us (0.85); the launches traced: 134 us -> 116 us
  waiting for transfers between devices: 47.5 us -> 28.2 us
    ppermute x14 -> x22, waiting for transfers between devices: 33.9 us -> 23.2 us  [along_z(): lax.ppermute(block, 'tile', [(i, (i + 2 * by) % tiles) for i in range(til...]
    all_to_all x1, waiting for transfers between devices: 7.3 us -> 0.79 us  [shards(): lax.all_to_all(packed, 'slab', split_axis=0, concat_axis=0, tiled=True)]
    ppermute x2, waiting for transfers between devices: 6.27 us -> 4.16 us  [along_y(): return lax.ppermute(block, 'tile', [(i, i ^ 1) for i in range(tiles)])]
    ppermute x14 -> x22, starting transfers between devices: 27 us -> 29.1 us  [along_z(): lax.ppermute(block, 'tile', [(i, (i + 2 * by) % tiles) for i in range(til...]
    ppermute x1, starting transfers between devices: 3.64 us -> 2.02 us  [shards(): above = lax.ppermute(bottom, 'slab', [(i + 1, i) for i in range(slabs - 1)])]
    pallas_call x3 -> x4, Pallas kernels: 7.43 us -> 7.6 us  [the longest x1 7.28 us: forward(): pl.pallas_call(kernel, out_shape=[jax.ShapeDtypeStruct(shape, BF16) for s...]
  transfers between devices with their start and end apart: 19 -> 27, of which waited for: 9 -> 18; matrix products, arithmetic and copies ran while one was open for 0% -> 1% of each run, Pallas kernels for 22% -> 26%
where the time goes in v5:
time: 117 us; the launch traced here: 116 us
  starting transfers between devices  43.9 us (38%)
  Pallas kernels  41.6 us (36%)
  waiting for transfers between devices  28.2 us (24%)
  local copies, waits for them, and re-layouts  1.27 us (1%)
    ppermute x22, starting transfers between devices, along_z(): lax.ppermute(block, 'tile', [(i, (i + 2 * by) % tiles) for i in range(til...  29.1 us
    ppermute x22, waiting for transfers between devices, along_z(): lax.ppermute(block, 'tile', [(i, (i + 2 * by) % tiles) for i in range(til...  23.2 us
    pallas_call x4, Pallas kernels, regularizer(): pl.pallas_call(functools.partial(regularizer_kernel, origin, count), grid...  21.8 us
    pallas_call x1, Pallas kernels, gradient(): pl.pallas_call(gradient_kernel, out_shape=jax.ShapeDtypeStruct(regular.sh...  7.69 us
    pallas_call x1, Pallas kernels, forward(): pl.pallas_call(kernel, out_shape=[jax.ShapeDtypeStruct(shape, BF16) for s...  7.28 us
    all_to_all x1, starting transfers between devices, shards(): lax.all_to_all(packed, 'slab', split_axis=0, concat_axis=0, tiled=True)  5.77 us
    ppermute x2, starting transfers between devices, along_y(): return lax.ppermute(block, 'tile', [(i, i ^ 1) for i in range(tiles)])  4.66 us
    ppermute x2, waiting for transfers between devices, along_y(): return lax.ppermute(block, 'tile', [(i, i ^ 1) for i in range(tiles)])  4.16 us
  transfers between devices with their start and end apart: 27, of which 18 were waited for; matrix products, arithmetic and copies ran while one was open for 1% of the time, Pallas kernels for 26%

profile of v5, /device:TPU:8, one launch (start us, length us, event | category | flops | bytes accessed | tf_op | source)
XLA Modules:
  0.0 115.9 jit_solution(10472308910386545589)
XLA Ops:
  0.0 1.7 %pack_messages.1 = bf16[16,4,16,128]{3,2,1,0:T(8,128)(2,1)} custom-call(s32[2,12]{1,0:T(2,128)} %bitcast.9, s32[2,12]{1,0:T(2,128)} %offset_ref.1, s32[2,12]{1,0:T(2,128)} %width_ref.1, bf16[12,2,128]{2,1,0:T(2,128)(2,1)} %bitcast.8, bf16[2,12,8,128]{3,2,1,0:T(8,128)(2,1)} %measured_ref.1), custom_call_target="tpu_custom_call" | custom-call | tf_op jit(solution)/shard_map/pack_messages/pallas_call | solution.py:67
  1.7 5.8 %all-to-all-start = ((bf16[16,4,16,128]{3,2,1,0:T(8,128)(2,1)}), bf16[16,4,16,128]{3,2,1,0:T(8,128)(2,1)S(1)}, u32[]{:S(2)}, u32[]{:S(2)}) async-start(bf16[16,4,16,128]{3,2,1,0:T(8,128)(2,1)} %pack_messages.1), calls=%async_computation | async-start | bytes 524288 | tf_op jit(solution)/shard_map/all_to_all | solution.py:550
  8.7 2.0 %collective-permute-start.5 = (bf16[1,2048,128]{2,1,0:T(8,128)(2,1)S(1)}, bf16[1,2048,128]{2,1,0:T(8,128)(2,1)S(1)}, u32[]{:S(2)}, u32[]{:S(2)}) collective-permute-start(bf16[1,2048,128]{2,1,0:T(8,128)(2,1)S(1)} %get-tuple-element.63.refs_1_), channel_id=1, source_target_pairs={{16,0},{32,16},{48,32},{64,48},{80,64},{96,80},{112,96},{128,112},... | collective-permute-start | bytes 1572872 | tf_op jit(solution)/shard_map/ppermute | solution.py:553
  10.8 2.3 %collective-permute-start.4 = (bf16[1,2048,128]{2,1,0:T(8,128)(2,1)S(1)}, bf16[1,2048,128]{2,1,0:T(8,128)(2,1)S(1)}, u32[]{:S(2)}, u32[]{:S(2)}) collective-permute-start(bf16[1,2048,128]{2,1,0:T(8,128)(2,1)S(1)} %get-tuple-element.64.refs_0_), channel_id=1, source_target_pairs={{0,16},{16,32},{32,48},{48,64},{64,80},{80,96},{96,112},{112,128},... | collective-permute-start | bytes 1572872 | tf_op jit(solution)/shard_map/ppermute | solution.py:552
  14.0 7.3 %forward.1 = (bf16[64,2176]{1,0:T(8,128)(2,1)S(1)}, bf16[64,2432]{1,0:T(8,128)(2,1)S(1)}, bf16[64,2432]{1,0:T(8,128)(2,1)S(1)}, bf16[64,2176]{1,0:T(8,128)(2,1)S...) custom-call(s32[4]{0:T(128)S(1)} %pad_add_fusion.place_ref, ...), custom_call_target="tpu_custom_call" | custom-call | flops 2147483648 | bytes 6291456 | tf_op jit(solution)/shard_map/forward/pallas_call | solution.py:220
  21.2 2.0 %collective-permute-start = (bf16[32,2176]{1,0:T(8,128)(2,1)S(1)}, bf16[32,2176]{1,0:T(8,128)(2,1)S(1)}, u32[]{:S(2)}, u32[]{:S(2)}) collective-permute-start(bf16[32,2176]{1,0:T(8,128)(2,1)S(1)} %get-tuple-element.38), channel_id=1, source_target_pairs={{0,2},{1,3},{2,4},{3,5},{4,6},{5,7},{6,8},{7,9},{8,10},{9,11},{10,... | collective-permute-start | bytes 417800 | tf_op jit(solution)/shard_map/ppermute | solution.py:543
  23.2 4.0 %collective-permute-start.1 = (bf16[32,2176]{1,0:T(8,128)(2,1)S(1)}, bf16[32,2176]{1,0:T(8,128)(2,1)S(1)}, u32[]{:S(2)}, u32[]{:S(2)}) collective-permute-start(bf16[32,2176]{1,0:T(8,128)(2,1)S(1)} %get-tuple-element.40), channel_id=1, source_target_pairs={{0,14},{1,15},{2,0},{3,1},{4,2},{5,3},{6,4},{7,5},{8,6},{9,7},{10,... | collective-permute-start | bytes 417800 | tf_op jit(solution)/shard_map/ppermute | solution.py:543
  28.0 2.9 %collective-permute-done.from_below_ref = bf16[32,2176]{1,0:T(8,128)(2,1)S(1)} collective-permute-done((bf16[32,2176]{1,0:T(8,128)(2,1)S(1)}, bf16[32,2176]{1,0:T(8,128)(2,1)S(1)}, u32[]{:S(2)}, u32[]{:S(2)}) %collective-permute-start) | collective-permute-done | bytes 139296 | tf_op jit(solution)/shard_map/ppermute | solution.py:543
  31.0 3.7 %collective-permute-start.3 = (bf16[64,2304]{1,0:T(8,128)(2,1)S(1)}, bf16[64,2304]{1,0:T(8,128)(2,1)S(1)}, u32[]{:S(2)}, u32[]{:S(2)}) collective-permute-start(bf16[64,2304]{1,0:T(8,128)(2,1)S(1)} %get-tuple-element.44), channel_id=1, source_target_pairs={{0,14},{1,15},{2,0},{3,1},{4,2},{5,3},{6,4},{7,5},{8,6},{9,7},{10,... | collective-permute-start | bytes 884744 | tf_op jit(solution)/shard_map/ppermute | solution.py:543
  35.3 5.5 %regularizer.4 = (bf16[8,2048,128]{2,1,0:T(8,128)(2,1)}, f32[8,128]{1,0:T(8,128)S(1)}) custom-call(s32[4]{0:T(128)S(1)} %pad_add_fusion.place_ref, f32[1]{0:T(128)S(6)} %copy.14.beta_ref, bf16[8,2048,128]{2,1,0:T(8,128)(2,1)} %volume_ref.9, bf16[1,2048,128]{2,1,0:T(8,128)(2,1)S(1)} %collective-permute-done.4.below_ref, ...), custom_call_target="tpu_custom_call" | custom-call | flops 15728640 | bytes 4194304 | tf_op jit(solution)/shard_map/regularizer/pallas_call | solution.py:459
  41.4 3.4 %collective-permute-done.2.from_below_ref = bf16[64,2304]{1,0:T(8,128)(2,1)S(1)} collective-permute-done((bf16[64,2304]{1,0:T(8,128)(2,1)S(1)}, bf16[64,2304]{1,0:T(8,128)(2,1)S(1)}, u32[]{:S(2)}, u32[]{:S(2)}) %collective-permute-start.2) | collective-permute-done | bytes 294944 | tf_op jit(solution)/shard_map/ppermute | solution.py:543
  45.3 1.7 %collective-permute-start.6 = (bf16[64,2432]{1,0:T(8,128)(2,1)S(1)}, bf16[64,2432]{1,0:T(8,128)(2,1)S(1)}, u32[]{:S(2)}, u32[]{:S(2)}) collective-permute-start(bf16[64,2432]{1,0:T(8,128)(2,1)S(1)} %get-tuple-element.47.refs_0_), channel_id=1, source_target_pairs={{0,2},{1,3},{2,4},{3,5},{4,6},{5,7},{6,8},{7,9},{8,10},{9,11},{10,... | collective-permute-start | bytes 933896 | tf_op jit(solution)/shard_map/ppermute | solution.py:543
  47.1 5.4 %regularizer.5 = (bf16[8,2048,128]{2,1,0:T(8,128)(2,1)}, f32[8,128]{1,0:T(8,128)S(1)}) custom-call(s32[4]{0:T(128)S(1)} %pad_add_fusion.place_ref, f32[1]{0:T(128)S(6)} %copy.14.beta_ref, bf16[8,2048,128]{2,1,0:T(8,128)(2,1)} %volume_ref.9, bf16[1,2048,128]{2,1,0:T(8,128)(2,1)S(1)} %collective-permute-done.4.below_ref, ...), custom_call_target="tpu_custom_call", output_to_operand_aliasing={{0}: (6, {})} | custom-call | flops 15728640 | bytes 4194304 | tf_op jit(solution)/shard_map/regularizer/pallas_call | solution.py:459
  53.5 1.5 %collective-permute-done.6.from_below_ref = bf16[64,2432]{1,0:T(8,128)(2,1)S(1)} collective-permute-done((bf16[64,2432]{1,0:T(8,128)(2,1)S(1)}, bf16[64,2432]{1,0:T(8,128)(2,1)S(1)}, u32[]{:S(2)}, u32[]{:S(2)}) %collective-permute-start.6) | collective-permute-done | bytes 311328 | tf_op jit(solution)/shard_map/ppermute | solution.py:543
  55.5 1.7 %collective-permute-start.8 = (bf16[64,2816]{1,0:T(8,128)(2,1)S(1)}, bf16[64,2816]{1,0:T(8,128)(2,1)S(1)}, u32[]{:S(2)}, u32[]{:S(2)}) collective-permute-start(bf16[64,2816]{1,0:T(8,128)(2,1)S(1)} %get-tuple-element.53.refs_0_), channel_id=1, source_target_pairs={{0,2},{1,3},{2,4},{3,5},{4,6},{5,7},{6,8},{7,9},{8,10},{9,11},{10,... | collective-permute-start | bytes 1081352 | tf_op jit(solution)/shard_map/ppermute | solution.py:543
  57.2 5.4 %regularizer.6 = (bf16[8,2048,128]{2,1,0:T(8,128)(2,1)}, f32[8,128]{1,0:T(8,128)S(1)}) custom-call(s32[4]{0:T(128)S(1)} %pad_add_fusion.place_ref, f32[1]{0:T(128)S(6)} %copy.14.beta_ref, bf16[8,2048,128]{2,1,0:T(8,128)(2,1)} %volume_ref.9, bf16[1,2048,128]{2,1,0:T(8,128)(2,1)S(1)} %collective-permute-done.4.below_ref, ...), custom_call_target="tpu_custom_call", output_to_operand_aliasing={{0}: (6, {})} | custom-call | flops 15728640 | bytes 4194304 | tf_op jit(solution)/shard_map/regularizer/pallas_call | solution.py:459
  63.8 1.5 %collective-permute-done.8.below_ref = bf16[64,2816]{1,0:T(8,128)(2,1)S(1)} collective-permute-done((bf16[64,2816]{1,0:T(8,128)(2,1)S(1)}, bf16[64,2816]{1,0:T(8,128)(2,1)S(1)}, u32[]{:S(2)}, u32[]{:S(2)}) %collective-permute-start.8) | collective-permute-done | bytes 360480 | tf_op jit(solution)/shard_map/ppermute | solution.py:543
  66.0 2.3 %collective-permute-start.10 = (bf16[64,2048]{1,0:T(8,128)(2,1)S(1)}, bf16[64,2048]{1,0:T(8,128)(2,1)S(1)}, u32[]{:S(2)}, u32[]{:S(2)}) collective-permute-start(bf16[64,2048]{1,0:T(8,128)(2,1)S(1)} %get-tuple-element.57.refs_0_), channel_id=1, source_target_pairs={{0,1},{1,0},{2,3},{3,2},{4,5},{5,4},{6,7},{7,6},{8,9},{9,8},{10,11... | collective-permute-start | bytes 786440 | tf_op jit(solution)/shard_map/ppermute | solution.py:546
  68.3 5.4 %regularizer.7 = (bf16[8,2048,128]{2,1,0:T(8,128)(2,1)}, f32[8,128]{1,0:T(8,128)S(1)}) custom-call(s32[4]{0:T(128)S(1)} %pad_add_fusion.place_ref, f32[1]{0:T(128)S(6)} %copy.14.beta_ref, bf16[8,2048,128]{2,1,0:T(8,128)(2,1)} %volume_ref.9, bf16[1,2048,128]{2,1,0:T(8,128)(2,1)S(1)} %collective-permute-done.4.below_ref, ...), custom_call_target="tpu_custom_call", output_to_operand_aliasing={{0}: (6, {})} | custom-call | flops 15728640 | bytes 4194304 | tf_op jit(solution)/shard_map/regularizer/pallas_call | solution.py:459
  75.4 2.3 %collective-permute-start.11 = (bf16[32,2048]{1,0:T(8,128)(2,1)S(1)}, bf16[32,2048]{1,0:T(8,128)(2,1)S(1)}, u32[]{:S(2)}, u32[]{:S(2)}) collective-permute-start(bf16[32,2048]{1,0:T(8,128)(2,1)S(1)} %residual_images.1.refs_0_), channel_id=1, source_target_pairs={{0,1},{1,0},{2,3},{3,2},{4,5},{5,4},{6,7},{7,6},{8,9},{9,8},{10,11... | collective-permute-start | bytes 393224 | tf_op jit(solution)/shard_map/ppermute | solution.py:546
  78.0 4.0 %collective-permute-done.11.refs_1_ = bf16[32,2048]{1,0:T(8,128)(2,1)S(1)} collective-permute-done((bf16[32,2048]{1,0:T(8,128)(2,1)S(1)}, bf16[32,2048]{1,0:T(8,128)(2,1)S(1)}, u32[]{:S(2)}, u32[]{:S(2)}) %collective-permute-start.11) | collective-permute-done | bytes 131104 | tf_op jit(solution)/shard_map/ppermute | solution.py:546
  82.4 1.9 %collective-permute-start.12 = (bf16[32,2048]{1,0:T(8,128)(2,1)S(1)}, bf16[32,2048]{1,0:T(8,128)(2,1)S(1)}, u32[]{:S(2)}, u32[]{:S(2)}) collective-permute-start(bf16[32,2048]{1,0:T(8,128)(2,1)S(1)} %residual_images.1.refs_0_), channel_id=1, source_target_pairs={{0,14},{1,15},{2,0},{3,1},{4,2},{5,3},{6,4},{7,5},{8,6},{9,7},{10,... | collective-permute-start | bytes 393224 | tf_op jit(solution)/shard_map/ppermute | solution.py:543
  86.0 2.3 %collective-permute-done.13.refs_3_ = bf16[32,2048]{1,0:T(8,128)(2,1)S(1)} collective-permute-done((bf16[32,2048]{1,0:T(8,128)(2,1)S(1)}, bf16[32,2048]{1,0:T(8,128)(2,1)S(1)}, u32[]{:S(2)}, u32[]{:S(2)}) %collective-permute-start.13) | collective-permute-done | bytes 131104 | tf_op jit(solution)/shard_map/ppermute | solution.py:543
  88.3 1.6 %collective-permute-start.17 = (bf16[32,2048]{1,0:T(8,128)(2,1)S(1)}, bf16[32,2048]{1,0:T(8,128)(2,1)S(1)}, u32[]{:S(2)}, u32[]{:S(2)}) collective-permute-start(bf16[32,2048]{1,0:T(8,128)(2,1)S(1)} %collective-permute-done.13.refs_3_), channel_id=1, source_target_pairs={{0,14},{1,15},{2,0},{3,1},{4,2},{5,3},{6,4},{7,5},{8,6},{9,7},{10,... | collective-permute-start | bytes 393224 | tf_op jit(solution)/shard_map/ppermute | solution.py:543
  90.8 1.9 %collective-permute-start.16 = (bf16[32,2048]{1,0:T(8,128)(2,1)S(1)}, bf16[32,2048]{1,0:T(8,128)(2,1)S(1)}, u32[]{:S(2)}, u32[]{:S(2)}) collective-permute-start(bf16[32,2048]{1,0:T(8,128)(2,1)S(1)} %collective-permute-done.12.refs_2_), channel_id=1, source_target_pairs={{0,14},{1,15},{2,0},{3,1},{4,2},{5,3},{6,4},{7,5},{8,6},{9,7},{10,... | collective-permute-start | bytes 393224 | tf_op jit(solution)/shard_map/ppermute | solution.py:543
  92.9 1.7 %collective-permute-done.15.refs_5_ = bf16[32,2048]{1,0:T(8,128)(2,1)S(1)} collective-permute-done((bf16[32,2048]{1,0:T(8,128)(2,1)S(1)}, bf16[32,2048]{1,0:T(8,128)(2,1)S(1)}, u32[]{:S(2)}, u32[]{:S(2)}) %collective-permute-start.15) | collective-permute-done | bytes 131104 | tf_op jit(solution)/shard_map/ppermute | solution.py:543
  94.6 3.2 %collective-permute-start.21 = (bf16[32,2048]{1,0:T(8,128)(2,1)S(1)}, bf16[32,2048]{1,0:T(8,128)(2,1)S(1)}, u32[]{:S(2)}, u32[]{:S(2)}) collective-permute-start(bf16[32,2048]{1,0:T(8,128)(2,1)S(1)} %collective-permute-done.17.refs_7_), channel_id=1, source_target_pairs={{0,14},{1,15},{2,0},{3,1},{4,2},{5,3},{6,4},{7,5},{8,6},{9,7},{10,... | collective-permute-start | bytes 393224 | tf_op jit(solution)/shard_map/ppermute | solution.py:543
  97.8 1.5 %collective-permute-start.20 = (bf16[32,2048]{1,0:T(8,128)(2,1)S(1)}, bf16[32,2048]{1,0:T(8,128)(2,1)S(1)}, u32[]{:S(2)}, u32[]{:S(2)}) collective-permute-start(bf16[32,2048]{1,0:T(8,128)(2,1)S(1)} %collective-permute-done.16.refs_6_), channel_id=1, source_target_pairs={{0,14},{1,15},{2,0},{3,1},{4,2},{5,3},{6,4},{7,5},{8,6},{9,7},{10,... | collective-permute-start | bytes 393224 | tf_op jit(solution)/shard_map/ppermute | solution.py:543
  100.3 1.6 %collective-permute-done.19.refs_9_ = bf16[32,2048]{1,0:T(8,128)(2,1)S(1)} collective-permute-done((bf16[32,2048]{1,0:T(8,128)(2,1)S(1)}, bf16[32,2048]{1,0:T(8,128)(2,1)S(1)}, u32[]{:S(2)}, u32[]{:S(2)}) %collective-permute-start.19) | collective-permute-done | bytes 131104 | tf_op jit(solution)/shard_map/ppermute | solution.py:543
  101.9 3.2 %collective-permute-start.25 = (bf16[32,2048]{1,0:T(8,128)(2,1)S(1)}, bf16[32,2048]{1,0:T(8,128)(2,1)S(1)}, u32[]{:S(2)}, u32[]{:S(2)}) collective-permute-start(bf16[32,2048]{1,0:T(8,128)(2,1)S(1)} %collective-permute-done.21.refs_11_), channel_id=1, source_target_pairs={{0,14},{1,15},{2,0},{3,1},{4,2},{5,3},{6,4},{7,5},{8,6},{9,7},{10,... | collective-permute-start | bytes 393224 | tf_op jit(solution)/shard_map/ppermute | solution.py:543
  106.5 1.6 %collective-permute-done.23.refs_13_ = bf16[32,2048]{1,0:T(8,128)(2,1)S(1)} collective-permute-done((bf16[32,2048]{1,0:T(8,128)(2,1)S(1)}, bf16[32,2048]{1,0:T(8,128)(2,1)S(1)}, u32[]{:S(2)}, u32[]{:S(2)}) %collective-permute-start.23) | collective-permute-done | bytes 131104 | tf_op jit(solution)/shard_map/ppermute | solution.py:543
  108.1 7.7 %gradient.1 = bf16[8,2048,128]{2,1,0:T(8,128)(2,1)} custom-call(s32[4]{0:T(128)S(1)} %pad_add_fusion.place_ref, f32[1]{0:T(128)S(6)} %copy.14.beta_ref, bf16[528,1024]{1,0:T(8,128)(2,1)S(1)} %spread_rows.1.refs_0_.spread_ref, bf16[16,2048]{1,0:T(8,128)(2,1)S(1)} %get-tuple-element.36.order_ref.ends_ref.mine_ref, ...), custom_call_target="tpu_custom_call" | custom-call | flops 2214592512 | bytes 10485760 | tf_op jit(solution)/shard_map/gradient/pallas_call | solution.py:522
  (38 shorter events, 14.8 us)
Async XLA Ops:
  1.7 12.3 %all-to-all-start = ((bf16[16,4,16,128]{3,2,1,0:T(8,128)(2,1)}), bf16[16,4,16,128]{3,2,1,0:T(8,128)(2,1)S(1)}, u32[]{:S(2)}, u32[]{:S(2)}) async-start(bf16[16,4,16,128]{3,2,1,0:T(8,128)(2,1)} %pack_messages.1), calls=%async_computation | async-start | bytes 524288 | tf_op jit(solution)/shard_map/all_to_all | solution.py:550
  8.7 26.6 %collective-permute-start.5 = (bf16[1,2048,128]{2,1,0:T(8,128)(2,1)S(1)}, bf16[1,2048,128]{2,1,0:T(8,128)(2,1)S(1)}, u32[]{:S(2)}, u32[]{:S(2)}) collective-permute-start(bf16[1,2048,128]{2,1,0:T(8,128)(2,1)S(1)} %get-tuple-element.63.refs_1_), channel_id=1, source_target_pairs={{16,0},{32,16},{48,32},{64,48},{80,64},{96,80},{112,96},{128,112},... | collective-permute-start | bytes 1572872 | tf_op jit(solution)/shard_map/ppermute | solution.py:553
  10.8 24.6 %collective-permute-start.4 = (bf16[1,2048,128]{2,1,0:T(8,128)(2,1)S(1)}, bf16[1,2048,128]{2,1,0:T(8,128)(2,1)S(1)}, u32[]{:S(2)}, u32[]{:S(2)}) collective-permute-start(bf16[1,2048,128]{2,1,0:T(8,128)(2,1)S(1)} %get-tuple-element.64.refs_0_), channel_id=1, source_target_pairs={{0,16},{16,32},{32,48},{48,64},{64,80},{80,96},{96,112},{112,128},... | collective-permute-start | bytes 1572872 | tf_op jit(solution)/shard_map/ppermute | solution.py:552
  21.2 9.6 %collective-permute-start = (bf16[32,2176]{1,0:T(8,128)(2,1)S(1)}, bf16[32,2176]{1,0:T(8,128)(2,1)S(1)}, u32[]{:S(2)}, u32[]{:S(2)}) collective-permute-start(bf16[32,2176]{1,0:T(8,128)(2,1)S(1)} %get-tuple-element.38), channel_id=1, source_target_pairs={{0,2},{1,3},{2,4},{3,5},{4,6},{5,7},{6,8},{7,9},{8,10},{9,11},{10,... | collective-permute-start | bytes 417800 | tf_op jit(solution)/shard_map/ppermute | solution.py:543
  23.2 7.7 %collective-permute-start.1 = (bf16[32,2176]{1,0:T(8,128)(2,1)S(1)}, bf16[32,2176]{1,0:T(8,128)(2,1)S(1)}, u32[]{:S(2)}, u32[]{:S(2)}) collective-permute-start(bf16[32,2176]{1,0:T(8,128)(2,1)S(1)} %get-tuple-element.40), channel_id=1, source_target_pairs={{0,14},{1,15},{2,0},{3,1},{4,2},{5,3},{6,4},{7,5},{8,6},{9,7},{10,... | collective-permute-start | bytes 417800 | tf_op jit(solution)/shard_map/ppermute | solution.py:543
  31.0 10.4 %collective-permute-start.3 = (bf16[64,2304]{1,0:T(8,128)(2,1)S(1)}, bf16[64,2304]{1,0:T(8,128)(2,1)S(1)}, u32[]{:S(2)}, u32[]{:S(2)}) collective-permute-start(bf16[64,2304]{1,0:T(8,128)(2,1)S(1)} %get-tuple-element.44), channel_id=1, source_target_pairs={{0,14},{1,15},{2,0},{3,1},{4,2},{5,3},{6,4},{7,5},{8,6},{9,7},{10,... | collective-permute-start | bytes 884744 | tf_op jit(solution)/shard_map/ppermute | solution.py:543
  34.7 10.1 %collective-permute-start.2 = (bf16[64,2304]{1,0:T(8,128)(2,1)S(1)}, bf16[64,2304]{1,0:T(8,128)(2,1)S(1)}, u32[]{:S(2)}, u32[]{:S(2)}) collective-permute-start(bf16[64,2304]{1,0:T(8,128)(2,1)S(1)} %get-tuple-element.42.refs_0_), channel_id=1, source_target_pairs={{0,2},{1,3},{2,4},{3,5},{4,6},{5,7},{6,8},{7,9},{8,10},{9,11},{10,... | collective-permute-start | bytes 884744 | tf_op jit(solution)/shard_map/ppermute | solution.py:543
  45.0 8.5 %collective-permute-start.7 = (bf16[64,2432]{1,0:T(8,128)(2,1)S(1)}, bf16[64,2432]{1,0:T(8,128)(2,1)S(1)}, u32[]{:S(2)}, u32[]{:S(2)}) collective-permute-start(bf16[64,2432]{1,0:T(8,128)(2,1)S(1)} %get-tuple-element.49), channel_id=1, source_target_pairs={{0,14},{1,15},{2,0},{3,1},{4,2},{5,3},{6,4},{7,5},{8,6},{9,7},{10,... | collective-permute-start | bytes 933896 | tf_op jit(solution)/shard_map/ppermute | solution.py:543
  45.3 9.7 %collective-permute-start.6 = (bf16[64,2432]{1,0:T(8,128)(2,1)S(1)}, bf16[64,2432]{1,0:T(8,128)(2,1)S(1)}, u32[]{:S(2)}, u32[]{:S(2)}) collective-permute-start(bf16[64,2432]{1,0:T(8,128)(2,1)S(1)} %get-tuple-element.47.refs_0_), channel_id=1, source_target_pairs={{0,2},{1,3},{2,4},{3,5},{4,6},{5,7},{6,8},{7,9},{8,10},{9,11},{10,... | collective-permute-start | bytes 933896 | tf_op jit(solution)/shard_map/ppermute | solution.py:543
  55.1 8.7 %collective-permute-start.9 = (bf16[64,2816]{1,0:T(8,128)(2,1)S(1)}, bf16[64,2816]{1,0:T(8,128)(2,1)S(1)}, u32[]{:S(2)}, u32[]{:S(2)}) collective-permute-start(bf16[64,2816]{1,0:T(8,128)(2,1)S(1)} %get-tuple-element.54), channel_id=1, source_target_pairs={{0,14},{1,15},{2,0},{3,1},{4,2},{5,3},{6,4},{7,5},{8,6},{9,7},{10,... | collective-permute-start | bytes 1081352 | tf_op jit(solution)/shard_map/ppermute | solution.py:543
  55.5 9.8 %collective-permute-start.8 = (bf16[64,2816]{1,0:T(8,128)(2,1)S(1)}, bf16[64,2816]{1,0:T(8,128)(2,1)S(1)}, u32[]{:S(2)}, u32[]{:S(2)}) collective-permute-start(bf16[64,2816]{1,0:T(8,128)(2,1)S(1)} %get-tuple-element.53.refs_0_), channel_id=1, source_target_pairs={{0,2},{1,3},{2,4},{3,5},{4,6},{5,7},{6,8},{7,9},{8,10},{9,11},{10,... | collective-permute-start | bytes 1081352 | tf_op jit(solution)/shard_map/ppermute | solution.py:543
  66.0 8.0 %collective-permute-start.10 = (bf16[64,2048]{1,0:T(8,128)(2,1)S(1)}, bf16[64,2048]{1,0:T(8,128)(2,1)S(1)}, u32[]{:S(2)}, u32[]{:S(2)}) collective-permute-start(bf16[64,2048]{1,0:T(8,128)(2,1)S(1)} %get-tuple-element.57.refs_0_), channel_id=1, source_target_pairs={{0,1},{1,0},{2,3},{3,2},{4,5},{5,4},{6,7},{7,6},{8,9},{9,8},{10,11... | collective-permute-start | bytes 786440 | tf_op jit(solution)/shard_map/ppermute | solution.py:546
  75.4 6.6 %collective-permute-start.11 = (bf16[32,2048]{1,0:T(8,128)(2,1)S(1)}, bf16[32,2048]{1,0:T(8,128)(2,1)S(1)}, u32[]{:S(2)}, u32[]{:S(2)}) collective-permute-start(bf16[32,2048]{1,0:T(8,128)(2,1)S(1)} %residual_images.1.refs_0_), channel_id=1, source_target_pairs={{0,1},{1,0},{2,3},{3,2},{4,5},{5,4},{6,7},{7,6},{8,9},{9,8},{10,11... | collective-permute-start | bytes 393224 | tf_op jit(solution)/shard_map/ppermute | solution.py:546
  77.7 7.3 %collective-permute-start.14 = (bf16[32,2048]{1,0:T(8,128)(2,1)S(1)}, bf16[32,2048]{1,0:T(8,128)(2,1)S(1)}, u32[]{:S(2)}, u32[]{:S(2)}) collective-permute-start(bf16[32,2048]{1,0:T(8,128)(2,1)S(1)} %residual_images.1.refs_0_), channel_id=1, source_target_pairs={{0,2},{1,3},{2,4},{3,5},{4,6},{5,7},{6,8},{7,9},{8,10},{9,11},{10,... | collective-permute-start | bytes 393224 | tf_op jit(solution)/shard_map/ppermute | solution.py:543
  82.0 6.4 %collective-permute-start.13 = (bf16[32,2048]{1,0:T(8,128)(2,1)S(1)}, bf16[32,2048]{1,0:T(8,128)(2,1)S(1)}, u32[]{:S(2)}, u32[]{:S(2)}) collective-permute-start(bf16[32,2048]{1,0:T(8,128)(2,1)S(1)} %collective-permute-done.11.refs_1_), channel_id=1, source_target_pairs={{0,14},{1,15},{2,0},{3,1},{4,2},{5,3},{6,4},{7,5},{8,6},{9,7},{10,... | collective-permute-start | bytes 393224 | tf_op jit(solution)/shard_map/ppermute | solution.py:543
  82.4 8.5 %collective-permute-start.12 = (bf16[32,2048]{1,0:T(8,128)(2,1)S(1)}, bf16[32,2048]{1,0:T(8,128)(2,1)S(1)}, u32[]{:S(2)}, u32[]{:S(2)}) collective-permute-start(bf16[32,2048]{1,0:T(8,128)(2,1)S(1)} %residual_images.1.refs_0_), channel_id=1, source_target_pairs={{0,14},{1,15},{2,0},{3,1},{4,2},{5,3},{6,4},{7,5},{8,6},{9,7},{10,... | collective-permute-start | bytes 393224 | tf_op jit(solution)/shard_map/ppermute | solution.py:543
  85.0 7.7 %collective-permute-start.18 = (bf16[32,2048]{1,0:T(8,128)(2,1)S(1)}, bf16[32,2048]{1,0:T(8,128)(2,1)S(1)}, u32[]{:S(2)}, u32[]{:S(2)}) collective-permute-start(bf16[32,2048]{1,0:T(8,128)(2,1)S(1)} %collective-permute-done.14.refs_4_), channel_id=1, source_target_pairs={{0,2},{1,3},{2,4},{3,5},{4,6},{5,7},{6,8},{7,9},{8,10},{9,11},{10,... | collective-permute-start | bytes 393224 | tf_op jit(solution)/shard_map/ppermute | solution.py:543
  85.0 9.5 %collective-permute-start.15 = (bf16[32,2048]{1,0:T(8,128)(2,1)S(1)}, bf16[32,2048]{1,0:T(8,128)(2,1)S(1)}, u32[]{:S(2)}, u32[]{:S(2)}) collective-permute-start(bf16[32,2048]{1,0:T(8,128)(2,1)S(1)} %collective-permute-done.11.refs_1_), channel_id=1, source_target_pairs={{0,2},{1,3},{2,4},{3,5},{4,6},{5,7},{6,8},{7,9},{8,10},{9,11},{10,... | collective-permute-start | bytes 393224 | tf_op jit(solution)/shard_map/ppermute | solution.py:543
  88.3 6.2 %collective-permute-start.17 = (bf16[32,2048]{1,0:T(8,128)(2,1)S(1)}, bf16[32,2048]{1,0:T(8,128)(2,1)S(1)}, u32[]{:S(2)}, u32[]{:S(2)}) collective-permute-start(bf16[32,2048]{1,0:T(8,128)(2,1)S(1)} %collective-permute-done.13.refs_3_), channel_id=1, source_target_pairs={{0,14},{1,15},{2,0},{3,1},{4,2},{5,3},{6,4},{7,5},{8,6},{9,7},{10,... | collective-permute-start | bytes 393224 | tf_op jit(solution)/shard_map/ppermute | solution.py:543
  90.8 7.0 %collective-permute-start.16 = (bf16[32,2048]{1,0:T(8,128)(2,1)S(1)}, bf16[32,2048]{1,0:T(8,128)(2,1)S(1)}, u32[]{:S(2)}, u32[]{:S(2)}) collective-permute-start(bf16[32,2048]{1,0:T(8,128)(2,1)S(1)} %collective-permute-done.12.refs_2_), channel_id=1, source_target_pairs={{0,14},{1,15},{2,0},{3,1},{4,2},{5,3},{6,4},{7,5},{8,6},{9,7},{10,... | collective-permute-start | bytes 393224 | tf_op jit(solution)/shard_map/ppermute | solution.py:543
  92.7 7.6 %collective-permute-start.22 = (bf16[32,2048]{1,0:T(8,128)(2,1)S(1)}, bf16[32,2048]{1,0:T(8,128)(2,1)S(1)}, u32[]{:S(2)}, u32[]{:S(2)}) collective-permute-start(bf16[32,2048]{1,0:T(8,128)(2,1)S(1)} %collective-permute-done.18.refs_8_), channel_id=1, source_target_pairs={{0,2},{1,3},{2,4},{3,5},{4,6},{5,7},{6,8},{7,9},{8,10},{9,11},{10,... | collective-permute-start | bytes 393224 | tf_op jit(solution)/shard_map/ppermute | solution.py:543
  94.6 7.3 %collective-permute-start.19 = (bf16[32,2048]{1,0:T(8,128)(2,1)S(1)}, bf16[32,2048]{1,0:T(8,128)(2,1)S(1)}, u32[]{:S(2)}, u32[]{:S(2)}) collective-permute-start(bf16[32,2048]{1,0:T(8,128)(2,1)S(1)} %collective-permute-done.15.refs_5_), channel_id=1, source_target_pairs={{0,2},{1,3},{2,4},{3,5},{4,6},{5,7},{6,8},{7,9},{8,10},{9,11},{10,... | collective-permute-start | bytes 393224 | tf_op jit(solution)/shard_map/ppermute | solution.py:543
  94.6 7.3 %collective-permute-start.21 = (bf16[32,2048]{1,0:T(8,128)(2,1)S(1)}, bf16[32,2048]{1,0:T(8,128)(2,1)S(1)}, u32[]{:S(2)}, u32[]{:S(2)}) collective-permute-start(bf16[32,2048]{1,0:T(8,128)(2,1)S(1)} %collective-permute-done.17.refs_7_), channel_id=1, source_target_pairs={{0,14},{1,15},{2,0},{3,1},{4,2},{5,3},{6,4},{7,5},{8,6},{9,7},{10,... | collective-permute-start | bytes 393224 | tf_op jit(solution)/shard_map/ppermute | solution.py:543
  97.8 7.3 %collective-permute-start.20 = (bf16[32,2048]{1,0:T(8,128)(2,1)S(1)}, bf16[32,2048]{1,0:T(8,128)(2,1)S(1)}, u32[]{:S(2)}, u32[]{:S(2)}) collective-permute-start(bf16[32,2048]{1,0:T(8,128)(2,1)S(1)} %collective-permute-done.16.refs_6_), channel_id=1, source_target_pairs={{0,14},{1,15},{2,0},{3,1},{4,2},{5,3},{6,4},{7,5},{8,6},{9,7},{10,... | collective-permute-start | bytes 393224 | tf_op jit(solution)/shard_map/ppermute | solution.py:543
  100.3 6.2 %collective-permute-start.24 = (bf16[32,2048]{1,0:T(8,128)(2,1)S(1)}, bf16[32,2048]{1,0:T(8,128)(2,1)S(1)}, u32[]{:S(2)}, u32[]{:S(2)}) collective-permute-start(bf16[32,2048]{1,0:T(8,128)(2,1)S(1)} %collective-permute-done.22.refs_12_), channel_id=1, source_target_pairs={{0,2},{1,3},{2,4},{3,5},{4,6},{5,7},{6,8},{7,9},{8,10},{9,11},{10,... | collective-permute-start | bytes 393224 | tf_op jit(solution)/shard_map/ppermute | solution.py:543
  101.9 6.2 %collective-permute-start.23 = (bf16[32,2048]{1,0:T(8,128)(2,1)S(1)}, bf16[32,2048]{1,0:T(8,128)(2,1)S(1)}, u32[]{:S(2)}, u32[]{:S(2)}) collective-permute-start(bf16[32,2048]{1,0:T(8,128)(2,1)S(1)} %collective-permute-done.19.refs_9_), channel_id=1, source_target_pairs={{0,2},{1,3},{2,4},{3,5},{4,6},{5,7},{6,8},{7,9},{8,10},{9,11},{10,... | collective-permute-start | bytes 393224 | tf_op jit(solution)/shard_map/ppermute | solution.py:543
  101.9 6.2 %collective-permute-start.25 = (bf16[32,2048]{1,0:T(8,128)(2,1)S(1)}, bf16[32,2048]{1,0:T(8,128)(2,1)S(1)}, u32[]{:S(2)}, u32[]{:S(2)}) collective-permute-start(bf16[32,2048]{1,0:T(8,128)(2,1)S(1)} %collective-permute-done.21.refs_11_), channel_id=1, source_target_pairs={{0,14},{1,15},{2,0},{3,1},{4,2},{5,3},{6,4},{7,5},{8,6},{9,7},{10,... | collective-permute-start | bytes 393224 | tf_op jit(solution)/shard_map/ppermute | solution.py:543

commit v6 on v5

--- a/solution.py
+++ b/solution.py
@@ -23,6 +23,7 @@
     return pltpu.CompilerParams(vmem_limit_bytes=mib << 20)
 
 XT = 256
+WIDE = 512
 F32 = jnp.float32
 BF16 = jnp.bfloat16
 VMEM = pl.BlockSpec(memory_space=pltpu.VMEM)
@@ -78,14 +79,14 @@
     return jnp.concatenate([block[z] for z in range(block.shape[0])], axis=1)
 
 
-def tile_copies(ref, buffer_ref, sem_ref, index, first=0, edge=0):
+def tile_copies(ref, buffer_ref, sem_ref, index, first=0, edge=0, tile=XT):
     slot = lax.rem(index, 2)
     extent = ref.shape[1]
-    start = (first + index) * XT
-    parts = [(start, edge, XT)]
+    start = (first + index) * tile
+    parts = [(start, edge, tile)]
     if edge:
         parts.append((jnp.maximum(start - edge, 0), 0, edge))
-        parts.append((jnp.minimum(start + XT, extent - edge), edge + XT, edge))
+        parts.append((jnp.minimum(start + tile, extent - edge), edge + tile, edge))
     return [
         pltpu.make_async_copy(
             ref.at[:, pl.ds(pl.multiple_of(source, 16), size)],
@@ -101,19 +102,19 @@
         copy.start()
 
 
-def streamed(ref, buffer_ref, sem_ref, step, steps, first=0, edge=0):
+def streamed(ref, buffer_ref, sem_ref, step, steps, first=0, edge=0, tile=XT):
     @pl.when(step + 1 < steps)
     def _():
-        start(tile_copies(ref, buffer_ref, sem_ref, step + 1, first, edge))
-
-    for copy in tile_copies(ref, buffer_ref, sem_ref, step, first, edge):
+        start(tile_copies(ref, buffer_ref, sem_ref, step + 1, first, edge, tile))
+
+    for copy in tile_copies(ref, buffer_ref, sem_ref, step, first, edge, tile):
         copy.wait()
     return buffer_ref.at[lax.rem(step, 2)]
 
 
-def stream_scratch(depth, strip, edge=0):
+def stream_scratch(depth, strip, edge=0, tile=XT):
     return [
-        pltpu.VMEM((2, depth, XT + 2 * edge, strip), BF16),
+        pltpu.VMEM((2, depth, tile + 2 * edge, strip), BF16),
         pltpu.SemaphoreType.DMA((2, 3 if edge else 1)),
     ]
 
@@ -474,21 +475,21 @@
     chunk_refs = refs[:-6]
     whole_ref, out_ref, buffer_ref, sem_ref, result_ref, result_sem_ref = refs[-6:]
     depth, extent, strip = whole_ref.shape
-    steps = extent // XT
+    steps = extent // WIDE
     beta = beta_ref[0]
     has_left = (place_ref[1] > 0).astype(F32)
     has_right = (place_ref[1] < place_ref[2] - 1).astype(F32)
-    start(tile_copies(whole_ref, buffer_ref, sem_ref, 0))
+    start(tile_copies(whole_ref, buffer_ref, sem_ref, 0, tile=WIDE))
 
     def result(step):
         slot = lax.rem(step, 2)
-        here = pl.ds(pl.multiple_of(step * XT, XT), XT)
+        here = pl.ds(pl.multiple_of(step * WIDE, WIDE), WIDE)
         return pltpu.make_async_copy(
             result_ref.at[slot], out_ref.at[:, here], result_sem_ref.at[slot]
         )
 
     def body(step, carry):
-        here = pl.ds(pl.multiple_of(step * XT, XT), XT)
+        here = pl.ds(pl.multiple_of(step * WIDE, WIDE), WIDE)
         mine = mine_ref[:, here].astype(F32)
         beside = beside_ref[RUN : RUN + LINES, here].astype(F32)
         on_left = penalty(mine[:8] - beside[:8]) * (has_left * beta)
@@ -498,7 +499,7 @@
         out = lax.dot_general(
             rows, spread_ref[...], (((0,), (0,)), ((), ())), preferred_element_type=F32
         )
-        regular_ref = streamed(whole_ref, buffer_ref, sem_ref, step, steps)
+        regular_ref = streamed(whole_ref, buffer_ref, sem_ref, step, steps, tile=WIDE)
 
         @pl.when(step >= 2)
         def _():
@@ -524,9 +525,9 @@
         out_shape=jax.ShapeDtypeStruct(regular.shape, BF16),
         in_specs=[SMEM, SMEM] + [VMEM] * (3 + len(chunks)) + [HBM],
         out_specs=ANY,
-        scratch_shapes=stream_scratch(depth, strip)
-        + [pltpu.VMEM((2, depth, XT, strip), BF16), pltpu.SemaphoreType.DMA((2,))],
-        compiler_params=limit(12),
+        scratch_shapes=stream_scratch(depth, strip, tile=WIDE)
+        + [pltpu.VMEM((2, depth, WIDE, strip), BF16), pltpu.SemaphoreType.DMA((2,))],
+        compiler_params=limit(16),
         cost_estimate=cost(2 * spread.shape[0] * size, 5 * size),
         name="gradient",
     )(place, beta, spread, mine, arrived, *chunks, regular)
@@ -579,7 +580,7 @@
         for hop in range(1, tiles // 4):
             up, down = along_z(up, 1), along_z(down, -1)
             ring[-hop], ring[hop] = up, down
-        ring[tiles // 4] = along_z(up, 1) if past == 1 else along_z(down, -1)
+        ring[tiles // 4] = along_z(ring[-2 * past], 2 * past)
         rings.append(ring)
     chunks = [ring[hop] for hop in hops(tiles) for ring in rings]
     regular = pltpu.with_memory_space_constraint(regular, pltpu.HBM)

time: 117 us -> 116 us (level)
  starting transfers between devices: 43.9 us -> 49.1 us
  waiting for transfers between devices: 28.2 us -> 23.1 us
    ppermute x22, starting transfers between devices: 29.1 us -> 34.3 us  [along_z(): lax.ppermute(block, 'tile', [(i, (i + 2 * by) % tiles) for i in range(til...]
    ppermute x2, waiting for transfers between devices: 4.16 us -> 1.18 us  [along_y(): return lax.ppermute(block, 'tile', [(i, i ^ 1) for i in range(tiles)])]
    ppermute x22, waiting for transfers between devices: 23.2 us -> 21.2 us  [along_z(): lax.ppermute(block, 'tile', [(i, (i + 2 * by) % tiles) for i in range(til...]
  transfers between devices with their start and end apart: 27 -> 27, of which waited for: 18 -> 16; matrix products, arithmetic and copies ran while one was open for 1% -> 1% of each run, Pallas kernels for 26% -> 26%
where the time goes in v6:
time: 116 us; the launch traced here: 115 us
  starting transfers between devices  49.1 us (42%)
  Pallas kernels  40.5 us (35%)
  waiting for transfers between devices  23.1 us (20%)
  local copies, waits for them, and re-layouts  1.27 us (1%)
    ppermute x22, starting transfers between devices, along_z(): lax.ppermute(block, 'tile', [(i, (i + 2 * by) % tiles) for i in range(til...  34.3 us
    pallas_call x4, Pallas kernels, regularizer(): pl.pallas_call(functools.partial(regularizer_kernel, origin, count), grid...  21.8 us
    ppermute x22, waiting for transfers between devices, along_z(): lax.ppermute(block, 'tile', [(i, (i + 2 * by) % tiles) for i in range(til...  21.2 us
    pallas_call x1, Pallas kernels, forward(): pl.pallas_call(kernel, out_shape=[jax.ShapeDtypeStruct(shape, BF16) for s...  7.28 us
    pallas_call x1, Pallas kernels, gradient(): pl.pallas_call(gradient_kernel, out_shape=jax.ShapeDtypeStruct(regular.sh...  6.62 us
    all_to_all x1, starting transfers between devices, shards(): lax.all_to_all(packed, 'slab', split_axis=0, concat_axis=0, tiled=True)  5.77 us
    ppermute x2, starting transfers between devices, along_y(): return lax.ppermute(block, 'tile', [(i, i ^ 1) for i in range(tiles)])  4.66 us
  transfers between devices with their start and end apart: 27, of which 16 were waited for; matrix products, arithmetic and copies ran while one was open for 1% of the time, Pallas kernels for 26%

profile of v6, /device:TPU:8, one launch (start us, length us, event | category | flops | bytes accessed | tf_op | source)
XLA Modules:
  0.0 115.1 jit_solution(6187113158801758042)
XLA Ops:
  0.0 1.7 %pack_messages.1 = bf16[16,4,16,128]{3,2,1,0:T(8,128)(2,1)} custom-call(s32[2,12]{1,0:T(2,128)} %bitcast.9, s32[2,12]{1,0:T(2,128)} %offset_ref.1, s32[2,12]{1,0:T(2,128)} %width_ref.1, bf16[12,2,128]{2,1,0:T(2,128)(2,1)} %bitcast.8, bf16[2,12,8,128]{3,2,1,0:T(8,128)(2,1)} %measured_ref.1), custom_call_target="tpu_custom_call" | custom-call | tf_op jit(solution)/shard_map/pack_messages/pallas_call | solution.py:68
  1.7 5.8 %all-to-all-start = ((bf16[16,4,16,128]{3,2,1,0:T(8,128)(2,1)}), bf16[16,4,16,128]{3,2,1,0:T(8,128)(2,1)S(1)}, u32[]{:S(2)}, u32[]{:S(2)}) async-start(bf16[16,4,16,128]{3,2,1,0:T(8,128)(2,1)} %pack_messages.1), calls=%async_computation | async-start | bytes 524288 | tf_op jit(solution)/shard_map/all_to_all | solution.py:551
  8.7 2.0 %collective-permute-start.5 = (bf16[1,2048,128]{2,1,0:T(8,128)(2,1)S(1)}, bf16[1,2048,128]{2,1,0:T(8,128)(2,1)S(1)}, u32[]{:S(2)}, u32[]{:S(2)}) collective-permute-start(bf16[1,2048,128]{2,1,0:T(8,128)(2,1)S(1)} %get-tuple-element.63.refs_1_), channel_id=1, source_target_pairs={{16,0},{32,16},{48,32},{64,48},{80,64},{96,80},{112,96},{128,112},... | collective-permute-start | bytes 1572872 | tf_op jit(solution)/shard_map/ppermute | solution.py:554
  10.8 2.3 %collective-permute-start.4 = (bf16[1,2048,128]{2,1,0:T(8,128)(2,1)S(1)}, bf16[1,2048,128]{2,1,0:T(8,128)(2,1)S(1)}, u32[]{:S(2)}, u32[]{:S(2)}) collective-permute-start(bf16[1,2048,128]{2,1,0:T(8,128)(2,1)S(1)} %get-tuple-element.64.refs_0_), channel_id=1, source_target_pairs={{0,16},{16,32},{32,48},{48,64},{64,80},{80,96},{96,112},{112,128},... | collective-permute-start | bytes 1572872 | tf_op jit(solution)/shard_map/ppermute | solution.py:553
  14.0 7.3 %forward.1 = (bf16[64,2176]{1,0:T(8,128)(2,1)S(1)}, bf16[64,2432]{1,0:T(8,128)(2,1)S(1)}, bf16[64,2432]{1,0:T(8,128)(2,1)S(1)}, bf16[64,2176]{1,0:T(8,128)(2,1)S...) custom-call(s32[4]{0:T(128)S(1)} %pad_add_fusion.place_ref, ...), custom_call_target="tpu_custom_call" | custom-call | flops 2147483648 | bytes 6291456 | tf_op jit(solution)/shard_map/forward/pallas_call | solution.py:221
  21.2 2.0 %collective-permute-start = (bf16[32,2176]{1,0:T(8,128)(2,1)S(1)}, bf16[32,2176]{1,0:T(8,128)(2,1)S(1)}, u32[]{:S(2)}, u32[]{:S(2)}) collective-permute-start(bf16[32,2176]{1,0:T(8,128)(2,1)S(1)} %get-tuple-element.38), channel_id=1, source_target_pairs={{0,2},{1,3},{2,4},{3,5},{4,6},{5,7},{6,8},{7,9},{8,10},{9,11},{10,... | collective-permute-start | bytes 417800 | tf_op jit(solution)/shard_map/ppermute | solution.py:544
  23.2 4.0 %collective-permute-start.1 = (bf16[32,2176]{1,0:T(8,128)(2,1)S(1)}, bf16[32,2176]{1,0:T(8,128)(2,1)S(1)}, u32[]{:S(2)}, u32[]{:S(2)}) collective-permute-start(bf16[32,2176]{1,0:T(8,128)(2,1)S(1)} %get-tuple-element.40), channel_id=1, source_target_pairs={{0,14},{1,15},{2,0},{3,1},{4,2},{5,3},{6,4},{7,5},{8,6},{9,7},{10,... | collective-permute-start | bytes 417800 | tf_op jit(solution)/shard_map/ppermute | solution.py:544
  28.0 2.9 %collective-permute-done.from_below_ref = bf16[32,2176]{1,0:T(8,128)(2,1)S(1)} collective-permute-done((bf16[32,2176]{1,0:T(8,128)(2,1)S(1)}, bf16[32,2176]{1,0:T(8,128)(2,1)S(1)}, u32[]{:S(2)}, u32[]{:S(2)}) %collective-permute-start) | collective-permute-done | bytes 139296 | tf_op jit(solution)/shard_map/ppermute | solution.py:544
  31.0 3.7 %collective-permute-start.3 = (bf16[64,2304]{1,0:T(8,128)(2,1)S(1)}, bf16[64,2304]{1,0:T(8,128)(2,1)S(1)}, u32[]{:S(2)}, u32[]{:S(2)}) collective-permute-start(bf16[64,2304]{1,0:T(8,128)(2,1)S(1)} %get-tuple-element.44), channel_id=1, source_target_pairs={{0,14},{1,15},{2,0},{3,1},{4,2},{5,3},{6,4},{7,5},{8,6},{9,7},{10,... | collective-permute-start | bytes 884744 | tf_op jit(solution)/shard_map/ppermute | solution.py:544
  35.4 5.5 %regularizer.4 = (bf16[8,2048,128]{2,1,0:T(8,128)(2,1)}, f32[8,128]{1,0:T(8,128)S(1)}) custom-call(s32[4]{0:T(128)S(1)} %pad_add_fusion.place_ref, f32[1]{0:T(128)S(6)} %copy.14.beta_ref, bf16[8,2048,128]{2,1,0:T(8,128)(2,1)} %volume_ref.9, bf16[1,2048,128]{2,1,0:T(8,128)(2,1)S(1)} %collective-permute-done.4.below_ref, ...), custom_call_target="tpu_custom_call" | custom-call | flops 15728640 | bytes 4194304 | tf_op jit(solution)/shard_map/regularizer/pallas_call | solution.py:460
  41.4 3.4 %collective-permute-done.2.from_below_ref = bf16[64,2304]{1,0:T(8,128)(2,1)S(1)} collective-permute-done((bf16[64,2304]{1,0:T(8,128)(2,1)S(1)}, bf16[64,2304]{1,0:T(8,128)(2,1)S(1)}, u32[]{:S(2)}, u32[]{:S(2)}) %collective-permute-start.2) | collective-permute-done | bytes 294944 | tf_op jit(solution)/shard_map/ppermute | solution.py:544
  45.3 1.7 %collective-permute-start.6 = (bf16[64,2432]{1,0:T(8,128)(2,1)S(1)}, bf16[64,2432]{1,0:T(8,128)(2,1)S(1)}, u32[]{:S(2)}, u32[]{:S(2)}) collective-permute-start(bf16[64,2432]{1,0:T(8,128)(2,1)S(1)} %get-tuple-element.47.refs_0_), channel_id=1, source_target_pairs={{0,2},{1,3},{2,4},{3,5},{4,6},{5,7},{6,8},{7,9},{8,10},{9,11},{10,... | collective-permute-start | bytes 933896 | tf_op jit(solution)/shard_map/ppermute | solution.py:544
  47.1 5.4 %regularizer.5 = (bf16[8,2048,128]{2,1,0:T(8,128)(2,1)}, f32[8,128]{1,0:T(8,128)S(1)}) custom-call(s32[4]{0:T(128)S(1)} %pad_add_fusion.place_ref, f32[1]{0:T(128)S(6)} %copy.14.beta_ref, bf16[8,2048,128]{2,1,0:T(8,128)(2,1)} %volume_ref.9, bf16[1,2048,128]{2,1,0:T(8,128)(2,1)S(1)} %collective-permute-done.4.below_ref, ...), custom_call_target="tpu_custom_call", output_to_operand_aliasing={{0}: (6, {})} | custom-call | flops 15728640 | bytes 4194304 | tf_op jit(solution)/shard_map/regularizer/pallas_call | solution.py:460
  53.5 1.5 %collective-permute-done.6.from_below_ref = bf16[64,2432]{1,0:T(8,128)(2,1)S(1)} collective-permute-done((bf16[64,2432]{1,0:T(8,128)(2,1)S(1)}, bf16[64,2432]{1,0:T(8,128)(2,1)S(1)}, u32[]{:S(2)}, u32[]{:S(2)}) %collective-permute-start.6) | collective-permute-done | bytes 311328 | tf_op jit(solution)/shard_map/ppermute | solution.py:544
  55.5 1.7 %collective-permute-start.8 = (bf16[64,2816]{1,0:T(8,128)(2,1)S(1)}, bf16[64,2816]{1,0:T(8,128)(2,1)S(1)}, u32[]{:S(2)}, u32[]{:S(2)}) collective-permute-start(bf16[64,2816]{1,0:T(8,128)(2,1)S(1)} %get-tuple-element.53.refs_0_), channel_id=1, source_target_pairs={{0,2},{1,3},{2,4},{3,5},{4,6},{5,7},{6,8},{7,9},{8,10},{9,11},{10,... | collective-permute-start | bytes 1081352 | tf_op jit(solution)/shard_map/ppermute | solution.py:544
  57.2 5.4 %regularizer.6 = (bf16[8,2048,128]{2,1,0:T(8,128)(2,1)}, f32[8,128]{1,0:T(8,128)S(1)}) custom-call(s32[4]{0:T(128)S(1)} %pad_add_fusion.place_ref, f32[1]{0:T(128)S(6)} %copy.14.beta_ref, bf16[8,2048,128]{2,1,0:T(8,128)(2,1)} %volume_ref.9, bf16[1,2048,128]{2,1,0:T(8,128)(2,1)S(1)} %collective-permute-done.4.below_ref, ...), custom_call_target="tpu_custom_call", output_to_operand_aliasing={{0}: (6, {})} | custom-call | flops 15728640 | bytes 4194304 | tf_op jit(solution)/shard_map/regularizer/pallas_call | solution.py:460
  63.8 1.5 %collective-permute-done.8.below_ref = bf16[64,2816]{1,0:T(8,128)(2,1)S(1)} collective-permute-done((bf16[64,2816]{1,0:T(8,128)(2,1)S(1)}, bf16[64,2816]{1,0:T(8,128)(2,1)S(1)}, u32[]{:S(2)}, u32[]{:S(2)}) %collective-permute-start.8) | collective-permute-done | bytes 360480 | tf_op jit(solution)/shard_map/ppermute | solution.py:544
  66.0 2.3 %collective-permute-start.10 = (bf16[64,2048]{1,0:T(8,128)(2,1)S(1)}, bf16[64,2048]{1,0:T(8,128)(2,1)S(1)}, u32[]{:S(2)}, u32[]{:S(2)}) collective-permute-start(bf16[64,2048]{1,0:T(8,128)(2,1)S(1)} %get-tuple-element.57.refs_0_), channel_id=1, source_target_pairs={{0,1},{1,0},{2,3},{3,2},{4,5},{5,4},{6,7},{7,6},{8,9},{9,8},{10,11... | collective-permute-start | bytes 786440 | tf_op jit(solution)/shard_map/ppermute | solution.py:547
  68.3 5.4 %regularizer.7 = (bf16[8,2048,128]{2,1,0:T(8,128)(2,1)}, f32[8,128]{1,0:T(8,128)S(1)}) custom-call(s32[4]{0:T(128)S(1)} %pad_add_fusion.place_ref, f32[1]{0:T(128)S(6)} %copy.14.beta_ref, bf16[8,2048,128]{2,1,0:T(8,128)(2,1)} %volume_ref.9, bf16[1,2048,128]{2,1,0:T(8,128)(2,1)S(1)} %collective-permute-done.4.below_ref, ...), custom_call_target="tpu_custom_call", output_to_operand_aliasing={{0}: (6, {})} | custom-call | flops 15728640 | bytes 4194304 | tf_op jit(solution)/shard_map/regularizer/pallas_call | solution.py:460
  73.9 1.4 %residual_images.1.refs_0_ = bf16[32,2048]{1,0:T(8,128)(2,1)S(1)} custom-call(s32[4]{0:T(128)S(1)} %pad_add_fusion.place_ref, f32[32,2048]{1,0:T(8,128)S(1)} %get-tuple-element.58.kept_ref, bf16[32,1024]{1,0:T(8,128)(2,1)S(1)} %get-tuple-element.59.strips_ref, bf16[64,2048]{1,0:T(8,128)(2,1)S(1)} %collective-permute-done.10.arrived_ref.beside_ref, ...), custom_call_target="tpu_custom_call" | custom-call | flops 100663296 | bytes 786432 | tf_op jit(solution)/shard_map/residual_images/pallas_call | solution.py:379
  75.4 2.3 %collective-permute-start.11 = (bf16[32,2048]{1,0:T(8,128)(2,1)S(1)}, bf16[32,2048]{1,0:T(8,128)(2,1)S(1)}, u32[]{:S(2)}, u32[]{:S(2)}) collective-permute-start(bf16[32,2048]{1,0:T(8,128)(2,1)S(1)} %residual_images.1.refs_0_), channel_id=1, source_target_pairs={{0,1},{1,0},{2,3},{3,2},{4,5},{5,4},{6,7},{7,6},{8,9},{9,8},{10,11... | collective-permute-start | bytes 393224 | tf_op jit(solution)/shard_map/ppermute | solution.py:547
  78.0 3.0 %collective-permute-start.12 = (bf16[32,2048]{1,0:T(8,128)(2,1)S(1)}, bf16[32,2048]{1,0:T(8,128)(2,1)S(1)}, u32[]{:S(2)}, u32[]{:S(2)}) collective-permute-start(bf16[32,2048]{1,0:T(8,128)(2,1)S(1)} %residual_images.1.refs_0_), channel_id=1, source_target_pairs={{0,14},{1,15},{2,0},{3,1},{4,2},{5,3},{6,4},{7,5},{8,6},{9,7},{10,... | collective-permute-start | bytes 393224 | tf_op jit(solution)/shard_map/ppermute | solution.py:544
  82.2 3.0 %collective-permute-start.13 = (bf16[32,2048]{1,0:T(8,128)(2,1)S(1)}, bf16[32,2048]{1,0:T(8,128)(2,1)S(1)}, u32[]{:S(2)}, u32[]{:S(2)}) collective-permute-start(bf16[32,2048]{1,0:T(8,128)(2,1)S(1)} %collective-permute-done.11.refs_1_), channel_id=1, source_target_pairs={{0,14},{1,15},{2,0},{3,1},{4,2},{5,3},{6,4},{7,5},{8,6},{9,7},{10,... | collective-permute-start | bytes 393224 | tf_op jit(solution)/shard_map/ppermute | solution.py:544
  85.2 3.2 %collective-permute-start.16 = (bf16[32,2048]{1,0:T(8,128)(2,1)S(1)}, bf16[32,2048]{1,0:T(8,128)(2,1)S(1)}, u32[]{:S(2)}, u32[]{:S(2)}) collective-permute-start(bf16[32,2048]{1,0:T(8,128)(2,1)S(1)} %collective-permute-done.12.refs_2_), channel_id=1, source_target_pairs={{0,14},{1,15},{2,0},{3,1},{4,2},{5,3},{6,4},{7,5},{8,6},{9,7},{10,... | collective-permute-start | bytes 393224 | tf_op jit(solution)/shard_map/ppermute | solution.py:544
  89.1 3.4 %collective-permute-start.17 = (bf16[32,2048]{1,0:T(8,128)(2,1)S(1)}, bf16[32,2048]{1,0:T(8,128)(2,1)S(1)}, u32[]{:S(2)}, u32[]{:S(2)}) collective-permute-start(bf16[32,2048]{1,0:T(8,128)(2,1)S(1)} %collective-permute-done.13.refs_3_), channel_id=1, source_target_pairs={{0,14},{1,15},{2,0},{3,1},{4,2},{5,3},{6,4},{7,5},{8,6},{9,7},{10,... | collective-permute-start | bytes 393224 | tf_op jit(solution)/shard_map/ppermute | solution.py:544
  92.6 1.7 %collective-permute-done.18.refs_8_ = bf16[32,2048]{1,0:T(8,128)(2,1)S(1)} collective-permute-done((bf16[32,2048]{1,0:T(8,128)(2,1)S(1)}, bf16[32,2048]{1,0:T(8,128)(2,1)S(1)}, u32[]{:S(2)}, u32[]{:S(2)}) %collective-permute-start.18) | collective-permute-done | bytes 131104 | tf_op jit(solution)/shard_map/ppermute | solution.py:544
  94.3 1.4 %collective-permute-start.22 = (bf16[32,2048]{1,0:T(8,128)(2,1)S(1)}, bf16[32,2048]{1,0:T(8,128)(2,1)S(1)}, u32[]{:S(2)}, u32[]{:S(2)}) collective-permute-start(bf16[32,2048]{1,0:T(8,128)(2,1)S(1)} %collective-permute-done.18.refs_8_), channel_id=1, source_target_pairs={{0,2},{1,3},{2,4},{3,5},{4,6},{5,7},{6,8},{7,9},{8,10},{9,11},{10,... | collective-permute-start | bytes 393224 | tf_op jit(solution)/shard_map/ppermute | solution.py:544
  95.6 1.9 %collective-permute-start.20 = (bf16[32,2048]{1,0:T(8,128)(2,1)S(1)}, bf16[32,2048]{1,0:T(8,128)(2,1)S(1)}, u32[]{:S(2)}, u32[]{:S(2)}) collective-permute-start(bf16[32,2048]{1,0:T(8,128)(2,1)S(1)} %collective-permute-done.16.refs_6_), channel_id=1, source_target_pairs={{0,14},{1,15},{2,0},{3,1},{4,2},{5,3},{6,4},{7,5},{8,6},{9,7},{10,... | collective-permute-start | bytes 393224 | tf_op jit(solution)/shard_map/ppermute | solution.py:544
  97.5 2.1 %collective-permute-start.23 = (bf16[32,2048]{1,0:T(8,128)(2,1)S(1)}, bf16[32,2048]{1,0:T(8,128)(2,1)S(1)}, u32[]{:S(2)}, u32[]{:S(2)}) collective-permute-start(bf16[32,2048]{1,0:T(8,128)(2,1)S(1)} %collective-permute-done.19.refs_9_), channel_id=1, source_target_pairs={{0,2},{1,3},{2,4},{3,5},{4,6},{5,7},{6,8},{7,9},{8,10},{9,11},{10,... | collective-permute-start | bytes 393224 | tf_op jit(solution)/shard_map/ppermute | solution.py:544
  103.7 1.9 %collective-permute-done.25.refs_15_ = bf16[32,2048]{1,0:T(8,128)(2,1)S(1)} collective-permute-done((bf16[32,2048]{1,0:T(8,128)(2,1)S(1)}, bf16[32,2048]{1,0:T(8,128)(2,1)S(1)}, u32[]{:S(2)}, u32[]{:S(2)}) %collective-permute-start.25) | collective-permute-done | bytes 131104 | tf_op jit(solution)/shard_map/ppermute | solution.py:544
  105.5 2.8 %collective-permute-done.21.refs_11_ = bf16[32,2048]{1,0:T(8,128)(2,1)S(1)} collective-permute-done((bf16[32,2048]{1,0:T(8,128)(2,1)S(1)}, bf16[32,2048]{1,0:T(8,128)(2,1)S(1)}, u32[]{:S(2)}, u32[]{:S(2)}) %collective-permute-start.21) | collective-permute-done | bytes 131104 | tf_op jit(solution)/shard_map/ppermute | solution.py:544
  108.3 6.6 %gradient.1 = bf16[8,2048,128]{2,1,0:T(8,128)(2,1)} custom-call(s32[4]{0:T(128)S(1)} %pad_add_fusion.place_ref, f32[1]{0:T(128)S(6)} %copy.14.beta_ref, bf16[528,1024]{1,0:T(8,128)(2,1)S(1)} %spread_rows.1.refs_0_.spread_ref, bf16[16,2048]{1,0:T(8,128)(2,1)S(1)} %get-tuple-element.36.order_ref.ends_ref.mine_ref, ...), custom_call_target="tpu_custom_call" | custom-call | flops 2214592512 | bytes 10485760 | tf_op jit(solution)/shard_map/gradient/pallas_call | solution.py:523
  (38 shorter events, 13.8 us)
Async XLA Ops:
  1.7 12.3 %all-to-all-start = ((bf16[16,4,16,128]{3,2,1,0:T(8,128)(2,1)}), bf16[16,4,16,128]{3,2,1,0:T(8,128)(2,1)S(1)}, u32[]{:S(2)}, u32[]{:S(2)}) async-start(bf16[16,4,16,128]{3,2,1,0:T(8,128)(2,1)} %pack_messages.1), calls=%async_computation | async-start | bytes 524288 | tf_op jit(solution)/shard_map/all_to_all | solution.py:551
  8.7 26.6 %collective-permute-start.5 = (bf16[1,2048,128]{2,1,0:T(8,128)(2,1)S(1)}, bf16[1,2048,128]{2,1,0:T(8,128)(2,1)S(1)}, u32[]{:S(2)}, u32[]{:S(2)}) collective-permute-start(bf16[1,2048,128]{2,1,0:T(8,128)(2,1)S(1)} %get-tuple-element.63.refs_1_), channel_id=1, source_target_pairs={{16,0},{32,16},{48,32},{64,48},{80,64},{96,80},{112,96},{128,112},... | collective-permute-start | bytes 1572872 | tf_op jit(solution)/shard_map/ppermute | solution.py:554
  10.8 24.6 %collective-permute-start.4 = (bf16[1,2048,128]{2,1,0:T(8,128)(2,1)S(1)}, bf16[1,2048,128]{2,1,0:T(8,128)(2,1)S(1)}, u32[]{:S(2)}, u32[]{:S(2)}) collective-permute-start(bf16[1,2048,128]{2,1,0:T(8,128)(2,1)S(1)} %get-tuple-element.64.refs_0_), channel_id=1, source_target_pairs={{0,16},{16,32},{32,48},{48,64},{64,80},{80,96},{96,112},{112,128},... | collective-permute-start | bytes 1572872 | tf_op jit(solution)/shard_map/ppermute | solution.py:553
  21.2 9.6 %collective-permute-start = (bf16[32,2176]{1,0:T(8,128)(2,1)S(1)}, bf16[32,2176]{1,0:T(8,128)(2,1)S(1)}, u32[]{:S(2)}, u32[]{:S(2)}) collective-permute-start(bf16[32,2176]{1,0:T(8,128)(2,1)S(1)} %get-tuple-element.38), channel_id=1, source_target_pairs={{0,2},{1,3},{2,4},{3,5},{4,6},{5,7},{6,8},{7,9},{8,10},{9,11},{10,... | collective-permute-start | bytes 417800 | tf_op jit(solution)/shard_map/ppermute | solution.py:544
  23.2 7.7 %collective-permute-start.1 = (bf16[32,2176]{1,0:T(8,128)(2,1)S(1)}, bf16[32,2176]{1,0:T(8,128)(2,1)S(1)}, u32[]{:S(2)}, u32[]{:S(2)}) collective-permute-start(bf16[32,2176]{1,0:T(8,128)(2,1)S(1)} %get-tuple-element.40), channel_id=1, source_target_pairs={{0,14},{1,15},{2,0},{3,1},{4,2},{5,3},{6,4},{7,5},{8,6},{9,7},{10,... | collective-permute-start | bytes 417800 | tf_op jit(solution)/shard_map/ppermute | solution.py:544
  31.0 10.4 %collective-permute-start.3 = (bf16[64,2304]{1,0:T(8,128)(2,1)S(1)}, bf16[64,2304]{1,0:T(8,128)(2,1)S(1)}, u32[]{:S(2)}, u32[]{:S(2)}) collective-permute-start(bf16[64,2304]{1,0:T(8,128)(2,1)S(1)} %get-tuple-element.44), channel_id=1, source_target_pairs={{0,14},{1,15},{2,0},{3,1},{4,2},{5,3},{6,4},{7,5},{8,6},{9,7},{10,... | collective-permute-start | bytes 884744 | tf_op jit(solution)/shard_map/ppermute | solution.py:544
  34.7 10.1 %collective-permute-start.2 = (bf16[64,2304]{1,0:T(8,128)(2,1)S(1)}, bf16[64,2304]{1,0:T(8,128)(2,1)S(1)}, u32[]{:S(2)}, u32[]{:S(2)}) collective-permute-start(bf16[64,2304]{1,0:T(8,128)(2,1)S(1)} %get-tuple-element.42.refs_0_), channel_id=1, source_target_pairs={{0,2},{1,3},{2,4},{3,5},{4,6},{5,7},{6,8},{7,9},{8,10},{9,11},{10,... | collective-permute-start | bytes 884744 | tf_op jit(solution)/shard_map/ppermute | solution.py:544
  45.0 8.5 %collective-permute-start.7 = (bf16[64,2432]{1,0:T(8,128)(2,1)S(1)}, bf16[64,2432]{1,0:T(8,128)(2,1)S(1)}, u32[]{:S(2)}, u32[]{:S(2)}) collective-permute-start(bf16[64,2432]{1,0:T(8,128)(2,1)S(1)} %get-tuple-element.49), channel_id=1, source_target_pairs={{0,14},{1,15},{2,0},{3,1},{4,2},{5,3},{6,4},{7,5},{8,6},{9,7},{10,... | collective-permute-start | bytes 933896 | tf_op jit(solution)/shard_map/ppermute | solution.py:544
  45.3 9.7 %collective-permute-start.6 = (bf16[64,2432]{1,0:T(8,128)(2,1)S(1)}, bf16[64,2432]{1,0:T(8,128)(2,1)S(1)}, u32[]{:S(2)}, u32[]{:S(2)}) collective-permute-start(bf16[64,2432]{1,0:T(8,128)(2,1)S(1)} %get-tuple-element.47.refs_0_), channel_id=1, source_target_pairs={{0,2},{1,3},{2,4},{3,5},{4,6},{5,7},{6,8},{7,9},{8,10},{9,11},{10,... | collective-permute-start | bytes 933896 | tf_op jit(solution)/shard_map/ppermute | solution.py:544
  55.1 8.7 %collective-permute-start.9 = (bf16[64,2816]{1,0:T(8,128)(2,1)S(1)}, bf16[64,2816]{1,0:T(8,128)(2,1)S(1)}, u32[]{:S(2)}, u32[]{:S(2)}) collective-permute-start(bf16[64,2816]{1,0:T(8,128)(2,1)S(1)} %get-tuple-element.54), channel_id=1, source_target_pairs={{0,14},{1,15},{2,0},{3,1},{4,2},{5,3},{6,4},{7,5},{8,6},{9,7},{10,... | collective-permute-start | bytes 1081352 | tf_op jit(solution)/shard_map/ppermute | solution.py:544
  55.5 9.8 %collective-permute-start.8 = (bf16[64,2816]{1,0:T(8,128)(2,1)S(1)}, bf16[64,2816]{1,0:T(8,128)(2,1)S(1)}, u32[]{:S(2)}, u32[]{:S(2)}) collective-permute-start(bf16[64,2816]{1,0:T(8,128)(2,1)S(1)} %get-tuple-element.53.refs_0_), channel_id=1, source_target_pairs={{0,2},{1,3},{2,4},{3,5},{4,6},{5,7},{6,8},{7,9},{8,10},{9,11},{10,... | collective-permute-start | bytes 1081352 | tf_op jit(solution)/shard_map/ppermute | solution.py:544
  66.0 8.0 %collective-permute-start.10 = (bf16[64,2048]{1,0:T(8,128)(2,1)S(1)}, bf16[64,2048]{1,0:T(8,128)(2,1)S(1)}, u32[]{:S(2)}, u32[]{:S(2)}) collective-permute-start(bf16[64,2048]{1,0:T(8,128)(2,1)S(1)} %get-tuple-element.57.refs_0_), channel_id=1, source_target_pairs={{0,1},{1,0},{2,3},{3,2},{4,5},{5,4},{6,7},{7,6},{8,9},{9,8},{10,11... | collective-permute-start | bytes 786440 | tf_op jit(solution)/shard_map/ppermute | solution.py:547
  75.4 6.6 %collective-permute-start.11 = (bf16[32,2048]{1,0:T(8,128)(2,1)S(1)}, bf16[32,2048]{1,0:T(8,128)(2,1)S(1)}, u32[]{:S(2)}, u32[]{:S(2)}) collective-permute-start(bf16[32,2048]{1,0:T(8,128)(2,1)S(1)} %residual_images.1.refs_0_), channel_id=1, source_target_pairs={{0,1},{1,0},{2,3},{3,2},{4,5},{5,4},{6,7},{7,6},{8,9},{9,8},{10,11... | collective-permute-start | bytes 393224 | tf_op jit(solution)/shard_map/ppermute | solution.py:547
  77.7 7.5 %collective-permute-start.14 = (bf16[32,2048]{1,0:T(8,128)(2,1)S(1)}, bf16[32,2048]{1,0:T(8,128)(2,1)S(1)}, u32[]{:S(2)}, u32[]{:S(2)}) collective-permute-start(bf16[32,2048]{1,0:T(8,128)(2,1)S(1)} %residual_images.1.refs_0_), channel_id=1, source_target_pairs={{0,2},{1,3},{2,4},{3,5},{4,6},{5,7},{6,8},{7,9},{8,10},{9,11},{10,... | collective-permute-start | bytes 393224 | tf_op jit(solution)/shard_map/ppermute | solution.py:544
  78.0 7.2 %collective-permute-start.12 = (bf16[32,2048]{1,0:T(8,128)(2,1)S(1)}, bf16[32,2048]{1,0:T(8,128)(2,1)S(1)}, u32[]{:S(2)}, u32[]{:S(2)}) collective-permute-start(bf16[32,2048]{1,0:T(8,128)(2,1)S(1)} %residual_images.1.refs_0_), channel_id=1, source_target_pairs={{0,14},{1,15},{2,0},{3,1},{4,2},{5,3},{6,4},{7,5},{8,6},{9,7},{10,... | collective-permute-start | bytes 393224 | tf_op jit(solution)/shard_map/ppermute | solution.py:544
  82.0 7.2 %collective-permute-start.15 = (bf16[32,2048]{1,0:T(8,128)(2,1)S(1)}, bf16[32,2048]{1,0:T(8,128)(2,1)S(1)}, u32[]{:S(2)}, u32[]{:S(2)}) collective-permute-start(bf16[32,2048]{1,0:T(8,128)(2,1)S(1)} %collective-permute-done.11.refs_1_), channel_id=1, source_target_pairs={{0,2},{1,3},{2,4},{3,5},{4,6},{5,7},{6,8},{7,9},{8,10},{9,11},{10,... | collective-permute-start | bytes 393224 | tf_op jit(solution)/shard_map/ppermute | solution.py:544
  82.2 6.9 %collective-permute-start.13 = (bf16[32,2048]{1,0:T(8,128)(2,1)S(1)}, bf16[32,2048]{1,0:T(8,128)(2,1)S(1)}, u32[]{:S(2)}, u32[]{:S(2)}) collective-permute-start(bf16[32,2048]{1,0:T(8,128)(2,1)S(1)} %collective-permute-done.11.refs_1_), channel_id=1, source_target_pairs={{0,14},{1,15},{2,0},{3,1},{4,2},{5,3},{6,4},{7,5},{8,6},{9,7},{10,... | collective-permute-start | bytes 393224 | tf_op jit(solution)/shard_map/ppermute | solution.py:544
  85.2 9.0 %collective-permute-start.18 = (bf16[32,2048]{1,0:T(8,128)(2,1)S(1)}, bf16[32,2048]{1,0:T(8,128)(2,1)S(1)}, u32[]{:S(2)}, u32[]{:S(2)}) collective-permute-start(bf16[32,2048]{1,0:T(8,128)(2,1)S(1)} %collective-permute-done.14.refs_4_), channel_id=1, source_target_pairs={{0,2},{1,3},{2,4},{3,5},{4,6},{5,7},{6,8},{7,9},{8,10},{9,11},{10,... | collective-permute-start | bytes 393224 | tf_op jit(solution)/shard_map/ppermute | solution.py:544
  85.2 10.4 %collective-permute-start.16 = (bf16[32,2048]{1,0:T(8,128)(2,1)S(1)}, bf16[32,2048]{1,0:T(8,128)(2,1)S(1)}, u32[]{:S(2)}, u32[]{:S(2)}) collective-permute-start(bf16[32,2048]{1,0:T(8,128)(2,1)S(1)} %collective-permute-done.12.refs_2_), channel_id=1, source_target_pairs={{0,14},{1,15},{2,0},{3,1},{4,2},{5,3},{6,4},{7,5},{8,6},{9,7},{10,... | collective-permute-start | bytes 393224 | tf_op jit(solution)/shard_map/ppermute | solution.py:544
  89.1 8.4 %collective-permute-start.19 = (bf16[32,2048]{1,0:T(8,128)(2,1)S(1)}, bf16[32,2048]{1,0:T(8,128)(2,1)S(1)}, u32[]{:S(2)}, u32[]{:S(2)}) collective-permute-start(bf16[32,2048]{1,0:T(8,128)(2,1)S(1)} %collective-permute-done.15.refs_5_), channel_id=1, source_target_pairs={{0,2},{1,3},{2,4},{3,5},{4,6},{5,7},{6,8},{7,9},{8,10},{9,11},{10,... | collective-permute-start | bytes 393224 | tf_op jit(solution)/shard_map/ppermute | solution.py:544
  89.1 10.4 %collective-permute-start.17 = (bf16[32,2048]{1,0:T(8,128)(2,1)S(1)}, bf16[32,2048]{1,0:T(8,128)(2,1)S(1)}, u32[]{:S(2)}, u32[]{:S(2)}) collective-permute-start(bf16[32,2048]{1,0:T(8,128)(2,1)S(1)} %collective-permute-done.13.refs_3_), channel_id=1, source_target_pairs={{0,14},{1,15},{2,0},{3,1},{4,2},{5,3},{6,4},{7,5},{8,6},{9,7},{10,... | collective-permute-start | bytes 393224 | tf_op jit(solution)/shard_map/ppermute | solution.py:544
  94.2 7.2 %collective-permute-start.24 = (bf16[32,2048]{1,0:T(8,128)(2,1)S(1)}, bf16[32,2048]{1,0:T(8,128)(2,1)S(1)}, u32[]{:S(2)}, u32[]{:S(2)}) collective-permute-start(bf16[32,2048]{1,0:T(8,128)(2,1)S(1)} %collective-permute-done.18.refs_8_), channel_id=1, source_target_pairs={{0,4},{1,5},{2,6},{3,7},{4,8},{5,9},{6,10},{7,11},{8,12},{9,13},{1... | collective-permute-start | bytes 393224 | tf_op jit(solution)/shard_map/ppermute | solution.py:544
  94.3 8.2 %collective-permute-start.22 = (bf16[32,2048]{1,0:T(8,128)(2,1)S(1)}, bf16[32,2048]{1,0:T(8,128)(2,1)S(1)}, u32[]{:S(2)}, u32[]{:S(2)}) collective-permute-start(bf16[32,2048]{1,0:T(8,128)(2,1)S(1)} %collective-permute-done.18.refs_8_), channel_id=1, source_target_pairs={{0,2},{1,3},{2,4},{3,5},{4,6},{5,7},{6,8},{7,9},{8,10},{9,11},{10,... | collective-permute-start | bytes 393224 | tf_op jit(solution)/shard_map/ppermute | solution.py:544
  95.6 6.8 %collective-permute-start.20 = (bf16[32,2048]{1,0:T(8,128)(2,1)S(1)}, bf16[32,2048]{1,0:T(8,128)(2,1)S(1)}, u32[]{:S(2)}, u32[]{:S(2)}) collective-permute-start(bf16[32,2048]{1,0:T(8,128)(2,1)S(1)} %collective-permute-done.16.refs_6_), channel_id=1, source_target_pairs={{0,14},{1,15},{2,0},{3,1},{4,2},{5,3},{6,4},{7,5},{8,6},{9,7},{10,... | collective-permute-start | bytes 393224 | tf_op jit(solution)/shard_map/ppermute | solution.py:544
  97.5 6.2 %collective-permute-start.23 = (bf16[32,2048]{1,0:T(8,128)(2,1)S(1)}, bf16[32,2048]{1,0:T(8,128)(2,1)S(1)}, u32[]{:S(2)}, u32[]{:S(2)}) collective-permute-start(bf16[32,2048]{1,0:T(8,128)(2,1)S(1)} %collective-permute-done.19.refs_9_), channel_id=1, source_target_pairs={{0,2},{1,3},{2,4},{3,5},{4,6},{5,7},{6,8},{7,9},{8,10},{9,11},{10,... | collective-permute-start | bytes 393224 | tf_op jit(solution)/shard_map/ppermute | solution.py:544
  99.6 6.0 %collective-permute-start.25 = (bf16[32,2048]{1,0:T(8,128)(2,1)S(1)}, bf16[32,2048]{1,0:T(8,128)(2,1)S(1)}, u32[]{:S(2)}, u32[]{:S(2)}) collective-permute-start(bf16[32,2048]{1,0:T(8,128)(2,1)S(1)} %collective-permute-done.17.refs_7_), channel_id=1, source_target_pairs={{0,12},{1,13},{2,14},{3,15},{4,0},{5,1},{6,2},{7,3},{8,4},{9,5},{1... | collective-permute-start | bytes 393224 | tf_op jit(solution)/shard_map/ppermute | solution.py:544
  101.4 6.9 %collective-permute-start.21 = (bf16[32,2048]{1,0:T(8,128)(2,1)S(1)}, bf16[32,2048]{1,0:T(8,128)(2,1)S(1)}, u32[]{:S(2)}, u32[]{:S(2)}) collective-permute-start(bf16[32,2048]{1,0:T(8,128)(2,1)S(1)} %collective-permute-done.17.refs_7_), channel_id=1, source_target_pairs={{0,14},{1,15},{2,0},{3,1},{4,2},{5,3},{6,4},{7,5},{8,6},{9,7},{10,... | collective-permute-start | bytes 393224 | tf_op jit(solution)/shard_map/ppermute | solution.py:544

commit v7 on v6

--- a/solution.py
+++ b/solution.py
@@ -40,7 +40,26 @@
     return lax.broadcasted_iota(jnp.int32, shape, dim)
 
 
-def pack_kernel(owner_ref, offset_ref, width_ref, weight_ref, measured_ref, out_ref, count_ref):
+def pack_kernel(
+    owner_ref,
+    offset_ref,
+    width_ref,
+    weight_ref,
+    measured_ref,
+    volume_ref,
+    out_ref,
+    top_ref,
+    bottom_ref,
+    count_ref,
+    sem_ref,
+):
+    depth = volume_ref.shape[0]
+    slices = [
+        pltpu.make_async_copy(volume_ref.at[pl.ds(z, 1)], ref, sem_ref.at[index])
+        for index, (z, ref) in enumerate(((depth - 1, top_ref), (0, bottom_ref)))
+    ]
+    for copy in slices:
+        copy.start()
     out_ref[...] = jnp.zeros_like(out_ref)
     slabs = out_ref.shape[0]
     views = owner_ref.shape[1]
@@ -62,17 +81,24 @@
             )
             rows = jnp.where(row == 8, weight_ref[view].astype(F32)[batch : batch + 1], jnp.where(row == 9, band, rows))
             out_ref[owner, batch * CAPP + rank] = rows.astype(BF16)
-
-
-def pack(owner, offset, width, weight, measured, slabs):
+    for copy in slices:
+        copy.wait()
+
+
+def pack(owner, offset, width, weight, measured, volume, slabs):
+    plane = jax.ShapeDtypeStruct((1,) + volume.shape[1:], BF16)
     return pl.pallas_call(
         pack_kernel,
-        out_shape=jax.ShapeDtypeStruct((slabs, SLOTS, ROWS, BAND), BF16),
-        in_specs=[SMEM, SMEM, SMEM, VMEM, VMEM],
-        out_specs=VMEM,
-        scratch_shapes=[pltpu.SMEM((slabs,), jnp.int32)],
+        out_shape=(
+            jax.ShapeDtypeStruct((slabs, SLOTS, ROWS, BAND), BF16),
+            plane,
+            plane,
+        ),
+        in_specs=[SMEM, SMEM, SMEM, VMEM, VMEM, HBM],
+        out_specs=(VMEM, ANY, ANY),
+        scratch_shapes=[pltpu.SMEM((slabs,), jnp.int32), pltpu.SemaphoreType.DMA((2,))],
         name="pack_messages",
-    )(owner, offset, width, jnp.transpose(weight, (1, 0, 2)), measured)
+    )(owner, offset, width, jnp.transpose(weight, (1, 0, 2)), measured, volume)
 
 
 def joined(block):
@@ -90,7 +116,7 @@
     return [
         pltpu.make_async_copy(
             ref.at[:, pl.ds(pl.multiple_of(source, 16), size)],
-            buffer_ref.at[slot, :, pl.ds(target, size)],
+            buffer_ref.at[slot, pl.ds(0, ref.shape[0]), pl.ds(target, size)],
             sem_ref.at[slot, part],
         )
         for part, (source, target, size) in enumerate(parts)
@@ -114,7 +140,7 @@
 
 def stream_scratch(depth, strip, edge=0, tile=XT):
     return [
-        pltpu.VMEM((2, depth, tile + 2 * edge, strip), BF16),
+        pltpu.VMEM((2, depth + (1 if edge else 0), tile + 2 * edge, strip), BF16),
         pltpu.SemaphoreType.DMA((2, 3 if edge else 1)),
     ]
 
@@ -175,7 +201,7 @@
     outs, (ends_ref, spread_ref, buffer_ref, sem_ref, last_ref, first_ref) = refs[:-6], refs[-6:]
     extent = volume_ref.shape[1]
     me = place_ref[1]
-    start(tile_copies(volume_ref, buffer_ref, sem_ref, 0))
+    start(tile_copies(volume_ref, buffer_ref, sem_ref, 0, tile=WIDE))
     fill_spread(tiles, me, got_ref, spread_ref)
     where = [(ref, row) for ref in outs for row in range(0, ref.shape[0], RUN)]
     beyond = pl.ds(extent, BAND)
@@ -184,24 +210,26 @@
         for turn, source in enumerate((tile, tile ^ 1)):
             ref, row = where[2 * index + turn]
             ref[row : row + RUN, beyond] = measured_rows(got_ref, source)
-    steps = extent // XT
+    steps = extent // WIDE
 
     def body(step, carry):
-        block_ref = streamed(volume_ref, buffer_ref, sem_ref, step, steps)
+        block_ref = streamed(volume_ref, buffer_ref, sem_ref, step, steps, tile=WIDE)
         out = lax.dot_general(
             spread_ref[...],
             joined(block_ref),
             (((1,), (1,)), ((), ())),
             preferred_element_type=F32,
         ).astype(BF16)
-        here = pl.ds(pl.multiple_of(step * XT, XT), XT)
+        here = pl.ds(pl.multiple_of(step * WIDE, WIDE), WIDE)
         for index, (ref, row) in enumerate(where):
             ref[row : row + RUN, here] = out[index * RUN : (index + 1) * RUN]
         ends_ref[:, here] = out[-LINES:]
         ends = out[-LINES:].astype(F32)
-        there = pl.ds(pl.multiple_of(step * 8, 8), 8)
-        first_ref[there] = ends[:8]
-        last_ref[there] = ends[8:]
+        count = WIDE // XT
+        for part in range(count):
+            there = pl.ds(pl.multiple_of((step * count + part) * 8, 8), 8)
+            first_ref[there] = ends[:8, part * XT : (part + 1) * XT]
+            last_ref[there] = ends[8:, part * XT : (part + 1) * XT]
         return carry
 
     lax.fori_loop(0, steps, body, 0)
@@ -225,9 +253,9 @@
         in_specs=[SMEM, VMEM, HBM] + [ANY] * len(order),
         out_specs=[VMEM] * (len(rows) + 1),
         scratch_shapes=[pltpu.VMEM((slots * depth + LINES, depth * strip), BF16)]
-        + stream_scratch(depth, strip)
+        + stream_scratch(depth, strip, tile=WIDE)
         + [pltpu.VMEM((extent // XT * 8, XT), F32)] * 2,
-        compiler_params=limit(10),
+        compiler_params=limit(12),
         cost_estimate=cost(2 * slots * depth * volume.size, 3 * volume.size),
         name="forward",
     )(place, got, volume, *order)
@@ -410,32 +438,29 @@
         start(tile_copies(volume_ref, buffer_ref, sem_ref, 0, first_tile, EDGE))
 
     block_ref = streamed(volume_ref, buffer_ref, sem_ref, step, steps, first_tile, EDGE)
-    depth, strip, tile = block_ref.shape[0], block_ref.shape[2], XT
+    depth, strip, tile = volume_ref.shape[0], volume_ref.shape[2], XT
     at = pl.program_id(0) + first_tile
     beta = beta_ref[0]
-    has_below = (place_ref[0] > 0).astype(F32)
-    has_above = (place_ref[0] < place_ref[3] - 1).astype(F32)
-    has_before = (at > 0).astype(F32)
-    has_after = (at < count - 1).astype(F32)
+    has_below, has_above = place_ref[0] > 0, place_ref[0] < place_ref[3] - 1
     here = pl.ds(EDGE, tile)
-    under_ref[...] = (
-        penalty(block_ref[0, here].astype(F32) - below_ref[0].astype(F32)) * has_below
-    )
+    bottom, top = block_ref[0, here], block_ref[depth - 1, here]
+    below = jnp.where(has_below, below_ref[0], bottom).astype(F32)
+    block_ref[depth, here] = jnp.where(has_above, above_ref[0], top)
+    under_ref[...] = penalty(bottom.astype(F32) - below)
     row = iota((tile, strip), 0)
     lane = iota((tile, strip), 1)
 
     def body(z, carry):
         center = block_ref[z, here].astype(F32)
-        top = z == depth - 1
-        upper = jnp.where(top, above_ref[0], block_ref[jnp.minimum(z + 1, depth - 1), here])
-        over = penalty(upper.astype(F32) - center) * jnp.where(top, has_above, 1.0)
+        over = penalty(block_ref[z + 1, here].astype(F32) - center)
         total = under_ref[...] - over
         under_ref[...] = over
-        ahead = block_ref[z, pl.ds(EDGE + tile, EDGE)].astype(F32)[0:1]
-        behind = block_ref[z, pl.ds(0, EDGE)].astype(F32)[EDGE - 1 :]
-        behind = penalty(center[0:1] - behind) * has_before
+        behind = block_ref[z, pl.ds(0, EDGE)].astype(F32)
+        behind = jnp.where(at > 0, behind[EDGE - 1 :], behind[:1])
+        ahead = block_ref[z, pl.ds(EDGE + tile, EDGE)].astype(F32)
+        ahead = jnp.where(at < count - 1, ahead[:1], ahead[EDGE - 1 :])
         along = penalty(jnp.where(row == tile - 1, ahead, pltpu.roll(center, tile - 1, 0)) - center)
-        along = jnp.where(row == tile - 1, along * has_after, along)
+        behind = penalty(center[:1] - behind)
         total = total + jnp.where(row == 0, behind, pltpu.roll(along, 1, 0)) - along
         across = penalty(pltpu.roll(center, strip - 1, 1) - center)
         across = jnp.where(lane == strip - 1, 0.0, across)
@@ -537,7 +562,6 @@
     slabs = lax.axis_size("slab")
     tiles = lax.axis_size("tile")
     slab, tile = lax.axis_index("slab"), lax.axis_index("tile")
-    depth = volume.shape[0]
     place = jnp.stack([slab, tile, jnp.int32(tiles), jnp.int32(slabs)])
 
     def along_z(block, by):
@@ -546,18 +570,16 @@
     def along_y(block):
         return lax.ppermute(block, "tile", [(i, i ^ 1) for i in range(tiles)])
 
-    packed = pack(view_owner[:, :, 0], band_offset, band_width, ray_weight, measured, slabs)
-    packed, after = lax.optimization_barrier((packed, volume))
+    volume = pltpu.with_memory_space_constraint(volume, pltpu.HBM)
+    packed, top, bottom = pack(
+        view_owner[:, :, 0], band_offset, band_width, ray_weight, measured, volume, slabs
+    )
     got = lax.all_to_all(packed, "slab", split_axis=0, concat_axis=0, tiled=True)
-    top, bottom = after[depth - 1 :], after[:1]
     below = lax.ppermute(top, "slab", [(i, i + 1) for i in range(slabs - 1)])
     above = lax.ppermute(bottom, "slab", [(i + 1, i) for i in range(slabs - 1)])
     flat = got.reshape(slabs * SLOTS, ROWS, BAND)
-    volume = pltpu.with_memory_space_constraint(volume, pltpu.HBM)
-
-    own, up1, down1, up2, down2, up3, down3, up, down, ends = forward(
-        place, flat, volume, tiles, top, bottom
-    )
+
+    own, up1, down1, up2, down2, up3, down3, up, down, ends = forward(place, flat, volume, tiles)
     extent = ends.shape[1]
     spread = spread_rows(place, flat, tiles, ends)
     order, regular = [spread], None

time: 116 us -> 143 us (1.23)
  Pallas kernels: 40.5 us -> 70.7 us
  waiting for transfers between devices: 23.1 us -> 21.4 us
    pallas_call x1, Pallas kernels: 1.68 us -> 34.4 us  [pack(): pl.pallas_call(pack_kernel, out_shape=(jax.ShapeDtypeStruct((slabs, SLOTS...]
    pallas_call x1, Pallas kernels: 7.28 us -> 5.38 us  [forward(): pl.pallas_call(kernel, out_shape=[jax.ShapeDtypeStruct(shape, BF16) for s...]
    ppermute x22, waiting for transfers between devices: 21.2 us -> 19.4 us  [along_z(): lax.ppermute(block, 'tile', [(i, (i + 2 * by) % tiles) for i in range(til...]
    ppermute x1, starting transfers between devices: 2.02 us -> 3.5 us  [shards(): above = lax.ppermute(bottom, 'slab', [(i + 1, i) for i in range(slabs - 1)])]
  transfers between devices with their start and end apart: 27 -> 27, of which waited for: 16 -> 15; matrix products, arithmetic and copies ran while one was open for 1% -> 0% of each run, Pallas kernels for 26% -> 19%
where the time goes in v7:
time: 143 us
  Pallas kernels  70.7 us (49%)
  starting transfers between devices  49.7 us (35%)
  waiting for transfers between devices  21.4 us (15%)
    pallas_call x1, Pallas kernels, pack(): pl.pallas_call(pack_kernel, out_shape=(jax.ShapeDtypeStruct((slabs, SLOTS...  34.4 us
    ppermute x22, starting transfers between devices, along_z(): lax.ppermute(block, 'tile', [(i, (i + 2 * by) % tiles) for i in range(til...  33.5 us
    pallas_call x4, Pallas kernels, regularizer(): pl.pallas_call(functools.partial(regularizer_kernel, origin, count), grid...  21.1 us
    ppermute x22, waiting for transfers between devices, along_z(): lax.ppermute(block, 'tile', [(i, (i + 2 * by) % tiles) for i in range(til...  19.4 us
    pallas_call x1, Pallas kernels, gradient(): pl.pallas_call(gradient_kernel, out_shape=jax.ShapeDtypeStruct(regular.sh...  6.63 us
    all_to_all x1, starting transfers between devices, shards(): lax.all_to_all(packed, 'slab', split_axis=0, concat_axis=0, tiled=True)  5.79 us
    pallas_call x1, Pallas kernels, forward(): pl.pallas_call(kernel, out_shape=[jax.ShapeDtypeStruct(shape, BF16) for s...  5.38 us
    ppermute x2, starting transfers between devices, along_y(): return lax.ppermute(block, 'tile', [(i, i ^ 1) for i in range(tiles)])  4.77 us
  transfers between devices with their start and end apart: 27, of which 15 were waited for; matrix products, arithmetic and copies ran while one was open for 0% of the time, Pallas kernels for 19%

profile of v7, /device:TPU:8, one launch (start us, length us, event | category | flops | bytes accessed | tf_op | source)
XLA Modules:
  0.0 142.9 jit_solution(4218590050495512188)
XLA Ops:
  0.0 34.4 %pack_messages.1 = (bf16[16,4,16,128]{3,2,1,0:T(8,128)(2,1)}, bf16[1,2048,128]{2,1,0:T(8,128)(2,1)}, bf16[1,2048,128]{2,1,0:T(8,128)(2,1)}) custom-call(s32[2,12]{1,0:T(2,128)} %bitcast.9, s32[2,12]{1,0:T(2,128)} %offset_ref.1, s32[2,12]{1,0:T(2,128)} %width_ref.1, bf16[12,2,128]{2,1,0:T(2,128)(2,1)} %bitcast.8, bf16[2,12,8,128]{3,2,1,0:T(8,128)(2,1)} %measured_ref.1, ...), custom_call_target="tpu_custom_call" | custom-call | tf_op jit(solution)/shard_map/pack_messages/pallas_call | solution.py:90
  34.4 5.8 %all-to-all-start = ((bf16[16,4,16,128]{3,2,1,0:T(8,128)(2,1)}), bf16[16,4,16,128]{3,2,1,0:T(8,128)(2,1)S(1)}, u32[]{:S(2)}, u32[]{:S(2)}) async-start(bf16[16,4,16,128]{3,2,1,0:T(8,128)(2,1)} %get-tuple-element.35), calls=%async_computation | async-start | bytes 524288 | tf_op jit(solution)/shard_map/all_to_all | solution.py:577
  40.2 2.0 %collective-permute-start.4 = (bf16[1,2048,128]{2,1,0:T(8,128)(2,1)}, bf16[1,2048,128]{2,1,0:T(8,128)(2,1)S(1)}, u32[]{:S(2)}, u32[]{:S(2)}) collective-permute-start(bf16[1,2048,128]{2,1,0:T(8,128)(2,1)} %get-tuple-element.46), channel_id=1, source_target_pairs={{0,16},{16,32},{32,48},{48,64},{64,80},{80,96},{96,112},{112,128},... | collective-permute-start | bytes 1572872 | tf_op jit(solution)/shard_map/ppermute | solution.py:578
  42.2 3.5 %collective-permute-start.5 = (bf16[1,2048,128]{2,1,0:T(8,128)(2,1)}, bf16[1,2048,128]{2,1,0:T(8,128)(2,1)S(1)}, u32[]{:S(2)}, u32[]{:S(2)}) collective-permute-start(bf16[1,2048,128]{2,1,0:T(8,128)(2,1)} %get-tuple-element.47), channel_id=1, source_target_pairs={{16,0},{32,16},{48,32},{64,48},{80,64},{96,80},{112,96},{128,112},... | collective-permute-start | bytes 1572872 | tf_op jit(solution)/shard_map/ppermute | solution.py:579
  46.7 5.4 %forward.1 = (bf16[64,2176]{1,0:T(8,128)(2,1)S(1)}, bf16[64,2432]{1,0:T(8,128)(2,1)S(1)}, bf16[64,2432]{1,0:T(8,128)(2,1)S(1)}, bf16[64,2176]{1,0:T(8,128)(2,1)S...) custom-call(s32[4]{0:T(128)S(1)} %pad_add_fusion.place_ref, ...), custom_call_target="tpu_custom_call" | custom-call | flops 2147483648 | bytes 6291456 | tf_op jit(solution)/shard_map/forward/pallas_call | solution.py:249
  52.1 2.0 %collective-permute-start = (bf16[32,2176]{1,0:T(8,128)(2,1)S(1)}, bf16[32,2176]{1,0:T(8,128)(2,1)S(1)}, u32[]{:S(2)}, u32[]{:S(2)}) collective-permute-start(bf16[32,2176]{1,0:T(8,128)(2,1)S(1)} %get-tuple-element.38), channel_id=1, source_target_pairs={{0,2},{1,3},{2,4},{3,5},{4,6},{5,7},{6,8},{7,9},{8,10},{9,11},{10,... | collective-permute-start | bytes 417800 | tf_op jit(solution)/shard_map/ppermute | solution.py:568
  54.1 4.0 %collective-permute-start.1 = (bf16[32,2176]{1,0:T(8,128)(2,1)S(1)}, bf16[32,2176]{1,0:T(8,128)(2,1)S(1)}, u32[]{:S(2)}, u32[]{:S(2)}) collective-permute-start(bf16[32,2176]{1,0:T(8,128)(2,1)S(1)} %get-tuple-element.40), channel_id=1, source_target_pairs={{0,14},{1,15},{2,0},{3,1},{4,2},{5,3},{6,4},{7,5},{8,6},{9,7},{10,... | collective-permute-start | bytes 417800 | tf_op jit(solution)/shard_map/ppermute | solution.py:568
  58.9 3.3 %collective-permute-done.from_below_ref = bf16[32,2176]{1,0:T(8,128)(2,1)S(1)} collective-permute-done((bf16[32,2176]{1,0:T(8,128)(2,1)S(1)}, bf16[32,2176]{1,0:T(8,128)(2,1)S(1)}, u32[]{:S(2)}, u32[]{:S(2)}) %collective-permute-start) | collective-permute-done | bytes 139296 | tf_op jit(solution)/shard_map/ppermute | solution.py:568
  62.3 3.1 %collective-permute-start.3 = (bf16[64,2304]{1,0:T(8,128)(2,1)S(1)}, bf16[64,2304]{1,0:T(8,128)(2,1)S(1)}, u32[]{:S(2)}, u32[]{:S(2)}) collective-permute-start(bf16[64,2304]{1,0:T(8,128)(2,1)S(1)} %get-tuple-element.44), channel_id=1, source_target_pairs={{0,14},{1,15},{2,0},{3,1},{4,2},{5,3},{6,4},{7,5},{8,6},{9,7},{10,... | collective-permute-start | bytes 884744 | tf_op jit(solution)/shard_map/ppermute | solution.py:568
  66.0 5.3 %regularizer.4 = (bf16[8,2048,128]{2,1,0:T(8,128)(2,1)}, f32[8,128]{1,0:T(8,128)S(1)}) custom-call(s32[4]{0:T(128)S(1)} %pad_add_fusion.place_ref, f32[1]{0:T(128)S(6)} %copy.14.beta_ref, bf16[8,2048,128]{2,1,0:T(8,128)(2,1)} %volume_ref.11, bf16[1,2048,128]{2,1,0:T(8,128)(2,1)S(1)} %collective-permute-done.4.below_ref, ...), custom_call_target="tpu_custom_call" | custom-call | flops 15728640 | bytes 4194304 | tf_op jit(solution)/shard_map/regularizer/pallas_call | solution.py:485
  71.4 3.4 %collective-permute-done.2.from_below_ref = bf16[64,2304]{1,0:T(8,128)(2,1)S(1)} collective-permute-done((bf16[64,2304]{1,0:T(8,128)(2,1)S(1)}, bf16[64,2304]{1,0:T(8,128)(2,1)S(1)}, u32[]{:S(2)}, u32[]{:S(2)}) %collective-permute-start.2) | collective-permute-done | bytes 294944 | tf_op jit(solution)/shard_map/ppermute | solution.py:568
  75.2 1.7 %collective-permute-start.6 = (bf16[64,2432]{1,0:T(8,128)(2,1)S(1)}, bf16[64,2432]{1,0:T(8,128)(2,1)S(1)}, u32[]{:S(2)}, u32[]{:S(2)}) collective-permute-start(bf16[64,2432]{1,0:T(8,128)(2,1)S(1)} %get-tuple-element.49.refs_0_), channel_id=1, source_target_pairs={{0,2},{1,3},{2,4},{3,5},{4,6},{5,7},{6,8},{7,9},{8,10},{9,11},{10,... | collective-permute-start | bytes 933896 | tf_op jit(solution)/shard_map/ppermute | solution.py:568
  77.0 5.3 %regularizer.5 = (bf16[8,2048,128]{2,1,0:T(8,128)(2,1)}, f32[8,128]{1,0:T(8,128)S(1)}) custom-call(s32[4]{0:T(128)S(1)} %pad_add_fusion.place_ref, f32[1]{0:T(128)S(6)} %copy.14.beta_ref, bf16[8,2048,128]{2,1,0:T(8,128)(2,1)} %volume_ref.11, bf16[1,2048,128]{2,1,0:T(8,128)(2,1)S(1)} %collective-permute-done.4.below_ref, ...), custom_call_target="tpu_custom_call", output_to_operand_aliasing={{0}: (6, {})} | custom-call | flops 15728640 | bytes 4194304 | tf_op jit(solution)/shard_map/regularizer/pallas_call | solution.py:485
  82.5 1.5 %collective-permute-done.6.from_below_ref = bf16[64,2432]{1,0:T(8,128)(2,1)S(1)} collective-permute-done((bf16[64,2432]{1,0:T(8,128)(2,1)S(1)}, bf16[64,2432]{1,0:T(8,128)(2,1)S(1)}, u32[]{:S(2)}, u32[]{:S(2)}) %collective-permute-start.6) | collective-permute-done | bytes 311328 | tf_op jit(solution)/shard_map/ppermute | solution.py:568
  84.5 1.7 %collective-permute-start.8 = (bf16[64,2816]{1,0:T(8,128)(2,1)S(1)}, bf16[64,2816]{1,0:T(8,128)(2,1)S(1)}, u32[]{:S(2)}, u32[]{:S(2)}) collective-permute-start(bf16[64,2816]{1,0:T(8,128)(2,1)S(1)} %get-tuple-element.55.refs_0_), channel_id=1, source_target_pairs={{0,2},{1,3},{2,4},{3,5},{4,6},{5,7},{6,8},{7,9},{8,10},{9,11},{10,... | collective-permute-start | bytes 1081352 | tf_op jit(solution)/shard_map/ppermute | solution.py:568
  86.2 5.3 %regularizer.6 = (bf16[8,2048,128]{2,1,0:T(8,128)(2,1)}, f32[8,128]{1,0:T(8,128)S(1)}) custom-call(s32[4]{0:T(128)S(1)} %pad_add_fusion.place_ref, f32[1]{0:T(128)S(6)} %copy.14.beta_ref, bf16[8,2048,128]{2,1,0:T(8,128)(2,1)} %volume_ref.11, bf16[1,2048,128]{2,1,0:T(8,128)(2,1)S(1)} %collective-permute-done.4.below_ref, ...), custom_call_target="tpu_custom_call", output_to_operand_aliasing={{0}: (6, {})} | custom-call | flops 15728640 | bytes 4194304 | tf_op jit(solution)/shard_map/regularizer/pallas_call | solution.py:485
  91.9 1.5 %collective-permute-done.8.below_ref = bf16[64,2816]{1,0:T(8,128)(2,1)S(1)} collective-permute-done((bf16[64,2816]{1,0:T(8,128)(2,1)S(1)}, bf16[64,2816]{1,0:T(8,128)(2,1)S(1)}, u32[]{:S(2)}, u32[]{:S(2)}) %collective-permute-start.8) | collective-permute-done | bytes 360480 | tf_op jit(solution)/shard_map/ppermute | solution.py:568
  94.1 2.4 %collective-permute-start.10 = (bf16[64,2048]{1,0:T(8,128)(2,1)S(1)}, bf16[64,2048]{1,0:T(8,128)(2,1)S(1)}, u32[]{:S(2)}, u32[]{:S(2)}) collective-permute-start(bf16[64,2048]{1,0:T(8,128)(2,1)S(1)} %get-tuple-element.59.refs_0_), channel_id=1, source_target_pairs={{0,1},{1,0},{2,3},{3,2},{4,5},{5,4},{6,7},{7,6},{8,9},{9,8},{10,11... | collective-permute-start | bytes 786440 | tf_op jit(solution)/shard_map/ppermute | solution.py:571
  96.4 5.3 %regularizer.7 = (bf16[8,2048,128]{2,1,0:T(8,128)(2,1)}, f32[8,128]{1,0:T(8,128)S(1)}) custom-call(s32[4]{0:T(128)S(1)} %pad_add_fusion.place_ref, f32[1]{0:T(128)S(6)} %copy.14.beta_ref, bf16[8,2048,128]{2,1,0:T(8,128)(2,1)} %volume_ref.11, bf16[1,2048,128]{2,1,0:T(8,128)(2,1)S(1)} %collective-permute-done.4.below_ref, ...), custom_call_target="tpu_custom_call", output_to_operand_aliasing={{0}: (6, {})} | custom-call | flops 15728640 | bytes 4194304 | tf_op jit(solution)/shard_map/regularizer/pallas_call | solution.py:485
  102.0 1.4 %residual_images.1.refs_0_ = bf16[32,2048]{1,0:T(8,128)(2,1)S(1)} custom-call(s32[4]{0:T(128)S(1)} %pad_add_fusion.place_ref, f32[32,2048]{1,0:T(8,128)S(1)} %get-tuple-element.60.kept_ref, bf16[32,1024]{1,0:T(8,128)(2,1)S(1)} %get-tuple-element.61.strips_ref, bf16[64,2048]{1,0:T(8,128)(2,1)S(1)} %collective-permute-done.10.arrived_ref.beside_ref, ...), custom_call_target="tpu_custom_call" | custom-call | flops 100663296 | bytes 786432 | tf_op jit(solution)/shard_map/residual_images/pallas_call | solution.py:407
  103.5 2.4 %collective-permute-start.11 = (bf16[32,2048]{1,0:T(8,128)(2,1)S(1)}, bf16[32,2048]{1,0:T(8,128)(2,1)S(1)}, u32[]{:S(2)}, u32[]{:S(2)}) collective-permute-start(bf16[32,2048]{1,0:T(8,128)(2,1)S(1)} %residual_images.1.refs_0_), channel_id=1, source_target_pairs={{0,1},{1,0},{2,3},{3,2},{4,5},{5,4},{6,7},{7,6},{8,9},{9,8},{10,11... | collective-permute-start | bytes 393224 | tf_op jit(solution)/shard_map/ppermute | solution.py:571
  106.1 3.0 %collective-permute-start.12 = (bf16[32,2048]{1,0:T(8,128)(2,1)S(1)}, bf16[32,2048]{1,0:T(8,128)(2,1)S(1)}, u32[]{:S(2)}, u32[]{:S(2)}) collective-permute-start(bf16[32,2048]{1,0:T(8,128)(2,1)S(1)} %residual_images.1.refs_0_), channel_id=1, source_target_pairs={{0,14},{1,15},{2,0},{3,1},{4,2},{5,3},{6,4},{7,5},{8,6},{9,7},{10,... | collective-permute-start | bytes 393224 | tf_op jit(solution)/shard_map/ppermute | solution.py:568
  110.3 3.0 %collective-permute-start.13 = (bf16[32,2048]{1,0:T(8,128)(2,1)S(1)}, bf16[32,2048]{1,0:T(8,128)(2,1)S(1)}, u32[]{:S(2)}, u32[]{:S(2)}) collective-permute-start(bf16[32,2048]{1,0:T(8,128)(2,1)S(1)} %collective-permute-done.11.refs_1_), channel_id=1, source_target_pairs={{0,14},{1,15},{2,0},{3,1},{4,2},{5,3},{6,4},{7,5},{8,6},{9,7},{10,... | collective-permute-start | bytes 393224 | tf_op jit(solution)/shard_map/ppermute | solution.py:568
  113.3 3.2 %collective-permute-start.16 = (bf16[32,2048]{1,0:T(8,128)(2,1)S(1)}, bf16[32,2048]{1,0:T(8,128)(2,1)S(1)}, u32[]{:S(2)}, u32[]{:S(2)}) collective-permute-start(bf16[32,2048]{1,0:T(8,128)(2,1)S(1)} %collective-permute-done.12.refs_2_), channel_id=1, source_target_pairs={{0,14},{1,15},{2,0},{3,1},{4,2},{5,3},{6,4},{7,5},{8,6},{9,7},{10,... | collective-permute-start | bytes 393224 | tf_op jit(solution)/shard_map/ppermute | solution.py:568
  117.6 3.2 %collective-permute-start.17 = (bf16[32,2048]{1,0:T(8,128)(2,1)S(1)}, bf16[32,2048]{1,0:T(8,128)(2,1)S(1)}, u32[]{:S(2)}, u32[]{:S(2)}) collective-permute-start(bf16[32,2048]{1,0:T(8,128)(2,1)S(1)} %collective-permute-done.13.refs_3_), channel_id=1, source_target_pairs={{0,14},{1,15},{2,0},{3,1},{4,2},{5,3},{6,4},{7,5},{8,6},{9,7},{10,... | collective-permute-start | bytes 393224 | tf_op jit(solution)/shard_map/ppermute | solution.py:568
  120.8 1.5 %collective-permute-done.18.refs_8_ = bf16[32,2048]{1,0:T(8,128)(2,1)S(1)} collective-permute-done((bf16[32,2048]{1,0:T(8,128)(2,1)S(1)}, bf16[32,2048]{1,0:T(8,128)(2,1)S(1)}, u32[]{:S(2)}, u32[]{:S(2)}) %collective-permute-start.18) | collective-permute-done | bytes 131104 | tf_op jit(solution)/shard_map/ppermute | solution.py:568
  123.6 2.0 %collective-permute-start.20 = (bf16[32,2048]{1,0:T(8,128)(2,1)S(1)}, bf16[32,2048]{1,0:T(8,128)(2,1)S(1)}, u32[]{:S(2)}, u32[]{:S(2)}) collective-permute-start(bf16[32,2048]{1,0:T(8,128)(2,1)S(1)} %collective-permute-done.16.refs_6_), channel_id=1, source_target_pairs={{0,14},{1,15},{2,0},{3,1},{4,2},{5,3},{6,4},{7,5},{8,6},{9,7},{10,... | collective-permute-start | bytes 393224 | tf_op jit(solution)/shard_map/ppermute | solution.py:568
  125.6 1.8 %collective-permute-start.23 = (bf16[32,2048]{1,0:T(8,128)(2,1)S(1)}, bf16[32,2048]{1,0:T(8,128)(2,1)S(1)}, u32[]{:S(2)}, u32[]{:S(2)}) collective-permute-start(bf16[32,2048]{1,0:T(8,128)(2,1)S(1)} %collective-permute-done.19.refs_9_), channel_id=1, source_target_pairs={{0,2},{1,3},{2,4},{3,5},{4,6},{5,7},{6,8},{7,9},{8,10},{9,11},{10,... | collective-permute-start | bytes 393224 | tf_op jit(solution)/shard_map/ppermute | solution.py:568
  127.4 1.2 collective-permute-start.25
  131.8 1.6 %collective-permute-done.25.refs_15_ = bf16[32,2048]{1,0:T(8,128)(2,1)S(1)} collective-permute-done((bf16[32,2048]{1,0:T(8,128)(2,1)S(1)}, bf16[32,2048]{1,0:T(8,128)(2,1)S(1)}, u32[]{:S(2)}, u32[]{:S(2)}) %collective-permute-start.25) | collective-permute-done | bytes 131104 | tf_op jit(solution)/shard_map/ppermute | solution.py:568
  133.3 2.8 %collective-permute-done.21.refs_11_ = bf16[32,2048]{1,0:T(8,128)(2,1)S(1)} collective-permute-done((bf16[32,2048]{1,0:T(8,128)(2,1)S(1)}, bf16[32,2048]{1,0:T(8,128)(2,1)S(1)}, u32[]{:S(2)}, u32[]{:S(2)}) %collective-permute-start.21) | collective-permute-done | bytes 131104 | tf_op jit(solution)/shard_map/ppermute | solution.py:568
  136.1 6.6 %gradient.1 = bf16[8,2048,128]{2,1,0:T(8,128)(2,1)} custom-call(s32[4]{0:T(128)S(1)} %pad_add_fusion.place_ref, f32[1]{0:T(128)S(6)} %copy.14.beta_ref, bf16[528,1024]{1,0:T(8,128)(2,1)S(1)} %spread_rows.1.refs_0_.spread_ref, bf16[16,2048]{1,0:T(8,128)(2,1)S(1)} %get-tuple-element.36.order_ref.ends_ref.mine_ref, ...), custom_call_target="tpu_custom_call" | custom-call | flops 2214592512 | bytes 10485760 | tf_op jit(solution)/shard_map/gradient/pallas_call | solution.py:548
  (37 shorter events, 11.3 us)
Async XLA Ops:
  34.4 12.3 %all-to-all-start = ((bf16[16,4,16,128]{3,2,1,0:T(8,128)(2,1)}), bf16[16,4,16,128]{3,2,1,0:T(8,128)(2,1)S(1)}, u32[]{:S(2)}, u32[]{:S(2)}) async-start(bf16[16,4,16,128]{3,2,1,0:T(8,128)(2,1)} %get-tuple-element.35), calls=%async_computation | async-start | bytes 524288 | tf_op jit(solution)/shard_map/all_to_all | solution.py:577
  40.2 25.8 %collective-permute-start.4 = (bf16[1,2048,128]{2,1,0:T(8,128)(2,1)}, bf16[1,2048,128]{2,1,0:T(8,128)(2,1)S(1)}, u32[]{:S(2)}, u32[]{:S(2)}) collective-permute-start(bf16[1,2048,128]{2,1,0:T(8,128)(2,1)} %get-tuple-element.46), channel_id=1, source_target_pairs={{0,16},{16,32},{32,48},{48,64},{64,80},{80,96},{96,112},{112,128},... | collective-permute-start | bytes 1572872 | tf_op jit(solution)/shard_map/ppermute | solution.py:578
  42.2 23.8 %collective-permute-start.5 = (bf16[1,2048,128]{2,1,0:T(8,128)(2,1)}, bf16[1,2048,128]{2,1,0:T(8,128)(2,1)S(1)}, u32[]{:S(2)}, u32[]{:S(2)}) collective-permute-start(bf16[1,2048,128]{2,1,0:T(8,128)(2,1)} %get-tuple-element.47), channel_id=1, source_target_pairs={{16,0},{32,16},{48,32},{64,48},{80,64},{96,80},{112,96},{128,112},... | collective-permute-start | bytes 1572872 | tf_op jit(solution)/shard_map/ppermute | solution.py:579
  52.1 10.1 %collective-permute-start = (bf16[32,2176]{1,0:T(8,128)(2,1)S(1)}, bf16[32,2176]{1,0:T(8,128)(2,1)S(1)}, u32[]{:S(2)}, u32[]{:S(2)}) collective-permute-start(bf16[32,2176]{1,0:T(8,128)(2,1)S(1)} %get-tuple-element.38), channel_id=1, source_target_pairs={{0,2},{1,3},{2,4},{3,5},{4,6},{5,7},{6,8},{7,9},{8,10},{9,11},{10,... | collective-permute-start | bytes 417800 | tf_op jit(solution)/shard_map/ppermute | solution.py:568
  54.1 8.1 %collective-permute-start.1 = (bf16[32,2176]{1,0:T(8,128)(2,1)S(1)}, bf16[32,2176]{1,0:T(8,128)(2,1)S(1)}, u32[]{:S(2)}, u32[]{:S(2)}) collective-permute-start(bf16[32,2176]{1,0:T(8,128)(2,1)S(1)} %get-tuple-element.40), channel_id=1, source_target_pairs={{0,14},{1,15},{2,0},{3,1},{4,2},{5,3},{6,4},{7,5},{8,6},{9,7},{10,... | collective-permute-start | bytes 417800 | tf_op jit(solution)/shard_map/ppermute | solution.py:568
  62.3 9.1 %collective-permute-start.3 = (bf16[64,2304]{1,0:T(8,128)(2,1)S(1)}, bf16[64,2304]{1,0:T(8,128)(2,1)S(1)}, u32[]{:S(2)}, u32[]{:S(2)}) collective-permute-start(bf16[64,2304]{1,0:T(8,128)(2,1)S(1)} %get-tuple-element.44), channel_id=1, source_target_pairs={{0,14},{1,15},{2,0},{3,1},{4,2},{5,3},{6,4},{7,5},{8,6},{9,7},{10,... | collective-permute-start | bytes 884744 | tf_op jit(solution)/shard_map/ppermute | solution.py:568
  65.4 9.3 %collective-permute-start.2 = (bf16[64,2304]{1,0:T(8,128)(2,1)S(1)}, bf16[64,2304]{1,0:T(8,128)(2,1)S(1)}, u32[]{:S(2)}, u32[]{:S(2)}) collective-permute-start(bf16[64,2304]{1,0:T(8,128)(2,1)S(1)} %get-tuple-element.42.refs_0_), channel_id=1, source_target_pairs={{0,2},{1,3},{2,4},{3,5},{4,6},{5,7},{6,8},{7,9},{8,10},{9,11},{10,... | collective-permute-start | bytes 884744 | tf_op jit(solution)/shard_map/ppermute | solution.py:568
  74.9 7.6 %collective-permute-start.7 = (bf16[64,2432]{1,0:T(8,128)(2,1)S(1)}, bf16[64,2432]{1,0:T(8,128)(2,1)S(1)}, u32[]{:S(2)}, u32[]{:S(2)}) collective-permute-start(bf16[64,2432]{1,0:T(8,128)(2,1)S(1)} %get-tuple-element.51), channel_id=1, source_target_pairs={{0,14},{1,15},{2,0},{3,1},{4,2},{5,3},{6,4},{7,5},{8,6},{9,7},{10,... | collective-permute-start | bytes 933896 | tf_op jit(solution)/shard_map/ppermute | solution.py:568
  75.2 8.8 %collective-permute-start.6 = (bf16[64,2432]{1,0:T(8,128)(2,1)S(1)}, bf16[64,2432]{1,0:T(8,128)(2,1)S(1)}, u32[]{:S(2)}, u32[]{:S(2)}) collective-permute-start(bf16[64,2432]{1,0:T(8,128)(2,1)S(1)} %get-tuple-element.49.refs_0_), channel_id=1, source_target_pairs={{0,2},{1,3},{2,4},{3,5},{4,6},{5,7},{6,8},{7,9},{8,10},{9,11},{10,... | collective-permute-start | bytes 933896 | tf_op jit(solution)/shard_map/ppermute | solution.py:568
  84.1 7.8 %collective-permute-start.9 = (bf16[64,2816]{1,0:T(8,128)(2,1)S(1)}, bf16[64,2816]{1,0:T(8,128)(2,1)S(1)}, u32[]{:S(2)}, u32[]{:S(2)}) collective-permute-start(bf16[64,2816]{1,0:T(8,128)(2,1)S(1)} %get-tuple-element.56), channel_id=1, source_target_pairs={{0,14},{1,15},{2,0},{3,1},{4,2},{5,3},{6,4},{7,5},{8,6},{9,7},{10,... | collective-permute-start | bytes 1081352 | tf_op jit(solution)/shard_map/ppermute | solution.py:568
  84.5 8.9 %collective-permute-start.8 = (bf16[64,2816]{1,0:T(8,128)(2,1)S(1)}, bf16[64,2816]{1,0:T(8,128)(2,1)S(1)}, u32[]{:S(2)}, u32[]{:S(2)}) collective-permute-start(bf16[64,2816]{1,0:T(8,128)(2,1)S(1)} %get-tuple-element.55.refs_0_), channel_id=1, source_target_pairs={{0,2},{1,3},{2,4},{3,5},{4,6},{5,7},{6,8},{7,9},{8,10},{9,11},{10,... | collective-permute-start | bytes 1081352 | tf_op jit(solution)/shard_map/ppermute | solution.py:568
  94.1 8.0 %collective-permute-start.10 = (bf16[64,2048]{1,0:T(8,128)(2,1)S(1)}, bf16[64,2048]{1,0:T(8,128)(2,1)S(1)}, u32[]{:S(2)}, u32[]{:S(2)}) collective-permute-start(bf16[64,2048]{1,0:T(8,128)(2,1)S(1)} %get-tuple-element.59.refs_0_), channel_id=1, source_target_pairs={{0,1},{1,0},{2,3},{3,2},{4,5},{5,4},{6,7},{7,6},{8,9},{9,8},{10,11... | collective-permute-start | bytes 786440 | tf_op jit(solution)/shard_map/ppermute | solution.py:571
  103.5 6.6 %collective-permute-start.11 = (bf16[32,2048]{1,0:T(8,128)(2,1)S(1)}, bf16[32,2048]{1,0:T(8,128)(2,1)S(1)}, u32[]{:S(2)}, u32[]{:S(2)}) collective-permute-start(bf16[32,2048]{1,0:T(8,128)(2,1)S(1)} %residual_images.1.refs_0_), channel_id=1, source_target_pairs={{0,1},{1,0},{2,3},{3,2},{4,5},{5,4},{6,7},{7,6},{8,9},{9,8},{10,11... | collective-permute-start | bytes 393224 | tf_op jit(solution)/shard_map/ppermute | solution.py:571
  105.9 7.4 %collective-permute-start.14 = (bf16[32,2048]{1,0:T(8,128)(2,1)S(1)}, bf16[32,2048]{1,0:T(8,128)(2,1)S(1)}, u32[]{:S(2)}, u32[]{:S(2)}) collective-permute-start(bf16[32,2048]{1,0:T(8,128)(2,1)S(1)} %residual_images.1.refs_0_), channel_id=1, source_target_pairs={{0,2},{1,3},{2,4},{3,5},{4,6},{5,7},{6,8},{7,9},{8,10},{9,11},{10,... | collective-permute-start | bytes 393224 | tf_op jit(solution)/shard_map/ppermute | solution.py:568
  106.1 7.2 %collective-permute-start.12 = (bf16[32,2048]{1,0:T(8,128)(2,1)S(1)}, bf16[32,2048]{1,0:T(8,128)(2,1)S(1)}, u32[]{:S(2)}, u32[]{:S(2)}) collective-permute-start(bf16[32,2048]{1,0:T(8,128)(2,1)S(1)} %residual_images.1.refs_0_), channel_id=1, source_target_pairs={{0,14},{1,15},{2,0},{3,1},{4,2},{5,3},{6,4},{7,5},{8,6},{9,7},{10,... | collective-permute-start | bytes 393224 | tf_op jit(solution)/shard_map/ppermute | solution.py:568
  110.0 7.6 %collective-permute-start.15 = (bf16[32,2048]{1,0:T(8,128)(2,1)S(1)}, bf16[32,2048]{1,0:T(8,128)(2,1)S(1)}, u32[]{:S(2)}, u32[]{:S(2)}) collective-permute-start(bf16[32,2048]{1,0:T(8,128)(2,1)S(1)} %collective-permute-done.11.refs_1_), channel_id=1, source_target_pairs={{0,2},{1,3},{2,4},{3,5},{4,6},{5,7},{6,8},{7,9},{8,10},{9,11},{10,... | collective-permute-start | bytes 393224 | tf_op jit(solution)/shard_map/ppermute | solution.py:568
  110.3 7.3 %collective-permute-start.13 = (bf16[32,2048]{1,0:T(8,128)(2,1)S(1)}, bf16[32,2048]{1,0:T(8,128)(2,1)S(1)}, u32[]{:S(2)}, u32[]{:S(2)}) collective-permute-start(bf16[32,2048]{1,0:T(8,128)(2,1)S(1)} %collective-permute-done.11.refs_1_), channel_id=1, source_target_pairs={{0,14},{1,15},{2,0},{3,1},{4,2},{5,3},{6,4},{7,5},{8,6},{9,7},{10,... | collective-permute-start | bytes 393224 | tf_op jit(solution)/shard_map/ppermute | solution.py:568
  113.3 9.1 %collective-permute-start.18 = (bf16[32,2048]{1,0:T(8,128)(2,1)S(1)}, bf16[32,2048]{1,0:T(8,128)(2,1)S(1)}, u32[]{:S(2)}, u32[]{:S(2)}) collective-permute-start(bf16[32,2048]{1,0:T(8,128)(2,1)S(1)} %collective-permute-done.14.refs_4_), channel_id=1, source_target_pairs={{0,2},{1,3},{2,4},{3,5},{4,6},{5,7},{6,8},{7,9},{8,10},{9,11},{10,... | collective-permute-start | bytes 393224 | tf_op jit(solution)/shard_map/ppermute | solution.py:568
  113.3 10.3 %collective-permute-start.16 = (bf16[32,2048]{1,0:T(8,128)(2,1)S(1)}, bf16[32,2048]{1,0:T(8,128)(2,1)S(1)}, u32[]{:S(2)}, u32[]{:S(2)}) collective-permute-start(bf16[32,2048]{1,0:T(8,128)(2,1)S(1)} %collective-permute-done.12.refs_2_), channel_id=1, source_target_pairs={{0,14},{1,15},{2,0},{3,1},{4,2},{5,3},{6,4},{7,5},{8,6},{9,7},{10,... | collective-permute-start | bytes 393224 | tf_op jit(solution)/shard_map/ppermute | solution.py:568
  117.6 8.0 %collective-permute-start.19 = (bf16[32,2048]{1,0:T(8,128)(2,1)S(1)}, bf16[32,2048]{1,0:T(8,128)(2,1)S(1)}, u32[]{:S(2)}, u32[]{:S(2)}) collective-permute-start(bf16[32,2048]{1,0:T(8,128)(2,1)S(1)} %collective-permute-done.15.refs_5_), channel_id=1, source_target_pairs={{0,2},{1,3},{2,4},{3,5},{4,6},{5,7},{6,8},{7,9},{8,10},{9,11},{10,... | collective-permute-start | bytes 393224 | tf_op jit(solution)/shard_map/ppermute | solution.py:568
  117.6 9.7 %collective-permute-start.17 = (bf16[32,2048]{1,0:T(8,128)(2,1)S(1)}, bf16[32,2048]{1,0:T(8,128)(2,1)S(1)}, u32[]{:S(2)}, u32[]{:S(2)}) collective-permute-start(bf16[32,2048]{1,0:T(8,128)(2,1)S(1)} %collective-permute-done.13.refs_3_), channel_id=1, source_target_pairs={{0,14},{1,15},{2,0},{3,1},{4,2},{5,3},{6,4},{7,5},{8,6},{9,7},{10,... | collective-permute-start | bytes 393224 | tf_op jit(solution)/shard_map/ppermute | solution.py:568
  122.3 7.2 %collective-permute-start.24 = (bf16[32,2048]{1,0:T(8,128)(2,1)S(1)}, bf16[32,2048]{1,0:T(8,128)(2,1)S(1)}, u32[]{:S(2)}, u32[]{:S(2)}) collective-permute-start(bf16[32,2048]{1,0:T(8,128)(2,1)S(1)} %collective-permute-done.18.refs_8_), channel_id=1, source_target_pairs={{0,4},{1,5},{2,6},{3,7},{4,8},{5,9},{6,10},{7,11},{8,12},{9,13},{1... | collective-permute-start | bytes 393224 | tf_op jit(solution)/shard_map/ppermute | solution.py:568
  122.3 8.2 %collective-permute-start.22 = (bf16[32,2048]{1,0:T(8,128)(2,1)S(1)}, bf16[32,2048]{1,0:T(8,128)(2,1)S(1)}, u32[]{:S(2)}, u32[]{:S(2)}) collective-permute-start(bf16[32,2048]{1,0:T(8,128)(2,1)S(1)} %collective-permute-done.18.refs_8_), channel_id=1, source_target_pairs={{0,2},{1,3},{2,4},{3,5},{4,6},{5,7},{6,8},{7,9},{8,10},{9,11},{10,... | collective-permute-start | bytes 393224 | tf_op jit(solution)/shard_map/ppermute | solution.py:568
  123.6 7.0 %collective-permute-start.20 = (bf16[32,2048]{1,0:T(8,128)(2,1)S(1)}, bf16[32,2048]{1,0:T(8,128)(2,1)S(1)}, u32[]{:S(2)}, u32[]{:S(2)}) collective-permute-start(bf16[32,2048]{1,0:T(8,128)(2,1)S(1)} %collective-permute-done.16.refs_6_), channel_id=1, source_target_pairs={{0,14},{1,15},{2,0},{3,1},{4,2},{5,3},{6,4},{7,5},{8,6},{9,7},{10,... | collective-permute-start | bytes 393224 | tf_op jit(solution)/shard_map/ppermute | solution.py:568
  125.6 6.2 %collective-permute-start.23 = (bf16[32,2048]{1,0:T(8,128)(2,1)S(1)}, bf16[32,2048]{1,0:T(8,128)(2,1)S(1)}, u32[]{:S(2)}, u32[]{:S(2)}) collective-permute-start(bf16[32,2048]{1,0:T(8,128)(2,1)S(1)} %collective-permute-done.19.refs_9_), channel_id=1, source_target_pairs={{0,2},{1,3},{2,4},{3,5},{4,6},{5,7},{6,8},{7,9},{8,10},{9,11},{10,... | collective-permute-start | bytes 393224 | tf_op jit(solution)/shard_map/ppermute | solution.py:568
  127.4 6.0 %collective-permute-start.25 = (bf16[32,2048]{1,0:T(8,128)(2,1)S(1)}, bf16[32,2048]{1,0:T(8,128)(2,1)S(1)}, u32[]{:S(2)}, u32[]{:S(2)}) collective-permute-start(bf16[32,2048]{1,0:T(8,128)(2,1)S(1)} %collective-permute-done.17.refs_7_), channel_id=1, source_target_pairs={{0,12},{1,13},{2,14},{3,15},{4,0},{5,1},{6,2},{7,3},{8,4},{9,5},{1... | collective-permute-start | bytes 393224 | tf_op jit(solution)/shard_map/ppermute | solution.py:568
  129.5 6.6 %collective-permute-start.21 = (bf16[32,2048]{1,0:T(8,128)(2,1)S(1)}, bf16[32,2048]{1,0:T(8,128)(2,1)S(1)}, u32[]{:S(2)}, u32[]{:S(2)}) collective-permute-start(bf16[32,2048]{1,0:T(8,128)(2,1)S(1)} %collective-permute-done.17.refs_7_), channel_id=1, source_target_pairs={{0,14},{1,15},{2,0},{3,1},{4,2},{5,3},{6,4},{7,5},{8,6},{9,7},{10,... | collective-permute-start | bytes 393224 | tf_op jit(solution)/shard_map/ppermute | solution.py:568

commit v8 on v6

--- a/solution.py
+++ b/solution.py
@@ -24,6 +24,7 @@
 
 XT = 256
 WIDE = 512
+TALL = 1024
 F32 = jnp.float32
 BF16 = jnp.bfloat16
 VMEM = pl.BlockSpec(memory_space=pltpu.VMEM)
@@ -90,7 +91,7 @@
     return [
         pltpu.make_async_copy(
             ref.at[:, pl.ds(pl.multiple_of(source, 16), size)],
-            buffer_ref.at[slot, :, pl.ds(target, size)],
+            buffer_ref.at[slot, pl.ds(0, ref.shape[0]), pl.ds(target, size)],
             sem_ref.at[slot, part],
         )
         for part, (source, target, size) in enumerate(parts)
@@ -114,7 +115,7 @@
 
 def stream_scratch(depth, strip, edge=0, tile=XT):
     return [
-        pltpu.VMEM((2, depth, tile + 2 * edge, strip), BF16),
+        pltpu.VMEM((2, depth + (1 if edge else 0), tile + 2 * edge, strip), BF16),
         pltpu.SemaphoreType.DMA((2, 3 if edge else 1)),
     ]
 
@@ -175,7 +176,7 @@
     outs, (ends_ref, spread_ref, buffer_ref, sem_ref, last_ref, first_ref) = refs[:-6], refs[-6:]
     extent = volume_ref.shape[1]
     me = place_ref[1]
-    start(tile_copies(volume_ref, buffer_ref, sem_ref, 0))
+    start(tile_copies(volume_ref, buffer_ref, sem_ref, 0, tile=TALL))
     fill_spread(tiles, me, got_ref, spread_ref)
     where = [(ref, row) for ref in outs for row in range(0, ref.shape[0], RUN)]
     beyond = pl.ds(extent, BAND)
@@ -184,24 +185,26 @@
         for turn, source in enumerate((tile, tile ^ 1)):
             ref, row = where[2 * index + turn]
             ref[row : row + RUN, beyond] = measured_rows(got_ref, source)
-    steps = extent // XT
+    steps = extent // TALL
 
     def body(step, carry):
-        block_ref = streamed(volume_ref, buffer_ref, sem_ref, step, steps)
+        block_ref = streamed(volume_ref, buffer_ref, sem_ref, step, steps, tile=TALL)
         out = lax.dot_general(
             spread_ref[...],
             joined(block_ref),
             (((1,), (1,)), ((), ())),
             preferred_element_type=F32,
         ).astype(BF16)
-        here = pl.ds(pl.multiple_of(step * XT, XT), XT)
+        here = pl.ds(pl.multiple_of(step * TALL, TALL), TALL)
         for index, (ref, row) in enumerate(where):
             ref[row : row + RUN, here] = out[index * RUN : (index + 1) * RUN]
         ends_ref[:, here] = out[-LINES:]
         ends = out[-LINES:].astype(F32)
-        there = pl.ds(pl.multiple_of(step * 8, 8), 8)
-        first_ref[there] = ends[:8]
-        last_ref[there] = ends[8:]
+        count = TALL // XT
+        for part in range(count):
+            there = pl.ds(pl.multiple_of((step * count + part) * 8, 8), 8)
+            first_ref[there] = ends[:8, part * XT : (part + 1) * XT]
+            last_ref[there] = ends[8:, part * XT : (part + 1) * XT]
         return carry
 
     lax.fori_loop(0, steps, body, 0)
@@ -225,9 +228,9 @@
         in_specs=[SMEM, VMEM, HBM] + [ANY] * len(order),
         out_specs=[VMEM] * (len(rows) + 1),
         scratch_shapes=[pltpu.VMEM((slots * depth + LINES, depth * strip), BF16)]
-        + stream_scratch(depth, strip)
+        + stream_scratch(depth, strip, tile=TALL)
         + [pltpu.VMEM((extent // XT * 8, XT), F32)] * 2,
-        compiler_params=limit(10),
+        compiler_params=limit(16),
         cost_estimate=cost(2 * slots * depth * volume.size, 3 * volume.size),
         name="forward",
     )(place, got, volume, *order)
@@ -410,32 +413,29 @@
         start(tile_copies(volume_ref, buffer_ref, sem_ref, 0, first_tile, EDGE))
 
     block_ref = streamed(volume_ref, buffer_ref, sem_ref, step, steps, first_tile, EDGE)
-    depth, strip, tile = block_ref.shape[0], block_ref.shape[2], XT
+    depth, strip, tile = volume_ref.shape[0], volume_ref.shape[2], XT
     at = pl.program_id(0) + first_tile
     beta = beta_ref[0]
-    has_below = (place_ref[0] > 0).astype(F32)
-    has_above = (place_ref[0] < place_ref[3] - 1).astype(F32)
-    has_before = (at > 0).astype(F32)
-    has_after = (at < count - 1).astype(F32)
+    has_below, has_above = place_ref[0] > 0, place_ref[0] < place_ref[3] - 1
     here = pl.ds(EDGE, tile)
-    under_ref[...] = (
-        penalty(block_ref[0, here].astype(F32) - below_ref[0].astype(F32)) * has_below
-    )
+    bottom, top = block_ref[0, here], block_ref[depth - 1, here]
+    below = jnp.where(has_below, below_ref[0], bottom).astype(F32)
+    block_ref[depth, here] = jnp.where(has_above, above_ref[0], top)
+    under_ref[...] = penalty(bottom.astype(F32) - below)
     row = iota((tile, strip), 0)
     lane = iota((tile, strip), 1)
 
     def body(z, carry):
         center = block_ref[z, here].astype(F32)
-        top = z == depth - 1
-        upper = jnp.where(top, above_ref[0], block_ref[jnp.minimum(z + 1, depth - 1), here])
-        over = penalty(upper.astype(F32) - center) * jnp.where(top, has_above, 1.0)
+        over = penalty(block_ref[z + 1, here].astype(F32) - center)
         total = under_ref[...] - over
         under_ref[...] = over
-        ahead = block_ref[z, pl.ds(EDGE + tile, EDGE)].astype(F32)[0:1]
-        behind = block_ref[z, pl.ds(0, EDGE)].astype(F32)[EDGE - 1 :]
-        behind = penalty(center[0:1] - behind) * has_before
+        behind = block_ref[z, pl.ds(0, EDGE)].astype(F32)
+        behind = jnp.where(at > 0, behind[EDGE - 1 :], behind[:1])
+        ahead = block_ref[z, pl.ds(EDGE + tile, EDGE)].astype(F32)
+        ahead = jnp.where(at < count - 1, ahead[:1], ahead[EDGE - 1 :])
         along = penalty(jnp.where(row == tile - 1, ahead, pltpu.roll(center, tile - 1, 0)) - center)
-        along = jnp.where(row == tile - 1, along * has_after, along)
+        behind = penalty(center[:1] - behind)
         total = total + jnp.where(row == 0, behind, pltpu.roll(along, 1, 0)) - along
         across = penalty(pltpu.roll(center, strip - 1, 1) - center)
         across = jnp.where(lane == strip - 1, 0.0, across)

time: 116 us -> 113 us (0.974)
  Pallas kernels: 40.5 us -> 37.4 us
    pallas_call x1, Pallas kernels: 7.28 us -> 4.8 us  [forward(): pl.pallas_call(kernel, out_shape=[jax.ShapeDtypeStruct(shape, BF16) for s...]
  transfers between devices with their start and end apart: 27 -> 27, of which waited for: 16 -> 16; matrix products, arithmetic and copies ran while one was open for 1% -> 1% of each run, Pallas kernels for 26% -> 24%
where the time goes in v8:
time: 113 us
  starting transfers between devices  49.3 us (44%)
  Pallas kernels  37.4 us (33%)
  waiting for transfers between devices  23.7 us (21%)
  local copies, waits for them, and re-layouts  1.27 us (1%)
    ppermute x22, starting transfers between devices, along_z(): lax.ppermute(block, 'tile', [(i, (i + 2 * by) % tiles) for i in range(til...  34.3 us
    ppermute x22, waiting for transfers between devices, along_z(): lax.ppermute(block, 'tile', [(i, (i + 2 * by) % tiles) for i in range(til...  21.6 us
    pallas_call x4, Pallas kernels, regularizer(): pl.pallas_call(functools.partial(regularizer_kernel, origin, count), grid...  21.1 us
    pallas_call x1, Pallas kernels, gradient(): pl.pallas_call(gradient_kernel, out_shape=jax.ShapeDtypeStruct(regular.sh...  6.63 us
    all_to_all x1, starting transfers between devices, shards(): lax.all_to_all(packed, 'slab', split_axis=0, concat_axis=0, tiled=True)  5.77 us
    ppermute x2, starting transfers between devices, along_y(): return lax.ppermute(block, 'tile', [(i, i ^ 1) for i in range(tiles)])  4.89 us
    pallas_call x1, Pallas kernels, forward(): pl.pallas_call(kernel, out_shape=[jax.ShapeDtypeStruct(shape, BF16) for s...  4.8 us
    ppermute x1, starting transfers between devices, shards(): below = lax.ppermute(top, 'slab', [(i, i + 1) for i in range(slabs - 1)])  2.3 us
  transfers between devices with their start and end apart: 27, of which 16 were waited for; matrix products, arithmetic and copies ran while one was open for 1% of the time, Pallas kernels for 24%

profile of v8, /device:TPU:8, one launch (start us, length us, event | category | flops | bytes accessed | tf_op | source)
XLA Modules:
  0.0 112.8 jit_solution(12396498201002222944)
XLA Ops:
  0.0 1.7 %pack_messages.1 = bf16[16,4,16,128]{3,2,1,0:T(8,128)(2,1)} custom-call(s32[2,12]{1,0:T(2,128)} %bitcast.9, s32[2,12]{1,0:T(2,128)} %offset_ref.1, s32[2,12]{1,0:T(2,128)} %width_ref.1, bf16[12,2,128]{2,1,0:T(2,128)(2,1)} %bitcast.8, bf16[2,12,8,128]{3,2,1,0:T(8,128)(2,1)} %measured_ref.1), custom_call_target="tpu_custom_call" | custom-call | tf_op jit(solution)/shard_map/pack_messages/pallas_call | solution.py:69
  1.7 5.8 %all-to-all-start = ((bf16[16,4,16,128]{3,2,1,0:T(8,128)(2,1)}), bf16[16,4,16,128]{3,2,1,0:T(8,128)(2,1)S(1)}, u32[]{:S(2)}, u32[]{:S(2)}) async-start(bf16[16,4,16,128]{3,2,1,0:T(8,128)(2,1)} %pack_messages.1), calls=%async_computation | async-start | bytes 524288 | tf_op jit(solution)/shard_map/all_to_all | solution.py:551
  8.7 2.0 %collective-permute-start.5 = (bf16[1,2048,128]{2,1,0:T(8,128)(2,1)S(1)}, bf16[1,2048,128]{2,1,0:T(8,128)(2,1)S(1)}, u32[]{:S(2)}, u32[]{:S(2)}) collective-permute-start(bf16[1,2048,128]{2,1,0:T(8,128)(2,1)S(1)} %get-tuple-element.63.refs_1_), channel_id=1, source_target_pairs={{16,0},{32,16},{48,32},{64,48},{80,64},{96,80},{112,96},{128,112},... | collective-permute-start | bytes 1572872 | tf_op jit(solution)/shard_map/ppermute | solution.py:554
  10.8 2.3 %collective-permute-start.4 = (bf16[1,2048,128]{2,1,0:T(8,128)(2,1)S(1)}, bf16[1,2048,128]{2,1,0:T(8,128)(2,1)S(1)}, u32[]{:S(2)}, u32[]{:S(2)}) collective-permute-start(bf16[1,2048,128]{2,1,0:T(8,128)(2,1)S(1)} %get-tuple-element.64.refs_0_), channel_id=1, source_target_pairs={{0,16},{16,32},{32,48},{48,64},{64,80},{80,96},{96,112},{112,128},... | collective-permute-start | bytes 1572872 | tf_op jit(solution)/shard_map/ppermute | solution.py:553
  14.0 4.8 %forward.1 = (bf16[64,2176]{1,0:T(8,128)(2,1)S(1)}, bf16[64,2432]{1,0:T(8,128)(2,1)S(1)}, bf16[64,2432]{1,0:T(8,128)(2,1)S(1)}, bf16[64,2176]{1,0:T(8,128)(2,1)S...) custom-call(s32[4]{0:T(128)S(1)} %pad_add_fusion.place_ref, ...), custom_call_target="tpu_custom_call" | custom-call | flops 2147483648 | bytes 6291456 | tf_op jit(solution)/shard_map/forward/pallas_call | solution.py:224
  18.8 2.0 %collective-permute-start = (bf16[32,2176]{1,0:T(8,128)(2,1)S(1)}, bf16[32,2176]{1,0:T(8,128)(2,1)S(1)}, u32[]{:S(2)}, u32[]{:S(2)}) collective-permute-start(bf16[32,2176]{1,0:T(8,128)(2,1)S(1)} %get-tuple-element.38), channel_id=1, source_target_pairs={{0,2},{1,3},{2,4},{3,5},{4,6},{5,7},{6,8},{7,9},{8,10},{9,11},{10,... | collective-permute-start | bytes 417800 | tf_op jit(solution)/shard_map/ppermute | solution.py:544
  20.8 4.0 %collective-permute-start.1 = (bf16[32,2176]{1,0:T(8,128)(2,1)S(1)}, bf16[32,2176]{1,0:T(8,128)(2,1)S(1)}, u32[]{:S(2)}, u32[]{:S(2)}) collective-permute-start(bf16[32,2176]{1,0:T(8,128)(2,1)S(1)} %get-tuple-element.40), channel_id=1, source_target_pairs={{0,14},{1,15},{2,0},{3,1},{4,2},{5,3},{6,4},{7,5},{8,6},{9,7},{10,... | collective-permute-start | bytes 417800 | tf_op jit(solution)/shard_map/ppermute | solution.py:544
  25.5 2.9 %collective-permute-done.from_below_ref = bf16[32,2176]{1,0:T(8,128)(2,1)S(1)} collective-permute-done((bf16[32,2176]{1,0:T(8,128)(2,1)S(1)}, bf16[32,2176]{1,0:T(8,128)(2,1)S(1)}, u32[]{:S(2)}, u32[]{:S(2)}) %collective-permute-start) | collective-permute-done | bytes 139296 | tf_op jit(solution)/shard_map/ppermute | solution.py:544
  28.5 3.7 %collective-permute-start.3 = (bf16[64,2304]{1,0:T(8,128)(2,1)S(1)}, bf16[64,2304]{1,0:T(8,128)(2,1)S(1)}, u32[]{:S(2)}, u32[]{:S(2)}) collective-permute-start(bf16[64,2304]{1,0:T(8,128)(2,1)S(1)} %get-tuple-element.44), channel_id=1, source_target_pairs={{0,14},{1,15},{2,0},{3,1},{4,2},{5,3},{6,4},{7,5},{8,6},{9,7},{10,... | collective-permute-start | bytes 884744 | tf_op jit(solution)/shard_map/ppermute | solution.py:544
  32.9 5.3 %regularizer.4 = (bf16[8,2048,128]{2,1,0:T(8,128)(2,1)}, f32[8,128]{1,0:T(8,128)S(1)}) custom-call(s32[4]{0:T(128)S(1)} %pad_add_fusion.place_ref, f32[1]{0:T(128)S(6)} %copy.14.beta_ref, bf16[8,2048,128]{2,1,0:T(8,128)(2,1)} %volume_ref.9, bf16[1,2048,128]{2,1,0:T(8,128)(2,1)S(1)} %collective-permute-done.4.below_ref, ...), custom_call_target="tpu_custom_call" | custom-call | flops 15728640 | bytes 4194304 | tf_op jit(solution)/shard_map/regularizer/pallas_call | solution.py:460
  39.0 3.4 %collective-permute-done.2.from_below_ref = bf16[64,2304]{1,0:T(8,128)(2,1)S(1)} collective-permute-done((bf16[64,2304]{1,0:T(8,128)(2,1)S(1)}, bf16[64,2304]{1,0:T(8,128)(2,1)S(1)}, u32[]{:S(2)}, u32[]{:S(2)}) %collective-permute-start.2) | collective-permute-done | bytes 294944 | tf_op jit(solution)/shard_map/ppermute | solution.py:544
  42.9 1.7 %collective-permute-start.6 = (bf16[64,2432]{1,0:T(8,128)(2,1)S(1)}, bf16[64,2432]{1,0:T(8,128)(2,1)S(1)}, u32[]{:S(2)}, u32[]{:S(2)}) collective-permute-start(bf16[64,2432]{1,0:T(8,128)(2,1)S(1)} %get-tuple-element.47.refs_0_), channel_id=1, source_target_pairs={{0,2},{1,3},{2,4},{3,5},{4,6},{5,7},{6,8},{7,9},{8,10},{9,11},{10,... | collective-permute-start | bytes 933896 | tf_op jit(solution)/shard_map/ppermute | solution.py:544
  44.6 5.3 %regularizer.5 = (bf16[8,2048,128]{2,1,0:T(8,128)(2,1)}, f32[8,128]{1,0:T(8,128)S(1)}) custom-call(s32[4]{0:T(128)S(1)} %pad_add_fusion.place_ref, f32[1]{0:T(128)S(6)} %copy.14.beta_ref, bf16[8,2048,128]{2,1,0:T(8,128)(2,1)} %volume_ref.9, bf16[1,2048,128]{2,1,0:T(8,128)(2,1)S(1)} %collective-permute-done.4.below_ref, ...), custom_call_target="tpu_custom_call", output_to_operand_aliasing={{0}: (6, {})} | custom-call | flops 15728640 | bytes 4194304 | tf_op jit(solution)/shard_map/regularizer/pallas_call | solution.py:460
  51.0 1.5 %collective-permute-done.6.from_below_ref = bf16[64,2432]{1,0:T(8,128)(2,1)S(1)} collective-permute-done((bf16[64,2432]{1,0:T(8,128)(2,1)S(1)}, bf16[64,2432]{1,0:T(8,128)(2,1)S(1)}, u32[]{:S(2)}, u32[]{:S(2)}) %collective-permute-start.6) | collective-permute-done | bytes 311328 | tf_op jit(solution)/shard_map/ppermute | solution.py:544
  53.0 1.7 %collective-permute-start.8 = (bf16[64,2816]{1,0:T(8,128)(2,1)S(1)}, bf16[64,2816]{1,0:T(8,128)(2,1)S(1)}, u32[]{:S(2)}, u32[]{:S(2)}) collective-permute-start(bf16[64,2816]{1,0:T(8,128)(2,1)S(1)} %get-tuple-element.53.refs_0_), channel_id=1, source_target_pairs={{0,2},{1,3},{2,4},{3,5},{4,6},{5,7},{6,8},{7,9},{8,10},{9,11},{10,... | collective-permute-start | bytes 1081352 | tf_op jit(solution)/shard_map/ppermute | solution.py:544
  54.8 5.3 %regularizer.6 = (bf16[8,2048,128]{2,1,0:T(8,128)(2,1)}, f32[8,128]{1,0:T(8,128)S(1)}) custom-call(s32[4]{0:T(128)S(1)} %pad_add_fusion.place_ref, f32[1]{0:T(128)S(6)} %copy.14.beta_ref, bf16[8,2048,128]{2,1,0:T(8,128)(2,1)} %volume_ref.9, bf16[1,2048,128]{2,1,0:T(8,128)(2,1)S(1)} %collective-permute-done.4.below_ref, ...), custom_call_target="tpu_custom_call", output_to_operand_aliasing={{0}: (6, {})} | custom-call | flops 15728640 | bytes 4194304 | tf_op jit(solution)/shard_map/regularizer/pallas_call | solution.py:460
  61.3 1.5 %collective-permute-done.8.below_ref = bf16[64,2816]{1,0:T(8,128)(2,1)S(1)} collective-permute-done((bf16[64,2816]{1,0:T(8,128)(2,1)S(1)}, bf16[64,2816]{1,0:T(8,128)(2,1)S(1)}, u32[]{:S(2)}, u32[]{:S(2)}) %collective-permute-start.8) | collective-permute-done | bytes 360480 | tf_op jit(solution)/shard_map/ppermute | solution.py:544
  63.5 2.4 %collective-permute-start.10 = (bf16[64,2048]{1,0:T(8,128)(2,1)S(1)}, bf16[64,2048]{1,0:T(8,128)(2,1)S(1)}, u32[]{:S(2)}, u32[]{:S(2)}) collective-permute-start(bf16[64,2048]{1,0:T(8,128)(2,1)S(1)} %get-tuple-element.57.refs_0_), channel_id=1, source_target_pairs={{0,1},{1,0},{2,3},{3,2},{4,5},{5,4},{6,7},{7,6},{8,9},{9,8},{10,11... | collective-permute-start | bytes 786440 | tf_op jit(solution)/shard_map/ppermute | solution.py:547
  65.8 5.3 %regularizer.7 = (bf16[8,2048,128]{2,1,0:T(8,128)(2,1)}, f32[8,128]{1,0:T(8,128)S(1)}) custom-call(s32[4]{0:T(128)S(1)} %pad_add_fusion.place_ref, f32[1]{0:T(128)S(6)} %copy.14.beta_ref, bf16[8,2048,128]{2,1,0:T(8,128)(2,1)} %volume_ref.9, bf16[1,2048,128]{2,1,0:T(8,128)(2,1)S(1)} %collective-permute-done.4.below_ref, ...), custom_call_target="tpu_custom_call", output_to_operand_aliasing={{0}: (6, {})} | custom-call | flops 15728640 | bytes 4194304 | tf_op jit(solution)/shard_map/regularizer/pallas_call | solution.py:460
  71.5 1.4 %residual_images.1.refs_0_ = bf16[32,2048]{1,0:T(8,128)(2,1)S(1)} custom-call(s32[4]{0:T(128)S(1)} %pad_add_fusion.place_ref, f32[32,2048]{1,0:T(8,128)S(1)} %get-tuple-element.58.kept_ref, bf16[32,1024]{1,0:T(8,128)(2,1)S(1)} %get-tuple-element.59.strips_ref, bf16[64,2048]{1,0:T(8,128)(2,1)S(1)} %collective-permute-done.10.arrived_ref.beside_ref, ...), custom_call_target="tpu_custom_call" | custom-call | flops 100663296 | bytes 786432 | tf_op jit(solution)/shard_map/residual_images/pallas_call | solution.py:382
  72.9 2.5 %collective-permute-start.11 = (bf16[32,2048]{1,0:T(8,128)(2,1)S(1)}, bf16[32,2048]{1,0:T(8,128)(2,1)S(1)}, u32[]{:S(2)}, u32[]{:S(2)}) collective-permute-start(bf16[32,2048]{1,0:T(8,128)(2,1)S(1)} %residual_images.1.refs_0_), channel_id=1, source_target_pairs={{0,1},{1,0},{2,3},{3,2},{4,5},{5,4},{6,7},{7,6},{8,9},{9,8},{10,11... | collective-permute-start | bytes 393224 | tf_op jit(solution)/shard_map/ppermute | solution.py:547
  75.7 3.0 %collective-permute-start.12 = (bf16[32,2048]{1,0:T(8,128)(2,1)S(1)}, bf16[32,2048]{1,0:T(8,128)(2,1)S(1)}, u32[]{:S(2)}, u32[]{:S(2)}) collective-permute-start(bf16[32,2048]{1,0:T(8,128)(2,1)S(1)} %residual_images.1.refs_0_), channel_id=1, source_target_pairs={{0,14},{1,15},{2,0},{3,1},{4,2},{5,3},{6,4},{7,5},{8,6},{9,7},{10,... | collective-permute-start | bytes 393224 | tf_op jit(solution)/shard_map/ppermute | solution.py:544
  79.9 3.0 %collective-permute-start.13 = (bf16[32,2048]{1,0:T(8,128)(2,1)S(1)}, bf16[32,2048]{1,0:T(8,128)(2,1)S(1)}, u32[]{:S(2)}, u32[]{:S(2)}) collective-permute-start(bf16[32,2048]{1,0:T(8,128)(2,1)S(1)} %collective-permute-done.11.refs_1_), channel_id=1, source_target_pairs={{0,14},{1,15},{2,0},{3,1},{4,2},{5,3},{6,4},{7,5},{8,6},{9,7},{10,... | collective-permute-start | bytes 393224 | tf_op jit(solution)/shard_map/ppermute | solution.py:544
  82.9 3.2 %collective-permute-start.16 = (bf16[32,2048]{1,0:T(8,128)(2,1)S(1)}, bf16[32,2048]{1,0:T(8,128)(2,1)S(1)}, u32[]{:S(2)}, u32[]{:S(2)}) collective-permute-start(bf16[32,2048]{1,0:T(8,128)(2,1)S(1)} %collective-permute-done.12.refs_2_), channel_id=1, source_target_pairs={{0,14},{1,15},{2,0},{3,1},{4,2},{5,3},{6,4},{7,5},{8,6},{9,7},{10,... | collective-permute-start | bytes 393224 | tf_op jit(solution)/shard_map/ppermute | solution.py:544
  87.1 3.4 %collective-permute-start.17 = (bf16[32,2048]{1,0:T(8,128)(2,1)S(1)}, bf16[32,2048]{1,0:T(8,128)(2,1)S(1)}, u32[]{:S(2)}, u32[]{:S(2)}) collective-permute-start(bf16[32,2048]{1,0:T(8,128)(2,1)S(1)} %collective-permute-done.13.refs_3_), channel_id=1, source_target_pairs={{0,14},{1,15},{2,0},{3,1},{4,2},{5,3},{6,4},{7,5},{8,6},{9,7},{10,... | collective-permute-start | bytes 393224 | tf_op jit(solution)/shard_map/ppermute | solution.py:544
  90.5 1.5 %collective-permute-done.18.refs_8_ = bf16[32,2048]{1,0:T(8,128)(2,1)S(1)} collective-permute-done((bf16[32,2048]{1,0:T(8,128)(2,1)S(1)}, bf16[32,2048]{1,0:T(8,128)(2,1)S(1)}, u32[]{:S(2)}, u32[]{:S(2)}) %collective-permute-start.18) | collective-permute-done | bytes 131104 | tf_op jit(solution)/shard_map/ppermute | solution.py:544
  91.9 1.6 %collective-permute-start.22 = (bf16[32,2048]{1,0:T(8,128)(2,1)S(1)}, bf16[32,2048]{1,0:T(8,128)(2,1)S(1)}, u32[]{:S(2)}, u32[]{:S(2)}) collective-permute-start(bf16[32,2048]{1,0:T(8,128)(2,1)S(1)} %collective-permute-done.18.refs_8_), channel_id=1, source_target_pairs={{0,2},{1,3},{2,4},{3,5},{4,6},{5,7},{6,8},{7,9},{8,10},{9,11},{10,... | collective-permute-start | bytes 393224 | tf_op jit(solution)/shard_map/ppermute | solution.py:544
  93.5 1.7 %collective-permute-start.20 = (bf16[32,2048]{1,0:T(8,128)(2,1)S(1)}, bf16[32,2048]{1,0:T(8,128)(2,1)S(1)}, u32[]{:S(2)}, u32[]{:S(2)}) collective-permute-start(bf16[32,2048]{1,0:T(8,128)(2,1)S(1)} %collective-permute-done.16.refs_6_), channel_id=1, source_target_pairs={{0,14},{1,15},{2,0},{3,1},{4,2},{5,3},{6,4},{7,5},{8,6},{9,7},{10,... | collective-permute-start | bytes 393224 | tf_op jit(solution)/shard_map/ppermute | solution.py:544
  95.2 2.1 %collective-permute-start.23 = (bf16[32,2048]{1,0:T(8,128)(2,1)S(1)}, bf16[32,2048]{1,0:T(8,128)(2,1)S(1)}, u32[]{:S(2)}, u32[]{:S(2)}) collective-permute-start(bf16[32,2048]{1,0:T(8,128)(2,1)S(1)} %collective-permute-done.19.refs_9_), channel_id=1, source_target_pairs={{0,2},{1,3},{2,4},{3,5},{4,6},{5,7},{6,8},{7,9},{8,10},{9,11},{10,... | collective-permute-start | bytes 393224 | tf_op jit(solution)/shard_map/ppermute | solution.py:544
  101.4 1.9 %collective-permute-done.25.refs_15_ = bf16[32,2048]{1,0:T(8,128)(2,1)S(1)} collective-permute-done((bf16[32,2048]{1,0:T(8,128)(2,1)S(1)}, bf16[32,2048]{1,0:T(8,128)(2,1)S(1)}, u32[]{:S(2)}, u32[]{:S(2)}) %collective-permute-start.25) | collective-permute-done | bytes 131104 | tf_op jit(solution)/shard_map/ppermute | solution.py:544
  103.2 2.8 %collective-permute-done.21.refs_11_ = bf16[32,2048]{1,0:T(8,128)(2,1)S(1)} collective-permute-done((bf16[32,2048]{1,0:T(8,128)(2,1)S(1)}, bf16[32,2048]{1,0:T(8,128)(2,1)S(1)}, u32[]{:S(2)}, u32[]{:S(2)}) %collective-permute-start.21) | collective-permute-done | bytes 131104 | tf_op jit(solution)/shard_map/ppermute | solution.py:544
  106.0 6.6 %gradient.1 = bf16[8,2048,128]{2,1,0:T(8,128)(2,1)} custom-call(s32[4]{0:T(128)S(1)} %pad_add_fusion.place_ref, f32[1]{0:T(128)S(6)} %copy.14.beta_ref, bf16[528,1024]{1,0:T(8,128)(2,1)S(1)} %spread_rows.1.refs_0_.spread_ref, bf16[16,2048]{1,0:T(8,128)(2,1)S(1)} %get-tuple-element.36.order_ref.ends_ref.mine_ref, ...), custom_call_target="tpu_custom_call" | custom-call | flops 2214592512 | bytes 10485760 | tf_op jit(solution)/shard_map/gradient/pallas_call | solution.py:523
  (38 shorter events, 14.5 us)
Async XLA Ops:
  1.7 12.3 %all-to-all-start = ((bf16[16,4,16,128]{3,2,1,0:T(8,128)(2,1)}), bf16[16,4,16,128]{3,2,1,0:T(8,128)(2,1)S(1)}, u32[]{:S(2)}, u32[]{:S(2)}) async-start(bf16[16,4,16,128]{3,2,1,0:T(8,128)(2,1)} %pack_messages.1), calls=%async_computation | async-start | bytes 524288 | tf_op jit(solution)/shard_map/all_to_all | solution.py:551
  8.7 24.2 %collective-permute-start.5 = (bf16[1,2048,128]{2,1,0:T(8,128)(2,1)S(1)}, bf16[1,2048,128]{2,1,0:T(8,128)(2,1)S(1)}, u32[]{:S(2)}, u32[]{:S(2)}) collective-permute-start(bf16[1,2048,128]{2,1,0:T(8,128)(2,1)S(1)} %get-tuple-element.63.refs_1_), channel_id=1, source_target_pairs={{16,0},{32,16},{48,32},{64,48},{80,64},{96,80},{112,96},{128,112},... | collective-permute-start | bytes 1572872 | tf_op jit(solution)/shard_map/ppermute | solution.py:554
  10.8 22.1 %collective-permute-start.4 = (bf16[1,2048,128]{2,1,0:T(8,128)(2,1)S(1)}, bf16[1,2048,128]{2,1,0:T(8,128)(2,1)S(1)}, u32[]{:S(2)}, u32[]{:S(2)}) collective-permute-start(bf16[1,2048,128]{2,1,0:T(8,128)(2,1)S(1)} %get-tuple-element.64.refs_0_), channel_id=1, source_target_pairs={{0,16},{16,32},{32,48},{48,64},{64,80},{80,96},{96,112},{112,128},... | collective-permute-start | bytes 1572872 | tf_op jit(solution)/shard_map/ppermute | solution.py:553
  18.8 9.7 %collective-permute-start = (bf16[32,2176]{1,0:T(8,128)(2,1)S(1)}, bf16[32,2176]{1,0:T(8,128)(2,1)S(1)}, u32[]{:S(2)}, u32[]{:S(2)}) collective-permute-start(bf16[32,2176]{1,0:T(8,128)(2,1)S(1)} %get-tuple-element.38), channel_id=1, source_target_pairs={{0,2},{1,3},{2,4},{3,5},{4,6},{5,7},{6,8},{7,9},{8,10},{9,11},{10,... | collective-permute-start | bytes 417800 | tf_op jit(solution)/shard_map/ppermute | solution.py:544
  20.8 7.7 %collective-permute-start.1 = (bf16[32,2176]{1,0:T(8,128)(2,1)S(1)}, bf16[32,2176]{1,0:T(8,128)(2,1)S(1)}, u32[]{:S(2)}, u32[]{:S(2)}) collective-permute-start(bf16[32,2176]{1,0:T(8,128)(2,1)S(1)} %get-tuple-element.40), channel_id=1, source_target_pairs={{0,14},{1,15},{2,0},{3,1},{4,2},{5,3},{6,4},{7,5},{8,6},{9,7},{10,... | collective-permute-start | bytes 417800 | tf_op jit(solution)/shard_map/ppermute | solution.py:544
  28.5 10.4 %collective-permute-start.3 = (bf16[64,2304]{1,0:T(8,128)(2,1)S(1)}, bf16[64,2304]{1,0:T(8,128)(2,1)S(1)}, u32[]{:S(2)}, u32[]{:S(2)}) collective-permute-start(bf16[64,2304]{1,0:T(8,128)(2,1)S(1)} %get-tuple-element.44), channel_id=1, source_target_pairs={{0,14},{1,15},{2,0},{3,1},{4,2},{5,3},{6,4},{7,5},{8,6},{9,7},{10,... | collective-permute-start | bytes 884744 | tf_op jit(solution)/shard_map/ppermute | solution.py:544
  32.2 10.1 %collective-permute-start.2 = (bf16[64,2304]{1,0:T(8,128)(2,1)S(1)}, bf16[64,2304]{1,0:T(8,128)(2,1)S(1)}, u32[]{:S(2)}, u32[]{:S(2)}) collective-permute-start(bf16[64,2304]{1,0:T(8,128)(2,1)S(1)} %get-tuple-element.42.refs_0_), channel_id=1, source_target_pairs={{0,2},{1,3},{2,4},{3,5},{4,6},{5,7},{6,8},{7,9},{8,10},{9,11},{10,... | collective-permute-start | bytes 884744 | tf_op jit(solution)/shard_map/ppermute | solution.py:544
  42.5 8.5 %collective-permute-start.7 = (bf16[64,2432]{1,0:T(8,128)(2,1)S(1)}, bf16[64,2432]{1,0:T(8,128)(2,1)S(1)}, u32[]{:S(2)}, u32[]{:S(2)}) collective-permute-start(bf16[64,2432]{1,0:T(8,128)(2,1)S(1)} %get-tuple-element.49), channel_id=1, source_target_pairs={{0,14},{1,15},{2,0},{3,1},{4,2},{5,3},{6,4},{7,5},{8,6},{9,7},{10,... | collective-permute-start | bytes 933896 | tf_op jit(solution)/shard_map/ppermute | solution.py:544
  42.9 9.7 %collective-permute-start.6 = (bf16[64,2432]{1,0:T(8,128)(2,1)S(1)}, bf16[64,2432]{1,0:T(8,128)(2,1)S(1)}, u32[]{:S(2)}, u32[]{:S(2)}) collective-permute-start(bf16[64,2432]{1,0:T(8,128)(2,1)S(1)} %get-tuple-element.47.refs_0_), channel_id=1, source_target_pairs={{0,2},{1,3},{2,4},{3,5},{4,6},{5,7},{6,8},{7,9},{8,10},{9,11},{10,... | collective-permute-start | bytes 933896 | tf_op jit(solution)/shard_map/ppermute | solution.py:544
  52.7 8.7 %collective-permute-start.9 = (bf16[64,2816]{1,0:T(8,128)(2,1)S(1)}, bf16[64,2816]{1,0:T(8,128)(2,1)S(1)}, u32[]{:S(2)}, u32[]{:S(2)}) collective-permute-start(bf16[64,2816]{1,0:T(8,128)(2,1)S(1)} %get-tuple-element.54), channel_id=1, source_target_pairs={{0,14},{1,15},{2,0},{3,1},{4,2},{5,3},{6,4},{7,5},{8,6},{9,7},{10,... | collective-permute-start | bytes 1081352 | tf_op jit(solution)/shard_map/ppermute | solution.py:544
  53.0 9.8 %collective-permute-start.8 = (bf16[64,2816]{1,0:T(8,128)(2,1)S(1)}, bf16[64,2816]{1,0:T(8,128)(2,1)S(1)}, u32[]{:S(2)}, u32[]{:S(2)}) collective-permute-start(bf16[64,2816]{1,0:T(8,128)(2,1)S(1)} %get-tuple-element.53.refs_0_), channel_id=1, source_target_pairs={{0,2},{1,3},{2,4},{3,5},{4,6},{5,7},{6,8},{7,9},{8,10},{9,11},{10,... | collective-permute-start | bytes 1081352 | tf_op jit(solution)/shard_map/ppermute | solution.py:544
  63.5 8.0 %collective-permute-start.10 = (bf16[64,2048]{1,0:T(8,128)(2,1)S(1)}, bf16[64,2048]{1,0:T(8,128)(2,1)S(1)}, u32[]{:S(2)}, u32[]{:S(2)}) collective-permute-start(bf16[64,2048]{1,0:T(8,128)(2,1)S(1)} %get-tuple-element.57.refs_0_), channel_id=1, source_target_pairs={{0,1},{1,0},{2,3},{3,2},{4,5},{5,4},{6,7},{7,6},{8,9},{9,8},{10,11... | collective-permute-start | bytes 786440 | tf_op jit(solution)/shard_map/ppermute | solution.py:547
  72.9 6.7 %collective-permute-start.11 = (bf16[32,2048]{1,0:T(8,128)(2,1)S(1)}, bf16[32,2048]{1,0:T(8,128)(2,1)S(1)}, u32[]{:S(2)}, u32[]{:S(2)}) collective-permute-start(bf16[32,2048]{1,0:T(8,128)(2,1)S(1)} %residual_images.1.refs_0_), channel_id=1, source_target_pairs={{0,1},{1,0},{2,3},{3,2},{4,5},{5,4},{6,7},{7,6},{8,9},{9,8},{10,11... | collective-permute-start | bytes 393224 | tf_op jit(solution)/shard_map/ppermute | solution.py:547
  75.4 7.4 %collective-permute-start.14 = (bf16[32,2048]{1,0:T(8,128)(2,1)S(1)}, bf16[32,2048]{1,0:T(8,128)(2,1)S(1)}, u32[]{:S(2)}, u32[]{:S(2)}) collective-permute-start(bf16[32,2048]{1,0:T(8,128)(2,1)S(1)} %residual_images.1.refs_0_), channel_id=1, source_target_pairs={{0,2},{1,3},{2,4},{3,5},{4,6},{5,7},{6,8},{7,9},{8,10},{9,11},{10,... | collective-permute-start | bytes 393224 | tf_op jit(solution)/shard_map/ppermute | solution.py:544
  75.7 7.2 %collective-permute-start.12 = (bf16[32,2048]{1,0:T(8,128)(2,1)S(1)}, bf16[32,2048]{1,0:T(8,128)(2,1)S(1)}, u32[]{:S(2)}, u32[]{:S(2)}) collective-permute-start(bf16[32,2048]{1,0:T(8,128)(2,1)S(1)} %residual_images.1.refs_0_), channel_id=1, source_target_pairs={{0,14},{1,15},{2,0},{3,1},{4,2},{5,3},{6,4},{7,5},{8,6},{9,7},{10,... | collective-permute-start | bytes 393224 | tf_op jit(solution)/shard_map/ppermute | solution.py:544
  79.6 7.4 %collective-permute-start.15 = (bf16[32,2048]{1,0:T(8,128)(2,1)S(1)}, bf16[32,2048]{1,0:T(8,128)(2,1)S(1)}, u32[]{:S(2)}, u32[]{:S(2)}) collective-permute-start(bf16[32,2048]{1,0:T(8,128)(2,1)S(1)} %collective-permute-done.11.refs_1_), channel_id=1, source_target_pairs={{0,2},{1,3},{2,4},{3,5},{4,6},{5,7},{6,8},{7,9},{8,10},{9,11},{10,... | collective-permute-start | bytes 393224 | tf_op jit(solution)/shard_map/ppermute | solution.py:544
  79.9 7.2 %collective-permute-start.13 = (bf16[32,2048]{1,0:T(8,128)(2,1)S(1)}, bf16[32,2048]{1,0:T(8,128)(2,1)S(1)}, u32[]{:S(2)}, u32[]{:S(2)}) collective-permute-start(bf16[32,2048]{1,0:T(8,128)(2,1)S(1)} %collective-permute-done.11.refs_1_), channel_id=1, source_target_pairs={{0,14},{1,15},{2,0},{3,1},{4,2},{5,3},{6,4},{7,5},{8,6},{9,7},{10,... | collective-permute-start | bytes 393224 | tf_op jit(solution)/shard_map/ppermute | solution.py:544
  82.9 9.0 %collective-permute-start.18 = (bf16[32,2048]{1,0:T(8,128)(2,1)S(1)}, bf16[32,2048]{1,0:T(8,128)(2,1)S(1)}, u32[]{:S(2)}, u32[]{:S(2)}) collective-permute-start(bf16[32,2048]{1,0:T(8,128)(2,1)S(1)} %collective-permute-done.14.refs_4_), channel_id=1, source_target_pairs={{0,2},{1,3},{2,4},{3,5},{4,6},{5,7},{6,8},{7,9},{8,10},{9,11},{10,... | collective-permute-start | bytes 393224 | tf_op jit(solution)/shard_map/ppermute | solution.py:544
  82.9 10.6 %collective-permute-start.16 = (bf16[32,2048]{1,0:T(8,128)(2,1)S(1)}, bf16[32,2048]{1,0:T(8,128)(2,1)S(1)}, u32[]{:S(2)}, u32[]{:S(2)}) collective-permute-start(bf16[32,2048]{1,0:T(8,128)(2,1)S(1)} %collective-permute-done.12.refs_2_), channel_id=1, source_target_pairs={{0,14},{1,15},{2,0},{3,1},{4,2},{5,3},{6,4},{7,5},{8,6},{9,7},{10,... | collective-permute-start | bytes 393224 | tf_op jit(solution)/shard_map/ppermute | solution.py:544
  87.0 8.1 %collective-permute-start.19 = (bf16[32,2048]{1,0:T(8,128)(2,1)S(1)}, bf16[32,2048]{1,0:T(8,128)(2,1)S(1)}, u32[]{:S(2)}, u32[]{:S(2)}) collective-permute-start(bf16[32,2048]{1,0:T(8,128)(2,1)S(1)} %collective-permute-done.15.refs_5_), channel_id=1, source_target_pairs={{0,2},{1,3},{2,4},{3,5},{4,6},{5,7},{6,8},{7,9},{8,10},{9,11},{10,... | collective-permute-start | bytes 393224 | tf_op jit(solution)/shard_map/ppermute | solution.py:544
  87.1 10.2 %collective-permute-start.17 = (bf16[32,2048]{1,0:T(8,128)(2,1)S(1)}, bf16[32,2048]{1,0:T(8,128)(2,1)S(1)}, u32[]{:S(2)}, u32[]{:S(2)}) collective-permute-start(bf16[32,2048]{1,0:T(8,128)(2,1)S(1)} %collective-permute-done.13.refs_3_), channel_id=1, source_target_pairs={{0,14},{1,15},{2,0},{3,1},{4,2},{5,3},{6,4},{7,5},{8,6},{9,7},{10,... | collective-permute-start | bytes 393224 | tf_op jit(solution)/shard_map/ppermute | solution.py:544
  91.9 7.2 %collective-permute-start.24 = (bf16[32,2048]{1,0:T(8,128)(2,1)S(1)}, bf16[32,2048]{1,0:T(8,128)(2,1)S(1)}, u32[]{:S(2)}, u32[]{:S(2)}) collective-permute-start(bf16[32,2048]{1,0:T(8,128)(2,1)S(1)} %collective-permute-done.18.refs_8_), channel_id=1, source_target_pairs={{0,4},{1,5},{2,6},{3,7},{4,8},{5,9},{6,10},{7,11},{8,12},{9,13},{1... | collective-permute-start | bytes 393224 | tf_op jit(solution)/shard_map/ppermute | solution.py:544
  91.9 8.2 %collective-permute-start.22 = (bf16[32,2048]{1,0:T(8,128)(2,1)S(1)}, bf16[32,2048]{1,0:T(8,128)(2,1)S(1)}, u32[]{:S(2)}, u32[]{:S(2)}) collective-permute-start(bf16[32,2048]{1,0:T(8,128)(2,1)S(1)} %collective-permute-done.18.refs_8_), channel_id=1, source_target_pairs={{0,2},{1,3},{2,4},{3,5},{4,6},{5,7},{6,8},{7,9},{8,10},{9,11},{10,... | collective-permute-start | bytes 393224 | tf_op jit(solution)/shard_map/ppermute | solution.py:544
  93.5 6.6 %collective-permute-start.20 = (bf16[32,2048]{1,0:T(8,128)(2,1)S(1)}, bf16[32,2048]{1,0:T(8,128)(2,1)S(1)}, u32[]{:S(2)}, u32[]{:S(2)}) collective-permute-start(bf16[32,2048]{1,0:T(8,128)(2,1)S(1)} %collective-permute-done.16.refs_6_), channel_id=1, source_target_pairs={{0,14},{1,15},{2,0},{3,1},{4,2},{5,3},{6,4},{7,5},{8,6},{9,7},{10,... | collective-permute-start | bytes 393224 | tf_op jit(solution)/shard_map/ppermute | solution.py:544
  95.2 6.2 %collective-permute-start.23 = (bf16[32,2048]{1,0:T(8,128)(2,1)S(1)}, bf16[32,2048]{1,0:T(8,128)(2,1)S(1)}, u32[]{:S(2)}, u32[]{:S(2)}) collective-permute-start(bf16[32,2048]{1,0:T(8,128)(2,1)S(1)} %collective-permute-done.19.refs_9_), channel_id=1, source_target_pairs={{0,2},{1,3},{2,4},{3,5},{4,6},{5,7},{6,8},{7,9},{8,10},{9,11},{10,... | collective-permute-start | bytes 393224 | tf_op jit(solution)/shard_map/ppermute | solution.py:544
  97.3 6.0 %collective-permute-start.25 = (bf16[32,2048]{1,0:T(8,128)(2,1)S(1)}, bf16[32,2048]{1,0:T(8,128)(2,1)S(1)}, u32[]{:S(2)}, u32[]{:S(2)}) collective-permute-start(bf16[32,2048]{1,0:T(8,128)(2,1)S(1)} %collective-permute-done.17.refs_7_), channel_id=1, source_target_pairs={{0,12},{1,13},{2,14},{3,15},{4,0},{5,1},{6,2},{7,3},{8,4},{9,5},{1... | collective-permute-start | bytes 393224 | tf_op jit(solution)/shard_map/ppermute | solution.py:544
  99.1 6.9 %collective-permute-start.21 = (bf16[32,2048]{1,0:T(8,128)(2,1)S(1)}, bf16[32,2048]{1,0:T(8,128)(2,1)S(1)}, u32[]{:S(2)}, u32[]{:S(2)}) collective-permute-start(bf16[32,2048]{1,0:T(8,128)(2,1)S(1)} %collective-permute-done.17.refs_7_), channel_id=1, source_target_pairs={{0,14},{1,15},{2,0},{3,1},{4,2},{5,3},{6,4},{7,5},{8,6},{9,7},{10,... | collective-permute-start | bytes 393224 | tf_op jit(solution)/shard_map/ppermute | solution.py:544

commit v9 on v8

--- a/solution.py
+++ b/solution.py
@@ -443,7 +443,7 @@
         out_ref[z] = (total * beta).astype(BF16)
         return carry
 
-    lax.fori_loop(0, depth, body, 0, unroll=2)
+    lax.fori_loop(0, depth, body, 0, unroll=4)
     token_ref[...] = under_ref[:8]
 
 

time: 113 us -> 113 us (level)
  waiting for transfers between devices: 23.7 us -> 25 us
    pallas_call x4, Pallas kernels: 21.1 us -> 20 us  [regularizer(): pl.pallas_call(functools.partial(regularizer_kernel, origin, count), grid...]
  transfers between devices with their start and end apart: 27 -> 27, of which waited for: 16 -> 16; matrix products, arithmetic and copies ran while one was open for 1% -> 1% of each run, Pallas kernels for 24% -> 23%
where the time goes in v9:
time: 113 us
  starting transfers between devices  49.1 us (43%)
  Pallas kernels  36.3 us (32%)
  waiting for transfers between devices  25 us (22%)
  local copies, waits for them, and re-layouts  1.27 us (1%)
    ppermute x22, starting transfers between devices, along_z(): lax.ppermute(block, 'tile', [(i, (i + 2 * by) % tiles) for i in range(til...  34.1 us
    ppermute x22, waiting for transfers between devices, along_z(): lax.ppermute(block, 'tile', [(i, (i + 2 * by) % tiles) for i in range(til...  22.6 us
    pallas_call x4, Pallas kernels, regularizer(): pl.pallas_call(functools.partial(regularizer_kernel, origin, count), grid...  20 us
    pallas_call x1, Pallas kernels, gradient(): pl.pallas_call(gradient_kernel, out_shape=jax.ShapeDtypeStruct(regular.sh...  6.62 us
    all_to_all x1, starting transfers between devices, shards(): lax.all_to_all(packed, 'slab', split_axis=0, concat_axis=0, tiled=True)  5.77 us
    ppermute x2, starting transfers between devices, along_y(): return lax.ppermute(block, 'tile', [(i, i ^ 1) for i in range(tiles)])  4.89 us
    pallas_call x1, Pallas kernels, forward(): pl.pallas_call(kernel, out_shape=[jax.ShapeDtypeStruct(shape, BF16) for s...  4.8 us
    ppermute x1, starting transfers between devices, shards(): below = lax.ppermute(top, 'slab', [(i, i + 1) for i in range(slabs - 1)])  2.3 us
  transfers between devices with their start and end apart: 27, of which 16 were waited for; matrix products, arithmetic and copies ran while one was open for 1% of the time, Pallas kernels for 23%

profile of v9, /device:TPU:8, one launch (start us, length us, event | category | flops | bytes accessed | tf_op | source)
XLA Modules:
  0.0 112.8 jit_solution(9395479546978724564)
XLA Ops:
  0.0 1.7 %pack_messages.1 = bf16[16,4,16,128]{3,2,1,0:T(8,128)(2,1)} custom-call(s32[2,12]{1,0:T(2,128)} %bitcast.9, s32[2,12]{1,0:T(2,128)} %offset_ref.1, s32[2,12]{1,0:T(2,128)} %width_ref.1, bf16[12,2,128]{2,1,0:T(2,128)(2,1)} %bitcast.8, bf16[2,12,8,128]{3,2,1,0:T(8,128)(2,1)} %measured_ref.1), custom_call_target="tpu_custom_call" | custom-call | tf_op jit(solution)/shard_map/pack_messages/pallas_call | solution.py:69
  1.7 5.8 %all-to-all-start = ((bf16[16,4,16,128]{3,2,1,0:T(8,128)(2,1)}), bf16[16,4,16,128]{3,2,1,0:T(8,128)(2,1)S(1)}, u32[]{:S(2)}, u32[]{:S(2)}) async-start(bf16[16,4,16,128]{3,2,1,0:T(8,128)(2,1)} %pack_messages.1), calls=%async_computation | async-start | bytes 524288 | tf_op jit(solution)/shard_map/all_to_all | solution.py:551
  8.7 2.0 %collective-permute-start.5 = (bf16[1,2048,128]{2,1,0:T(8,128)(2,1)S(1)}, bf16[1,2048,128]{2,1,0:T(8,128)(2,1)S(1)}, u32[]{:S(2)}, u32[]{:S(2)}) collective-permute-start(bf16[1,2048,128]{2,1,0:T(8,128)(2,1)S(1)} %get-tuple-element.63.refs_1_), channel_id=1, source_target_pairs={{16,0},{32,16},{48,32},{64,48},{80,64},{96,80},{112,96},{128,112},... | collective-permute-start | bytes 1572872 | tf_op jit(solution)/shard_map/ppermute | solution.py:554
  10.8 2.3 %collective-permute-start.4 = (bf16[1,2048,128]{2,1,0:T(8,128)(2,1)S(1)}, bf16[1,2048,128]{2,1,0:T(8,128)(2,1)S(1)}, u32[]{:S(2)}, u32[]{:S(2)}) collective-permute-start(bf16[1,2048,128]{2,1,0:T(8,128)(2,1)S(1)} %get-tuple-element.64.refs_0_), channel_id=1, source_target_pairs={{0,16},{16,32},{32,48},{48,64},{64,80},{80,96},{96,112},{112,128},... | collective-permute-start | bytes 1572872 | tf_op jit(solution)/shard_map/ppermute | solution.py:553
  14.0 4.8 %forward.1 = (bf16[64,2176]{1,0:T(8,128)(2,1)S(1)}, bf16[64,2432]{1,0:T(8,128)(2,1)S(1)}, bf16[64,2432]{1,0:T(8,128)(2,1)S(1)}, bf16[64,2176]{1,0:T(8,128)(2,1)S...) custom-call(s32[4]{0:T(128)S(1)} %pad_add_fusion.place_ref, ...), custom_call_target="tpu_custom_call" | custom-call | flops 2147483648 | bytes 6291456 | tf_op jit(solution)/shard_map/forward/pallas_call | solution.py:224
  18.8 2.0 %collective-permute-start = (bf16[32,2176]{1,0:T(8,128)(2,1)S(1)}, bf16[32,2176]{1,0:T(8,128)(2,1)S(1)}, u32[]{:S(2)}, u32[]{:S(2)}) collective-permute-start(bf16[32,2176]{1,0:T(8,128)(2,1)S(1)} %get-tuple-element.38), channel_id=1, source_target_pairs={{0,2},{1,3},{2,4},{3,5},{4,6},{5,7},{6,8},{7,9},{8,10},{9,11},{10,... | collective-permute-start | bytes 417800 | tf_op jit(solution)/shard_map/ppermute | solution.py:544
  20.8 4.0 %collective-permute-start.1 = (bf16[32,2176]{1,0:T(8,128)(2,1)S(1)}, bf16[32,2176]{1,0:T(8,128)(2,1)S(1)}, u32[]{:S(2)}, u32[]{:S(2)}) collective-permute-start(bf16[32,2176]{1,0:T(8,128)(2,1)S(1)} %get-tuple-element.40), channel_id=1, source_target_pairs={{0,14},{1,15},{2,0},{3,1},{4,2},{5,3},{6,4},{7,5},{8,6},{9,7},{10,... | collective-permute-start | bytes 417800 | tf_op jit(solution)/shard_map/ppermute | solution.py:544
  25.5 2.9 %collective-permute-done.from_below_ref = bf16[32,2176]{1,0:T(8,128)(2,1)S(1)} collective-permute-done((bf16[32,2176]{1,0:T(8,128)(2,1)S(1)}, bf16[32,2176]{1,0:T(8,128)(2,1)S(1)}, u32[]{:S(2)}, u32[]{:S(2)}) %collective-permute-start) | collective-permute-done | bytes 139296 | tf_op jit(solution)/shard_map/ppermute | solution.py:544
  28.5 3.7 %collective-permute-start.3 = (bf16[64,2304]{1,0:T(8,128)(2,1)S(1)}, bf16[64,2304]{1,0:T(8,128)(2,1)S(1)}, u32[]{:S(2)}, u32[]{:S(2)}) collective-permute-start(bf16[64,2304]{1,0:T(8,128)(2,1)S(1)} %get-tuple-element.44), channel_id=1, source_target_pairs={{0,14},{1,15},{2,0},{3,1},{4,2},{5,3},{6,4},{7,5},{8,6},{9,7},{10,... | collective-permute-start | bytes 884744 | tf_op jit(solution)/shard_map/ppermute | solution.py:544
  32.9 5.0 %regularizer.4 = (bf16[8,2048,128]{2,1,0:T(8,128)(2,1)}, f32[8,128]{1,0:T(8,128)S(1)}) custom-call(s32[4]{0:T(128)S(1)} %pad_add_fusion.place_ref, f32[1]{0:T(128)S(6)} %copy.14.beta_ref, bf16[8,2048,128]{2,1,0:T(8,128)(2,1)} %volume_ref.9, bf16[1,2048,128]{2,1,0:T(8,128)(2,1)S(1)} %collective-permute-done.4.below_ref, ...), custom_call_target="tpu_custom_call" | custom-call | flops 15728640 | bytes 4194304 | tf_op jit(solution)/shard_map/regularizer/pallas_call | solution.py:460
  39.0 3.4 %collective-permute-done.2.from_below_ref = bf16[64,2304]{1,0:T(8,128)(2,1)S(1)} collective-permute-done((bf16[64,2304]{1,0:T(8,128)(2,1)S(1)}, bf16[64,2304]{1,0:T(8,128)(2,1)S(1)}, u32[]{:S(2)}, u32[]{:S(2)}) %collective-permute-start.2) | collective-permute-done | bytes 294944 | tf_op jit(solution)/shard_map/ppermute | solution.py:544
  42.9 1.7 %collective-permute-start.6 = (bf16[64,2432]{1,0:T(8,128)(2,1)S(1)}, bf16[64,2432]{1,0:T(8,128)(2,1)S(1)}, u32[]{:S(2)}, u32[]{:S(2)}) collective-permute-start(bf16[64,2432]{1,0:T(8,128)(2,1)S(1)} %get-tuple-element.47.refs_0_), channel_id=1, source_target_pairs={{0,2},{1,3},{2,4},{3,5},{4,6},{5,7},{6,8},{7,9},{8,10},{9,11},{10,... | collective-permute-start | bytes 933896 | tf_op jit(solution)/shard_map/ppermute | solution.py:544
  44.6 5.0 %regularizer.5 = (bf16[8,2048,128]{2,1,0:T(8,128)(2,1)}, f32[8,128]{1,0:T(8,128)S(1)}) custom-call(s32[4]{0:T(128)S(1)} %pad_add_fusion.place_ref, f32[1]{0:T(128)S(6)} %copy.14.beta_ref, bf16[8,2048,128]{2,1,0:T(8,128)(2,1)} %volume_ref.9, bf16[1,2048,128]{2,1,0:T(8,128)(2,1)S(1)} %collective-permute-done.4.below_ref, ...), custom_call_target="tpu_custom_call", output_to_operand_aliasing={{0}: (6, {})} | custom-call | flops 15728640 | bytes 4194304 | tf_op jit(solution)/shard_map/regularizer/pallas_call | solution.py:460
  51.0 1.5 %collective-permute-done.6.from_below_ref = bf16[64,2432]{1,0:T(8,128)(2,1)S(1)} collective-permute-done((bf16[64,2432]{1,0:T(8,128)(2,1)S(1)}, bf16[64,2432]{1,0:T(8,128)(2,1)S(1)}, u32[]{:S(2)}, u32[]{:S(2)}) %collective-permute-start.6) | collective-permute-done | bytes 311328 | tf_op jit(solution)/shard_map/ppermute | solution.py:544
  53.0 1.7 %collective-permute-start.8 = (bf16[64,2816]{1,0:T(8,128)(2,1)S(1)}, bf16[64,2816]{1,0:T(8,128)(2,1)S(1)}, u32[]{:S(2)}, u32[]{:S(2)}) collective-permute-start(bf16[64,2816]{1,0:T(8,128)(2,1)S(1)} %get-tuple-element.53.refs_0_), channel_id=1, source_target_pairs={{0,2},{1,3},{2,4},{3,5},{4,6},{5,7},{6,8},{7,9},{8,10},{9,11},{10,... | collective-permute-start | bytes 1081352 | tf_op jit(solution)/shard_map/ppermute | solution.py:544
  54.8 5.0 %regularizer.6 = (bf16[8,2048,128]{2,1,0:T(8,128)(2,1)}, f32[8,128]{1,0:T(8,128)S(1)}) custom-call(s32[4]{0:T(128)S(1)} %pad_add_fusion.place_ref, f32[1]{0:T(128)S(6)} %copy.14.beta_ref, bf16[8,2048,128]{2,1,0:T(8,128)(2,1)} %volume_ref.9, bf16[1,2048,128]{2,1,0:T(8,128)(2,1)S(1)} %collective-permute-done.4.below_ref, ...), custom_call_target="tpu_custom_call", output_to_operand_aliasing={{0}: (6, {})} | custom-call | flops 15728640 | bytes 4194304 | tf_op jit(solution)/shard_map/regularizer/pallas_call | solution.py:460
  59.8 1.6 %collective-permute-done.9.above_ref = bf16[64,2816]{1,0:T(8,128)(2,1)S(1)} collective-permute-done((bf16[64,2816]{1,0:T(8,128)(2,1)S(1)}, bf16[64,2816]{1,0:T(8,128)(2,1)S(1)}, u32[]{:S(2)}, u32[]{:S(2)}) %collective-permute-start.9) | collective-permute-done | bytes 360480 | tf_op jit(solution)/shard_map/ppermute | solution.py:544
  61.3 1.5 %collective-permute-done.8.below_ref = bf16[64,2816]{1,0:T(8,128)(2,1)S(1)} collective-permute-done((bf16[64,2816]{1,0:T(8,128)(2,1)S(1)}, bf16[64,2816]{1,0:T(8,128)(2,1)S(1)}, u32[]{:S(2)}, u32[]{:S(2)}) %collective-permute-start.8) | collective-permute-done | bytes 360480 | tf_op jit(solution)/shard_map/ppermute | solution.py:544
  63.5 2.5 %collective-permute-start.10 = (bf16[64,2048]{1,0:T(8,128)(2,1)S(1)}, bf16[64,2048]{1,0:T(8,128)(2,1)S(1)}, u32[]{:S(2)}, u32[]{:S(2)}) collective-permute-start(bf16[64,2048]{1,0:T(8,128)(2,1)S(1)} %get-tuple-element.57.refs_0_), channel_id=1, source_target_pairs={{0,1},{1,0},{2,3},{3,2},{4,5},{5,4},{6,7},{7,6},{8,9},{9,8},{10,11... | collective-permute-start | bytes 786440 | tf_op jit(solution)/shard_map/ppermute | solution.py:547
  66.0 5.0 %regularizer.7 = (bf16[8,2048,128]{2,1,0:T(8,128)(2,1)}, f32[8,128]{1,0:T(8,128)S(1)}) custom-call(s32[4]{0:T(128)S(1)} %pad_add_fusion.place_ref, f32[1]{0:T(128)S(6)} %copy.14.beta_ref, bf16[8,2048,128]{2,1,0:T(8,128)(2,1)} %volume_ref.9, bf16[1,2048,128]{2,1,0:T(8,128)(2,1)S(1)} %collective-permute-done.4.below_ref, ...), custom_call_target="tpu_custom_call", output_to_operand_aliasing={{0}: (6, {})} | custom-call | flops 15728640 | bytes 4194304 | tf_op jit(solution)/shard_map/regularizer/pallas_call | solution.py:460
  73.1 2.4 %collective-permute-start.11 = (bf16[32,2048]{1,0:T(8,128)(2,1)S(1)}, bf16[32,2048]{1,0:T(8,128)(2,1)S(1)}, u32[]{:S(2)}, u32[]{:S(2)}) collective-permute-start(bf16[32,2048]{1,0:T(8,128)(2,1)S(1)} %residual_images.1.refs_0_), channel_id=1, source_target_pairs={{0,1},{1,0},{2,3},{3,2},{4,5},{5,4},{6,7},{7,6},{8,9},{9,8},{10,11... | collective-permute-start | bytes 393224 | tf_op jit(solution)/shard_map/ppermute | solution.py:547
  75.7 3.0 %collective-permute-start.12 = (bf16[32,2048]{1,0:T(8,128)(2,1)S(1)}, bf16[32,2048]{1,0:T(8,128)(2,1)S(1)}, u32[]{:S(2)}, u32[]{:S(2)}) collective-permute-start(bf16[32,2048]{1,0:T(8,128)(2,1)S(1)} %residual_images.1.refs_0_), channel_id=1, source_target_pairs={{0,14},{1,15},{2,0},{3,1},{4,2},{5,3},{6,4},{7,5},{8,6},{9,7},{10,... | collective-permute-start | bytes 393224 | tf_op jit(solution)/shard_map/ppermute | solution.py:544
  79.9 3.0 %collective-permute-start.13 = (bf16[32,2048]{1,0:T(8,128)(2,1)S(1)}, bf16[32,2048]{1,0:T(8,128)(2,1)S(1)}, u32[]{:S(2)}, u32[]{:S(2)}) collective-permute-start(bf16[32,2048]{1,0:T(8,128)(2,1)S(1)} %collective-permute-done.11.refs_1_), channel_id=1, source_target_pairs={{0,14},{1,15},{2,0},{3,1},{4,2},{5,3},{6,4},{7,5},{8,6},{9,7},{10,... | collective-permute-start | bytes 393224 | tf_op jit(solution)/shard_map/ppermute | solution.py:544
  82.9 3.2 %collective-permute-start.16 = (bf16[32,2048]{1,0:T(8,128)(2,1)S(1)}, bf16[32,2048]{1,0:T(8,128)(2,1)S(1)}, u32[]{:S(2)}, u32[]{:S(2)}) collective-permute-start(bf16[32,2048]{1,0:T(8,128)(2,1)S(1)} %collective-permute-done.12.refs_2_), channel_id=1, source_target_pairs={{0,14},{1,15},{2,0},{3,1},{4,2},{5,3},{6,4},{7,5},{8,6},{9,7},{10,... | collective-permute-start | bytes 393224 | tf_op jit(solution)/shard_map/ppermute | solution.py:544
  87.2 3.2 %collective-permute-start.17 = (bf16[32,2048]{1,0:T(8,128)(2,1)S(1)}, bf16[32,2048]{1,0:T(8,128)(2,1)S(1)}, u32[]{:S(2)}, u32[]{:S(2)}) collective-permute-start(bf16[32,2048]{1,0:T(8,128)(2,1)S(1)} %collective-permute-done.13.refs_3_), channel_id=1, source_target_pairs={{0,14},{1,15},{2,0},{3,1},{4,2},{5,3},{6,4},{7,5},{8,6},{9,7},{10,... | collective-permute-start | bytes 393224 | tf_op jit(solution)/shard_map/ppermute | solution.py:544
  90.5 1.5 %collective-permute-done.18.refs_8_ = bf16[32,2048]{1,0:T(8,128)(2,1)S(1)} collective-permute-done((bf16[32,2048]{1,0:T(8,128)(2,1)S(1)}, bf16[32,2048]{1,0:T(8,128)(2,1)S(1)}, u32[]{:S(2)}, u32[]{:S(2)}) %collective-permute-start.18) | collective-permute-done | bytes 131104 | tf_op jit(solution)/shard_map/ppermute | solution.py:544
  91.9 1.6 %collective-permute-start.22 = (bf16[32,2048]{1,0:T(8,128)(2,1)S(1)}, bf16[32,2048]{1,0:T(8,128)(2,1)S(1)}, u32[]{:S(2)}, u32[]{:S(2)}) collective-permute-start(bf16[32,2048]{1,0:T(8,128)(2,1)S(1)} %collective-permute-done.18.refs_8_), channel_id=1, source_target_pairs={{0,2},{1,3},{2,4},{3,5},{4,6},{5,7},{6,8},{7,9},{8,10},{9,11},{10,... | collective-permute-start | bytes 393224 | tf_op jit(solution)/shard_map/ppermute | solution.py:544
  93.5 1.7 %collective-permute-start.20 = (bf16[32,2048]{1,0:T(8,128)(2,1)S(1)}, bf16[32,2048]{1,0:T(8,128)(2,1)S(1)}, u32[]{:S(2)}, u32[]{:S(2)}) collective-permute-start(bf16[32,2048]{1,0:T(8,128)(2,1)S(1)} %collective-permute-done.16.refs_6_), channel_id=1, source_target_pairs={{0,14},{1,15},{2,0},{3,1},{4,2},{5,3},{6,4},{7,5},{8,6},{9,7},{10,... | collective-permute-start | bytes 393224 | tf_op jit(solution)/shard_map/ppermute | solution.py:544
  95.2 2.1 %collective-permute-start.23 = (bf16[32,2048]{1,0:T(8,128)(2,1)S(1)}, bf16[32,2048]{1,0:T(8,128)(2,1)S(1)}, u32[]{:S(2)}, u32[]{:S(2)}) collective-permute-start(bf16[32,2048]{1,0:T(8,128)(2,1)S(1)} %collective-permute-done.19.refs_9_), channel_id=1, source_target_pairs={{0,2},{1,3},{2,4},{3,5},{4,6},{5,7},{6,8},{7,9},{8,10},{9,11},{10,... | collective-permute-start | bytes 393224 | tf_op jit(solution)/shard_map/ppermute | solution.py:544
  101.4 1.9 %collective-permute-done.25.refs_15_ = bf16[32,2048]{1,0:T(8,128)(2,1)S(1)} collective-permute-done((bf16[32,2048]{1,0:T(8,128)(2,1)S(1)}, bf16[32,2048]{1,0:T(8,128)(2,1)S(1)}, u32[]{:S(2)}, u32[]{:S(2)}) %collective-permute-start.25) | collective-permute-done | bytes 131104 | tf_op jit(solution)/shard_map/ppermute | solution.py:544
  103.2 2.7 %collective-permute-done.21.refs_11_ = bf16[32,2048]{1,0:T(8,128)(2,1)S(1)} collective-permute-done((bf16[32,2048]{1,0:T(8,128)(2,1)S(1)}, bf16[32,2048]{1,0:T(8,128)(2,1)S(1)}, u32[]{:S(2)}, u32[]{:S(2)}) %collective-permute-start.21) | collective-permute-done | bytes 131104 | tf_op jit(solution)/shard_map/ppermute | solution.py:544
  106.0 6.6 %gradient.1 = bf16[8,2048,128]{2,1,0:T(8,128)(2,1)} custom-call(s32[4]{0:T(128)S(1)} %pad_add_fusion.place_ref, f32[1]{0:T(128)S(6)} %copy.14.beta_ref, bf16[528,1024]{1,0:T(8,128)(2,1)S(1)} %spread_rows.1.refs_0_.spread_ref, bf16[16,2048]{1,0:T(8,128)(2,1)S(1)} %get-tuple-element.36.order_ref.ends_ref.mine_ref, ...), custom_call_target="tpu_custom_call" | custom-call | flops 2214592512 | bytes 10485760 | tf_op jit(solution)/shard_map/gradient/pallas_call | solution.py:523
  (38 shorter events, 15.7 us)
Async XLA Ops:
  1.7 12.3 %all-to-all-start = ((bf16[16,4,16,128]{3,2,1,0:T(8,128)(2,1)}), bf16[16,4,16,128]{3,2,1,0:T(8,128)(2,1)S(1)}, u32[]{:S(2)}, u32[]{:S(2)}) async-start(bf16[16,4,16,128]{3,2,1,0:T(8,128)(2,1)} %pack_messages.1), calls=%async_computation | async-start | bytes 524288 | tf_op jit(solution)/shard_map/all_to_all | solution.py:551
  8.7 24.2 %collective-permute-start.5 = (bf16[1,2048,128]{2,1,0:T(8,128)(2,1)S(1)}, bf16[1,2048,128]{2,1,0:T(8,128)(2,1)S(1)}, u32[]{:S(2)}, u32[]{:S(2)}) collective-permute-start(bf16[1,2048,128]{2,1,0:T(8,128)(2,1)S(1)} %get-tuple-element.63.refs_1_), channel_id=1, source_target_pairs={{16,0},{32,16},{48,32},{64,48},{80,64},{96,80},{112,96},{128,112},... | collective-permute-start | bytes 1572872 | tf_op jit(solution)/shard_map/ppermute | solution.py:554
  10.8 22.1 %collective-permute-start.4 = (bf16[1,2048,128]{2,1,0:T(8,128)(2,1)S(1)}, bf16[1,2048,128]{2,1,0:T(8,128)(2,1)S(1)}, u32[]{:S(2)}, u32[]{:S(2)}) collective-permute-start(bf16[1,2048,128]{2,1,0:T(8,128)(2,1)S(1)} %get-tuple-element.64.refs_0_), channel_id=1, source_target_pairs={{0,16},{16,32},{32,48},{48,64},{64,80},{80,96},{96,112},{112,128},... | collective-permute-start | bytes 1572872 | tf_op jit(solution)/shard_map/ppermute | solution.py:553
  18.8 9.7 %collective-permute-start = (bf16[32,2176]{1,0:T(8,128)(2,1)S(1)}, bf16[32,2176]{1,0:T(8,128)(2,1)S(1)}, u32[]{:S(2)}, u32[]{:S(2)}) collective-permute-start(bf16[32,2176]{1,0:T(8,128)(2,1)S(1)} %get-tuple-element.38), channel_id=1, source_target_pairs={{0,2},{1,3},{2,4},{3,5},{4,6},{5,7},{6,8},{7,9},{8,10},{9,11},{10,... | collective-permute-start | bytes 417800 | tf_op jit(solution)/shard_map/ppermute | solution.py:544
  20.8 7.7 %collective-permute-start.1 = (bf16[32,2176]{1,0:T(8,128)(2,1)S(1)}, bf16[32,2176]{1,0:T(8,128)(2,1)S(1)}, u32[]{:S(2)}, u32[]{:S(2)}) collective-permute-start(bf16[32,2176]{1,0:T(8,128)(2,1)S(1)} %get-tuple-element.40), channel_id=1, source_target_pairs={{0,14},{1,15},{2,0},{3,1},{4,2},{5,3},{6,4},{7,5},{8,6},{9,7},{10,... | collective-permute-start | bytes 417800 | tf_op jit(solution)/shard_map/ppermute | solution.py:544
  28.5 10.4 %collective-permute-start.3 = (bf16[64,2304]{1,0:T(8,128)(2,1)S(1)}, bf16[64,2304]{1,0:T(8,128)(2,1)S(1)}, u32[]{:S(2)}, u32[]{:S(2)}) collective-permute-start(bf16[64,2304]{1,0:T(8,128)(2,1)S(1)} %get-tuple-element.44), channel_id=1, source_target_pairs={{0,14},{1,15},{2,0},{3,1},{4,2},{5,3},{6,4},{7,5},{8,6},{9,7},{10,... | collective-permute-start | bytes 884744 | tf_op jit(solution)/shard_map/ppermute | solution.py:544
  32.2 10.1 %collective-permute-start.2 = (bf16[64,2304]{1,0:T(8,128)(2,1)S(1)}, bf16[64,2304]{1,0:T(8,128)(2,1)S(1)}, u32[]{:S(2)}, u32[]{:S(2)}) collective-permute-start(bf16[64,2304]{1,0:T(8,128)(2,1)S(1)} %get-tuple-element.42.refs_0_), channel_id=1, source_target_pairs={{0,2},{1,3},{2,4},{3,5},{4,6},{5,7},{6,8},{7,9},{8,10},{9,11},{10,... | collective-permute-start | bytes 884744 | tf_op jit(solution)/shard_map/ppermute | solution.py:544
  42.5 8.5 %collective-permute-start.7 = (bf16[64,2432]{1,0:T(8,128)(2,1)S(1)}, bf16[64,2432]{1,0:T(8,128)(2,1)S(1)}, u32[]{:S(2)}, u32[]{:S(2)}) collective-permute-start(bf16[64,2432]{1,0:T(8,128)(2,1)S(1)} %get-tuple-element.49), channel_id=1, source_target_pairs={{0,14},{1,15},{2,0},{3,1},{4,2},{5,3},{6,4},{7,5},{8,6},{9,7},{10,... | collective-permute-start | bytes 933896 | tf_op jit(solution)/shard_map/ppermute | solution.py:544
  42.9 9.7 %collective-permute-start.6 = (bf16[64,2432]{1,0:T(8,128)(2,1)S(1)}, bf16[64,2432]{1,0:T(8,128)(2,1)S(1)}, u32[]{:S(2)}, u32[]{:S(2)}) collective-permute-start(bf16[64,2432]{1,0:T(8,128)(2,1)S(1)} %get-tuple-element.47.refs_0_), channel_id=1, source_target_pairs={{0,2},{1,3},{2,4},{3,5},{4,6},{5,7},{6,8},{7,9},{8,10},{9,11},{10,... | collective-permute-start | bytes 933896 | tf_op jit(solution)/shard_map/ppermute | solution.py:544
  52.7 8.7 %collective-permute-start.9 = (bf16[64,2816]{1,0:T(8,128)(2,1)S(1)}, bf16[64,2816]{1,0:T(8,128)(2,1)S(1)}, u32[]{:S(2)}, u32[]{:S(2)}) collective-permute-start(bf16[64,2816]{1,0:T(8,128)(2,1)S(1)} %get-tuple-element.54), channel_id=1, source_target_pairs={{0,14},{1,15},{2,0},{3,1},{4,2},{5,3},{6,4},{7,5},{8,6},{9,7},{10,... | collective-permute-start | bytes 1081352 | tf_op jit(solution)/shard_map/ppermute | solution.py:544
  53.0 9.8 %collective-permute-start.8 = (bf16[64,2816]{1,0:T(8,128)(2,1)S(1)}, bf16[64,2816]{1,0:T(8,128)(2,1)S(1)}, u32[]{:S(2)}, u32[]{:S(2)}) collective-permute-start(bf16[64,2816]{1,0:T(8,128)(2,1)S(1)} %get-tuple-element.53.refs_0_), channel_id=1, source_target_pairs={{0,2},{1,3},{2,4},{3,5},{4,6},{5,7},{6,8},{7,9},{8,10},{9,11},{10,... | collective-permute-start | bytes 1081352 | tf_op jit(solution)/shard_map/ppermute | solution.py:544
  63.5 8.1 %collective-permute-start.10 = (bf16[64,2048]{1,0:T(8,128)(2,1)S(1)}, bf16[64,2048]{1,0:T(8,128)(2,1)S(1)}, u32[]{:S(2)}, u32[]{:S(2)}) collective-permute-start(bf16[64,2048]{1,0:T(8,128)(2,1)S(1)} %get-tuple-element.57.refs_0_), channel_id=1, source_target_pairs={{0,1},{1,0},{2,3},{3,2},{4,5},{5,4},{6,7},{7,6},{8,9},{9,8},{10,11... | collective-permute-start | bytes 786440 | tf_op jit(solution)/shard_map/ppermute | solution.py:547
  73.1 6.6 %collective-permute-start.11 = (bf16[32,2048]{1,0:T(8,128)(2,1)S(1)}, bf16[32,2048]{1,0:T(8,128)(2,1)S(1)}, u32[]{:S(2)}, u32[]{:S(2)}) collective-permute-start(bf16[32,2048]{1,0:T(8,128)(2,1)S(1)} %residual_images.1.refs_0_), channel_id=1, source_target_pairs={{0,1},{1,0},{2,3},{3,2},{4,5},{5,4},{6,7},{7,6},{8,9},{9,8},{10,11... | collective-permute-start | bytes 393224 | tf_op jit(solution)/shard_map/ppermute | solution.py:547
  75.4 7.4 %collective-permute-start.14 = (bf16[32,2048]{1,0:T(8,128)(2,1)S(1)}, bf16[32,2048]{1,0:T(8,128)(2,1)S(1)}, u32[]{:S(2)}, u32[]{:S(2)}) collective-permute-start(bf16[32,2048]{1,0:T(8,128)(2,1)S(1)} %residual_images.1.refs_0_), channel_id=1, source_target_pairs={{0,2},{1,3},{2,4},{3,5},{4,6},{5,7},{6,8},{7,9},{8,10},{9,11},{10,... | collective-permute-start | bytes 393224 | tf_op jit(solution)/shard_map/ppermute | solution.py:544
  75.7 7.2 %collective-permute-start.12 = (bf16[32,2048]{1,0:T(8,128)(2,1)S(1)}, bf16[32,2048]{1,0:T(8,128)(2,1)S(1)}, u32[]{:S(2)}, u32[]{:S(2)}) collective-permute-start(bf16[32,2048]{1,0:T(8,128)(2,1)S(1)} %residual_images.1.refs_0_), channel_id=1, source_target_pairs={{0,14},{1,15},{2,0},{3,1},{4,2},{5,3},{6,4},{7,5},{8,6},{9,7},{10,... | collective-permute-start | bytes 393224 | tf_op jit(solution)/shard_map/ppermute | solution.py:544
  79.6 7.6 %collective-permute-start.15 = (bf16[32,2048]{1,0:T(8,128)(2,1)S(1)}, bf16[32,2048]{1,0:T(8,128)(2,1)S(1)}, u32[]{:S(2)}, u32[]{:S(2)}) collective-permute-start(bf16[32,2048]{1,0:T(8,128)(2,1)S(1)} %collective-permute-done.11.refs_1_), channel_id=1, source_target_pairs={{0,2},{1,3},{2,4},{3,5},{4,6},{5,7},{6,8},{7,9},{8,10},{9,11},{10,... | collective-permute-start | bytes 393224 | tf_op jit(solution)/shard_map/ppermute | solution.py:544
  79.9 7.3 %collective-permute-start.13 = (bf16[32,2048]{1,0:T(8,128)(2,1)S(1)}, bf16[32,2048]{1,0:T(8,128)(2,1)S(1)}, u32[]{:S(2)}, u32[]{:S(2)}) collective-permute-start(bf16[32,2048]{1,0:T(8,128)(2,1)S(1)} %collective-permute-done.11.refs_1_), channel_id=1, source_target_pairs={{0,14},{1,15},{2,0},{3,1},{4,2},{5,3},{6,4},{7,5},{8,6},{9,7},{10,... | collective-permute-start | bytes 393224 | tf_op jit(solution)/shard_map/ppermute | solution.py:544
  82.9 9.1 %collective-permute-start.18 = (bf16[32,2048]{1,0:T(8,128)(2,1)S(1)}, bf16[32,2048]{1,0:T(8,128)(2,1)S(1)}, u32[]{:S(2)}, u32[]{:S(2)}) collective-permute-start(bf16[32,2048]{1,0:T(8,128)(2,1)S(1)} %collective-permute-done.14.refs_4_), channel_id=1, source_target_pairs={{0,2},{1,3},{2,4},{3,5},{4,6},{5,7},{6,8},{7,9},{8,10},{9,11},{10,... | collective-permute-start | bytes 393224 | tf_op jit(solution)/shard_map/ppermute | solution.py:544
  82.9 10.6 %collective-permute-start.16 = (bf16[32,2048]{1,0:T(8,128)(2,1)S(1)}, bf16[32,2048]{1,0:T(8,128)(2,1)S(1)}, u32[]{:S(2)}, u32[]{:S(2)}) collective-permute-start(bf16[32,2048]{1,0:T(8,128)(2,1)S(1)} %collective-permute-done.12.refs_2_), channel_id=1, source_target_pairs={{0,14},{1,15},{2,0},{3,1},{4,2},{5,3},{6,4},{7,5},{8,6},{9,7},{10,... | collective-permute-start | bytes 393224 | tf_op jit(solution)/shard_map/ppermute | solution.py:544
  87.2 8.0 %collective-permute-start.19 = (bf16[32,2048]{1,0:T(8,128)(2,1)S(1)}, bf16[32,2048]{1,0:T(8,128)(2,1)S(1)}, u32[]{:S(2)}, u32[]{:S(2)}) collective-permute-start(bf16[32,2048]{1,0:T(8,128)(2,1)S(1)} %collective-permute-done.15.refs_5_), channel_id=1, source_target_pairs={{0,2},{1,3},{2,4},{3,5},{4,6},{5,7},{6,8},{7,9},{8,10},{9,11},{10,... | collective-permute-start | bytes 393224 | tf_op jit(solution)/shard_map/ppermute | solution.py:544
  87.2 10.0 %collective-permute-start.17 = (bf16[32,2048]{1,0:T(8,128)(2,1)S(1)}, bf16[32,2048]{1,0:T(8,128)(2,1)S(1)}, u32[]{:S(2)}, u32[]{:S(2)}) collective-permute-start(bf16[32,2048]{1,0:T(8,128)(2,1)S(1)} %collective-permute-done.13.refs_3_), channel_id=1, source_target_pairs={{0,14},{1,15},{2,0},{3,1},{4,2},{5,3},{6,4},{7,5},{8,6},{9,7},{10,... | collective-permute-start | bytes 393224 | tf_op jit(solution)/shard_map/ppermute | solution.py:544
  91.9 7.2 %collective-permute-start.24 = (bf16[32,2048]{1,0:T(8,128)(2,1)S(1)}, bf16[32,2048]{1,0:T(8,128)(2,1)S(1)}, u32[]{:S(2)}, u32[]{:S(2)}) collective-permute-start(bf16[32,2048]{1,0:T(8,128)(2,1)S(1)} %collective-permute-done.18.refs_8_), channel_id=1, source_target_pairs={{0,4},{1,5},{2,6},{3,7},{4,8},{5,9},{6,10},{7,11},{8,12},{9,13},{1... | collective-permute-start | bytes 393224 | tf_op jit(solution)/shard_map/ppermute | solution.py:544
  91.9 8.2 %collective-permute-start.22 = (bf16[32,2048]{1,0:T(8,128)(2,1)S(1)}, bf16[32,2048]{1,0:T(8,128)(2,1)S(1)}, u32[]{:S(2)}, u32[]{:S(2)}) collective-permute-start(bf16[32,2048]{1,0:T(8,128)(2,1)S(1)} %collective-permute-done.18.refs_8_), channel_id=1, source_target_pairs={{0,2},{1,3},{2,4},{3,5},{4,6},{5,7},{6,8},{7,9},{8,10},{9,11},{10,... | collective-permute-start | bytes 393224 | tf_op jit(solution)/shard_map/ppermute | solution.py:544
  93.5 6.7 %collective-permute-start.20 = (bf16[32,2048]{1,0:T(8,128)(2,1)S(1)}, bf16[32,2048]{1,0:T(8,128)(2,1)S(1)}, u32[]{:S(2)}, u32[]{:S(2)}) collective-permute-start(bf16[32,2048]{1,0:T(8,128)(2,1)S(1)} %collective-permute-done.16.refs_6_), channel_id=1, source_target_pairs={{0,14},{1,15},{2,0},{3,1},{4,2},{5,3},{6,4},{7,5},{8,6},{9,7},{10,... | collective-permute-start | bytes 393224 | tf_op jit(solution)/shard_map/ppermute | solution.py:544
  95.2 6.2 %collective-permute-start.23 = (bf16[32,2048]{1,0:T(8,128)(2,1)S(1)}, bf16[32,2048]{1,0:T(8,128)(2,1)S(1)}, u32[]{:S(2)}, u32[]{:S(2)}) collective-permute-start(bf16[32,2048]{1,0:T(8,128)(2,1)S(1)} %collective-permute-done.19.refs_9_), channel_id=1, source_target_pairs={{0,2},{1,3},{2,4},{3,5},{4,6},{5,7},{6,8},{7,9},{8,10},{9,11},{10,... | collective-permute-start | bytes 393224 | tf_op jit(solution)/shard_map/ppermute | solution.py:544
  97.3 6.0 %collective-permute-start.25 = (bf16[32,2048]{1,0:T(8,128)(2,1)S(1)}, bf16[32,2048]{1,0:T(8,128)(2,1)S(1)}, u32[]{:S(2)}, u32[]{:S(2)}) collective-permute-start(bf16[32,2048]{1,0:T(8,128)(2,1)S(1)} %collective-permute-done.17.refs_7_), channel_id=1, source_target_pairs={{0,12},{1,13},{2,14},{3,15},{4,0},{5,1},{6,2},{7,3},{8,4},{9,5},{1... | collective-permute-start | bytes 393224 | tf_op jit(solution)/shard_map/ppermute | solution.py:544
  99.1 6.8 %collective-permute-start.21 = (bf16[32,2048]{1,0:T(8,128)(2,1)S(1)}, bf16[32,2048]{1,0:T(8,128)(2,1)S(1)}, u32[]{:S(2)}, u32[]{:S(2)}) collective-permute-start(bf16[32,2048]{1,0:T(8,128)(2,1)S(1)} %collective-permute-done.17.refs_7_), channel_id=1, source_target_pairs={{0,14},{1,15},{2,0},{3,1},{4,2},{5,3},{6,4},{7,5},{8,6},{9,7},{10,... | collective-permute-start | bytes 393224 | tf_op jit(solution)/shard_map/ppermute | solution.py:544
